TPU v7x, 512 devices: a whole 4x8x8 slice. The times are simulated.
512 devices in a mesh: group: 64 (over x, y_lo, z), tensor: 8 (over y_hi, core).
Axes of the slice: x: 4, y: 8 (y_hi: 4, y_lo: 2; y = y_hi * 2 + y_lo), z: 8, core: 2. Of those that a mesh axis runs over, the one named last changes fastest.
Arguments:
- inputs: bfloat16 [4, 128, 8192], P(None, None, 'group'), may hold values from -160 to 160
- gain: float32 [8192], P('group'), may hold values from 0.1 to 1.9
- w_query: bfloat16 [8192, 8192], P('group', 'tensor'), may hold values from -0.0625 to 0.0625
- key_projection_weight: bfloat16 [8192, 1024], P('group', 'tensor'), may hold values from -0.0625 to 0.0625
- value_projection_weight: bfloat16 [8192, 1024], P('group', 'tensor'), may hold values from -0.0625 to 0.0625
- w_output: bfloat16 [8192, 8192], P('tensor', 'group'), may hold values from -0.0625 to 0.0625
- adapter_in: bfloat16 [8, 8192, 192], P(None, 'group'), may hold values from -0.0625 to 0.0625
- adapter_attn: bfloat16 [8, 8192, 64], P(None, 'tensor'), may hold values from -0.0625 to 0.0625
- adapter_out: bfloat16 [8, 64, 8192], P(None, None, 'group'), may hold values from -0.75 to 0.75
- pool_query: bfloat16 [64, 64, 8192], P('group', None, 'tensor'), may hold values from -0.75 to 0.75
- slot_keyvalue_matrices: bfloat16 [64, 64, 2, 1024], P('group', None, None, 'tensor'), may hold values from -0.75 to 0.75
- cache_keys: bfloat16 [128, 8, 1024, 128], P('group', 'tensor'), may hold values from -600 to 600
- value_cache: bfloat16 [128, 8, 1024, 128], P('group', 'tensor'), may hold values from -6 to 6
- tasks: int32 [128], replicated, may hold values from 0 to 7
- homes: int32 [8], replicated, may hold values from 0 to 63, as said below
- moves: int32 [16, 2], replicated, may hold values from 0 to 63, as said below
- lengths: int32 [128], P('group'), may hold values from 1 to 1024
Outputs:
- outputs: bfloat16 [4, 128, 8192], P(None, None, 'group')
Inputs may be any that keep to these rules, and one draw needn't show every extreme that they name: `homes`: 8 different groups, one a home for each adapter. `moves`: column 0 an adapter (0 to 7), column 1 a destination group; no group is named twice.
All inputs are finite; a program needn't handle non-finite values.
Results may differ from a plain program's by a relative error of at most 0.0071.
Values may be sent and summed in bfloat16 or wider, within the bound.
No kernel may reach another device: no remote copies, remote signals or barrier semaphores. Data moves between devices by JAX's collectives and lax.ppermute only.
A program may use at most 64 MiB of HBM per device.

v0:
```python
import math

import jax
import jax.numpy as jnp
from jax import lax
from jax.sharding import PartitionSpec as P

epsilon = 1e-05


def apply_rotary(vectors, token_positions):
    half_width = vectors.shape[-1] // 2
    frequency = jnp.exp(
        -jnp.log(500000.0) * jnp.arange(half_width, dtype=jnp.float32) * (2.0 / vectors.shape[-1])
    )
    angles = token_positions.astype(jnp.float32)[:, None] * frequency[None, :]
    cosine = jnp.cos(angles)[:, None, :]
    sine_part = jnp.sin(angles)[:, None, :]
    leading = vectors[..., :half_width]
    trailing = vectors[..., half_width:]
    return jnp.concatenate(
        [leading * cosine - trailing * sine_part, leading * sine_part + trailing * cosine], axis=-1
    )


def pick_tasks(tasks, moves, decode_step, per_group, step_total):
    if decode_step < step_total // 2:
        return tasks
    owners = jnp.arange(tasks.shape[0], dtype=jnp.int32) // per_group
    matched = moves[:, 1][None, :] == owners[:, None]
    moved = jnp.any(matched, axis=1)
    chosen = jnp.sum(jnp.where(matched, moves[:, 0][None, :], 0), axis=1)
    return jnp.where(moved, chosen, tasks)


def expand(marks, rows):
    return (marks[:, :, None] * rows[:, None, :]).reshape(
        rows.shape[0], marks.shape[1] * rows.shape[1]
    )


def attend(
    grouped_queries, cache_keys, value_cache, fresh_keys, fresh_values, lengths, decode_step
):
    scaling = 1.0 / math.sqrt(grouped_queries.shape[-1])
    old_scores = (
        jnp.einsum(
            "rkgd,rkjd->rkgj", grouped_queries, cache_keys, preferred_element_type=jnp.float32
        )
        * scaling
    )
    new_scores = (
        jnp.einsum(
            "rkgd,rkjd->rkgj", grouped_queries, fresh_keys, preferred_element_type=jnp.float32
        )
        * scaling
    )
    visible = jnp.arange(cache_keys.shape[2])[None, None, None, :] < lengths[:, None, None, None]
    old_scores = jnp.where(visible, old_scores, -1e30)
    new_scores = jnp.where(
        jnp.arange(fresh_keys.shape[2])[None, None, None, :] <= decode_step, new_scores, -1e30
    )
    highest = jnp.maximum(jnp.max(old_scores, axis=-1), jnp.max(new_scores, axis=-1))[..., None]
    old_exp = jnp.exp(old_scores - highest)
    new_exp = jnp.exp(new_scores - highest)
    denominator = jnp.sum(old_exp, axis=-1, keepdims=True) + jnp.sum(
        new_exp, axis=-1, keepdims=True
    )
    old_weights = (old_exp / denominator).astype(jnp.bfloat16)
    new_weights = (new_exp / denominator).astype(jnp.bfloat16)
    mixed = jnp.einsum(
        "rkgj,rkjd->rkgd", old_weights, value_cache, preferred_element_type=jnp.float32
    )
    mixed = mixed + jnp.einsum(
        "rkgj,rkjd->rkgd", new_weights, fresh_values, preferred_element_type=jnp.float32
    )
    return mixed.astype(jnp.bfloat16).reshape(grouped_queries.shape[0], -1)


def on_device(
    inputs,
    gain,
    w_query,
    key_projection_weight,
    value_projection_weight,
    w_output,
    adapter_in,
    adapter_attn,
    adapter_out,
    pool_query,
    slot_keyvalue_matrices,
    cache_keys,
    value_cache,
    tasks,
    homes,
    moves,
    lengths,
):
    steps_count, all_rows, width_part = inputs.shape
    own_rows = lengths.shape[0]
    task_count = homes.shape[0]
    rank_width = adapter_out.shape[1]
    head_dim = cache_keys.shape[3]
    kv_heads = cache_keys.shape[1]
    query_width = w_query.shape[1]
    key_total_width = key_projection_weight.shape[1]
    query_heads = query_width // head_dim
    first_row = lax.axis_index("group") * own_rows
    model_width = width_part * lax.axis_size("group")
    every_query, every_keyval = (
        lax.all_gather(pool_query, "group", axis=0, tiled=True),
        lax.all_gather(slot_keyvalue_matrices, "group", axis=0, tiled=True),
    )
    b_query = jnp.take(every_query, homes, axis=0)
    b_keyval = jnp.take(every_keyval, homes, axis=0)
    query_flat = b_query.reshape(task_count * rank_width, query_width)
    key_flat = b_keyval[:, :, 0, :].reshape(task_count * rank_width, key_total_width)
    value_flat = b_keyval[:, :, 1, :].reshape(task_count * rank_width, key_total_width)
    in_flat = adapter_in.reshape(task_count * width_part, 3 * rank_width)
    attn_flat = adapter_attn.reshape(task_count * query_width, rank_width)
    out_flat = adapter_out.reshape(task_count * rank_width, width_part)
    labels = jnp.arange(task_count, dtype=jnp.int32)
    appended_keys = jnp.zeros((own_rows, kv_heads, steps_count, head_dim), jnp.bfloat16)
    appended_values = jnp.zeros((own_rows, kv_heads, steps_count, head_dim), jnp.bfloat16)
    base_end = query_width + 2 * key_total_width
    results = []
    for decode_step in range(steps_count):
        active = pick_tasks(tasks, moves, decode_step, own_rows, steps_count)
        marks = (active[:, None] == labels[None, :]).astype(jnp.bfloat16)
        residual = inputs[decode_step]
        states = residual.astype(jnp.float32)
        squares = jnp.sum(states * states, axis=1)
        gained = (states * gain[None, :]).astype(jnp.bfloat16)
        total_squares = lax.psum(squares, "group")
        own_squares = lax.dynamic_slice_in_dim(total_squares, first_row, own_rows, 0)
        own_terms = lax.psum_scatter(
            jnp.concatenate(
                [
                    jnp.dot(gained, w_query, preferred_element_type=jnp.float32),
                    jnp.dot(gained, key_projection_weight, preferred_element_type=jnp.float32),
                    jnp.dot(gained, value_projection_weight, preferred_element_type=jnp.float32),
                    jnp.dot(expand(marks, gained), in_flat, preferred_element_type=jnp.float32),
                ],
                axis=1,
            ),
            "group",
            scatter_dimension=0,
            tiled=True,
        )
        inverse = lax.rsqrt(own_squares / model_width + epsilon)
        lowrank = (inverse[:, None] * own_terms[:, base_end:]).astype(jnp.bfloat16)
        marks_own = lax.dynamic_slice_in_dim(marks, first_row, own_rows, 0)
        raw_query = inverse[:, None] * own_terms[:, :query_width] + jnp.dot(
            expand(marks_own, lowrank[:, :rank_width]),
            query_flat,
            preferred_element_type=jnp.float32,
        )
        unrotated_key = inverse[:, None] * own_terms[
            :, query_width : query_width + key_total_width
        ] + jnp.dot(
            expand(marks_own, lowrank[:, rank_width : 2 * rank_width]),
            key_flat,
            preferred_element_type=jnp.float32,
        )
        projected_value = inverse[:, None] * own_terms[
            :, query_width + key_total_width : base_end
        ] + jnp.dot(
            expand(marks_own, lowrank[:, 2 * rank_width :]),
            value_flat,
            preferred_element_type=jnp.float32,
        )
        token_positions = lengths + decode_step
        query_vectors = apply_rotary(
            raw_query.reshape(own_rows, query_heads, head_dim), token_positions
        ).astype(jnp.bfloat16)
        current_keys = apply_rotary(
            unrotated_key.reshape(own_rows, kv_heads, head_dim), token_positions
        ).astype(jnp.bfloat16)
        current_values = projected_value.reshape(own_rows, kv_heads, head_dim).astype(jnp.bfloat16)
        appended_keys = appended_keys.at[:, :, decode_step, :].set(current_keys)
        appended_values = appended_values.at[:, :, decode_step, :].set(current_values)
        grouped_queries = query_vectors.reshape(
            own_rows, kv_heads, query_heads // kv_heads, head_dim
        )
        attended = attend(
            grouped_queries,
            cache_keys,
            value_cache,
            appended_keys,
            appended_values,
            lengths,
            decode_step,
        )
        piece_rows = lax.all_gather(attended, "group", axis=0, tiled=True)
        mixed = jnp.concatenate(
            [
                jnp.dot(piece_rows, w_output, preferred_element_type=jnp.float32),
                jnp.dot(expand(marks, piece_rows), attn_flat, preferred_element_type=jnp.float32),
            ],
            axis=1,
        )
        totals = lax.psum(mixed.astype(jnp.bfloat16), "tensor").astype(jnp.float32)
        reduced = totals[:, width_part:].astype(jnp.bfloat16)
        adapted = jnp.dot(expand(marks, reduced), out_flat, preferred_element_type=jnp.float32)
        finished = (residual.astype(jnp.float32) + totals[:, :width_part] + adapted).astype(
            jnp.bfloat16
        )
        results.append(finished)
    return jnp.stack(results, axis=0)


def solution(mesh):
    return jax.shard_map(
        on_device,
        mesh=mesh,
        in_specs=(
            P(None, None, "group"),
            P("group"),
            P("group", "tensor"),
            P("group", "tensor"),
            P("group", "tensor"),
            P("tensor", "group"),
            P(None, "group", None),
            P(None, "tensor", None),
            P(None, None, "group"),
            P("group", None, "tensor"),
            P("group", None, None, "tensor"),
            P("group", "tensor", None, None),
            P("group", "tensor", None, None),
            P(),
            P(),
            P(),
            P("group"),
        ),
        out_specs=P(None, None, "group"),
        check_vma=False,
    )
```

profile of v0, /device:TPU:1, one launch (start us, length us, event | category | flops | bytes accessed | tf_op | source)
XLA Modules:
  0.0 2032.8 jit_solution(4280882517574282367)
XLA Ops:
  25.9 1.3 dynamic-slice.66
  27.9 140.1 %all-reduce.6 = (f32[128]{0:T(128)S(1)}, f32[128]{0:T(128)S(1)}, f32[128]{0:T(128)S(1)}, f32[128]{0:T(128)S(1)}) all-reduce(f32[128]{0:T(128)S(1)} %get-tuple-element.210, f32[128]{0:T(128)S(1)} %get-tuple-element.123, f32[128]{0:T(128)S(1)} %get-tuple-element.208, ...), channel_id=1, replica_groups=mesh['group'=64,'tensor'=8] {'group'}, use_global_device_ids=true, to_apply=%region_27.28 | all-reduce | flops 512 | bytes 4096 | tf_op jit(solution)/shard_map/psum | solution.py:134
  170.2 434.5 %all-reduce.12.cloned.1.call-done = (f32[128,1472]{1,0:T(8,128)}, f32[128,1472]{1,0:T(8,128)}, f32[128,1472]{1,0:T(8,128)}, f32[128,1472]{1,0:T(8,128)}) async-done(((f32[128,1472]{1,0:T(8,128)}, f32[128,1472]{1,0:T(8,128)}, f32[128,1472]{1,0:T(8,128)}, f32[128,1472]{1,0:T(8,128)}), (f32[128,1472]{1,0:T(8,128)}, f32[128,1472]{1,0:T(8,128)}, f32[128,1472]{1,0:T(8,128)}, ...) | async-done | bytes 3014672
  610.0 298.5 %all-gather.9.cloned.1.call-done = bf16[64,64,2,128]{3,1,2,0:T(8,128)(2,1)} async-done(((bf16[1,64,2,128]{3,1,2,0:T(8,128)(2,1)}), bf16[64,64,2,128]{3,1,2,0:T(8,128)(2,1)}) %all-gather.9.cloned.1.call-update) | async-done | bytes 2097168 | tf_op jit(solution)/shard_map/all_gather | solution.py:112
  908.5 2.2 gather_fusion.1
  916.9 311.8 %all-gather.7.cloned.1.call-done = bf16[64,64,1024]{2,1,0:T(8,128)(2,1)} async-done(((bf16[1,64,1024]{2,1,0:T(8,128)(2,1)}), bf16[64,64,1024]{2,1,0:T(8,128)(2,1)}) %all-gather.7.cloned.1.call-update) | async-done | bytes 8388624 | tf_op jit(solution)/shard_map/all_gather | solution.py:111
  1228.7 4.0 gather_fusion
  1232.7 1.2 fusion.55
  1233.9 1.1 fusion.53
  1238.7 137.2 %all-gather = bf16[64,2,1024]{2,1,0:T(2,128)(2,1)} all-gather(bf16[1,2,1024]{2,1,0:T(2,128)(2,1)S(1)} %reshape.1531), channel_id=1, replica_groups=mesh['group'=64,'tensor'=8] {'group'}, dimensions={0}, use_global_device_ids=true | all-gather | bytes 266240 | tf_op jit(solution)/shard_map/all_gather | solution.py:194
  1375.9 1.8 reshape.1532
  1377.7 2.5 fusion.45
  1380.5 133.8 %all-gather.1 = bf16[64,2,1024]{2,1,0:T(2,128)(2,1)} all-gather(bf16[1,2,1024]{2,1,0:T(2,128)(2,1)S(1)} %reshape.1533), channel_id=1, replica_groups=mesh['group'=64,'tensor'=8] {'group'}, dimensions={0}, use_global_device_ids=true | all-gather | bytes 266240 | tf_op jit(solution)/shard_map/all_gather | solution.py:194
  1514.3 1.8 reshape.1534
  1516.0 2.5 fusion.42
  1518.9 1.1 fusion.51
  1520.0 1.3 scatter.34
  1524.3 134.9 %all-gather.2 = bf16[64,2,1024]{2,1,0:T(2,128)(2,1)} all-gather(bf16[1,2,1024]{2,1,0:T(2,128)(2,1)S(1)} %reshape.1535), channel_id=1, replica_groups=mesh['group'=64,'tensor'=8] {'group'}, dimensions={0}, use_global_device_ids=true | all-gather | bytes 266240 | tf_op jit(solution)/shard_map/all_gather | solution.py:194
  1659.2 1.8 reshape.1536
  1661.0 2.5 fusion.39
  1664.9 1.3 scatter.36
  1668.6 1.7 fusion.73
  1671.2 124.7 %all-gather.3 = bf16[64,2,1024]{2,1,0:T(2,128)(2,1)S(1)} all-gather(bf16[1,2,1024]{2,1,0:T(2,128)(2,1)S(1)} %reshape.1537), channel_id=1, replica_groups=mesh['group'=64,'tensor'=8] {'group'}, dimensions={0}, use_global_device_ids=true | all-gather | bytes 266240 | tf_op jit(solution)/shard_map/all_gather | solution.py:194
  1799.8 218.9 %all-reduce.14.cloned.1.call-done = (bf16[128,192]{0,1:T(8,128)(2,1)}, bf16[128,192]{0,1:T(8,128)(2,1)}, bf16[128,192]{0,1:T(8,128)(2,1)}, bf16[128,192]{0,1:T(8,128)(2,1)}) async-done(((bf16[128,192]{0,1:T(8,128)(2,1)}, bf16[128,192]{0,1:T(8,128)(2,1)}, bf16[128,192]{0,1:T(8,128)(2,1)}, bf16[128,192]{0,1:T(8,128)(2,1)}), (bf16[128,192]{0,1:T(8,128)(2,1)}, bf16[128,192]{0,1:T(8,128)(2,1)}, ...) | async-done | bytes 196624 | tf_op jit(solution)/shard_map/psum | solution.py:202
  (242 shorter events, 56.2 us)
Async XLA Ops:
  6.5 1371.1 %copy-start = (bf16[8,1024,64]{1,2,0:T(8,128)(2,1)S(1)}, bf16[8,1024,64]{1,2,0:T(8,128)(2,1)}, u32[]{:S(2)}) copy-start(bf16[8,1024,64]{1,2,0:T(8,128)(2,1)} %param.40) | copy-start | bytes 3145732
  6.5 598.2 %all-reduce.12.cloned.1.call-start = ((), (), s32[]{:S(2)}) async-start(), calls=%async_computation.2 | async-start | bytes 6291456
  24.1 145.2 %copy-start.35 = (s32[8]{0:T(128)S(1)}, s32[8]{0:T(128)}, u32[]{:S(2)}) copy-start(s32[8]{0:T(128)} %param.47) | copy-start | bytes 100
  24.1 145.3 %copy-start.20 = (s32[2]{0:T(128)S(1)}, s32[2]{0:T(128)}, u32[]{:S(2)}) copy-start(s32[2]{0:T(128)} %param.49) | copy-start | bytes 28
  24.1 884.4 %all-gather.9.cloned.1.call-start = ((), (), s32[]{:S(2)}) async-start(), calls=%async_computation.1 | async-start | bytes 2129920 | tf_op jit(solution)/shard_map/all_gather | solution.py:112
  24.9 1203.8 %all-gather.7.cloned.1.call-start = ((), (), s32[]{:S(2)}) async-start(), calls=%async_computation | async-start | bytes 8519680 | tf_op jit(solution)/shard_map/all_gather | solution.py:111
  25.6 1993.1 %all-reduce.14.cloned.1.call-start = ((), (), s32[]{:S(2)}) async-start(), calls=%async_computation.3 | async-start | bytes 393216 | tf_op jit(solution)/shard_map/psum | solution.py:202
  169.1 1063.6 %copy-start.29 = (f32[2]{0:T(128)}, f32[2]{0:T(128)S(1)}, u32[]{:S(2)}) copy-start(f32[2]{0:T(128)S(1)} %add_rsqrt_fusion) | copy-start | bytes 28
  169.2 1064.7 %copy-start.31 = (f32[2]{0:T(128)}, f32[2]{0:T(128)S(1)}, u32[]{:S(2)}) copy-start(f32[2]{0:T(128)S(1)} %add_rsqrt_fusion.2) | copy-start | bytes 28
  169.3 1063.3 %copy-start.30 = (f32[2]{0:T(128)}, f32[2]{0:T(128)S(1)}, u32[]{:S(2)}) copy-start(f32[2]{0:T(128)S(1)} %add_rsqrt_fusion.1) | copy-start | bytes 28
  169.4 1064.5 %copy-start.27 = (pred[8]{0:T(512)(128)(4,1)}, pred[8]{0:T(512)(128)(4,1)S(1)}, u32[]{:S(2)}) copy-start(pred[8]{0:T(512)(128)(4,1)S(1)} %compare_and_fusion) | copy-start | bytes 28
  910.8 321.9 %copy-start.14 = (bf16[8,64,1,128]{3,1,2,0:T(8,128)(2,1)}, bf16[8,64,1,128]{3,1,2,0:T(8,128)(2,1)S(1)}, u32[]{:S(2)}) copy-start(bf16[8,64,1,128]{3,1,2,0:T(8,128)(2,1)S(1)} %get-tuple-element.113) | copy-start | bytes 393220
  916.0 320.1 %copy-start.24 = (bf16[2,4,128]{2,1,0:T(4,128)(2,1)}, bf16[2,4,128]{2,1,0:T(4,128)(2,1)S(1)}, u32[]{:S(2)}) copy-start(bf16[2,4,128]{2,1,0:T(4,128)(2,1)S(1)} %scatter.30) | copy-start | bytes 6148
  1237.0 143.2 %copy-start.4 = (bf16[1024,128]{1,0:T(8,128)(2,1)S(1)}, bf16[1024,128]{1,0:T(8,128)(2,1)}, u32[]{:S(2)}) copy-start(bf16[1024,128]{1,0:T(8,128)(2,1)} %param.38) | copy-start | bytes 786436
  1238.5 275.8 %copy-start.21 = (bf16[2,4,128]{2,0,1:T(2,128)(2,1)}, bf16[2,4,128]{2,0,1:T(2,128)(2,1)S(1)}, u32[]{:S(2)}) copy-start(bf16[2,4,128]{2,0,1:T(2,128)(2,1)S(1)} %fusion.77) | copy-start | bytes 6148
  1380.5 138.4 %copy-start.28 = (pred[8]{0:T(512)(128)(4,1)S(1)}, pred[8]{0:T(512)(128)(4,1)}, u32[]{:S(2)}) copy-start(pred[8]{0:T(512)(128)(4,1)} %copy-done.27) | copy-start | bytes 28
  1524.1 136.8 %copy-start.23 = (bf16[2,4,128]{2,0,1:T(2,128)(2,1)}, bf16[2,4,128]{2,0,1:T(2,128)(2,1)S(1)}, u32[]{:S(2)}) copy-start(bf16[2,4,128]{2,0,1:T(2,128)(2,1)S(1)} %fusion.75) | copy-start | bytes 6148
  1668.6 128.6 %copy-start.16 = (bf16[128,64]{0,1:T(8,128)(2,1)S(1)}, bf16[128,64]{0,1:T(8,128)(2,1)}, u32[]{:S(2)}) copy-start(bf16[128,64]{0,1:T(8,128)(2,1)} %fusion.45) | copy-start | bytes 49156
  1670.3 127.6 %copy-start.17 = (bf16[128,64]{0,1:T(8,128)(2,1)S(1)}, bf16[128,64]{0,1:T(8,128)(2,1)}, u32[]{:S(2)}) copy-start(bf16[128,64]{0,1:T(8,128)(2,1)} %fusion.42) | copy-start | bytes 49156
  1671.2 127.3 %copy-start.18 = (bf16[128,64]{0,1:T(8,128)(2,1)S(1)}, bf16[128,64]{0,1:T(8,128)(2,1)}, u32[]{:S(2)}) copy-start(bf16[128,64]{0,1:T(8,128)(2,1)} %fusion.39) | copy-start | bytes 49156
  1795.9 224.2 %copy-start.9 = (bf16[1,128,128]{1,2,0:T(8,128)(2,1)S(1)}, bf16[1,128,128]{1,2,0:T(8,128)(2,1)}, u32[]{:S(2)}) copy-start(bf16[1,128,128]{1,2,0:T(8,128)(2,1)} %copy-done.8) | copy-start | bytes 98308
  1795.9 224.2 %copy-start.34 = (bf16[8,64,128]{2,1,0:T(8,128)(2,1)S(1)}, bf16[8,64,128]{2,1,0:T(8,128)(2,1)}, u32[]{:S(2)}) copy-start(bf16[8,64,128]{2,1,0:T(8,128)(2,1)} %param.41) | copy-start | bytes 393220
  1796.0 226.8 %copy-start.13 = (bf16[1,128,128]{1,2,0:T(8,128)(2,1)S(1)}, bf16[1,128,128]{1,2,0:T(8,128)(2,1)}, u32[]{:S(2)}) copy-start(bf16[1,128,128]{1,2,0:T(8,128)(2,1)} %copy-done.12) | copy-start | bytes 98308
  1796.0 228.5 %copy-start.11 = (bf16[1,128,128]{1,2,0:T(8,128)(2,1)S(1)}, bf16[1,128,128]{1,2,0:T(8,128)(2,1)}, u32[]{:S(2)}) copy-start(bf16[1,128,128]{1,2,0:T(8,128)(2,1)} %copy-done.10) | copy-start | bytes 98308
  (16 other events, 63.2 us)
Sparse Core Ops, SparseCore 0:
  24.2 580.4 all-reduce.11
  607.0 301.4 all-gather.8
  910.8 317.8 all-gather.6
  1799.9 218.7 all-reduce.13
where the time goes:
time: 2040 us; the launch traced here: 2030 us
  waiting for transfers between devices  1260 us (62%)
  blocking collectives  671 us (33%)
  matrix products  41.9 us (2%)
  local copies, waits for them, and re-layouts  25.3 us (1%)
    all_gather x4, blocking collectives, on_device(): piece_rows = lax.all_gather(attended, 'group', axis=0, tiled=True)  531 us
    unnamed x5, waiting for transfers between devices  435 us
    all_gather x1, waiting for transfers between devices, on_device(): lax.all_gather(pool_query, 'group', axis=0, tiled=True)  312 us
    all_gather x1, waiting for transfers between devices, on_device(): lax.all_gather(slot_keyvalue_matrices, 'group', axis=0, tiled=True)  298 us
    psum x1, waiting for transfers between devices, on_device(): totals = lax.psum(mixed.astype(jnp.bfloat16), 'tensor').astype(jnp.float32)  219 us
    psum x1, blocking collectives, on_device(): total_squares = lax.psum(squares, 'group')  140 us
  transfers between devices with their start and end apart: 4, of which 4 were waited for; matrix products, arithmetic and copies ran while one was open for 1% of the time, Pallas kernels for 0%

commit v1 on v0

v1 whole, which is shorter than its diff:
```python
import math

import jax
import jax.numpy as jnp
from jax import lax
from jax.sharding import Mesh
from jax.sharding import PartitionSpec as P

epsilon = 1e-05
GROUP = ("x", "y_lo", "z")
PLANE = ("x", "y_lo")
TENSOR = ("y_hi", "core")
PADDED_WIDTH = 256


def exchange(blocks, axes):
    return lax.all_to_all(blocks, axes, 0, 0, tiled=True)


def apply_rotary(vectors, token_positions):
    half_width = vectors.shape[-1] // 2
    frequency = jnp.exp(
        -jnp.log(500000.0) * jnp.arange(half_width, dtype=jnp.float32) * (2.0 / vectors.shape[-1])
    )
    angles = token_positions.astype(jnp.float32)[:, None] * frequency[None, :]
    cosine = jnp.cos(angles)[:, None, :]
    sine_part = jnp.sin(angles)[:, None, :]
    leading = vectors[..., :half_width]
    trailing = vectors[..., half_width:]
    return jnp.concatenate(
        [leading * cosine - trailing * sine_part, leading * sine_part + trailing * cosine], axis=-1
    )


def dot(left, right):
    return jnp.dot(left, right, preferred_element_type=jnp.float32)


def attend(queries, cache_keys, value_cache, fresh_keys, fresh_values, lengths, query_steps):
    scaling = 1.0 / math.sqrt(queries.shape[-1])
    old_scores = (
        jnp.einsum("rnd,rjd->rnj", queries, cache_keys, preferred_element_type=jnp.float32)
        * scaling
    )
    new_scores = (
        jnp.einsum("rnd,rjd->rnj", queries, fresh_keys, preferred_element_type=jnp.float32)
        * scaling
    )
    visible = jnp.arange(cache_keys.shape[1])[None, None, :] < lengths[:, None, None]
    old_scores = jnp.where(visible, old_scores, -1e30)
    fresh = jnp.arange(fresh_keys.shape[1])[None, None, :] <= query_steps[None, :, None]
    new_scores = jnp.where(fresh, new_scores, -1e30)
    highest = jnp.maximum(jnp.max(old_scores, axis=-1), jnp.max(new_scores, axis=-1))[..., None]
    old_exp = jnp.exp(old_scores - highest)
    new_exp = jnp.exp(new_scores - highest)
    denominator = jnp.sum(old_exp, axis=-1, keepdims=True) + jnp.sum(
        new_exp, axis=-1, keepdims=True
    )
    old_weights = (old_exp / denominator).astype(jnp.bfloat16)
    new_weights = (new_exp / denominator).astype(jnp.bfloat16)
    mixed = jnp.einsum(
        "rnj,rjd->rnd", old_weights, value_cache, preferred_element_type=jnp.float32
    )
    mixed = mixed + jnp.einsum(
        "rnj,rjd->rnd", new_weights, fresh_values, preferred_element_type=jnp.float32
    )
    return mixed.astype(jnp.bfloat16)


def on_device(
    inputs,
    gain,
    w_query,
    key_projection_weight,
    value_projection_weight,
    w_output,
    adapter_in,
    adapter_attn,
    adapter_out,
    pool_query,
    slot_keyvalue_matrices,
    cache_keys,
    value_cache,
    tasks,
    homes,
    moves,
    lengths,
):
    steps, all_rows, width_part = inputs.shape
    own_rows = lengths.shape[0]
    groups = all_rows // own_rows
    planes = lax.axis_size(PLANE)
    depth = lax.axis_size("z")
    task_count = homes.shape[0]
    rank = adapter_out.shape[1]
    head_dim = cache_keys.shape[3]
    query_width = w_query.shape[1]
    heads = query_width // head_dim
    key_end = query_width + head_dim
    base_end = key_end + head_dim
    per_group = steps * own_rows
    every_row = groups * per_group
    model_width = width_part * groups
    me = lax.axis_index(GROUP)

    group_tasks = tasks.reshape(groups, own_rows)
    matched = moves[:, 1][None, :] == jnp.arange(groups, dtype=jnp.int32)[:, None]
    moved = jnp.any(matched, axis=1)
    chosen = jnp.sum(jnp.where(matched, moves[:, 0][None, :], 0), axis=1)
    needed = jnp.concatenate([group_tasks, chosen[:, None]], axis=1)
    slots = own_rows + 1
    late = jnp.where(moved[:, None], chosen[:, None], group_tasks)
    active = jnp.stack([group_tasks if s < steps // 2 else late for s in range(steps)], axis=1)
    active = active.reshape(every_row)
    marks = active[:, None] == jnp.arange(task_count, dtype=jnp.int32)[None, :]

    up = jnp.concatenate(
        [
            pool_query.reshape(rank, query_width),
            slot_keyvalue_matrices.reshape(rank, 2 * head_dim),
        ],
        axis=1,
    )
    with jax.named_scope("up_rows"):
        up_rows = exchange(up, GROUP)
    sources = jnp.sum(
        jnp.where(
            needed.reshape(-1)[:, None] == jnp.arange(task_count, dtype=jnp.int32)[None, :],
            homes[None, :],
            0,
        ),
        axis=1,
    )
    pick = (sources[:, None] == jnp.arange(groups, dtype=jnp.int32)[None, :]).astype(jnp.bfloat16)
    chosen_rows = dot(pick, up_rows).astype(jnp.bfloat16)
    with jax.named_scope("up_needed"):
        up_needed = exchange(chosen_rows.reshape(groups, slots * base_end), GROUP)

    residual = (
        inputs.reshape(steps, groups, own_rows, width_part)
        .transpose(1, 0, 2, 3)
        .reshape(every_row, width_part)
    )
    states = residual.astype(jnp.float32)
    gained = (states * gain[None, :]).astype(jnp.bfloat16)
    squares = jnp.sum(states * states, axis=1, keepdims=True)
    squares_high = lax.reduce_precision(squares, 8, 7)
    spread = jnp.where(marks[:, :, None], gained[:, None, :], 0).reshape(
        every_row, task_count * width_part
    )
    partial = jnp.concatenate(
        [
            dot(gained, w_query),
            dot(gained, key_projection_weight),
            dot(gained, value_projection_weight),
            dot(spread, adapter_in.reshape(task_count * width_part, 3 * rank)),
            squares_high,
            squares - squares_high,
            jnp.zeros((every_row, PADDED_WIDTH - 3 * rank - 2), jnp.float32),
        ],
        axis=1,
    ).astype(jnp.bfloat16)
    with jax.named_scope("sum_plane"):
        by_plane = exchange(partial.reshape(planes, depth * per_group, -1), PLANE)
    plane_sum = jnp.sum(by_plane.astype(jnp.float32), axis=0).astype(jnp.bfloat16)
    with jax.named_scope("sum_z"):
        by_depth = exchange(plane_sum.reshape(depth, per_group, -1), "z")
    own = jnp.sum(by_depth.astype(jnp.float32), axis=0)

    low_end = base_end + 3 * rank
    inverse = lax.rsqrt((own[:, low_end] + own[:, low_end + 1]) / model_width + epsilon)[:, None]
    lowrank = (inverse * own[:, base_end:low_end]).astype(jnp.bfloat16)
    own_moved = lax.dynamic_index_in_dim(moved, me, 0, keepdims=False)
    row_step = jnp.arange(per_group) // own_rows
    row_slot = jnp.where(
        jnp.logical_and(row_step >= steps // 2, own_moved),
        own_rows,
        jnp.arange(per_group) % own_rows,
    )[:, None]

    def lift(block, first, last):
        total = jnp.zeros((per_group, last - first), jnp.float32)
        for slot in range(slots):
            matrix = up_needed[:, slot * base_end + first : slot * base_end + last]
            lifted = dot(lowrank[:, block * rank : (block + 1) * rank], matrix)
            total = jnp.where(row_slot == slot, lifted, total)
        return total

    raw_query = inverse * own[:, :query_width] + lift(0, 0, query_width)
    raw_key = inverse * own[:, query_width:key_end] + lift(1, query_width, key_end)
    raw_value = inverse * own[:, key_end:base_end] + lift(2, key_end, base_end)
    positions = jnp.tile(lengths, steps) + row_step
    queries = apply_rotary(raw_query.reshape(per_group, heads, head_dim), positions)
    new_keys = apply_rotary(raw_key.reshape(per_group, 1, head_dim), positions)

    def by_row(array):
        return (
            array.astype(jnp.bfloat16)
            .reshape(steps, own_rows, -1, head_dim)
            .transpose(1, 0, 2, 3)
            .reshape(own_rows, -1, head_dim)
        )

    attended = attend(
        by_row(queries),
        cache_keys.reshape(own_rows, -1, head_dim),
        value_cache.reshape(own_rows, -1, head_dim),
        by_row(new_keys),
        by_row(raw_value),
        lengths,
        jnp.arange(steps * heads) // heads,
    )
    attended = (
        attended.reshape(own_rows, steps, query_width)
        .transpose(1, 0, 2)
        .reshape(per_group, query_width)
    )

    with jax.named_scope("gather_z"):
        line = exchange(
            jnp.broadcast_to(attended[None], (depth, per_group, query_width)), "z"
        ).reshape(depth * per_group, query_width)
    with jax.named_scope("gather_plane"):
        piece_rows = exchange(
            jnp.broadcast_to(line[None], (planes, depth * per_group, query_width)), PLANE
        ).reshape(every_row, query_width)

    every_reduced = jnp.einsum(
        "rq,tqc->rtc", piece_rows, adapter_attn, preferred_element_type=jnp.float32
    )
    reduced = jnp.where(marks[:, :, None], every_reduced, 0).astype(jnp.bfloat16)
    mixed = dot(piece_rows, w_output) + dot(
        reduced.reshape(every_row, task_count * rank),
        adapter_out.reshape(task_count * rank, width_part),
    )
    mixed = mixed.astype(jnp.bfloat16)
    half = every_row // 2
    core = lax.axis_index("core")
    with jax.named_scope("sum_core"):
        pair = lax.all_gather(mixed, "core", axis=0)
    mine = lax.dynamic_slice_in_dim(pair, core * half, half, 1).astype(jnp.float32)
    mine = mine[0] + mine[1]
    for hop in (1, 2):
        with jax.named_scope("sum_y_hi"):
            ways = [(i, i ^ hop) for i in range(lax.axis_size("y_hi"))]
            mine = lax.reduce_precision(mine, 8, 7)
            mine = mine + lax.ppermute(mine.astype(jnp.bfloat16), "y_hi", ways).astype(jnp.float32)
    finished = lax.dynamic_slice_in_dim(states, core * half, half, 0) + mine
    with jax.named_scope("gather_core"):
        finished = lax.all_gather(finished.astype(jnp.bfloat16), "core", axis=0, tiled=True)
    return (
        finished.reshape(groups, steps, own_rows, width_part)
        .transpose(1, 0, 2, 3)
        .reshape(steps, all_rows, width_part)
    )


def solution(mesh):
    parts = Mesh(mesh.devices.reshape(4, 2, 8, 4, 2), GROUP + TENSOR)
    return jax.shard_map(
        on_device,
        mesh=parts,
        in_specs=(
            P(None, None, GROUP),
            P(GROUP),
            P(GROUP, TENSOR),
            P(GROUP, TENSOR),
            P(GROUP, TENSOR),
            P(TENSOR, GROUP),
            P(None, GROUP, None),
            P(None, TENSOR, None),
            P(None, None, GROUP),
            P(GROUP, None, TENSOR),
            P(GROUP, None, None, TENSOR),
            P(GROUP, TENSOR, None, None),
            P(GROUP, TENSOR, None, None),
            P(),
            P(),
            P(),
            P(GROUP),
        ),
        out_specs=P(None, None, GROUP),
        check_vma=False,
    )
```

time: 2040 us -> 155 us (0.08)
  waiting for transfers between devices: 1260 us -> 49.9 us
  blocking collectives: 671 us -> 21 us
  starting transfers between devices: 0.12 us -> 49.8 us
  matrix products: 41.9 us -> 8.06 us
    all_gather x2 -> x0, waiting for transfers between devices: 610 us -> none  [the longest x1 312 us: on_device(): lax.all_gather(pool_query, 'group', axis=0, tiled=True)]
    all_gather x4 -> x2, blocking collectives: 531 us -> 10.7 us  [the longest x1 6.69 us: on_device(): pair = lax.all_gather(mixed, 'core', axis=0)]
    unnamed x5 -> x0, waiting for transfers between devices: 435 us -> none
    psum x1 -> x0, waiting for transfers between devices: 219 us -> none  [on_device(): totals = lax.psum(mixed.astype(jnp.bfloat16), 'tensor').astype(jnp.float32)]
    psum x1 -> x0, blocking collectives: 140 us -> none  [on_device(): total_squares = lax.psum(squares, 'group')]
    all_to_all x0 -> x5, waiting for transfers between devices: none -> 43.7 us  [exchange(): return lax.all_to_all(blocks, axes, 0, 0, tiled=True)]
    all_to_all x0 -> x5, starting transfers between devices: none -> 39 us  [exchange(): return lax.all_to_all(blocks, axes, 0, 0, tiled=True)]
    dot_general x56 -> x20, matrix products: 41.9 us -> 7.32 us  [the longest x16 6.24 us: dot(): return jnp.dot(left, right, preferred_element_type=jnp.float32)]
  transfers between devices with their start and end apart: 4 -> 7, of which waited for: 4 -> 7; matrix products, arithmetic and copies ran while one was open for 1% -> 13% of each run, Pallas kernels for 0% -> 0%
where the time goes in v1:
time: 155 us; the launch traced here: 154 us
  waiting for transfers between devices  49.9 us (32%)
  starting transfers between devices  49.8 us (32%)
  blocking collectives  21 us (14%)
  local copies, waits for them, and re-layouts  13.3 us (9%)
  other arithmetic  11.9 us (8%)
  matrix products  8.06 us (5%)
    all_to_all x5, waiting for transfers between devices, exchange(): return lax.all_to_all(blocks, axes, 0, 0, tiled=True)  43.7 us
    all_to_all x5, starting transfers between devices, exchange(): return lax.all_to_all(blocks, axes, 0, 0, tiled=True)  39 us
    ppermute x2, starting transfers between devices, on_device(): lax.ppermute(mine.astype(jnp.bfloat16), 'y_hi', ways).astype(jnp.float32)  10.7 us
    all_to_all x1, blocking collectives, exchange(): return lax.all_to_all(blocks, axes, 0, 0, tiled=True)  10.3 us
    all_gather x1, blocking collectives, on_device(): pair = lax.all_gather(mixed, 'core', axis=0)  6.69 us
    dot_general x16, matrix products, dot(): return jnp.dot(left, right, preferred_element_type=jnp.float32)  6.24 us
    ppermute x2, waiting for transfers between devices, on_device(): lax.ppermute(mine.astype(jnp.bfloat16), 'y_hi', ways).astype(jnp.float32)  6.22 us
    all_to_all x3, other arithmetic, exchange(): return lax.all_to_all(blocks, axes, 0, 0, tiled=True)  6.18 us
  transfers between devices with their start and end apart: 7, of which 7 were waited for; matrix products, arithmetic and copies ran while one was open for 13% of the time, Pallas kernels for 0%

profile of v1, /device:TPU:1, one launch (start us, length us, event | category | flops | bytes accessed | tf_op | source)
XLA Modules:
  0.0 154.5 jit_solution(1514936374021401433)
XLA Ops:
  3.7 15.5 %all-to-all-start.2 = ((bf16[64,2,640]{2,1,0:T(2,128)(2,1)}), bf16[64,2,640]{2,1,0:T(2,128)(2,1)S(1)}, u32[]{:S(2)}, u32[]{:S(2)}) async-start(bf16[64,2,640]{2,1,0:T(2,128)(2,1)} %reshape.515), calls=%async_computation.2 | async-start | bytes 327680 | tf_op jit(solution)/shard_map/up_rows/all_to_all | solution.py:17
  22.3 1.1 fusion
  24.0 1.4 convolution_convert_fusion.1
  25.4 2.0 %concatenate.40 = bf16[8,64,1536]{2,1,0:T(8,128)(2,1)} concatenate(bf16[8,64,1024]{2,1,0:T(8,128)(2,1)S(1)} %convolution_convert_fusion.1, bf16[8,64,128]{2,1,0:T(8,128)(2,1)S(1)} %convolution_convert_fusion.3, bf16[8,64,128]{2,1,0:T(8,128)(2,1)S(1)} %convolution_convert_fusion.2, bf16[8,64,192]{2,1,0:T(8,128)(2,1)S(1)} %bitcast.130, bf16[8,64,1]{2,1,0:T(8,128)(2,1)S(1)} %copy.112, ...), dimensions={2} | concatenate | bytes 3145728 | tf_op jit(solution)/shard_map/concatenate | solution.py:151
  27.4 1.6 %all-to-all-done.2 = bf16[64,2,640]{2,1,0:T(2,128)(2,1)S(1)} async-done(((bf16[64,2,640]{2,1,0:T(2,128)(2,1)}), bf16[64,2,640]{2,1,0:T(2,128)(2,1)S(1)}, u32[]{:S(2)}, u32[]{:S(2)}) %all-to-all-start.2) | async-done | bytes 163872 | tf_op jit(solution)/shard_map/up_rows/all_to_all | solution.py:17
  29.0 4.2 %all-to-all-start = ((bf16[8,64,1536]{2,1,0:T(8,128)(2,1)}), bf16[8,64,1536]{2,1,0:T(8,128)(2,1)S(1)}, u32[]{:S(2)}, u32[]{:S(2)}) async-start(bf16[8,64,1536]{2,1,0:T(8,128)(2,1)} %concatenate.40), calls=%async_computation | async-start | bytes 3145728 | tf_op jit(solution)/shard_map/sum_plane/all_to_all | solution.py:17
  34.6 1.3 convolution_convert_fusion
  35.9 1.6 %all_to_all.38 = bf16[64,1,3840]{2,1,0:T(2,128)(2,1)} reshape(bf16[192,1280]{1,0:T(8,128)(2,1)S(1)} %convolution_convert_fusion) | data formatting | bytes 983040 | tf_op jit(solution)/shard_map/up_needed/all_to_all | solution.py:17
  37.5 4.6 %reduce.7 = bf16[64,3840]{1,0:T(8,128)(2,1)S(1)} reduce(bf16[64,1,3840]{2,1,0:T(2,128)(2,1)} %all_to_all.38, bf16[]{:T(256)} %broadcast.423), dimensions={1}, to_apply=%all_to_all.38.reduce_sub_computation | reduce | bytes 983042 | tf_op jit(solution)/shard_map/up_needed/all_to_all | solution.py:17
  43.0 9.5 %all-to-all-done = bf16[8,64,1536]{2,1,0:T(8,128)(2,1)S(1)} async-done(((bf16[8,64,1536]{2,1,0:T(8,128)(2,1)}), bf16[8,64,1536]{2,1,0:T(8,128)(2,1)S(1)}, u32[]{:S(2)}, u32[]{:S(2)}) %all-to-all-start) | async-done | bytes 1572896 | tf_op jit(solution)/shard_map/sum_plane/all_to_all | solution.py:17
  52.4 10.0 %all-to-all-start.3 = ((bf16[64,2,1920]{2,1,0:T(2,128)(2,1)}), bf16[64,2,1920]{2,1,0:T(2,128)(2,1)S(1)}, u32[]{:S(2)}, u32[]{:S(2)}) async-start(bf16[64,2,1920]{2,1,0:T(2,128)(2,1)} %reshape.517), calls=%async_computation.3 | async-start | bytes 983040 | tf_op jit(solution)/shard_map/up_needed/all_to_all | solution.py:17
  64.2 14.0 %all-to-all-done.3 = bf16[64,2,1920]{2,1,0:T(2,128)(2,1)S(1)} async-done(((bf16[64,2,1920]{2,1,0:T(2,128)(2,1)}), bf16[64,2,1920]{2,1,0:T(2,128)(2,1)S(1)}, u32[]{:S(2)}, u32[]{:S(2)}) %all-to-all-start.3) | async-done | bytes 491552 | tf_op jit(solution)/shard_map/up_needed/all_to_all | solution.py:17
  78.2 4.0 %all-to-all-start.1 = ((bf16[8,8,1536]{2,1,0:T(8,128)(2,1)}), bf16[8,8,1536]{2,1,0:T(8,128)(2,1)}, u32[]{:S(2)}, u32[]{:S(2)}) async-start(bf16[8,8,1536]{2,1,0:T(8,128)(2,1)} %bitcast.133), calls=%async_computation.1 | async-start | bytes 393216 | tf_op jit(solution)/shard_map/sum_z/all_to_all | solution.py:17
  84.2 6.9 %all-to-all-done.1 = bf16[8,8,1536]{2,1,0:T(8,128)(2,1)} async-done(((bf16[8,8,1536]{2,1,0:T(8,128)(2,1)}), bf16[8,8,1536]{2,1,0:T(8,128)(2,1)}, u32[]{:S(2)}, u32[]{:S(2)}) %all-to-all-start.1) | async-done | bytes 196640 | tf_op jit(solution)/shard_map/sum_z/all_to_all | solution.py:17
  95.3 10.3 %all_to_all.45 = bf16[8,8,1024]{2,1,0:T(8,128)(2,1)S(1)} all-to-all(bf16[8,8,1024]{2,1,0:T(8,128)(2,1)S(1)} %broadcast_in_dim.222), channel_id=1, replica_groups=mesh['x'=4,'y_lo'=2,'z'=8,'y_hi'=4,'core'=2] {'z'}, dimensions={0} | all-to-all | bytes 262144 | tf_op jit(solution)/shard_map/gather_z/all_to_all | solution.py:17
  105.6 1.1 broadcast_in_dim.224
  106.7 5.3 %all-to-all-start.5 = ((bf16[8,64,1024]{2,1,0:T(8,128)(2,1)}), bf16[8,64,1024]{2,1,0:T(8,128)(2,1)S(1)}, u32[]{:S(2)}, u32[]{:S(2)}) async-start(bf16[8,64,1024]{2,1,0:T(8,128)(2,1)} %broadcast_in_dim.224), calls=%async_computation.5 | async-start | bytes 2097152 | tf_op jit(solution)/shard_map/gather_plane/all_to_all | solution.py:17
  112.0 11.7 %all-to-all-done.5 = bf16[8,64,1024]{2,1,0:T(8,128)(2,1)S(1)} async-done(((bf16[8,64,1024]{2,1,0:T(8,128)(2,1)}), bf16[8,64,1024]{2,1,0:T(8,128)(2,1)S(1)}, u32[]{:S(2)}, u32[]{:S(2)}) %all-to-all-start.5) | async-done | bytes 1048608 | tf_op jit(solution)/shard_map/gather_plane/all_to_all | solution.py:17
  125.9 6.7 %all-gather = bf16[1024,128]{1,0:T(8,128)(2,1)S(1)} all-gather(bf16[512,128]{1,0:T(8,128)(2,1)S(1)} %fusion.2), channel_id=2, replica_groups=mesh['x'=4,'y_lo'=2,'z'=8,'y_hi'=4,'core'=2] {'core'}, dimensions={0}, use_global_device_ids=true | all-gather | bytes 393216 | tf_op jit(solution)/shard_map/sum_core/all_gather | solution.py:240
  132.6 4.2 %collective-permute-start = (bf16[256,128]{1,0:T(8,128)(2,1)S(1)}, bf16[256,128]{1,0:T(8,128)(2,1)S(1)}, u32[]{:S(2)}, u32[]{:S(2)}) collective-permute-start(bf16[256,128]{1,0:T(8,128)(2,1)S(1)} %fusion.88), channel_id=1, source_target_pairs={{0,2},{2,0},{4,6},{6,4},{1,3},{3,1},{5,7},{7,5},{8,10},{10,8},{12,... | collective-permute-start | bytes 196616 | tf_op jit(solution)/shard_map/sum_y_hi/ppermute | solution.py:247
  136.8 3.8 %collective-permute-done = bf16[256,128]{1,0:T(8,128)(2,1)S(1)} collective-permute-done((bf16[256,128]{1,0:T(8,128)(2,1)S(1)}, bf16[256,128]{1,0:T(8,128)(2,1)S(1)}, u32[]{:S(2)}, u32[]{:S(2)}) %collective-permute-start) | collective-permute-done | bytes 65568 | tf_op jit(solution)/shard_map/sum_y_hi/ppermute | solution.py:247
  140.7 6.5 %collective-permute-start.1 = (bf16[256,128]{1,0:T(8,128)(2,1)S(1)}, bf16[256,128]{1,0:T(8,128)(2,1)S(1)}, u32[]{:S(2)}, u32[]{:S(2)}) collective-permute-start(bf16[256,128]{1,0:T(8,128)(2,1)S(1)} %fusion.39), channel_id=1, source_target_pairs={{0,4},{2,6},{4,0},{6,2},{1,5},{3,7},{5,1},{7,3},{8,12},{10,14},{12... | collective-permute-start | bytes 196616 | tf_op jit(solution)/shard_map/sum_y_hi/ppermute | solution.py:247
  147.2 2.4 %collective-permute-done.1 = bf16[256,128]{1,0:T(8,128)(2,1)S(1)} collective-permute-done((bf16[256,128]{1,0:T(8,128)(2,1)S(1)}, bf16[256,128]{1,0:T(8,128)(2,1)S(1)}, u32[]{:S(2)}, u32[]{:S(2)}) %collective-permute-start.1) | collective-permute-done | bytes 65568 | tf_op jit(solution)/shard_map/sum_y_hi/ppermute | solution.py:247
  149.7 4.0 %all_gather.11 = bf16[512,128]{1,0:T(8,128)(2,1)S(1)} all-gather(bf16[256,128]{1,0:T(8,128)(2,1)S(1)} %add_convert_fusion), channel_id=1, replica_groups=mesh['x'=4,'y_lo'=2,'z'=8,'y_hi'=4,'core'=2] {'core'}, dimensions={0}, use_global_device_ids=true | all-gather | bytes 196608 | tf_op jit(solution)/shard_map/gather_core/all_gather | solution.py:250
  (116 shorter events, 20.2 us)
Async XLA Ops:
  0.0 123.7 %copy-start = (bf16[8,1024,64]{1,2,0:T(8,128)(2,1)S(1)}, bf16[8,1024,64]{1,2,0:T(8,128)(2,1)}, u32[]{:S(2)}) copy-start(bf16[8,1024,64]{1,2,0:T(8,128)(2,1)} %param.24) | copy-start | bytes 3145732
  0.0 20.1 %copy-start.2 = (bf16[4,128,128]{2,1,0:T(8,128)(2,1)S(1)}, bf16[4,128,128]{2,1,0:T(8,128)(2,1)}, u32[]{:S(2)}) copy-start(bf16[4,128,128]{2,1,0:T(8,128)(2,1)} %param.17) | copy-start | bytes 393220
  0.0 20.3 %copy-start.10 = (s32[16,2]{0,1:T(2,128)S(1)}, s32[16,2]{0,1:T(2,128)}, u32[]{:S(2)}) copy-start(s32[16,2]{0,1:T(2,128)} %param.32) | copy-start | bytes 388
  0.0 20.5 %copy-start.8 = (s32[128]{0:T(128)S(1)}, s32[128]{0:T(128)}, u32[]{:S(2)}) copy-start(s32[128]{0:T(128)} %param.30) | copy-start | bytes 1540
  0.0 21.1 %copy-start.7 = (f32[128]{0:T(128)S(1)}, f32[128]{0:T(128)}, u32[]{:S(2)}) copy-start(f32[128]{0:T(128)} %param.18) | copy-start | bytes 1540
  3.0 18.2 %copy-start.5 = (bf16[128,128]{1,0:T(8,128)(2,1)S(1)}, bf16[128,128]{1,0:T(8,128)(2,1)}, u32[]{:S(2)}) copy-start(bf16[128,128]{1,0:T(8,128)(2,1)} %param.21) | copy-start | bytes 98308
  3.7 17.7 %copy-start.6 = (bf16[128,128]{1,0:T(8,128)(2,1)S(1)}, bf16[128,128]{1,0:T(8,128)(2,1)}, u32[]{:S(2)}) copy-start(bf16[128,128]{1,0:T(8,128)(2,1)} %param.20) | copy-start | bytes 98308
  3.7 25.2 %all-to-all-start.2 = ((bf16[64,2,640]{2,1,0:T(2,128)(2,1)}), bf16[64,2,640]{2,1,0:T(2,128)(2,1)S(1)}, u32[]{:S(2)}, u32[]{:S(2)}) async-start(bf16[64,2,640]{2,1,0:T(2,128)(2,1)} %reshape.515), calls=%async_computation.2 | async-start | bytes 327680 | tf_op jit(solution)/shard_map/up_rows/all_to_all | solution.py:17
  20.2 2.2 %copy-start.13 = (bf16[8,128,192]{1,2,0:T(8,128)(2,1)S(1)}, bf16[8,128,192]{1,2,0:T(8,128)(2,1)}, u32[]{:S(2)}) copy-start(bf16[8,128,192]{1,2,0:T(8,128)(2,1)} %param.23) | copy-start | bytes 1179652
  27.4 6.3 %copy-start.11 = (s32[8]{0:T(128)S(1)}, s32[8]{0:T(128)}, u32[]{:S(2)}) copy-start(s32[8]{0:T(128)} %param.31) | copy-start | bytes 100
  29.0 23.5 %all-to-all-start = ((bf16[8,64,1536]{2,1,0:T(8,128)(2,1)}), bf16[8,64,1536]{2,1,0:T(8,128)(2,1)S(1)}, u32[]{:S(2)}, u32[]{:S(2)}) async-start(bf16[8,64,1536]{2,1,0:T(8,128)(2,1)} %concatenate.40), calls=%async_computation | async-start | bytes 3145728 | tf_op jit(solution)/shard_map/sum_plane/all_to_all | solution.py:17
  37.5 25.6 %copy-start.9 = (s32[2]{0:T(128)S(1)}, s32[2]{0:T(128)}, u32[]{:S(2)}) copy-start(s32[2]{0:T(128)} %param.33) | copy-start | bytes 28
  52.4 25.8 %all-to-all-start.3 = ((bf16[64,2,1920]{2,1,0:T(2,128)(2,1)}), bf16[64,2,1920]{2,1,0:T(2,128)(2,1)S(1)}, u32[]{:S(2)}, u32[]{:S(2)}) async-start(bf16[64,2,1920]{2,1,0:T(2,128)(2,1)} %reshape.517), calls=%async_computation.3 | async-start | bytes 983040 | tf_op jit(solution)/shard_map/up_needed/all_to_all | solution.py:17
  78.2 12.9 %all-to-all-start.1 = ((bf16[8,8,1536]{2,1,0:T(8,128)(2,1)}), bf16[8,8,1536]{2,1,0:T(8,128)(2,1)}, u32[]{:S(2)}, u32[]{:S(2)}) async-start(bf16[8,8,1536]{2,1,0:T(8,128)(2,1)} %bitcast.133), calls=%async_computation.1 | async-start | bytes 393216 | tf_op jit(solution)/shard_map/sum_z/all_to_all | solution.py:17
  84.1 9.7 %copy-start.1 = (bf16[2,1,1024,128]{3,2,1,0:T(8,128)(2,1)S(1)}, bf16[2,1,1024,128]{3,2,1,0:T(8,128)(2,1)}, u32[]{:S(2)}) copy-start(bf16[2,1,1024,128]{3,2,1,0:T(8,128)(2,1)} %param.28) | copy-start | bytes 1572868
  84.2 10.6 %copy-start.12 = (bf16[2,1,1024,128]{3,2,1,0:T(8,128)(2,1)S(1)}, bf16[2,1,1024,128]{3,2,1,0:T(8,128)(2,1)}, u32[]{:S(2)}) copy-start(bf16[2,1,1024,128]{3,2,1,0:T(8,128)(2,1)} %param.29) | copy-start | bytes 1572868
  106.7 17.0 %all-to-all-start.5 = ((bf16[8,64,1024]{2,1,0:T(8,128)(2,1)}), bf16[8,64,1024]{2,1,0:T(8,128)(2,1)S(1)}, u32[]{:S(2)}, u32[]{:S(2)}) async-start(bf16[8,64,1024]{2,1,0:T(8,128)(2,1)} %broadcast_in_dim.224), calls=%async_computation.5 | async-start | bytes 2097152 | tf_op jit(solution)/shard_map/gather_plane/all_to_all | solution.py:17
  123.7 0.9 copy-start.4
  124.5 1.0 copy-start.3
  132.6 8.0 %collective-permute-start = (bf16[256,128]{1,0:T(8,128)(2,1)S(1)}, bf16[256,128]{1,0:T(8,128)(2,1)S(1)}, u32[]{:S(2)}, u32[]{:S(2)}) collective-permute-start(bf16[256,128]{1,0:T(8,128)(2,1)S(1)} %fusion.88), channel_id=1, source_target_pairs={{0,2},{2,0},{4,6},{6,4},{1,3},{3,1},{5,7},{7,5},{8,10},{10,8},{12,... | collective-permute-start | bytes 196616 | tf_op jit(solution)/shard_map/sum_y_hi/ppermute | solution.py:247
  140.7 9.0 %collective-permute-start.1 = (bf16[256,128]{1,0:T(8,128)(2,1)S(1)}, bf16[256,128]{1,0:T(8,128)(2,1)S(1)}, u32[]{:S(2)}, u32[]{:S(2)}) collective-permute-start(bf16[256,128]{1,0:T(8,128)(2,1)S(1)} %fusion.39), channel_id=1, source_target_pairs={{0,4},{2,6},{4,0},{6,2},{1,5},{3,7},{5,1},{7,3},{8,12},{10,14},{12... | collective-permute-start | bytes 196616 | tf_op jit(solution)/shard_map/sum_y_hi/ppermute | solution.py:247

commit v2 on v1

--- a/solution.py
+++ b/solution.py
@@ -101,18 +101,18 @@
     per_group = steps * own_rows
     every_row = groups * per_group
     model_width = width_part * groups
-    me = lax.axis_index(GROUP)
+    line = lax.axis_size("x")
+    column_rows = depth * per_group
 
     group_tasks = tasks.reshape(groups, own_rows)
     matched = moves[:, 1][None, :] == jnp.arange(groups, dtype=jnp.int32)[:, None]
     moved = jnp.any(matched, axis=1)
     chosen = jnp.sum(jnp.where(matched, moves[:, 0][None, :], 0), axis=1)
-    needed = jnp.concatenate([group_tasks, chosen[:, None]], axis=1)
-    slots = own_rows + 1
     late = jnp.where(moved[:, None], chosen[:, None], group_tasks)
     active = jnp.stack([group_tasks if s < steps // 2 else late for s in range(steps)], axis=1)
     active = active.reshape(every_row)
     marks = active[:, None] == jnp.arange(task_count, dtype=jnp.int32)[None, :]
+    row_home = jnp.sum(jnp.where(marks, homes[None, :], 0), axis=1)
 
     up = jnp.concatenate(
         [
@@ -121,20 +121,8 @@
         ],
         axis=1,
     )
-    with jax.named_scope("up_rows"):
-        up_rows = exchange(up, GROUP)
-    sources = jnp.sum(
-        jnp.where(
-            needed.reshape(-1)[:, None] == jnp.arange(task_count, dtype=jnp.int32)[None, :],
-            homes[None, :],
-            0,
-        ),
-        axis=1,
-    )
-    pick = (sources[:, None] == jnp.arange(groups, dtype=jnp.int32)[None, :]).astype(jnp.bfloat16)
-    chosen_rows = dot(pick, up_rows).astype(jnp.bfloat16)
-    with jax.named_scope("up_needed"):
-        up_needed = exchange(chosen_rows.reshape(groups, slots * base_end), GROUP)
+    with jax.named_scope("up_x"):
+        up_line = exchange(jnp.broadcast_to(up[None], (line, rank, base_end)), "x")
 
     residual = (
         inputs.reshape(steps, groups, own_rows, width_part)
@@ -161,37 +149,72 @@
         axis=1,
     ).astype(jnp.bfloat16)
     with jax.named_scope("sum_plane"):
-        by_plane = exchange(partial.reshape(planes, depth * per_group, -1), PLANE)
-    plane_sum = jnp.sum(by_plane.astype(jnp.float32), axis=0).astype(jnp.bfloat16)
+        by_plane = exchange(partial.reshape(planes, column_rows, -1), PLANE)
+
+    up_line, by_plane = lax.optimization_barrier((up_line, by_plane))
+    with jax.named_scope("up_y_lo"):
+        up_other = lax.ppermute(up_line, "y_lo", [(0, 1), (1, 0)])
+    plane_sum = jnp.sum(by_plane.astype(jnp.float32), axis=0)
+
+    low_end = 3 * rank
+    low_part = plane_sum[:, base_end:]
+    squares = low_part[:, low_end : low_end + 1] + low_part[:, low_end + 1 : low_end + 2]
+    squares_high = lax.reduce_precision(squares, 8, 7)
+    low_part = jnp.concatenate(
+        [
+            low_part[:, :low_end],
+            squares_high,
+            squares - squares_high,
+            low_part[:, low_end + 2 :],
+        ],
+        axis=1,
+    ).astype(jnp.bfloat16)
+    with jax.named_scope("sum_low"):
+        low_sum = exchange(
+            jnp.broadcast_to(low_part[None], (depth, column_rows, PADDED_WIDTH)), "z"
+        )
+    low_sum = jnp.sum(low_sum.astype(jnp.float32), axis=0)
+    inverse = lax.rsqrt(
+        (low_sum[:, low_end : low_end + 1] + low_sum[:, low_end + 1 : low_end + 2]) / model_width
+        + epsilon
+    )
+    lowrank = (inverse * low_sum[:, :low_end]).astype(jnp.bfloat16)
+
+    x, y_lo, z = (lax.axis_index(name) for name in GROUP)
+    column_home = lax.dynamic_slice_in_dim(
+        row_home, (x * 2 + y_lo) * column_rows, column_rows, 0
+    )
+
+    def lift(block, first, last):
+        total = jnp.zeros((column_rows, last - first), jnp.float32)
+        rows = lowrank[:, block * rank : (block + 1) * rank]
+        for matrices, half in ((up_line, y_lo), (up_other, 1 - y_lo)):
+            slots = (jnp.arange(line) * 2 + half) * depth + z
+            use = column_home[:, None] == slots[None, :]
+            spread = jnp.where(use[:, :, None], rows[:, None, :], 0).reshape(
+                column_rows, line * rank
+            )
+            total = total + dot(
+                spread, matrices[:, :, first:last].reshape(line * rank, last - first)
+            )
+        return total
+
+    lifted = jnp.concatenate(
+        [lift(0, 0, query_width), lift(1, query_width, key_end), lift(2, key_end, base_end)],
+        axis=1,
+    )
+    raw_part = (inverse * plane_sum[:, :base_end] + lifted).astype(jnp.bfloat16)
     with jax.named_scope("sum_z"):
-        by_depth = exchange(plane_sum.reshape(depth, per_group, -1), "z")
-    own = jnp.sum(by_depth.astype(jnp.float32), axis=0)
-
-    low_end = base_end + 3 * rank
-    inverse = lax.rsqrt((own[:, low_end] + own[:, low_end + 1]) / model_width + epsilon)[:, None]
-    lowrank = (inverse * own[:, base_end:low_end]).astype(jnp.bfloat16)
-    own_moved = lax.dynamic_index_in_dim(moved, me, 0, keepdims=False)
+        by_depth = exchange(raw_part.reshape(depth, per_group, base_end), "z")
+    raw = jnp.sum(by_depth.astype(jnp.float32), axis=0)
+
     row_step = jnp.arange(per_group) // own_rows
-    row_slot = jnp.where(
-        jnp.logical_and(row_step >= steps // 2, own_moved),
-        own_rows,
-        jnp.arange(per_group) % own_rows,
-    )[:, None]
-
-    def lift(block, first, last):
-        total = jnp.zeros((per_group, last - first), jnp.float32)
-        for slot in range(slots):
-            matrix = up_needed[:, slot * base_end + first : slot * base_end + last]
-            lifted = dot(lowrank[:, block * rank : (block + 1) * rank], matrix)
-            total = jnp.where(row_slot == slot, lifted, total)
-        return total
-
-    raw_query = inverse * own[:, :query_width] + lift(0, 0, query_width)
-    raw_key = inverse * own[:, query_width:key_end] + lift(1, query_width, key_end)
-    raw_value = inverse * own[:, key_end:base_end] + lift(2, key_end, base_end)
     positions = jnp.tile(lengths, steps) + row_step
-    queries = apply_rotary(raw_query.reshape(per_group, heads, head_dim), positions)
-    new_keys = apply_rotary(raw_key.reshape(per_group, 1, head_dim), positions)
+    queries = apply_rotary(raw[:, :query_width].reshape(per_group, heads, head_dim), positions)
+    new_keys = apply_rotary(
+        raw[:, query_width:key_end].reshape(per_group, 1, head_dim), positions
+    )
+    raw_value = raw[:, key_end:]
 
     def by_row(array):
         return (
@@ -239,12 +262,12 @@
     with jax.named_scope("sum_core"):
         pair = lax.all_gather(mixed, "core", axis=0)
     mine = lax.dynamic_slice_in_dim(pair, core * half, half, 1).astype(jnp.float32)
-    mine = mine[0] + mine[1]
-    for hop in (1, 2):
-        with jax.named_scope("sum_y_hi"):
-            ways = [(i, i ^ hop) for i in range(lax.axis_size("y_hi"))]
-            mine = lax.reduce_precision(mine, 8, 7)
-            mine = mine + lax.ppermute(mine.astype(jnp.bfloat16), "y_hi", ways).astype(jnp.float32)
+    mine = (mine[0] + mine[1]).astype(jnp.bfloat16)
+    with jax.named_scope("sum_y_hi"):
+        mine = exchange(
+            jnp.broadcast_to(mine[None], (lax.axis_size("y_hi"), half, width_part)), "y_hi"
+        )
+    mine = jnp.sum(mine.astype(jnp.float32), axis=0)
     finished = lax.dynamic_slice_in_dim(states, core * half, half, 0) + mine
     with jax.named_scope("gather_core"):
         finished = lax.all_gather(finished.astype(jnp.bfloat16), "core", axis=0, tiled=True)

time: 155 us -> 150 us (0.968)
  blocking collectives: 21 us -> 37 us
  starting transfers between devices: 49.8 us -> 39 us
  other arithmetic: 11.9 us -> 3.76 us
  waiting for transfers between devices: 49.9 us -> 47.1 us
    all_to_all x1 -> x2, blocking collectives: 10.3 us -> 25.3 us  [exchange(): return lax.all_to_all(blocks, axes, 0, 0, tiled=True)]
    ppermute x2 -> x1, starting transfers between devices: 10.7 us -> 2.43 us  [on_device(): up_other = lax.ppermute(up_line, 'y_lo', [(0, 1), (1, 0)])]
    all_to_all x3 -> x0, other arithmetic: 6.18 us -> none  [exchange(): return lax.all_to_all(blocks, axes, 0, 0, tiled=True)]
    all_to_all x5, starting transfers between devices: 39 us -> 36.6 us  [exchange(): return lax.all_to_all(blocks, axes, 0, 0, tiled=True)]
    all_to_all x2 -> x0, local copies, waits for them, and re-layouts: 2.11 us -> none  [exchange(): return lax.all_to_all(blocks, axes, 0, 0, tiled=True)]
    unnamed x34 -> x35, local copies, waits for them, and re-layouts: 4.49 us -> 2.53 us
    all_to_all x5, waiting for transfers between devices: 43.7 us -> 42 us  [exchange(): return lax.all_to_all(blocks, axes, 0, 0, tiled=True)]
    reduce_sum x3 -> x5, other arithmetic: 1.96 us -> 0.39 us  [the longest x1 0.21 us: on_device(): plane_sum = jnp.sum(by_plane.astype(jnp.float32), axis=0)]
  transfers between devices with their start and end apart: 7 -> 6, of which waited for: 7 -> 5; matrix products, arithmetic and copies ran while one was open for 13% -> 8% of each run, Pallas kernels for 0% -> 0%
where the time goes in v2:
time: 150 us; the launch traced here: 149 us
  waiting for transfers between devices  47.1 us (31%)
  starting transfers between devices  39 us (26%)
  blocking collectives  37 us (25%)
  local copies, waits for them, and re-layouts  12.4 us (8%)
  matrix products  9.49 us (6%)
  other arithmetic  3.76 us (3%)
    all_to_all x5, waiting for transfers between devices, exchange(): return lax.all_to_all(blocks, axes, 0, 0, tiled=True)  42 us
    all_to_all x5, starting transfers between devices, exchange(): return lax.all_to_all(blocks, axes, 0, 0, tiled=True)  36.6 us
    all_to_all x2, blocking collectives, exchange(): return lax.all_to_all(blocks, axes, 0, 0, tiled=True)  25.3 us
    all_gather x1, blocking collectives, on_device(): pair = lax.all_gather(mixed, 'core', axis=0)  7.67 us
    dot_general x12, matrix products, dot(): return jnp.dot(left, right, preferred_element_type=jnp.float32)  6.61 us
    ppermute x1, waiting for transfers between devices, on_device(): up_other = lax.ppermute(up_line, 'y_lo', [(0, 1), (1, 0)])  5.18 us
    all_gather x1, blocking collectives, on_device(): lax.all_gather(finished.astype(jnp.bfloat16), 'core', axis=0, tiled=True)  4.07 us
    concatenate x1, local copies, waits for them, and re-layouts, on_device(): jnp.concatenate([dot(gained, w_query), dot(gained, key_projection_weight)...  3.34 us
  transfers between devices with their start and end apart: 6, of which 5 were waited for; matrix products, arithmetic and copies ran while one was open for 8% of the time, Pallas kernels for 0%

profile of v2, /device:TPU:1, one launch (start us, length us, event | category | flops | bytes accessed | tf_op | source)
XLA Modules:
  0.0 149.4 jit_solution(7592125020322906935)
XLA Ops:
  0.0 0.9 copy.180
  0.9 1.0 pad_maximum_fusion
  1.8 0.9 broadcast_in_dim.246
  2.7 5.0 %all-to-all-start = ((bf16[4,64,1280]{2,1,0:T(8,128)(2,1)}), bf16[4,64,1280]{2,1,0:T(8,128)(2,1)S(1)}, u32[]{:S(2)}, u32[]{:S(2)}) async-start(bf16[4,64,1280]{2,1,0:T(8,128)(2,1)} %broadcast_in_dim.246), calls=%async_computation | async-start | bytes 1310720 | tf_op jit(solution)/shard_map/up_x/all_to_all | solution.py:17
  8.7 1.1 fusion
  13.4 1.4 convolution_convert_fusion
  14.8 3.3 %concatenate.49 = bf16[8,64,1536]{2,1,0:T(8,128)(2,1)} concatenate(bf16[8,64,1024]{2,1,0:T(8,128)(2,1)S(1)} %convolution_convert_fusion, bf16[8,64,128]{2,1,0:T(8,128)(2,1)} %convolution_convert_fusion.2, bf16[8,64,128]{2,1,0:T(8,128)(2,1)} %convolution_convert_fusion.1, bf16[8,64,192]{2,1,0:T(8,128)(2,1)S(1)} %bitcast.134, bf16[8,64,1]{2,1,0:T(8,128)(2,1)S(1)} %copy.144, ...), dimensions={2} | concatenate | bytes 3145728 | tf_op jit(solution)/shard_map/concatenate | solution.py:139
  18.2 0.8 copy-done.1
  19.1 5.3 %all-to-all-start.1 = ((bf16[8,64,1536]{2,1,0:T(8,128)(2,1)}), bf16[8,64,1536]{2,1,0:T(8,128)(2,1)S(1)}, u32[]{:S(2)}, u32[]{:S(2)}) async-start(bf16[8,64,1536]{2,1,0:T(8,128)(2,1)} %concatenate.49), calls=%async_computation.1 | async-start | bytes 3145728 | tf_op jit(solution)/shard_map/sum_plane/all_to_all | solution.py:17
  24.5 16.2 %all-to-all-done.1 = bf16[8,64,1536]{2,1,0:T(8,128)(2,1)S(1)} async-done(((bf16[8,64,1536]{2,1,0:T(8,128)(2,1)}), bf16[8,64,1536]{2,1,0:T(8,128)(2,1)S(1)}, u32[]{:S(2)}, u32[]{:S(2)}) %all-to-all-start.1) | async-done | bytes 1572896 | tf_op jit(solution)/shard_map/sum_plane/all_to_all | solution.py:17
  42.3 13.5 %all-to-all-start.2 = ((bf16[8,64,256]{2,1,0:T(8,128)(2,1)}), bf16[8,64,256]{2,1,0:T(8,128)(2,1)S(1)}, u32[]{:S(2)}, u32[]{:S(2)}) async-start(bf16[8,64,256]{2,1,0:T(8,128)(2,1)} %broadcast_in_dim.256), calls=%async_computation.2 | async-start | bytes 524288 | tf_op jit(solution)/shard_map/sum_low/all_to_all | solution.py:17
  56.1 2.4 %collective-permute-start = (bf16[4,64,1280]{2,1,0:T(8,128)(2,1)}, bf16[4,64,1280]{2,1,0:T(8,128)(2,1)S(1)}, u32[]{:S(2)}, u32[]{:S(2)}) collective-permute-start(bf16[4,64,1280]{2,1,0:T(8,128)(2,1)} %copy-done.1), channel_id=1, source_target_pairs={{0,64},{64,0},{1,65},{65,1},{2,66},{66,2},{3,67},{67,3},{4,68},{68... | collective-permute-start | bytes 1966088 | tf_op jit(solution)/shard_map/up_y_lo/ppermute | solution.py:156
  58.6 6.7 %all-to-all-done.2 = bf16[8,64,256]{2,1,0:T(8,128)(2,1)S(1)} async-done(((bf16[8,64,256]{2,1,0:T(8,128)(2,1)}), bf16[8,64,256]{2,1,0:T(8,128)(2,1)S(1)}, u32[]{:S(2)}, u32[]{:S(2)}) %all-to-all-start.2) | async-done | bytes 262176 | tf_op jit(solution)/shard_map/sum_low/all_to_all | solution.py:17
  66.5 5.2 %collective-permute-done = bf16[4,64,1280]{2,1,0:T(8,128)(2,1)S(1)} collective-permute-done((bf16[4,64,1280]{2,1,0:T(8,128)(2,1)}, bf16[4,64,1280]{2,1,0:T(8,128)(2,1)S(1)}, u32[]{:S(2)}, u32[]{:S(2)}) %collective-permute-start) | collective-permute-done | bytes 655392 | tf_op jit(solution)/shard_map/up_y_lo/ppermute | solution.py:156
  73.4 6.4 %all-to-all-start.3 = ((bf16[8,8,1280]{2,1,0:T(8,128)(2,1)}), bf16[8,8,1280]{2,1,0:T(8,128)(2,1)S(1)}, u32[]{:S(2)}, u32[]{:S(2)}) async-start(bf16[8,8,1280]{2,1,0:T(8,128)(2,1)} %fusion.23), calls=%async_computation.3 | async-start | bytes 327680 | tf_op jit(solution)/shard_map/sum_z/all_to_all | solution.py:17
  79.8 8.2 %all-to-all-done.3 = bf16[8,8,1280]{2,1,0:T(8,128)(2,1)S(1)} async-done(((bf16[8,8,1280]{2,1,0:T(8,128)(2,1)}), bf16[8,8,1280]{2,1,0:T(8,128)(2,1)S(1)}, u32[]{:S(2)}, u32[]{:S(2)}) %all-to-all-start.3) | async-done | bytes 163872 | tf_op jit(solution)/shard_map/sum_z/all_to_all | solution.py:17
  89.2 1.3 fusion.11
  90.8 10.3 %all_to_all.35 = bf16[8,8,1024]{2,1,0:T(8,128)(2,1)S(1)} all-to-all(bf16[8,8,1024]{2,1,0:T(8,128)(2,1)S(1)} %broadcast_in_dim.269), channel_id=1, replica_groups=mesh['x'=4,'y_lo'=2,'z'=8,'y_hi'=4,'core'=2] {'z'}, dimensions={0} | all-to-all | bytes 262144 | tf_op jit(solution)/shard_map/gather_z/all_to_all | solution.py:17
  101.1 1.1 broadcast_in_dim.271
  102.2 6.5 %all-to-all-start.5 = ((bf16[8,64,1024]{2,1,0:T(8,128)(2,1)}), bf16[8,64,1024]{2,1,0:T(8,128)(2,1)S(1)}, u32[]{:S(2)}, u32[]{:S(2)}) async-start(bf16[8,64,1024]{2,1,0:T(8,128)(2,1)} %broadcast_in_dim.271), calls=%async_computation.5 | async-start | bytes 2097152 | tf_op jit(solution)/shard_map/gather_plane/all_to_all | solution.py:17
  108.7 10.9 %all-to-all-done.5 = bf16[8,64,1024]{2,1,0:T(8,128)(2,1)S(1)} async-done(((bf16[8,64,1024]{2,1,0:T(8,128)(2,1)}), bf16[8,64,1024]{2,1,0:T(8,128)(2,1)S(1)}, u32[]{:S(2)}, u32[]{:S(2)}) %all-to-all-start.5) | async-done | bytes 1048608 | tf_op jit(solution)/shard_map/gather_plane/all_to_all | solution.py:17
  121.8 7.7 %all-gather = bf16[1024,128]{1,0:T(8,128)(2,1)S(1)} all-gather(bf16[512,128]{1,0:T(8,128)(2,1)S(1)} %fusion.3), channel_id=2, replica_groups=mesh['x'=4,'y_lo'=2,'z'=8,'y_hi'=4,'core'=2] {'core'}, dimensions={0}, use_global_device_ids=true | all-gather | bytes 393216 | tf_op jit(solution)/shard_map/sum_core/all_gather | solution.py:263
  129.5 15.0 %all_to_all.36 = bf16[4,256,128]{2,1,0:T(8,128)(2,1)S(1)} all-to-all(bf16[4,256,128]{2,1,0:T(8,128)(2,1)S(1)} %broadcast_in_dim.275), channel_id=1, replica_groups=mesh['x'=4,'y_lo'=2,'z'=8,'y_hi'=4,'core'=2] {'y_hi'}, dimensions={0} | all-to-all | bytes 524288 | tf_op jit(solution)/shard_map/sum_y_hi/all_to_all | solution.py:17
  144.6 4.1 %all_gather.11 = bf16[512,128]{1,0:T(8,128)(2,1)S(1)} all-gather(bf16[256,128]{1,0:T(8,128)(2,1)S(1)} %add_convert_fusion), channel_id=1, replica_groups=mesh['x'=4,'y_lo'=2,'z'=8,'y_hi'=4,'core'=2] {'core'}, dimensions={0}, use_global_device_ids=true | all-gather | bytes 196608 | tf_op jit(solution)/shard_map/gather_core/all_gather | solution.py:273
  (117 shorter events, 13.9 us)
Async XLA Ops:
  0.0 119.6 %copy-start = (bf16[8,1024,64]{1,2,0:T(8,128)(2,1)S(1)}, bf16[8,1024,64]{1,2,0:T(8,128)(2,1)}, u32[]{:S(2)}) copy-start(bf16[8,1024,64]{1,2,0:T(8,128)(2,1)} %param.24) | copy-start | bytes 3145732
  0.0 7.7 %copy-start.11 = (s32[16,2]{0,1:T(2,128)S(1)}, s32[16,2]{0,1:T(2,128)}, u32[]{:S(2)}) copy-start(s32[16,2]{0,1:T(2,128)} %param.32) | copy-start | bytes 388
  0.0 7.9 %copy-start.12 = (s32[128]{0:T(128)S(1)}, s32[128]{0:T(128)}, u32[]{:S(2)}) copy-start(s32[128]{0:T(128)} %param.30) | copy-start | bytes 1540
  0.9 7.5 %copy-start.4 = (bf16[4,128,128]{2,1,0:T(8,128)(2,1)S(1)}, bf16[4,128,128]{2,1,0:T(8,128)(2,1)}, u32[]{:S(2)}) copy-start(bf16[4,128,128]{2,1,0:T(8,128)(2,1)} %param.17) | copy-start | bytes 393220
  1.8 6.8 %copy-start.9 = (f32[128]{0:T(128)S(1)}, f32[128]{0:T(128)}, u32[]{:S(2)}) copy-start(f32[128]{0:T(128)} %param.18) | copy-start | bytes 1540
  2.7 6.0 %copy-start.14 = (bf16[8,128,192]{1,2,0:T(8,128)(2,1)S(1)}, bf16[8,128,192]{1,2,0:T(8,128)(2,1)}, u32[]{:S(2)}) copy-start(bf16[8,128,192]{1,2,0:T(8,128)(2,1)} %param.23) | copy-start | bytes 1179652
  2.7 15.5 %all-to-all-start = ((bf16[4,64,1280]{2,1,0:T(8,128)(2,1)}), bf16[4,64,1280]{2,1,0:T(8,128)(2,1)S(1)}, u32[]{:S(2)}, u32[]{:S(2)}) async-start(bf16[4,64,1280]{2,1,0:T(8,128)(2,1)} %broadcast_in_dim.246), calls=%async_computation | async-start | bytes 1310720 | tf_op jit(solution)/shard_map/up_x/all_to_all | solution.py:17
  8.7 3.1 %copy-start.7 = (bf16[128,128]{1,0:T(8,128)(2,1)S(1)}, bf16[128,128]{1,0:T(8,128)(2,1)}, u32[]{:S(2)}) copy-start(bf16[128,128]{1,0:T(8,128)(2,1)} %param.21) | copy-start | bytes 98308
  8.7 3.9 %copy-start.8 = (bf16[128,128]{1,0:T(8,128)(2,1)S(1)}, bf16[128,128]{1,0:T(8,128)(2,1)}, u32[]{:S(2)}) copy-start(bf16[128,128]{1,0:T(8,128)(2,1)} %param.20) | copy-start | bytes 98308
  18.2 6.1 %copy-start.10 = (s32[2]{0:T(128)S(1)}, s32[2]{0:T(128)}, u32[]{:S(2)}) copy-start(s32[2]{0:T(128)} %param.33) | copy-start | bytes 28
  18.2 6.2 %copy-start.13 = (s32[8]{0:T(128)S(1)}, s32[8]{0:T(128)}, u32[]{:S(2)}) copy-start(s32[8]{0:T(128)} %param.31) | copy-start | bytes 100
  18.2 0.8 copy-start.1
  19.1 21.7 %all-to-all-start.1 = ((bf16[8,64,1536]{2,1,0:T(8,128)(2,1)}), bf16[8,64,1536]{2,1,0:T(8,128)(2,1)S(1)}, u32[]{:S(2)}, u32[]{:S(2)}) async-start(bf16[8,64,1536]{2,1,0:T(8,128)(2,1)} %concatenate.49), calls=%async_computation.1 | async-start | bytes 3145728 | tf_op jit(solution)/shard_map/sum_plane/all_to_all | solution.py:17
  40.9 24.7 %copy-start.2 = (bf16[4,64,1280]{2,1,0:T(8,128)(2,1)S(1)}, bf16[4,64,1280]{2,1,0:T(8,128)(2,1)}, u32[]{:S(2)}) copy-start(bf16[4,64,1280]{2,1,0:T(8,128)(2,1)} %copy-done.1) | copy-start | bytes 1966084
  42.3 22.9 %all-to-all-start.2 = ((bf16[8,64,256]{2,1,0:T(8,128)(2,1)}), bf16[8,64,256]{2,1,0:T(8,128)(2,1)S(1)}, u32[]{:S(2)}, u32[]{:S(2)}) async-start(bf16[8,64,256]{2,1,0:T(8,128)(2,1)} %broadcast_in_dim.256), calls=%async_computation.2 | async-start | bytes 524288 | tf_op jit(solution)/shard_map/sum_low/all_to_all | solution.py:17
  56.1 15.6 %collective-permute-start = (bf16[4,64,1280]{2,1,0:T(8,128)(2,1)}, bf16[4,64,1280]{2,1,0:T(8,128)(2,1)S(1)}, u32[]{:S(2)}, u32[]{:S(2)}) collective-permute-start(bf16[4,64,1280]{2,1,0:T(8,128)(2,1)} %copy-done.1), channel_id=1, source_target_pairs={{0,64},{64,0},{1,65},{65,1},{2,66},{66,2},{3,67},{67,3},{4,68},{68... | collective-permute-start | bytes 1966088 | tf_op jit(solution)/shard_map/up_y_lo/ppermute | solution.py:156
  66.5 21.8 %copy-start.3 = (bf16[2,1,1024,128]{3,2,1,0:T(8,128)(2,1)S(1)}, bf16[2,1,1024,128]{3,2,1,0:T(8,128)(2,1)}, u32[]{:S(2)}) copy-start(bf16[2,1,1024,128]{3,2,1,0:T(8,128)(2,1)} %param.28) | copy-start | bytes 1572868
  73.4 14.6 %all-to-all-start.3 = ((bf16[8,8,1280]{2,1,0:T(8,128)(2,1)}), bf16[8,8,1280]{2,1,0:T(8,128)(2,1)S(1)}, u32[]{:S(2)}, u32[]{:S(2)}) async-start(bf16[8,8,1280]{2,1,0:T(8,128)(2,1)} %fusion.23), calls=%async_computation.3 | async-start | bytes 327680 | tf_op jit(solution)/shard_map/sum_z/all_to_all | solution.py:17
  102.2 17.4 %all-to-all-start.5 = ((bf16[8,64,1024]{2,1,0:T(8,128)(2,1)}), bf16[8,64,1024]{2,1,0:T(8,128)(2,1)S(1)}, u32[]{:S(2)}, u32[]{:S(2)}) async-start(bf16[8,64,1024]{2,1,0:T(8,128)(2,1)} %broadcast_in_dim.271), calls=%async_computation.5 | async-start | bytes 2097152 | tf_op jit(solution)/shard_map/gather_plane/all_to_all | solution.py:17
  119.6 0.9 copy-start.6
  120.3 1.0 copy-start.5

commit v3 on v2

--- a/solution.py
+++ b/solution.py
@@ -1,8 +1,11 @@
+import functools
 import math
 
 import jax
 import jax.numpy as jnp
 from jax import lax
+from jax.experimental import pallas as pl
+from jax.experimental.pallas import tpu as pltpu
 from jax.sharding import Mesh
 from jax.sharding import PartitionSpec as P
 
@@ -34,6 +37,108 @@
 
 def dot(left, right):
     return jnp.dot(left, right, preferred_element_type=jnp.float32)
+
+
+def project_kernel(
+    own_rows,
+    inputs_ref,
+    gain_ref,
+    query_ref,
+    key_ref,
+    value_ref,
+    adapter_ref,
+    tasks_ref,
+    moves_ref,
+    out_ref,
+):
+    steps, all_rows, width = inputs_ref.shape
+    every_row = steps * all_rows
+    per_group = steps * own_rows
+    query_width = query_ref.shape[1]
+    head_dim = key_ref.shape[1]
+    low = adapter_ref.shape[1]
+    base_end = query_width + 2 * head_dim
+    block = 128
+    gathered = inputs_ref[...].reshape(every_row, width)
+
+    @pl.loop(0, every_row // block)
+    def _(index):
+        first = pl.multiple_of(index * block, block)
+        rows = pl.ds(first, block)
+
+        def row_of(width):
+            return first + lax.broadcasted_iota(jnp.int32, (block, width), 0)
+
+        def lane(width):
+            return lax.broadcasted_iota(jnp.int32, (block, width), 1)
+
+        def source_of(row):
+            return row // per_group * own_rows + row % own_rows
+
+        row = row_of(every_row)
+        place = row % per_group // own_rows * all_rows + source_of(row)
+        order = jnp.where(lane(every_row) == place, 1.0, 0.0).astype(jnp.bfloat16)
+        states = dot(order, gathered)
+        gained = (states * gain_ref[...]).astype(jnp.bfloat16)
+        squares = jnp.sum(states * states, axis=1, keepdims=True)
+        squares_high = squares.astype(jnp.bfloat16).astype(jnp.float32)
+
+        own = lane(all_rows) == source_of(row_of(all_rows))
+        task = jnp.sum(jnp.where(own, tasks_ref[...], 0), axis=1, keepdims=True)
+        moves = moves_ref.shape[1]
+        here = moves_ref[1:2, :] == row_of(moves) // per_group
+        moved = jnp.sum(jnp.where(here, 1, 0), axis=1, keepdims=True) > 0
+        chosen = jnp.sum(jnp.where(here, moves_ref[0:1, :], 0), axis=1, keepdims=True)
+        late = row_of(1) % per_group >= per_group // 2
+        task = jnp.where(jnp.logical_and(late, moved), chosen, task)
+
+        out_ref[rows, 0:query_width] = dot(gained, query_ref[...]).astype(jnp.bfloat16)
+        out_ref[rows, query_width : query_width + head_dim] = dot(gained, key_ref[...]).astype(
+            jnp.bfloat16
+        )
+        out_ref[rows, query_width + head_dim : base_end] = dot(gained, value_ref[...]).astype(
+            jnp.bfloat16
+        )
+        total = jnp.zeros((block, low), jnp.float32)
+        for adapter in range(adapter_ref.shape[0]):
+            mine = jnp.where(task == adapter, gained, jnp.zeros_like(gained))
+            total = total + lax.dot_general(
+                mine,
+                adapter_ref[adapter],
+                (((1,), (1,)), ((), ())),
+                preferred_element_type=jnp.float32,
+            )
+        rest = PADDED_WIDTH - low
+        extra = jnp.where(
+            lane(rest) == 0,
+            squares_high,
+            jnp.where(lane(rest) == 1, squares - squares_high, 0.0),
+        )
+        out_ref[rows, base_end : base_end + PADDED_WIDTH] = jnp.concatenate(
+            [total, extra], axis=1
+        ).astype(jnp.bfloat16)
+
+
+def project(inputs, gain, w_query, w_key, w_value, adapter_in, tasks, moves, own_rows):
+    steps, all_rows, width = inputs.shape
+    columns = w_query.shape[1] + w_key.shape[1] + w_value.shape[1] + PADDED_WIDTH
+    return pl.pallas_call(
+        functools.partial(project_kernel, own_rows),
+        out_shape=jax.ShapeDtypeStruct((steps * all_rows, columns), jnp.bfloat16),
+        compiler_params=pltpu.CompilerParams(vmem_limit_bytes=32 * 1024 * 1024),
+        cost_estimate=pl.CostEstimate(
+            flops=2 * steps * all_rows * width * 3328, bytes_accessed=3_000_000, transcendentals=0
+        ),
+    )(
+        inputs,
+        gain[None, :],
+        w_query,
+        w_key,
+        w_value,
+        jnp.swapaxes(adapter_in, 1, 2),
+        tasks[None, :],
+        moves.T,
+    )
 
 
 def attend(queries, cache_keys, value_cache, fresh_keys, fresh_values, lengths, query_steps):
@@ -121,39 +226,25 @@
         ],
         axis=1,
     )
+    with jax.named_scope("up_y_lo"):
+        up_pair = jnp.stack([up, lax.ppermute(up, "y_lo", [(0, 1), (1, 0)])])
     with jax.named_scope("up_x"):
-        up_line = exchange(jnp.broadcast_to(up[None], (line, rank, base_end)), "x")
-
-    residual = (
-        inputs.reshape(steps, groups, own_rows, width_part)
-        .transpose(1, 0, 2, 3)
-        .reshape(every_row, width_part)
-    )
-    states = residual.astype(jnp.float32)
-    gained = (states * gain[None, :]).astype(jnp.bfloat16)
-    squares = jnp.sum(states * states, axis=1, keepdims=True)
-    squares_high = lax.reduce_precision(squares, 8, 7)
-    spread = jnp.where(marks[:, :, None], gained[:, None, :], 0).reshape(
-        every_row, task_count * width_part
-    )
-    partial = jnp.concatenate(
-        [
-            dot(gained, w_query),
-            dot(gained, key_projection_weight),
-            dot(gained, value_projection_weight),
-            dot(spread, adapter_in.reshape(task_count * width_part, 3 * rank)),
-            squares_high,
-            squares - squares_high,
-            jnp.zeros((every_row, PADDED_WIDTH - 3 * rank - 2), jnp.float32),
-        ],
-        axis=1,
-    ).astype(jnp.bfloat16)
+        up_plane = lax.all_gather(up_pair, "x", axis=0)
+
+    partial = project(
+        inputs,
+        gain,
+        w_query,
+        key_projection_weight,
+        value_projection_weight,
+        adapter_in,
+        tasks,
+        moves,
+        own_rows,
+    )
     with jax.named_scope("sum_plane"):
         by_plane = exchange(partial.reshape(planes, column_rows, -1), PLANE)
 
-    up_line, by_plane = lax.optimization_barrier((up_line, by_plane))
-    with jax.named_scope("up_y_lo"):
-        up_other = lax.ppermute(up_line, "y_lo", [(0, 1), (1, 0)])
     plane_sum = jnp.sum(by_plane.astype(jnp.float32), axis=0)
 
     low_end = 3 * rank
@@ -185,19 +276,17 @@
         row_home, (x * 2 + y_lo) * column_rows, column_rows, 0
     )
 
+    halves = jnp.stack([y_lo, 1 - y_lo])
+    slots = ((jnp.arange(line)[:, None] * 2 + halves[None, :]) * depth + z).reshape(-1)
+    use = column_home[:, None] == slots[None, :]
+    up_flat = up_plane.reshape(planes * rank, base_end)
+
     def lift(block, first, last):
-        total = jnp.zeros((column_rows, last - first), jnp.float32)
         rows = lowrank[:, block * rank : (block + 1) * rank]
-        for matrices, half in ((up_line, y_lo), (up_other, 1 - y_lo)):
-            slots = (jnp.arange(line) * 2 + half) * depth + z
-            use = column_home[:, None] == slots[None, :]
-            spread = jnp.where(use[:, :, None], rows[:, None, :], 0).reshape(
-                column_rows, line * rank
-            )
-            total = total + dot(
-                spread, matrices[:, :, first:last].reshape(line * rank, last - first)
-            )
-        return total
+        spread = jnp.where(use[:, :, None], rows[:, None, :], 0).reshape(
+            column_rows, planes * rank
+        )
+        return dot(spread, up_flat[:, first:last])
 
     lifted = jnp.concatenate(
         [lift(0, 0, query_width), lift(1, query_width, key_end), lift(2, key_end, base_end)],
@@ -268,7 +357,13 @@
             jnp.broadcast_to(mine[None], (lax.axis_size("y_hi"), half, width_part)), "y_hi"
         )
     mine = jnp.sum(mine.astype(jnp.float32), axis=0)
-    finished = lax.dynamic_slice_in_dim(states, core * half, half, 0) + mine
+    residual = (
+        inputs.reshape(steps, groups, own_rows, width_part)
+        .transpose(1, 0, 2, 3)
+        .reshape(every_row, width_part)
+    )
+    residual = lax.dynamic_slice_in_dim(residual, core * half, half, 0)
+    finished = residual.astype(jnp.float32) + mine
     with jax.named_scope("gather_core"):
         finished = lax.all_gather(finished.astype(jnp.bfloat16), "core", axis=0, tiled=True)
     return (

time: 150 us -> 167 us (1.11)
  waiting for transfers between devices: 47.1 us -> 62.8 us
  blocking collectives: 37 us -> 22.3 us
  between operations: 0.49 us -> 13.8 us
  Pallas kernels: 0 us -> 4.15 us
  matrix products: 9.49 us -> 6.29 us
    all_to_all x2 -> x1, blocking collectives: 25.3 us -> 10.4 us  [exchange(): return lax.all_to_all(blocks, axes, 0, 0, tiled=True)]
    all_gather x0 -> x1, waiting for transfers between devices: none -> 12.1 us  [on_device(): up_plane = lax.all_gather(up_pair, 'x', axis=0)]
    ppermute x1, waiting for transfers between devices: 5.18 us -> 14 us  [on_device(): up_pair = jnp.stack([up, lax.ppermute(up, 'y_lo', [(0, 1), (1, 0)])])]
    all_to_all x5, waiting for transfers between devices: 42 us -> 36.7 us  [exchange(): return lax.all_to_all(blocks, axes, 0, 0, tiled=True)]
    unnamed x35 -> x45, local copies, waits for them, and re-layouts: 2.53 us -> 7.28 us
    pallas_call x0 -> x1, Pallas kernels: none -> 4.15 us  [project(): pl.pallas_call(functools.partial(project_kernel, own_rows), out_shape=jax...]
    concatenate x1 -> x0, local copies, waits for them, and re-layouts: 3.34 us -> none  [on_device(): jnp.concatenate([dot(gained, w_query), dot(gained, key_projection_weight)...]
    dot_general x12 -> x5, matrix products: 6.61 us -> 4.46 us  [dot(): return jnp.dot(left, right, preferred_element_type=jnp.float32)]
  transfers between devices with their start and end apart: 6 -> 7, of which waited for: 5 -> 6; matrix products, arithmetic and copies ran while one was open for 8% -> 3% of each run, Pallas kernels for 0% -> 0%
where the time goes in v3:
time: 167 us; the launch traced here: 166 us
  waiting for transfers between devices  62.8 us (38%)
  starting transfers between devices  40.5 us (24%)
  blocking collectives  22.3 us (13%)
  between operations  13.8 us (8%)
  local copies, waits for them, and re-layouts  12.3 us (7%)
  matrix products  6.29 us (4%)
  Pallas kernels  4.15 us (2%)
  other arithmetic  3.69 us (2%)
    all_to_all x5, starting transfers between devices, exchange(): return lax.all_to_all(blocks, axes, 0, 0, tiled=True)  37.1 us
    all_to_all x5, waiting for transfers between devices, exchange(): return lax.all_to_all(blocks, axes, 0, 0, tiled=True)  36.7 us
    ppermute x1, waiting for transfers between devices, on_device(): up_pair = jnp.stack([up, lax.ppermute(up, 'y_lo', [(0, 1), (1, 0)])])  14 us
    all_gather x1, waiting for transfers between devices, on_device(): up_plane = lax.all_gather(up_pair, 'x', axis=0)  12.1 us
    all_to_all x1, blocking collectives, exchange(): return lax.all_to_all(blocks, axes, 0, 0, tiled=True)  10.4 us
    all_gather x1, blocking collectives, on_device(): pair = lax.all_gather(mixed, 'core', axis=0)  7.55 us
    unnamed x45, local copies, waits for them, and re-layouts  7.28 us
    dot_general x5, matrix products, dot(): return jnp.dot(left, right, preferred_element_type=jnp.float32)  4.46 us
  transfers between devices with their start and end apart: 7, of which 6 were waited for; matrix products, arithmetic and copies ran while one was open for 3% of the time, Pallas kernels for 0%

profile of v3, /device:TPU:1, one launch (start us, length us, event | category | flops | bytes accessed | tf_op | source)
XLA Modules:
  0.0 165.8 jit_solution(4224021297351371884)
XLA Ops:
  6.5 1.0 copy-done.1
  7.5 1.0 copy-done.3
  8.5 0.9 copy-done.4
  13.0 4.1 %shard_map.163 = bf16[512,1536]{1,0:T(8,128)(2,1)} custom-call(bf16[4,128,128]{2,1,0:T(8,128)(2,1)S(1)} %copy-done.1, f32[1,128]{1,0:T(1,128)S(1)} %bitcast.105, bf16[128,1024]{1,0:T(8,128)(2,1)S(1)} %copy-done.4, bf16[128,128]{1,0:T(8,128)(2,1)S(1)} %copy-done.5, bf16[128,128]{1,0:T(8,128)(2,1)S(1)} %copy-done.6, bf16[8,192,128]{2,1,0:T(8,128)(2,1)S(1)} %bitcast.102, ...), custom_call_target="tpu_custom_call" | custom-call | flops 436207616 | bytes 3000000 | tf_op jit(solution)/shard_map/pallas_call | solution.py:125
  17.2 6.0 %all-to-all-start = ((bf16[8,64,1536]{2,1,0:T(8,128)(2,1)}), bf16[8,64,1536]{2,1,0:T(8,128)(2,1)S(1)}, u32[]{:S(2)}, u32[]{:S(2)}) async-start(bf16[8,64,1536]{2,1,0:T(8,128)(2,1)} %bitcast.7), calls=%async_computation | async-start | bytes 3145728 | tf_op jit(solution)/shard_map/sum_plane/all_to_all | solution.py:20
  23.3 3.3 %collective-permute-start = (bf16[64,1280]{1,0:T(8,128)(2,1)S(1)}, bf16[64,1280]{1,0:T(8,128)(2,1)S(1)}, u32[]{:S(2)}, u32[]{:S(2)}) collective-permute-start(bf16[64,1280]{1,0:T(8,128)(2,1)S(1)} %get-tuple-element.8), channel_id=1, source_target_pairs={{0,64},{64,0},{1,65},{65,1},{2,66},{66,2},{3,67},{67,3},{4,68},{68... | collective-permute-start | bytes 491528 | tf_op jit(solution)/shard_map/up_y_lo/ppermute | solution.py:230
  27.6 14.0 %collective-permute-done = bf16[64,1280]{1,0:T(8,128)(2,1)S(1)} collective-permute-done((bf16[64,1280]{1,0:T(8,128)(2,1)S(1)}, bf16[64,1280]{1,0:T(8,128)(2,1)S(1)}, u32[]{:S(2)}, u32[]{:S(2)}) %collective-permute-start) | collective-permute-done | bytes 163872 | tf_op jit(solution)/shard_map/up_y_lo/ppermute | solution.py:230
  41.6 0.8 pad_maximum_fusion
  44.0 14.1 %all-to-all-start.1 = ((bf16[8,64,256]{2,1,0:T(8,128)(2,1)}), bf16[8,64,256]{2,1,0:T(8,128)(2,1)S(1)}, u32[]{:S(2)}, u32[]{:S(2)}) async-start(bf16[8,64,256]{2,1,0:T(8,128)(2,1)} %broadcast_in_dim.183), calls=%async_computation.1 | async-start | bytes 524288 | tf_op jit(solution)/shard_map/sum_low/all_to_all | solution.py:20
  58.5 8.9 %all-to-all-done.1 = bf16[8,64,256]{2,1,0:T(8,128)(2,1)S(1)} async-done(((bf16[8,64,256]{2,1,0:T(8,128)(2,1)}), bf16[8,64,256]{2,1,0:T(8,128)(2,1)S(1)}, u32[]{:S(2)}, u32[]{:S(2)}) %all-to-all-start.1) | async-done | bytes 262176 | tf_op jit(solution)/shard_map/sum_low/all_to_all | solution.py:20
  68.3 12.1 %all-gather.4.cloned.1.call-done = bf16[8,64,1280]{2,1,0:T(8,128)(2,1)} async-done(((bf16[2,64,1280]{2,1,0:T(8,128)(2,1)}), bf16[8,64,1280]{2,1,0:T(8,128)(2,1)}) %all-gather.4.cloned.1.call-update) | async-done | bytes 1310736 | tf_op jit(solution)/shard_map/up_x/all_gather | solution.py:232
  80.4 1.5 fusion.4
  81.9 1.1 fusion.18
  83.2 1.1 fusion.16
  85.0 7.1 %all-to-all-start.2 = ((bf16[8,8,1280]{2,1,0:T(8,128)(2,1)}), bf16[8,8,1280]{2,1,0:T(8,128)(2,1)S(1)}, u32[]{:S(2)}, u32[]{:S(2)}) async-start(bf16[8,8,1280]{2,1,0:T(8,128)(2,1)} %fusion.14), calls=%async_computation.2 | async-start | bytes 327680 | tf_op jit(solution)/shard_map/sum_z/all_to_all | solution.py:20
  92.2 8.3 %all-to-all-done.2 = bf16[8,8,1280]{2,1,0:T(8,128)(2,1)S(1)} async-done(((bf16[8,8,1280]{2,1,0:T(8,128)(2,1)}), bf16[8,8,1280]{2,1,0:T(8,128)(2,1)S(1)}, u32[]{:S(2)}, u32[]{:S(2)}) %all-to-all-start.2) | async-done | bytes 163872 | tf_op jit(solution)/shard_map/sum_z/all_to_all | solution.py:20
  102.2 10.4 %all_to_all.30 = bf16[8,8,1024]{2,1,0:T(8,128)(2,1)S(1)} all-to-all(bf16[8,8,1024]{2,1,0:T(8,128)(2,1)S(1)} %broadcast_in_dim.200), channel_id=1, replica_groups=mesh['x'=4,'y_lo'=2,'z'=8,'y_hi'=4,'core'=2] {'z'}, dimensions={0} | all-to-all | bytes 262144 | tf_op jit(solution)/shard_map/gather_z/all_to_all | solution.py:20
  112.6 1.1 broadcast_in_dim.202
  113.7 4.2 %all-to-all-start.4 = ((bf16[8,64,1024]{2,1,0:T(8,128)(2,1)}), bf16[8,64,1024]{2,1,0:T(8,128)(2,1)S(1)}, u32[]{:S(2)}, u32[]{:S(2)}) async-start(bf16[8,64,1024]{2,1,0:T(8,128)(2,1)} %broadcast_in_dim.202), calls=%async_computation.4 | async-start | bytes 2097152 | tf_op jit(solution)/shard_map/gather_plane/all_to_all | solution.py:20
  118.0 11.0 %all-to-all-done.4 = bf16[8,64,1024]{2,1,0:T(8,128)(2,1)S(1)} async-done(((bf16[8,64,1024]{2,1,0:T(8,128)(2,1)}), bf16[8,64,1024]{2,1,0:T(8,128)(2,1)S(1)}, u32[]{:S(2)}, u32[]{:S(2)}) %all-to-all-start.4) | async-done | bytes 1048608 | tf_op jit(solution)/shard_map/gather_plane/all_to_all | solution.py:20
  131.2 7.5 %all-gather.1 = bf16[1024,128]{1,0:T(8,128)(2,1)S(1)} all-gather(bf16[512,128]{1,0:T(8,128)(2,1)S(1)} %fusion.1), channel_id=3, replica_groups=mesh['x'=4,'y_lo'=2,'z'=8,'y_hi'=4,'core'=2] {'core'}, dimensions={0}, use_global_device_ids=true | all-gather | bytes 393216 | tf_op jit(solution)/shard_map/sum_core/all_gather | solution.py:352
  139.5 5.7 %all-to-all-start.5 = ((bf16[4,256,128]{2,1,0:T(8,128)(2,1)}), bf16[4,256,128]{2,1,0:T(8,128)(2,1)S(1)}, u32[]{:S(2)}, u32[]{:S(2)}) async-start(bf16[4,256,128]{2,1,0:T(8,128)(2,1)} %broadcast_in_dim.206), calls=%async_computation.5 | async-start | bytes 524288 | tf_op jit(solution)/shard_map/sum_y_hi/all_to_all | solution.py:20
  145.3 8.5 %all-to-all-done.5 = bf16[4,256,128]{2,1,0:T(8,128)(2,1)S(1)} async-done(((bf16[4,256,128]{2,1,0:T(8,128)(2,1)}), bf16[4,256,128]{2,1,0:T(8,128)(2,1)S(1)}, u32[]{:S(2)}, u32[]{:S(2)}) %all-to-all-start.5) | async-done | bytes 262176 | tf_op jit(solution)/shard_map/sum_y_hi/all_to_all | solution.py:20
  153.9 4.3 %all_gather.19 = bf16[512,128]{1,0:T(8,128)(2,1)S(1)} all-gather(bf16[256,128]{1,0:T(8,128)(2,1)S(1)} %add_convert_fusion), channel_id=1, replica_groups=mesh['x'=4,'y_lo'=2,'z'=8,'y_hi'=4,'core'=2] {'core'}, dimensions={0}, use_global_device_ids=true | all-gather | bytes 196608 | tf_op jit(solution)/shard_map/gather_core/all_gather | solution.py:368
  (118 shorter events, 13.8 us)
Async XLA Ops:
  6.5 122.4 %copy-start = (bf16[8,1024,64]{1,2,0:T(8,128)(2,1)S(1)}, bf16[8,1024,64]{1,2,0:T(8,128)(2,1)}, u32[]{:S(2)}) copy-start(bf16[8,1024,64]{1,2,0:T(8,128)(2,1)} %param.24) | copy-start | bytes 3145732
  6.5 1.0 copy-start.1
  7.5 1.0 copy-start.3
  8.5 0.9 copy-start.4
  9.5 0.8 copy-start.5
  10.2 0.8 copy-start.6
  17.1 6.1 %copy-start.16 = (bf16[1,64,2,128]{3,2,1,0:T(2,128)(2,1)S(1)}, bf16[1,64,2,128]{3,2,1,0:T(2,128)(2,1)}, u32[]{:S(2)}) copy-start(bf16[1,64,2,128]{3,2,1,0:T(2,128)(2,1)} %param.27) | copy-start | bytes 98308
  17.1 6.1 %copy-start.14 = (bf16[1,64,1024]{2,1,0:T(8,128)(2,1)S(1)}, bf16[1,64,1024]{2,1,0:T(8,128)(2,1)}, u32[]{:S(2)}) copy-start(bf16[1,64,1024]{2,1,0:T(8,128)(2,1)} %param.26) | copy-start | bytes 393220
  17.1 9.5 %copy-start.10 = (s32[128]{0:T(128)S(1)}, s32[128]{0:T(128)}, u32[]{:S(2)}) copy-start(s32[128]{0:T(128)} %param.30) | copy-start | bytes 1540
  17.1 9.6 %copy-start.8 = (s32[16,2]{0,1:T(2,128)S(1)}, s32[16,2]{0,1:T(2,128)}, u32[]{:S(2)}) copy-start(s32[16,2]{0,1:T(2,128)} %param.32) | copy-start | bytes 388
  17.1 10.2 %copy-start.17 = (s32[2]{0:T(128)S(1)}, s32[2]{0:T(128)}, u32[]{:S(2)}) copy-start(s32[2]{0:T(128)} %param.33) | copy-start | bytes 28
  17.2 25.2 %all-to-all-start = ((bf16[8,64,1536]{2,1,0:T(8,128)(2,1)}), bf16[8,64,1536]{2,1,0:T(8,128)(2,1)S(1)}, u32[]{:S(2)}, u32[]{:S(2)}) async-start(bf16[8,64,1536]{2,1,0:T(8,128)(2,1)} %bitcast.7), calls=%async_computation | async-start | bytes 3145728 | tf_op jit(solution)/shard_map/sum_plane/all_to_all | solution.py:20
  23.2 57.2 %all-gather.4.cloned.1.call-start = ((), (), s32[]{:S(2)}) async-start(), calls=%async_computation.6 | async-start | bytes 1638400 | tf_op jit(solution)/shard_map/up_x/all_gather | solution.py:232
  23.3 18.3 %collective-permute-start = (bf16[64,1280]{1,0:T(8,128)(2,1)S(1)}, bf16[64,1280]{1,0:T(8,128)(2,1)S(1)}, u32[]{:S(2)}, u32[]{:S(2)}) collective-permute-start(bf16[64,1280]{1,0:T(8,128)(2,1)S(1)} %get-tuple-element.8), channel_id=1, source_target_pairs={{0,64},{64,0},{1,65},{65,1},{2,66},{66,2},{3,67},{67,3},{4,68},{68... | collective-permute-start | bytes 491528 | tf_op jit(solution)/shard_map/up_y_lo/ppermute | solution.py:230
  42.6 15.5 %copy-start.18 = (s32[8]{0:T(128)S(1)}, s32[8]{0:T(128)}, u32[]{:S(2)}) copy-start(s32[8]{0:T(128)} %param.31) | copy-start | bytes 100
  44.0 23.4 %all-to-all-start.1 = ((bf16[8,64,256]{2,1,0:T(8,128)(2,1)}), bf16[8,64,256]{2,1,0:T(8,128)(2,1)S(1)}, u32[]{:S(2)}, u32[]{:S(2)}) async-start(bf16[8,64,256]{2,1,0:T(8,128)(2,1)} %broadcast_in_dim.183), calls=%async_computation.1 | async-start | bytes 524288 | tf_op jit(solution)/shard_map/sum_low/all_to_all | solution.py:20
  81.9 18.9 %copy-start.12 = (bf16[2,1,1024,128]{3,2,1,0:T(8,128)(2,1)S(1)}, bf16[2,1,1024,128]{3,2,1,0:T(8,128)(2,1)}, u32[]{:S(2)}) copy-start(bf16[2,1,1024,128]{3,2,1,0:T(8,128)(2,1)} %param.28) | copy-start | bytes 1572868
  84.2 17.4 %copy-start.19 = (bf16[2,1,1024,128]{3,2,1,0:T(8,128)(2,1)S(1)}, bf16[2,1,1024,128]{3,2,1,0:T(8,128)(2,1)}, u32[]{:S(2)}) copy-start(bf16[2,1,1024,128]{3,2,1,0:T(8,128)(2,1)} %param.29) | copy-start | bytes 1572868
  85.0 15.5 %all-to-all-start.2 = ((bf16[8,8,1280]{2,1,0:T(8,128)(2,1)}), bf16[8,8,1280]{2,1,0:T(8,128)(2,1)S(1)}, u32[]{:S(2)}, u32[]{:S(2)}) async-start(bf16[8,8,1280]{2,1,0:T(8,128)(2,1)} %fusion.14), calls=%async_computation.2 | async-start | bytes 327680 | tf_op jit(solution)/shard_map/sum_z/all_to_all | solution.py:20
  113.7 15.3 %all-to-all-start.4 = ((bf16[8,64,1024]{2,1,0:T(8,128)(2,1)}), bf16[8,64,1024]{2,1,0:T(8,128)(2,1)S(1)}, u32[]{:S(2)}, u32[]{:S(2)}) async-start(bf16[8,64,1024]{2,1,0:T(8,128)(2,1)} %broadcast_in_dim.202), calls=%async_computation.4 | async-start | bytes 2097152 | tf_op jit(solution)/shard_map/gather_plane/all_to_all | solution.py:20
  129.0 0.9 copy-start.15
  129.7 1.0 copy-start.13
  131.1 14.0 %copy-start.2 = (bf16[4,128,128]{2,1,0:T(8,128)(2,1)S(1)}, bf16[4,128,128]{2,1,0:T(8,128)(2,1)}, u32[]{:S(2)}) copy-start(bf16[4,128,128]{2,1,0:T(8,128)(2,1)} %inputs_ref.1) | copy-start | bytes 393220
  139.5 14.3 %all-to-all-start.5 = ((bf16[4,256,128]{2,1,0:T(8,128)(2,1)}), bf16[4,256,128]{2,1,0:T(8,128)(2,1)S(1)}, u32[]{:S(2)}, u32[]{:S(2)}) async-start(bf16[4,256,128]{2,1,0:T(8,128)(2,1)} %broadcast_in_dim.206), calls=%async_computation.5 | async-start | bytes 524288 | tf_op jit(solution)/shard_map/sum_y_hi/all_to_all | solution.py:20
  (3 other events, 2.0 us)
Sparse Core Ops, SparseCore 0:
  42.5 37.8 all-gather.3

commit v4 on v3

--- a/solution.py
+++ b/solution.py
@@ -50,6 +50,12 @@
     tasks_ref,
     moves_ref,
     out_ref,
+    held_inputs,
+    held_query,
+    held_key,
+    held_value,
+    held_adapter,
+    arrived,
 ):
     steps, all_rows, width = inputs_ref.shape
     every_row = steps * all_rows
@@ -59,7 +65,22 @@
     low = adapter_ref.shape[1]
     base_end = query_width + 2 * head_dim
     block = 128
-    gathered = inputs_ref[...].reshape(every_row, width)
+    pairs = (
+        (inputs_ref, held_inputs),
+        (query_ref, held_query),
+        (key_ref, held_key),
+        (value_ref, held_value),
+        (adapter_ref, held_adapter),
+    )
+    copies = [
+        pltpu.make_async_copy(source, held, arrived.at[number])
+        for number, (source, held) in enumerate(pairs)
+    ]
+    for copy in copies:
+        copy.start()
+    for copy in copies:
+        copy.wait()
+    gathered = held_inputs[...].reshape(every_row, width)
 
     @pl.loop(0, every_row // block)
     def _(index):
@@ -92,11 +113,11 @@
         late = row_of(1) % per_group >= per_group // 2
         task = jnp.where(jnp.logical_and(late, moved), chosen, task)
 
-        out_ref[rows, 0:query_width] = dot(gained, query_ref[...]).astype(jnp.bfloat16)
-        out_ref[rows, query_width : query_width + head_dim] = dot(gained, key_ref[...]).astype(
+        out_ref[rows, 0:query_width] = dot(gained, held_query[...]).astype(jnp.bfloat16)
+        out_ref[rows, query_width : query_width + head_dim] = dot(gained, held_key[...]).astype(
             jnp.bfloat16
         )
-        out_ref[rows, query_width + head_dim : base_end] = dot(gained, value_ref[...]).astype(
+        out_ref[rows, query_width + head_dim : base_end] = dot(gained, held_value[...]).astype(
             jnp.bfloat16
         )
         total = jnp.zeros((block, low), jnp.float32)
@@ -104,7 +125,7 @@
             mine = jnp.where(task == adapter, gained, jnp.zeros_like(gained))
             total = total + lax.dot_general(
                 mine,
-                adapter_ref[adapter],
+                held_adapter[adapter],
                 (((1,), (1,)), ((), ())),
                 preferred_element_type=jnp.float32,
             )
@@ -121,10 +142,29 @@
 
 def project(inputs, gain, w_query, w_key, w_value, adapter_in, tasks, moves, own_rows):
     steps, all_rows, width = inputs.shape
+    down = jnp.swapaxes(adapter_in, 1, 2)
     columns = w_query.shape[1] + w_key.shape[1] + w_value.shape[1] + PADDED_WIDTH
     return pl.pallas_call(
         functools.partial(project_kernel, own_rows),
         out_shape=jax.ShapeDtypeStruct((steps * all_rows, columns), jnp.bfloat16),
+        in_specs=[
+            pl.BlockSpec(memory_space=pl.ANY),
+            pl.BlockSpec(memory_space=pltpu.VMEM),
+            pl.BlockSpec(memory_space=pl.ANY),
+            pl.BlockSpec(memory_space=pl.ANY),
+            pl.BlockSpec(memory_space=pl.ANY),
+            pl.BlockSpec(memory_space=pl.ANY),
+            pl.BlockSpec(memory_space=pltpu.VMEM),
+            pl.BlockSpec(memory_space=pltpu.VMEM),
+        ],
+        scratch_shapes=[
+            pltpu.VMEM(inputs.shape, jnp.bfloat16),
+            pltpu.VMEM(w_query.shape, jnp.bfloat16),
+            pltpu.VMEM(w_key.shape, jnp.bfloat16),
+            pltpu.VMEM(w_value.shape, jnp.bfloat16),
+            pltpu.VMEM(down.shape, jnp.bfloat16),
+            pltpu.SemaphoreType.DMA((5,)),
+        ],
         compiler_params=pltpu.CompilerParams(vmem_limit_bytes=32 * 1024 * 1024),
         cost_estimate=pl.CostEstimate(
             flops=2 * steps * all_rows * width * 3328, bytes_accessed=3_000_000, transcendentals=0
@@ -135,7 +175,7 @@
         w_query,
         w_key,
         w_value,
-        jnp.swapaxes(adapter_in, 1, 2),
+        down,
         tasks[None, :],
         moves.T,
     )
@@ -206,7 +246,6 @@
     per_group = steps * own_rows
     every_row = groups * per_group
     model_width = width_part * groups
-    line = lax.axis_size("x")
     column_rows = depth * per_group
 
     group_tasks = tasks.reshape(groups, own_rows)
@@ -226,10 +265,8 @@
         ],
         axis=1,
     )
-    with jax.named_scope("up_y_lo"):
-        up_pair = jnp.stack([up, lax.ppermute(up, "y_lo", [(0, 1), (1, 0)])])
-    with jax.named_scope("up_x"):
-        up_plane = lax.all_gather(up_pair, "x", axis=0)
+    with jax.named_scope("up_plane"):
+        up_plane = exchange(jnp.broadcast_to(up[None], (planes, rank, base_end)), PLANE)
 
     partial = project(
         inputs,
@@ -276,8 +313,7 @@
         row_home, (x * 2 + y_lo) * column_rows, column_rows, 0
     )
 
-    halves = jnp.stack([y_lo, 1 - y_lo])
-    slots = ((jnp.arange(line)[:, None] * 2 + halves[None, :]) * depth + z).reshape(-1)
+    slots = jnp.arange(planes) * depth + z
     use = column_home[:, None] == slots[None, :]
     up_flat = up_plane.reshape(planes * rank, base_end)
 

time: 167 us -> 159 us (0.952)
  between operations: 13.8 us -> 0.44 us
  local copies, waits for them, and re-layouts: 12.3 us -> 16 us
  waiting for transfers between devices: 62.8 us -> 66.2 us
  starting transfers between devices: 40.5 us -> 38.5 us
    all_to_all x5 -> x6, waiting for transfers between devices: 36.7 us -> 66.2 us  [exchange(): return lax.all_to_all(blocks, axes, 0, 0, tiled=True)]
    ppermute x1 -> x0, waiting for transfers between devices: 14 us -> none  [on_device(): up_pair = jnp.stack([up, lax.ppermute(up, 'y_lo', [(0, 1), (1, 0)])])]
    all_gather x1 -> x0, waiting for transfers between devices: 12.1 us -> none  [on_device(): up_plane = lax.all_gather(up_pair, 'x', axis=0)]
    ppermute x1 -> x0, starting transfers between devices: 3.32 us -> none  [on_device(): up_pair = jnp.stack([up, lax.ppermute(up, 'y_lo', [(0, 1), (1, 0)])])]
    select_n x3, local copies, waits for them, and re-layouts: 0.43 us -> 2.6 us  [lift(): jnp.where(use[:, :, None], rows[:, None, :], 0)]
    all_to_all x5 -> x6, starting transfers between devices: 37.1 us -> 38.5 us  [exchange(): return lax.all_to_all(blocks, axes, 0, 0, tiled=True)]
    unnamed x45 -> x49, local copies, waits for them, and re-layouts: 7.28 us -> 7.83 us
  transfers between devices with their start and end apart: 7 -> 6, of which waited for: 6 -> 6; matrix products, arithmetic and copies ran while one was open for 3% -> 2% of each run, Pallas kernels for 0% -> 0%
where the time goes in v4:
time: 159 us; the launch traced here: 158 us
  waiting for transfers between devices  66.2 us (42%)
  starting transfers between devices  38.5 us (24%)
  blocking collectives  22.4 us (14%)
  local copies, waits for them, and re-layouts  16 us (10%)
  other arithmetic  4.75 us (3%)
  matrix products  4.66 us (3%)
  Pallas kernels  4.59 us (3%)
    all_to_all x6, waiting for transfers between devices, exchange(): return lax.all_to_all(blocks, axes, 0, 0, tiled=True)  66.2 us
    all_to_all x6, starting transfers between devices, exchange(): return lax.all_to_all(blocks, axes, 0, 0, tiled=True)  38.5 us
    all_to_all x1, blocking collectives, exchange(): return lax.all_to_all(blocks, axes, 0, 0, tiled=True)  10.3 us
    all_gather x1, blocking collectives, on_device(): pair = lax.all_gather(mixed, 'core', axis=0)  7.85 us
    unnamed x49, local copies, waits for them, and re-layouts  7.83 us
    pallas_call x1, Pallas kernels, project(): pl.pallas_call(functools.partial(project_kernel, own_rows), out_shape=jax...  4.59 us
    all_gather x1, blocking collectives, on_device(): lax.all_gather(finished.astype(jnp.bfloat16), 'core', axis=0, tiled=True)  4.23 us
  transfers between devices with their start and end apart: 6, of which 6 were waited for; matrix products, arithmetic and copies ran while one was open for 2% of the time, Pallas kernels for 0%

profile of v4, /device:TPU:1, one launch (start us, length us, event | category | flops | bytes accessed | tf_op | source)
XLA Modules:
  0.0 157.6 jit_solution(6857238591984882557)
XLA Ops:
  0.0 1.0 copy-done.1
  1.0 1.0 copy-done.3
  2.0 0.9 copy-done.4
  6.5 4.6 %shard_map.163 = bf16[512,1536]{1,0:T(8,128)(2,1)} custom-call(bf16[4,128,128]{2,1,0:T(8,128)(2,1)S(1)} %copy-done.1, f32[1,128]{1,0:T(1,128)S(1)} %bitcast.100, bf16[128,1024]{1,0:T(8,128)(2,1)S(1)} %copy-done.4, bf16[128,128]{1,0:T(8,128)(2,1)S(1)} %copy-done.5, bf16[128,128]{1,0:T(8,128)(2,1)S(1)} %copy-done.6, bf16[8,192,128]{2,1,0:T(8,128)(2,1)S(1)} %bitcast.97, ...), custom_call_target="tpu_custom_call" | custom-call | flops 436207616 | bytes 3000000 | tf_op jit(solution)/shard_map/pallas_call | solution.py:147
  11.1 6.0 %all-to-all-start = ((bf16[8,64,1536]{2,1,0:T(8,128)(2,1)}), bf16[8,64,1536]{2,1,0:T(8,128)(2,1)S(1)}, u32[]{:S(2)}, u32[]{:S(2)}) async-start(bf16[8,64,1536]{2,1,0:T(8,128)(2,1)} %bitcast.7), calls=%async_computation | async-start | bytes 3145728 | tf_op jit(solution)/shard_map/sum_plane/all_to_all | solution.py:20
  17.3 16.7 %all-to-all-done = bf16[8,64,1536]{2,1,0:T(8,128)(2,1)S(1)} async-done(((bf16[8,64,1536]{2,1,0:T(8,128)(2,1)}), bf16[8,64,1536]{2,1,0:T(8,128)(2,1)S(1)}, u32[]{:S(2)}, u32[]{:S(2)}) %all-to-all-start) | async-done | bytes 1572896 | tf_op jit(solution)/shard_map/sum_plane/all_to_all | solution.py:20
  35.6 13.6 %all-to-all-start.1 = ((bf16[8,64,256]{2,1,0:T(8,128)(2,1)}), bf16[8,64,256]{2,1,0:T(8,128)(2,1)S(1)}, u32[]{:S(2)}, u32[]{:S(2)}) async-start(bf16[8,64,256]{2,1,0:T(8,128)(2,1)} %broadcast_in_dim.188), calls=%async_computation.1 | async-start | bytes 524288 | tf_op jit(solution)/shard_map/sum_low/all_to_all | solution.py:20
  49.4 9.1 %all-to-all-done.1 = bf16[8,64,256]{2,1,0:T(8,128)(2,1)S(1)} async-done(((bf16[8,64,256]{2,1,0:T(8,128)(2,1)}), bf16[8,64,256]{2,1,0:T(8,128)(2,1)S(1)}, u32[]{:S(2)}, u32[]{:S(2)}) %all-to-all-start.1) | async-done | bytes 262176 | tf_op jit(solution)/shard_map/sum_low/all_to_all | solution.py:20
  58.5 1.2 broadcast_in_dim.199
  59.7 5.3 %all-to-all-start.2 = ((bf16[8,64,1280]{2,1,0:T(8,128)(2,1)}), bf16[8,64,1280]{2,1,0:T(8,128)(2,1)S(1)}, u32[]{:S(2)}, u32[]{:S(2)}) async-start(bf16[8,64,1280]{2,1,0:T(8,128)(2,1)} %broadcast_in_dim.199), calls=%async_computation.2 | async-start | bytes 2621440 | tf_op jit(solution)/shard_map/up_plane/all_to_all | solution.py:20
  68.5 12.8 %all-to-all-done.2 = bf16[8,64,1280]{2,1,0:T(8,128)(2,1)S(1)} async-done(((bf16[8,64,1280]{2,1,0:T(8,128)(2,1)}), bf16[8,64,1280]{2,1,0:T(8,128)(2,1)S(1)}, u32[]{:S(2)}, u32[]{:S(2)}) %all-to-all-start.2) | async-done | bytes 1310752 | tf_op jit(solution)/shard_map/up_plane/all_to_all | solution.py:20
  82.8 1.7 %select_n.86 = bf16[64,512]{1,0:T(8,128)(2,1)} reshape(bf16[64,8,64]{2,1,0:T(8,128)(2,1)} %get-tuple-element.13) | data formatting | bytes 131072 | tf_op jit(solution)/shard_map/jit(_where)/select_n | solution.py:322
  84.5 1.0 fusion.18
  85.5 1.6 fusion.14
  87.1 3.4 %all-to-all-start.3 = ((bf16[8,8,1280]{2,1,0:T(8,128)(2,1)}), bf16[8,8,1280]{2,1,0:T(8,128)(2,1)S(1)}, u32[]{:S(2)}, u32[]{:S(2)}) async-start(bf16[8,8,1280]{2,1,0:T(8,128)(2,1)} %fusion.14), calls=%async_computation.3 | async-start | bytes 327680 | tf_op jit(solution)/shard_map/sum_z/all_to_all | solution.py:20
  90.6 8.2 %all-to-all-done.3 = bf16[8,8,1280]{2,1,0:T(8,128)(2,1)S(1)} async-done(((bf16[8,8,1280]{2,1,0:T(8,128)(2,1)}), bf16[8,8,1280]{2,1,0:T(8,128)(2,1)S(1)}, u32[]{:S(2)}, u32[]{:S(2)}) %all-to-all-start.3) | async-done | bytes 163872 | tf_op jit(solution)/shard_map/sum_z/all_to_all | solution.py:20
  100.5 10.3 %all_to_all.35 = bf16[8,8,1024]{2,1,0:T(8,128)(2,1)S(1)} all-to-all(bf16[8,8,1024]{2,1,0:T(8,128)(2,1)S(1)} %broadcast_in_dim.206), channel_id=1, replica_groups=mesh['x'=4,'y_lo'=2,'z'=8,'y_hi'=4,'core'=2] {'z'}, dimensions={0} | all-to-all | bytes 262144 | tf_op jit(solution)/shard_map/gather_z/all_to_all | solution.py:20
  110.8 1.1 broadcast_in_dim.208
  111.9 4.3 %all-to-all-start.5 = ((bf16[8,64,1024]{2,1,0:T(8,128)(2,1)}), bf16[8,64,1024]{2,1,0:T(8,128)(2,1)S(1)}, u32[]{:S(2)}, u32[]{:S(2)}) async-start(bf16[8,64,1024]{2,1,0:T(8,128)(2,1)} %broadcast_in_dim.208), calls=%async_computation.5 | async-start | bytes 2097152 | tf_op jit(solution)/shard_map/gather_plane/all_to_all | solution.py:20
  116.3 10.9 %all-to-all-done.5 = bf16[8,64,1024]{2,1,0:T(8,128)(2,1)S(1)} async-done(((bf16[8,64,1024]{2,1,0:T(8,128)(2,1)}), bf16[8,64,1024]{2,1,0:T(8,128)(2,1)S(1)}, u32[]{:S(2)}, u32[]{:S(2)}) %all-to-all-start.5) | async-done | bytes 1048608 | tf_op jit(solution)/shard_map/gather_plane/all_to_all | solution.py:20
  129.3 7.9 %all-gather = bf16[1024,128]{1,0:T(8,128)(2,1)S(1)} all-gather(bf16[512,128]{1,0:T(8,128)(2,1)S(1)} %fusion.1), channel_id=2, replica_groups=mesh['x'=4,'y_lo'=2,'z'=8,'y_hi'=4,'core'=2] {'core'}, dimensions={0}, use_global_device_ids=true | all-gather | bytes 393216 | tf_op jit(solution)/shard_map/sum_core/all_gather | solution.py:388
  137.9 5.9 %all-to-all-start.6 = ((bf16[4,256,128]{2,1,0:T(8,128)(2,1)}), bf16[4,256,128]{2,1,0:T(8,128)(2,1)S(1)}, u32[]{:S(2)}, u32[]{:S(2)}) async-start(bf16[4,256,128]{2,1,0:T(8,128)(2,1)} %broadcast_in_dim.212), calls=%async_computation.6 | async-start | bytes 524288 | tf_op jit(solution)/shard_map/sum_y_hi/all_to_all | solution.py:20
  143.9 8.6 %all-to-all-done.6 = bf16[4,256,128]{2,1,0:T(8,128)(2,1)S(1)} async-done(((bf16[4,256,128]{2,1,0:T(8,128)(2,1)}), bf16[4,256,128]{2,1,0:T(8,128)(2,1)S(1)}, u32[]{:S(2)}, u32[]{:S(2)}) %all-to-all-start.6) | async-done | bytes 262176 | tf_op jit(solution)/shard_map/sum_y_hi/all_to_all | solution.py:20
  152.6 4.2 %all_gather.11 = bf16[512,128]{1,0:T(8,128)(2,1)S(1)} all-gather(bf16[256,128]{1,0:T(8,128)(2,1)S(1)} %add_convert_fusion), channel_id=1, replica_groups=mesh['x'=4,'y_lo'=2,'z'=8,'y_hi'=4,'core'=2] {'core'}, dimensions={0}, use_global_device_ids=true | all-gather | bytes 196608 | tf_op jit(solution)/shard_map/gather_core/all_gather | solution.py:404
  (116 shorter events, 16.0 us)
Async XLA Ops:
  0.0 127.1 %copy-start = (bf16[8,1024,64]{1,2,0:T(8,128)(2,1)S(1)}, bf16[8,1024,64]{1,2,0:T(8,128)(2,1)}, u32[]{:S(2)}) copy-start(bf16[8,1024,64]{1,2,0:T(8,128)(2,1)} %param.24) | copy-start | bytes 3145732
  0.0 1.0 copy-start.1
  1.0 1.0 copy-start.3
  2.0 0.9 copy-start.4
  2.9 0.8 copy-start.5
  11.1 6.1 %copy-start.10 = (s32[128]{0:T(128)S(1)}, s32[128]{0:T(128)}, u32[]{:S(2)}) copy-start(s32[128]{0:T(128)} %param.30) | copy-start | bytes 1540
  11.1 6.2 %copy-start.17 = (bf16[1,64,2,128]{3,2,1,0:T(2,128)(2,1)S(1)}, bf16[1,64,2,128]{3,2,1,0:T(2,128)(2,1)}, u32[]{:S(2)}) copy-start(bf16[1,64,2,128]{3,2,1,0:T(2,128)(2,1)} %param.27) | copy-start | bytes 98308
  11.1 6.2 %copy-start.8 = (s32[16,2]{0,1:T(2,128)S(1)}, s32[16,2]{0,1:T(2,128)}, u32[]{:S(2)}) copy-start(s32[16,2]{0,1:T(2,128)} %param.32) | copy-start | bytes 388
  11.1 22.9 %all-to-all-start = ((bf16[8,64,1536]{2,1,0:T(8,128)(2,1)}), bf16[8,64,1536]{2,1,0:T(8,128)(2,1)S(1)}, u32[]{:S(2)}, u32[]{:S(2)}) async-start(bf16[8,64,1536]{2,1,0:T(8,128)(2,1)} %bitcast.7), calls=%async_computation | async-start | bytes 3145728 | tf_op jit(solution)/shard_map/sum_plane/all_to_all | solution.py:20
  34.2 15.2 %copy-start.15 = (bf16[1,64,1024]{2,1,0:T(8,128)(2,1)S(1)}, bf16[1,64,1024]{2,1,0:T(8,128)(2,1)}, u32[]{:S(2)}) copy-start(bf16[1,64,1024]{2,1,0:T(8,128)(2,1)} %param.26) | copy-start | bytes 393220
  35.6 22.9 %all-to-all-start.1 = ((bf16[8,64,256]{2,1,0:T(8,128)(2,1)}), bf16[8,64,256]{2,1,0:T(8,128)(2,1)S(1)}, u32[]{:S(2)}, u32[]{:S(2)}) async-start(bf16[8,64,256]{2,1,0:T(8,128)(2,1)} %broadcast_in_dim.188), calls=%async_computation.1 | async-start | bytes 524288 | tf_op jit(solution)/shard_map/sum_low/all_to_all | solution.py:20
  59.7 5.7 %copy-start.18 = (s32[2]{0:T(128)S(1)}, s32[2]{0:T(128)}, u32[]{:S(2)}) copy-start(s32[2]{0:T(128)} %param.33) | copy-start | bytes 28
  59.7 5.8 %copy-start.19 = (s32[8]{0:T(128)S(1)}, s32[8]{0:T(128)}, u32[]{:S(2)}) copy-start(s32[8]{0:T(128)} %param.31) | copy-start | bytes 100
  59.7 21.5 %all-to-all-start.2 = ((bf16[8,64,1280]{2,1,0:T(8,128)(2,1)}), bf16[8,64,1280]{2,1,0:T(8,128)(2,1)S(1)}, u32[]{:S(2)}, u32[]{:S(2)}) async-start(bf16[8,64,1280]{2,1,0:T(8,128)(2,1)} %broadcast_in_dim.199), calls=%async_computation.2 | async-start | bytes 2621440 | tf_op jit(solution)/shard_map/up_plane/all_to_all | solution.py:20
  81.2 0.8 copy-start.13
  82.1 17.0 %copy-start.12 = (bf16[2,1,1024,128]{3,2,1,0:T(8,128)(2,1)S(1)}, bf16[2,1,1024,128]{3,2,1,0:T(8,128)(2,1)}, u32[]{:S(2)}) copy-start(bf16[2,1,1024,128]{3,2,1,0:T(8,128)(2,1)} %param.28) | copy-start | bytes 1572868
  85.5 14.0 %copy-start.21 = (pred[32,4]{0,1:T(4,128)(4,1)S(1)}, pred[32,4]{0,1:T(4,128)(4,1)}, u32[]{:S(2)}) copy-start(pred[32,4]{0,1:T(4,128)(4,1)} %iota_compare_fusion.3) | copy-start | bytes 388
  85.5 14.4 %copy-start.20 = (bf16[2,1,1024,128]{3,2,1,0:T(8,128)(2,1)S(1)}, bf16[2,1,1024,128]{3,2,1,0:T(8,128)(2,1)}, u32[]{:S(2)}) copy-start(bf16[2,1,1024,128]{3,2,1,0:T(8,128)(2,1)} %param.29) | copy-start | bytes 1572868
  87.1 11.7 %all-to-all-start.3 = ((bf16[8,8,1280]{2,1,0:T(8,128)(2,1)}), bf16[8,8,1280]{2,1,0:T(8,128)(2,1)S(1)}, u32[]{:S(2)}, u32[]{:S(2)}) async-start(bf16[8,8,1280]{2,1,0:T(8,128)(2,1)} %fusion.14), calls=%async_computation.3 | async-start | bytes 327680 | tf_op jit(solution)/shard_map/sum_z/all_to_all | solution.py:20
  111.9 15.2 %all-to-all-start.5 = ((bf16[8,64,1024]{2,1,0:T(8,128)(2,1)}), bf16[8,64,1024]{2,1,0:T(8,128)(2,1)S(1)}, u32[]{:S(2)}, u32[]{:S(2)}) async-start(bf16[8,64,1024]{2,1,0:T(8,128)(2,1)} %broadcast_in_dim.208), calls=%async_computation.5 | async-start | bytes 2097152 | tf_op jit(solution)/shard_map/gather_plane/all_to_all | solution.py:20
  127.1 0.9 copy-start.16
  127.9 1.0 copy-start.14
  129.3 14.6 %copy-start.2 = (bf16[4,128,128]{2,1,0:T(8,128)(2,1)S(1)}, bf16[4,128,128]{2,1,0:T(8,128)(2,1)}, u32[]{:S(2)}) copy-start(bf16[4,128,128]{2,1,0:T(8,128)(2,1)} %inputs_ref.1) | copy-start | bytes 393220
  137.9 14.6 %all-to-all-start.6 = ((bf16[4,256,128]{2,1,0:T(8,128)(2,1)}), bf16[4,256,128]{2,1,0:T(8,128)(2,1)S(1)}, u32[]{:S(2)}, u32[]{:S(2)}) async-start(bf16[4,256,128]{2,1,0:T(8,128)(2,1)} %broadcast_in_dim.212), calls=%async_computation.6 | async-start | bytes 524288 | tf_op jit(solution)/shard_map/sum_y_hi/all_to_all | solution.py:20
  (4 other events, 2.7 us)

commit v5 on v4

--- a/solution.py
+++ b/solution.py
@@ -165,7 +165,6 @@
             pltpu.VMEM(down.shape, jnp.bfloat16),
             pltpu.SemaphoreType.DMA((5,)),
         ],
-        compiler_params=pltpu.CompilerParams(vmem_limit_bytes=32 * 1024 * 1024),
         cost_estimate=pl.CostEstimate(
             flops=2 * steps * all_rows * width * 3328, bytes_accessed=3_000_000, transcendentals=0
         ),
@@ -235,6 +234,7 @@
     own_rows = lengths.shape[0]
     groups = all_rows // own_rows
     planes = lax.axis_size(PLANE)
+    line = lax.axis_size("x")
     depth = lax.axis_size("z")
     task_count = homes.shape[0]
     rank = adapter_out.shape[1]
@@ -258,16 +258,6 @@
     marks = active[:, None] == jnp.arange(task_count, dtype=jnp.int32)[None, :]
     row_home = jnp.sum(jnp.where(marks, homes[None, :], 0), axis=1)
 
-    up = jnp.concatenate(
-        [
-            pool_query.reshape(rank, query_width),
-            slot_keyvalue_matrices.reshape(rank, 2 * head_dim),
-        ],
-        axis=1,
-    )
-    with jax.named_scope("up_plane"):
-        up_plane = exchange(jnp.broadcast_to(up[None], (planes, rank, base_end)), PLANE)
-
     partial = project(
         inputs,
         gain,
@@ -279,9 +269,23 @@
         moves,
         own_rows,
     )
+    partial, pool_query, slot_keyvalue_matrices = lax.optimization_barrier(
+        (partial, pool_query, slot_keyvalue_matrices)
+    )
     with jax.named_scope("sum_plane"):
         by_plane = exchange(partial.reshape(planes, column_rows, -1), PLANE)
 
+    up = jnp.concatenate(
+        [
+            pool_query.reshape(rank, query_width),
+            slot_keyvalue_matrices.reshape(rank, 2 * head_dim),
+        ],
+        axis=1,
+    )
+    with jax.named_scope("up_x"):
+        up_line = lax.all_gather(up, "x", axis=0)
+    with jax.named_scope("up_y_lo"):
+        up_other = lax.ppermute(up_line, "y_lo", [(0, 1), (1, 0)])
     plane_sum = jnp.sum(by_plane.astype(jnp.float32), axis=0)
 
     low_end = 3 * rank
@@ -313,16 +317,20 @@
         row_home, (x * 2 + y_lo) * column_rows, column_rows, 0
     )
 
-    slots = jnp.arange(planes) * depth + z
-    use = column_home[:, None] == slots[None, :]
-    up_flat = up_plane.reshape(planes * rank, base_end)
+    use = [
+        column_home[:, None] == ((jnp.arange(line) * 2 + half) * depth + z)[None, :]
+        for half in (y_lo, 1 - y_lo)
+    ]
 
     def lift(block, first, last):
         rows = lowrank[:, block * rank : (block + 1) * rank]
-        spread = jnp.where(use[:, :, None], rows[:, None, :], 0).reshape(
-            column_rows, planes * rank
-        )
-        return dot(spread, up_flat[:, first:last])
+        total = jnp.zeros((column_rows, last - first), jnp.float32)
+        for mask, matrices in zip(use, (up_line, up_other), strict=True):
+            spread = jnp.where(mask[:, :, None], rows[:, None, :], 0).reshape(
+                column_rows, line * rank
+            )
+            total = total + dot(spread, matrices.reshape(line * rank, base_end)[:, first:last])
+        return total
 
     lifted = jnp.concatenate(
         [lift(0, 0, query_width), lift(1, query_width, key_end), lift(2, key_end, base_end)],

time: 159 us -> 146 us (0.918)
  waiting for transfers between devices: 66.2 us -> 36 us
  blocking collectives: 22.4 us -> 51.5 us
  local copies, waits for them, and re-layouts: 16 us -> 6 us
  starting transfers between devices: 38.5 us -> 33.1 us
  matrix products: 4.66 us -> 9.11 us
  other arithmetic: 4.75 us -> 2.89 us
    all_to_all x6 -> x5, waiting for transfers between devices: 66.2 us -> 36 us  [exchange(): return lax.all_to_all(blocks, axes, 0, 0, tiled=True)]
    all_gather x0 -> x1, blocking collectives: none -> 26.4 us  [on_device(): up_line = lax.all_gather(up, 'x', axis=0)]
    all_to_all x6 -> x5, starting transfers between devices: 38.5 us -> 30.6 us  [exchange(): return lax.all_to_all(blocks, axes, 0, 0, tiled=True)]
    unnamed x49 -> x29, local copies, waits for them, and re-layouts: 7.83 us -> 0.85 us
    dot_general x5 -> x8, matrix products: 2.83 us -> 7.28 us  [dot(): return jnp.dot(left, right, preferred_element_type=jnp.float32)]
    all_gather x1, blocking collectives: 7.85 us -> 10.5 us  [on_device(): pair = lax.all_gather(mixed, 'core', axis=0)]
    ppermute x0 -> x1, starting transfers between devices: none -> 2.57 us  [on_device(): up_other = lax.ppermute(up_line, 'y_lo', [(0, 1), (1, 0)])]
    select_n x3 -> x6, local copies, waits for them, and re-layouts: 2.6 us -> 0.67 us  [lift(): jnp.where(mask[:, :, None], rows[:, None, :], 0)]
  transfers between devices with their start and end apart: 6 -> 6, of which waited for: 6 -> 4; matrix products, arithmetic and copies ran while one was open for 2% -> 5% of each run, Pallas kernels for 0% -> 0%
where the time goes in v5:
time: 146 us; the launch traced here: 145 us
  blocking collectives  51.5 us (35%)
  waiting for transfers between devices  36 us (25%)
  starting transfers between devices  33.1 us (23%)
  matrix products  9.11 us (6%)
  Pallas kernels  6.13 us (4%)
  local copies, waits for them, and re-layouts  6 us (4%)
  other arithmetic  2.89 us (2%)
    all_to_all x5, waiting for transfers between devices, exchange(): return lax.all_to_all(blocks, axes, 0, 0, tiled=True)  36 us
    all_to_all x5, starting transfers between devices, exchange(): return lax.all_to_all(blocks, axes, 0, 0, tiled=True)  30.6 us
    all_gather x1, blocking collectives, on_device(): up_line = lax.all_gather(up, 'x', axis=0)  26.4 us
    all_gather x1, blocking collectives, on_device(): pair = lax.all_gather(mixed, 'core', axis=0)  10.5 us
    all_to_all x1, blocking collectives, exchange(): return lax.all_to_all(blocks, axes, 0, 0, tiled=True)  10.3 us
    dot_general x8, matrix products, dot(): return jnp.dot(left, right, preferred_element_type=jnp.float32)  7.28 us
    pallas_call x1, Pallas kernels, project(): pl.pallas_call(functools.partial(project_kernel, own_rows), out_shape=jax...  6.13 us
    all_gather x1, blocking collectives, on_device(): lax.all_gather(finished.astype(jnp.bfloat16), 'core', axis=0, tiled=True)  4.34 us
  transfers between devices with their start and end apart: 6, of which 4 were waited for; matrix products, arithmetic and copies ran while one was open for 5% of the time, Pallas kernels for 0%

profile of v5, /device:TPU:1, one launch (start us, length us, event | category | flops | bytes accessed | tf_op | source)
XLA Modules:
  0.0 145.3 jit_solution(3115455614135089075)
XLA Ops:
  0.0 6.1 %shard_map.163 = bf16[512,1536]{1,0:T(8,128)(2,1)} custom-call(bf16[4,128,128]{2,1,0:T(8,128)(2,1)} %inputs_ref.1, f32[1,128]{1,0:T(1,128)} %bitcast.124, bf16[128,1024]{1,0:T(8,128)(2,1)} %query_ref.1, bf16[128,128]{1,0:T(8,128)(2,1)} %key_ref.1, bf16[128,128]{1,0:T(8,128)(2,1)} %value_ref.1, bf16[8,192,128]{2,1,0:T(8,128)(2,1)} %bitcast.108, ...), custom_call_target="tpu_custom_call" | custom-call | flops 436207616 | bytes 3000000 | tf_op jit(solution)/shard_map/pallas_call | solution.py:147
  6.2 6.0 %all-to-all-start = ((bf16[8,64,1536]{2,1,0:T(8,128)(2,1)}), bf16[8,64,1536]{2,1,0:T(8,128)(2,1)S(1)}, u32[]{:S(2)}, u32[]{:S(2)}) async-start(bf16[8,64,1536]{2,1,0:T(8,128)(2,1)} %bitcast.100), calls=%async_computation | async-start | bytes 3145728 | tf_op jit(solution)/shard_map/sum_plane/all_to_all | solution.py:20
  12.3 26.4 %all-gather = bf16[256,1280]{1,0:T(8,128)(2,1)} all-gather(bf16[64,1280]{1,0:T(8,128)(2,1)S(1)} %pad_maximum_fusion), channel_id=2, replica_groups=mesh['x'=4,'y_lo'=2,'z'=8,'y_hi'=4,'core'=2] {'x'}, dimensions={0}, use_global_device_ids=true | all-gather | bytes 819200 | tf_op jit(solution)/shard_map/up_x/all_gather | solution.py:286
  38.6 2.6 %collective-permute-start = (bf16[4,64,1280]{2,1,0:T(8,128)(2,1)}, bf16[4,64,1280]{2,1,0:T(8,128)(2,1)}, u32[]{:S(2)}, u32[]{:S(2)}) collective-permute-start(bf16[4,64,1280]{2,1,0:T(8,128)(2,1)} %bitcast.11), channel_id=1, source_target_pairs={{0,64},{64,0},{1,65},{65,1},{2,66},{66,2},{3,67},{67,3},{4,68},{68... | collective-permute-start | bytes 1966088 | tf_op jit(solution)/shard_map/up_y_lo/ppermute | solution.py:288
  43.8 11.7 %all-to-all-start.1 = ((bf16[8,64,256]{2,1,0:T(8,128)(2,1)}), bf16[8,64,256]{2,1,0:T(8,128)(2,1)S(1)}, u32[]{:S(2)}, u32[]{:S(2)}) async-start(bf16[8,64,256]{2,1,0:T(8,128)(2,1)} %broadcast_in_dim.213), calls=%async_computation.1 | async-start | bytes 524288 | tf_op jit(solution)/shard_map/sum_low/all_to_all | solution.py:20
  55.7 9.1 %all-to-all-done.1 = bf16[8,64,256]{2,1,0:T(8,128)(2,1)S(1)} async-done(((bf16[8,64,256]{2,1,0:T(8,128)(2,1)}), bf16[8,64,256]{2,1,0:T(8,128)(2,1)S(1)}, u32[]{:S(2)}, u32[]{:S(2)}) %all-to-all-start.1) | async-done | bytes 262176 | tf_op jit(solution)/shard_map/sum_low/all_to_all | solution.py:20
  66.2 1.0 fusion.24
  67.1 1.0 fusion.21
  68.1 1.3 fusion.5
  69.4 1.3 convolution_add_fusion
  70.7 1.0 convolution_add_fusion.4
  71.7 1.0 convolution_add_fusion.3
  72.7 0.8 fusion.15
  73.5 3.4 %all-to-all-start.2 = ((bf16[8,8,1280]{2,1,0:T(8,128)(2,1)}), bf16[8,8,1280]{2,1,0:T(8,128)(2,1)S(1)}, u32[]{:S(2)}, u32[]{:S(2)}) async-start(bf16[8,8,1280]{2,1,0:T(8,128)(2,1)} %fusion.15), calls=%async_computation.2 | async-start | bytes 327680 | tf_op jit(solution)/shard_map/sum_z/all_to_all | solution.py:20
  77.0 8.1 %all-to-all-done.2 = bf16[8,8,1280]{2,1,0:T(8,128)(2,1)S(1)} async-done(((bf16[8,8,1280]{2,1,0:T(8,128)(2,1)}), bf16[8,8,1280]{2,1,0:T(8,128)(2,1)S(1)}, u32[]{:S(2)}, u32[]{:S(2)}) %all-to-all-start.2) | async-done | bytes 163872 | tf_op jit(solution)/shard_map/sum_z/all_to_all | solution.py:20
  86.8 10.3 %all_to_all.30 = bf16[8,8,1024]{2,1,0:T(8,128)(2,1)S(1)} all-to-all(bf16[8,8,1024]{2,1,0:T(8,128)(2,1)S(1)} %broadcast_in_dim.231), channel_id=1, replica_groups=mesh['x'=4,'y_lo'=2,'z'=8,'y_hi'=4,'core'=2] {'z'}, dimensions={0} | all-to-all | bytes 262144 | tf_op jit(solution)/shard_map/gather_z/all_to_all | solution.py:20
  97.1 1.1 broadcast_in_dim.233
  98.2 3.6 %all-to-all-start.4 = ((bf16[8,64,1024]{2,1,0:T(8,128)(2,1)}), bf16[8,64,1024]{2,1,0:T(8,128)(2,1)S(1)}, u32[]{:S(2)}, u32[]{:S(2)}) async-start(bf16[8,64,1024]{2,1,0:T(8,128)(2,1)} %broadcast_in_dim.233), calls=%async_computation.4 | async-start | bytes 2097152 | tf_op jit(solution)/shard_map/gather_plane/all_to_all | solution.py:20
  101.8 10.3 %all-to-all-done.4 = bf16[8,64,1024]{2,1,0:T(8,128)(2,1)S(1)} async-done(((bf16[8,64,1024]{2,1,0:T(8,128)(2,1)}), bf16[8,64,1024]{2,1,0:T(8,128)(2,1)S(1)}, u32[]{:S(2)}, u32[]{:S(2)}) %all-to-all-start.4) | async-done | bytes 1048608 | tf_op jit(solution)/shard_map/gather_plane/all_to_all | solution.py:20
  114.3 10.5 %all-gather.1 = bf16[1024,128]{1,0:T(8,128)(2,1)S(1)} all-gather(bf16[512,128]{1,0:T(8,128)(2,1)S(1)} %fusion.1), channel_id=3, replica_groups=mesh['x'=4,'y_lo'=2,'z'=8,'y_hi'=4,'core'=2] {'core'}, dimensions={0}, use_global_device_ids=true | all-gather | bytes 393216 | tf_op jit(solution)/shard_map/sum_core/all_gather | solution.py:396
  125.6 5.9 %all-to-all-start.5 = ((bf16[4,256,128]{2,1,0:T(8,128)(2,1)}), bf16[4,256,128]{2,1,0:T(8,128)(2,1)S(1)}, u32[]{:S(2)}, u32[]{:S(2)}) async-start(bf16[4,256,128]{2,1,0:T(8,128)(2,1)} %broadcast_in_dim.237), calls=%async_computation.5 | async-start | bytes 524288 | tf_op jit(solution)/shard_map/sum_y_hi/all_to_all | solution.py:20
  131.6 8.6 %all-to-all-done.5 = bf16[4,256,128]{2,1,0:T(8,128)(2,1)S(1)} async-done(((bf16[4,256,128]{2,1,0:T(8,128)(2,1)}), bf16[4,256,128]{2,1,0:T(8,128)(2,1)S(1)}, u32[]{:S(2)}, u32[]{:S(2)}) %all-to-all-start.5) | async-done | bytes 262176 | tf_op jit(solution)/shard_map/sum_y_hi/all_to_all | solution.py:20
  140.2 4.3 %all_gather.19 = bf16[512,128]{1,0:T(8,128)(2,1)S(1)} all-gather(bf16[256,128]{1,0:T(8,128)(2,1)S(1)} %add_convert_fusion), channel_id=1, replica_groups=mesh['x'=4,'y_lo'=2,'z'=8,'y_hi'=4,'core'=2] {'core'}, dimensions={0}, use_global_device_ids=true | all-gather | bytes 196608 | tf_op jit(solution)/shard_map/gather_core/all_gather | solution.py:412
  144.6 0.7 copy.115
  (102 shorter events, 8.9 us)
Async XLA Ops:
  0.0 112.1 %copy-start = (bf16[8,1024,64]{1,2,0:T(8,128)(2,1)S(1)}, bf16[8,1024,64]{1,2,0:T(8,128)(2,1)}, u32[]{:S(2)}) copy-start(bf16[8,1024,64]{1,2,0:T(8,128)(2,1)} %param.24) | copy-start | bytes 3145732
  6.1 6.1 %copy-start.6 = (bf16[1,64,2,128]{3,2,1,0:T(2,128)(2,1)S(1)}, bf16[1,64,2,128]{3,2,1,0:T(2,128)(2,1)}, u32[]{:S(2)}) copy-start(bf16[1,64,2,128]{3,2,1,0:T(2,128)(2,1)} %param.27) | copy-start | bytes 98308
  6.2 6.1 %copy-start.4 = (bf16[1,64,1024]{2,1,0:T(8,128)(2,1)S(1)}, bf16[1,64,1024]{2,1,0:T(8,128)(2,1)}, u32[]{:S(2)}) copy-start(bf16[1,64,1024]{2,1,0:T(8,128)(2,1)} %param.26) | copy-start | bytes 393220
  6.2 35.1 %copy-start.9 = (s32[128]{0:T(128)S(1)}, s32[128]{0:T(128)}, u32[]{:S(2)}) copy-start(s32[128]{0:T(128)} %param.30) | copy-start | bytes 1540
  6.2 35.2 %copy-start.7 = (s32[16,2]{0,1:T(2,128)S(1)}, s32[16,2]{0,1:T(2,128)}, u32[]{:S(2)}) copy-start(s32[16,2]{0,1:T(2,128)} %param.32) | copy-start | bytes 388
  6.2 36.0 %all-to-all-start = ((bf16[8,64,1536]{2,1,0:T(8,128)(2,1)}), bf16[8,64,1536]{2,1,0:T(8,128)(2,1)S(1)}, u32[]{:S(2)}, u32[]{:S(2)}) async-start(bf16[8,64,1536]{2,1,0:T(8,128)(2,1)} %bitcast.100), calls=%async_computation | async-start | bytes 3145728 | tf_op jit(solution)/shard_map/sum_plane/all_to_all | solution.py:20
  12.2 29.7 %copy-start.8 = (s32[2]{0:T(128)S(1)}, s32[2]{0:T(128)}, u32[]{:S(2)}) copy-start(s32[2]{0:T(128)} %param.33) | copy-start | bytes 28
  12.2 29.8 %copy-start.10 = (s32[8]{0:T(128)S(1)}, s32[8]{0:T(128)}, u32[]{:S(2)}) copy-start(s32[8]{0:T(128)} %param.31) | copy-start | bytes 100
  38.6 30.7 %collective-permute-start = (bf16[4,64,1280]{2,1,0:T(8,128)(2,1)}, bf16[4,64,1280]{2,1,0:T(8,128)(2,1)}, u32[]{:S(2)}, u32[]{:S(2)}) collective-permute-start(bf16[4,64,1280]{2,1,0:T(8,128)(2,1)} %bitcast.11), channel_id=1, source_target_pairs={{0,64},{64,0},{1,65},{65,1},{2,66},{66,2},{3,67},{67,3},{4,68},{68... | collective-permute-start | bytes 1966088 | tf_op jit(solution)/shard_map/up_y_lo/ppermute | solution.py:288
  43.8 21.0 %all-to-all-start.1 = ((bf16[8,64,256]{2,1,0:T(8,128)(2,1)}), bf16[8,64,256]{2,1,0:T(8,128)(2,1)S(1)}, u32[]{:S(2)}, u32[]{:S(2)}) async-start(bf16[8,64,256]{2,1,0:T(8,128)(2,1)} %broadcast_in_dim.213), calls=%async_computation.1 | async-start | bytes 524288 | tf_op jit(solution)/shard_map/sum_low/all_to_all | solution.py:20
  69.4 16.0 %copy-start.1 = (bf16[2,1,1024,128]{3,2,1,0:T(8,128)(2,1)S(1)}, bf16[2,1,1024,128]{3,2,1,0:T(8,128)(2,1)}, u32[]{:S(2)}) copy-start(bf16[2,1,1024,128]{3,2,1,0:T(8,128)(2,1)} %param.28) | copy-start | bytes 1572868
  70.7 15.5 %copy-start.11 = (bf16[2,1,1024,128]{3,2,1,0:T(8,128)(2,1)S(1)}, bf16[2,1,1024,128]{3,2,1,0:T(8,128)(2,1)}, u32[]{:S(2)}) copy-start(bf16[2,1,1024,128]{3,2,1,0:T(8,128)(2,1)} %param.29) | copy-start | bytes 1572868
  73.5 11.6 %all-to-all-start.2 = ((bf16[8,8,1280]{2,1,0:T(8,128)(2,1)}), bf16[8,8,1280]{2,1,0:T(8,128)(2,1)S(1)}, u32[]{:S(2)}, u32[]{:S(2)}) async-start(bf16[8,8,1280]{2,1,0:T(8,128)(2,1)} %fusion.15), calls=%async_computation.2 | async-start | bytes 327680 | tf_op jit(solution)/shard_map/sum_z/all_to_all | solution.py:20
  98.2 13.9 %all-to-all-start.4 = ((bf16[8,64,1024]{2,1,0:T(8,128)(2,1)}), bf16[8,64,1024]{2,1,0:T(8,128)(2,1)S(1)}, u32[]{:S(2)}, u32[]{:S(2)}) async-start(bf16[8,64,1024]{2,1,0:T(8,128)(2,1)} %broadcast_in_dim.233), calls=%async_computation.4 | async-start | bytes 2097152 | tf_op jit(solution)/shard_map/gather_plane/all_to_all | solution.py:20
  112.1 0.9 copy-start.5
  112.9 1.0 copy-start.3
  113.8 17.7 %copy-start.2 = (bf16[4,128,128]{2,1,0:T(8,128)(2,1)S(1)}, bf16[4,128,128]{2,1,0:T(8,128)(2,1)}, u32[]{:S(2)}) copy-start(bf16[4,128,128]{2,1,0:T(8,128)(2,1)} %inputs_ref.1) | copy-start | bytes 393220
  125.6 14.6 %all-to-all-start.5 = ((bf16[4,256,128]{2,1,0:T(8,128)(2,1)}), bf16[4,256,128]{2,1,0:T(8,128)(2,1)S(1)}, u32[]{:S(2)}, u32[]{:S(2)}) async-start(bf16[4,256,128]{2,1,0:T(8,128)(2,1)} %broadcast_in_dim.237), calls=%async_computation.5 | async-start | bytes 524288 | tf_op jit(solution)/shard_map/sum_y_hi/all_to_all | solution.py:20

commit v6 on v3

--- a/solution.py
+++ b/solution.py
@@ -39,51 +39,78 @@
     return jnp.dot(left, right, preferred_element_type=jnp.float32)
 
 
+def start_copies(pairs, arrived):
+    copies = [
+        pltpu.make_async_copy(source, held, arrived.at[number])
+        for number, (source, held) in enumerate(pairs)
+    ]
+    for copy in copies:
+        copy.start()
+    return copies
+
+
 def project_kernel(
     own_rows,
+    gain_ref,
+    tasks_ref,
+    moves_ref,
     inputs_ref,
-    gain_ref,
+    adapter_ref,
     query_ref,
     key_ref,
     value_ref,
-    adapter_ref,
-    tasks_ref,
-    moves_ref,
     out_ref,
+    held_inputs,
+    held_adapter,
+    held_query,
+    held_key,
+    held_value,
+    gained_ref,
+    arrived,
 ):
     steps, all_rows, width = inputs_ref.shape
     every_row = steps * all_rows
     per_group = steps * own_rows
     query_width = query_ref.shape[1]
     head_dim = key_ref.shape[1]
-    low = adapter_ref.shape[1]
-    base_end = query_width + 2 * head_dim
+    adapters, low, _ = adapter_ref.shape
+    key_end = query_width + head_dim
+    base_end = key_end + head_dim
     block = 128
-    gathered = inputs_ref[...].reshape(every_row, width)
-
-    @pl.loop(0, every_row // block)
-    def _(index):
-        first = pl.multiple_of(index * block, block)
-        rows = pl.ds(first, block)
+    copies = start_copies(
+        (
+            (inputs_ref, held_inputs),
+            (adapter_ref, held_adapter),
+            (query_ref, held_query),
+            (key_ref, held_key),
+            (value_ref, held_value),
+        ),
+        arrived,
+    )
+
+    def lane(width):
+        return lax.broadcasted_iota(jnp.int32, (block, width), 1)
+
+    copies[0].wait()
+    gathered = held_inputs[...].reshape(every_row, width)
+    squares_of = []
+    for first in range(0, every_row, block):
+        row = first + lax.broadcasted_iota(jnp.int32, (block, every_row), 0)
+        place = row % per_group // own_rows * all_rows + row // per_group * own_rows + row % own_rows
+        order = jnp.where(lane(every_row) == place, 1.0, 0.0).astype(jnp.bfloat16)
+        states = dot(order, gathered)
+        gained_ref[first : first + block, :] = (states * gain_ref[...]).astype(jnp.bfloat16)
+        squares_of.append(jnp.sum(states * states, axis=1, keepdims=True))
+
+    copies[1].wait()
+    for index, squares in enumerate(squares_of):
+        first = index * block
 
         def row_of(width):
             return first + lax.broadcasted_iota(jnp.int32, (block, width), 0)
 
-        def lane(width):
-            return lax.broadcasted_iota(jnp.int32, (block, width), 1)
-
-        def source_of(row):
-            return row // per_group * own_rows + row % own_rows
-
-        row = row_of(every_row)
-        place = row % per_group // own_rows * all_rows + source_of(row)
-        order = jnp.where(lane(every_row) == place, 1.0, 0.0).astype(jnp.bfloat16)
-        states = dot(order, gathered)
-        gained = (states * gain_ref[...]).astype(jnp.bfloat16)
-        squares = jnp.sum(states * states, axis=1, keepdims=True)
-        squares_high = squares.astype(jnp.bfloat16).astype(jnp.float32)
-
-        own = lane(all_rows) == source_of(row_of(all_rows))
+        row = row_of(all_rows)
+        own = lane(all_rows) == row // per_group * own_rows + row % own_rows
         task = jnp.sum(jnp.where(own, tasks_ref[...], 0), axis=1, keepdims=True)
         moves = moves_ref.shape[1]
         here = moves_ref[1:2, :] == row_of(moves) // per_group
@@ -91,54 +118,169 @@
         chosen = jnp.sum(jnp.where(here, moves_ref[0:1, :], 0), axis=1, keepdims=True)
         late = row_of(1) % per_group >= per_group // 2
         task = jnp.where(jnp.logical_and(late, moved), chosen, task)
-
-        out_ref[rows, 0:query_width] = dot(gained, query_ref[...]).astype(jnp.bfloat16)
-        out_ref[rows, query_width : query_width + head_dim] = dot(gained, key_ref[...]).astype(
-            jnp.bfloat16
-        )
-        out_ref[rows, query_width + head_dim : base_end] = dot(gained, value_ref[...]).astype(
-            jnp.bfloat16
-        )
+        gained = gained_ref[first : first + block, :]
         total = jnp.zeros((block, low), jnp.float32)
-        for adapter in range(adapter_ref.shape[0]):
-            mine = jnp.where(task == adapter, gained, jnp.zeros_like(gained))
+        for adapter in range(0, adapters, 2):
+            both = [
+                jnp.where(task == number, gained, jnp.zeros_like(gained))
+                for number in (adapter, adapter + 1)
+            ]
             total = total + lax.dot_general(
-                mine,
-                adapter_ref[adapter],
+                jnp.concatenate(both, axis=1),
+                jnp.concatenate([held_adapter[adapter], held_adapter[adapter + 1]], axis=1),
                 (((1,), (1,)), ((), ())),
                 preferred_element_type=jnp.float32,
             )
         rest = PADDED_WIDTH - low
+        squares_high = squares.astype(jnp.bfloat16).astype(jnp.float32)
         extra = jnp.where(
             lane(rest) == 0,
             squares_high,
             jnp.where(lane(rest) == 1, squares - squares_high, 0.0),
         )
-        out_ref[rows, base_end : base_end + PADDED_WIDTH] = jnp.concatenate(
+        out_ref[first : first + block, base_end : base_end + PADDED_WIDTH] = jnp.concatenate(
             [total, extra], axis=1
         ).astype(jnp.bfloat16)
+
+    for copy in copies[2:]:
+        copy.wait()
+
+    @pl.loop(0, every_row // block)
+    def _(index):
+        rows = pl.ds(pl.multiple_of(index * block, block), block)
+        gained = gained_ref[rows, :]
+        out_ref[rows, 0:query_width] = dot(gained, held_query[...]).astype(jnp.bfloat16)
+        out_ref[rows, query_width:key_end] = dot(gained, held_key[...]).astype(jnp.bfloat16)
+        out_ref[rows, key_end:base_end] = dot(gained, held_value[...]).astype(jnp.bfloat16)
 
 
 def project(inputs, gain, w_query, w_key, w_value, adapter_in, tasks, moves, own_rows):
     steps, all_rows, width = inputs.shape
     columns = w_query.shape[1] + w_key.shape[1] + w_value.shape[1] + PADDED_WIDTH
+    large = (inputs, jnp.swapaxes(adapter_in, 1, 2), w_query, w_key, w_value)
     return pl.pallas_call(
         functools.partial(project_kernel, own_rows),
         out_shape=jax.ShapeDtypeStruct((steps * all_rows, columns), jnp.bfloat16),
-        compiler_params=pltpu.CompilerParams(vmem_limit_bytes=32 * 1024 * 1024),
+        in_specs=[pl.BlockSpec(memory_space=pltpu.VMEM)] * 3
+        + [pl.BlockSpec(memory_space=pl.ANY)] * len(large),
+        scratch_shapes=[pltpu.VMEM(array.shape, jnp.bfloat16) for array in large]
+        + [
+            pltpu.VMEM((steps * all_rows, width), jnp.bfloat16),
+            pltpu.SemaphoreType.DMA((len(large),)),
+        ],
         cost_estimate=pl.CostEstimate(
             flops=2 * steps * all_rows * width * 3328, bytes_accessed=3_000_000, transcendentals=0
         ),
-    )(
-        inputs,
-        gain[None, :],
-        w_query,
-        w_key,
-        w_value,
-        jnp.swapaxes(adapter_in, 1, 2),
-        tasks[None, :],
-        moves.T,
-    )
+    )(gain[None, :], tasks[None, :], moves.T, *large)
+
+
+def plane_kernel(low, parts_ref, base_ref, low_ref):
+    sources, rows, columns = parts_ref.shape
+    base_end = base_ref.shape[1]
+    @pl.loop(0, rows // 16)
+    def _(index):
+        part = pl.ds(pl.multiple_of(index * 16, 16), 16)
+        total = parts_ref[0, part, :].astype(jnp.float32)
+        for source in range(1, sources):
+            total = total + parts_ref[source, part, :].astype(jnp.float32)
+        base_ref[part, :] = total[:, :base_end]
+        last = total[:, base_end:]
+        lane = lax.broadcasted_iota(jnp.int32, last.shape, 1)
+        squares = jnp.sum(jnp.where(lane >= low, last, 0.0), axis=1, keepdims=True)
+        squares_high = squares.astype(jnp.bfloat16).astype(jnp.float32)
+        last = jnp.where(
+            lane < low,
+            last,
+            jnp.where(
+                lane == low, squares_high, jnp.where(lane == low + 1, squares - squares_high, 0.0)
+            ),
+        ).astype(jnp.bfloat16)
+        for target in range(low_ref.shape[0]):
+            low_ref[target, part, :] = last
+
+
+def sum_plane(parts, base_end, low, depth):
+    sources, rows, columns = parts.shape
+    return pl.pallas_call(
+        functools.partial(plane_kernel, low),
+        out_shape=[
+            jax.ShapeDtypeStruct((rows, base_end), jnp.float32),
+            jax.ShapeDtypeStruct((depth, rows, columns - base_end), jnp.bfloat16),
+        ],
+        in_specs=[pl.BlockSpec(memory_space=pltpu.VMEM)],
+        out_specs=[pl.BlockSpec(memory_space=pltpu.VMEM)] * 2,
+        compiler_params=pltpu.CompilerParams(vmem_limit_bytes=16 * 1024 * 1024),
+        cost_estimate=pl.CostEstimate(
+            flops=parts.size, bytes_accessed=2 * parts.size, transcendentals=0
+        ),
+    )(parts)
+
+
+def lift_kernel(
+    rank,
+    head_dim,
+    model_width,
+    slot_ref,
+    low_ref,
+    line_ref,
+    other_ref,
+    base_ref,
+    out_ref,
+    held_base,
+    arrived,
+):
+    copy = pltpu.make_async_copy(base_ref, held_base, arrived)
+    copy.start()
+    rows, columns = out_ref.shape
+    line = line_ref.shape[0]
+    low = 3 * rank
+    total = low_ref[0].astype(jnp.float32)
+    for source in range(1, low_ref.shape[0]):
+        total = total + low_ref[source].astype(jnp.float32)
+    lane = lax.broadcasted_iota(jnp.int32, total.shape, 1)
+    squares = jnp.sum(jnp.where(lane >= low, total, 0.0), axis=1, keepdims=True)
+    inverse = lax.rsqrt(squares / model_width + epsilon)
+    lowrank = (inverse * total).astype(jnp.bfloat16)
+    from_lane = lax.broadcasted_iota(jnp.int32, (PADDED_WIDTH, line * rank), 0)
+    to_lane = lax.broadcasted_iota(jnp.int32, (PADDED_WIDTH, line * rank), 1)
+    slot_lane = lax.broadcasted_iota(jnp.int32, (rows, line * rank), 1) // rank
+    slot = slot_ref[...]
+    spreads = []
+    for number in range(3):
+        pick = jnp.where(from_lane == number * rank + to_lane % rank, 1.0, 0.0)
+        tiled = dot(lowrank, pick.astype(jnp.bfloat16))
+        spreads.append(
+            [
+                jnp.where(slot == slot_lane + half * line, tiled, 0.0).astype(jnp.bfloat16)
+                for half in range(2)
+            ]
+        )
+    copy.wait()
+    key_first, value_first = columns - 2 * head_dim, columns - head_dim
+    bounds = ((0, key_first), (key_first, value_first), (value_first, columns))
+    for (first, last), (near, far) in zip(bounds, spreads, strict=True):
+        lifted = dot(near, line_ref[:, :, first:last].reshape(line * rank, last - first))
+        lifted = lifted + dot(
+            far, other_ref[:, :, first:last].reshape(line * rank, last - first)
+        )
+        out_ref[:, first:last] = (inverse * held_base[:, first:last] + lifted).astype(jnp.bfloat16)
+
+
+def lift(slot, low_parts, base, up_line, up_other, rank, head_dim, model_width):
+    return pl.pallas_call(
+        functools.partial(lift_kernel, rank, head_dim, model_width),
+        out_shape=jax.ShapeDtypeStruct(base.shape, jnp.bfloat16),
+        in_specs=[pl.BlockSpec(memory_space=pltpu.VMEM)] * 4
+        + [pl.BlockSpec(memory_space=pl.ANY)],
+        out_specs=pl.BlockSpec(memory_space=pltpu.VMEM),
+        scratch_shapes=[pltpu.VMEM(base.shape, jnp.float32), pltpu.SemaphoreType.DMA(())],
+        compiler_params=pltpu.CompilerParams(vmem_limit_bytes=16 * 1024 * 1024),
+        cost_estimate=pl.CostEstimate(
+            flops=2 * base.size * up_line.shape[0] * 2 * rank,
+            bytes_accessed=2_000_000,
+            transcendentals=0,
+        ),
+    )(slot, low_parts, up_line, up_other, base)
 
 
 def attend(queries, cache_keys, value_cache, fresh_keys, fresh_values, lengths, query_steps):
@@ -195,6 +337,7 @@
     own_rows = lengths.shape[0]
     groups = all_rows // own_rows
     planes = lax.axis_size(PLANE)
+    line = lax.axis_size("x")
     depth = lax.axis_size("z")
     task_count = homes.shape[0]
     rank = adapter_out.shape[1]
@@ -206,7 +349,6 @@
     per_group = steps * own_rows
     every_row = groups * per_group
     model_width = width_part * groups
-    line = lax.axis_size("x")
     column_rows = depth * per_group
 
     group_tasks = tasks.reshape(groups, own_rows)
@@ -218,18 +360,6 @@
     active = active.reshape(every_row)
     marks = active[:, None] == jnp.arange(task_count, dtype=jnp.int32)[None, :]
     row_home = jnp.sum(jnp.where(marks, homes[None, :], 0), axis=1)
-
-    up = jnp.concatenate(
-        [
-            pool_query.reshape(rank, query_width),
-            slot_keyvalue_matrices.reshape(rank, 2 * head_dim),
-        ],
-        axis=1,
-    )
-    with jax.named_scope("up_y_lo"):
-        up_pair = jnp.stack([up, lax.ppermute(up, "y_lo", [(0, 1), (1, 0)])])
-    with jax.named_scope("up_x"):
-        up_plane = lax.all_gather(up_pair, "x", axis=0)
 
     partial = project(
         inputs,
@@ -242,57 +372,37 @@
         moves,
         own_rows,
     )
+    partial, pool_query, slot_keyvalue_matrices = lax.optimization_barrier(
+        (partial, pool_query, slot_keyvalue_matrices)
+    )
     with jax.named_scope("sum_plane"):
         by_plane = exchange(partial.reshape(planes, column_rows, -1), PLANE)
 
-    plane_sum = jnp.sum(by_plane.astype(jnp.float32), axis=0)
-
-    low_end = 3 * rank
-    low_part = plane_sum[:, base_end:]
-    squares = low_part[:, low_end : low_end + 1] + low_part[:, low_end + 1 : low_end + 2]
-    squares_high = lax.reduce_precision(squares, 8, 7)
-    low_part = jnp.concatenate(
+    up = jnp.concatenate(
         [
-            low_part[:, :low_end],
-            squares_high,
-            squares - squares_high,
-            low_part[:, low_end + 2 :],
+            pool_query.reshape(rank, query_width),
+            slot_keyvalue_matrices.reshape(rank, 2 * head_dim),
         ],
         axis=1,
-    ).astype(jnp.bfloat16)
+    )
+    with jax.named_scope("up_x"):
+        up_line = lax.all_gather(up, "x", axis=0)
+    with jax.named_scope("up_y_lo"):
+        up_other = lax.ppermute(up_line, "y_lo", [(0, 1), (1, 0)])
+    plane_sum, low_part = sum_plane(by_plane, base_end, 3 * rank, depth)
     with jax.named_scope("sum_low"):
-        low_sum = exchange(
-            jnp.broadcast_to(low_part[None], (depth, column_rows, PADDED_WIDTH)), "z"
-        )
-    low_sum = jnp.sum(low_sum.astype(jnp.float32), axis=0)
-    inverse = lax.rsqrt(
-        (low_sum[:, low_end : low_end + 1] + low_sum[:, low_end + 1 : low_end + 2]) / model_width
-        + epsilon
-    )
-    lowrank = (inverse * low_sum[:, :low_end]).astype(jnp.bfloat16)
+        low_parts = exchange(low_part, "z")
 
     x, y_lo, z = (lax.axis_index(name) for name in GROUP)
     column_home = lax.dynamic_slice_in_dim(
         row_home, (x * 2 + y_lo) * column_rows, column_rows, 0
     )
-
-    halves = jnp.stack([y_lo, 1 - y_lo])
-    slots = ((jnp.arange(line)[:, None] * 2 + halves[None, :]) * depth + z).reshape(-1)
-    use = column_home[:, None] == slots[None, :]
-    up_flat = up_plane.reshape(planes * rank, base_end)
-
-    def lift(block, first, last):
-        rows = lowrank[:, block * rank : (block + 1) * rank]
-        spread = jnp.where(use[:, :, None], rows[:, None, :], 0).reshape(
-            column_rows, planes * rank
-        )
-        return dot(spread, up_flat[:, first:last])
-
-    lifted = jnp.concatenate(
-        [lift(0, 0, query_width), lift(1, query_width, key_end), lift(2, key_end, base_end)],
-        axis=1,
-    )
-    raw_part = (inverse * plane_sum[:, :base_end] + lifted).astype(jnp.bfloat16)
+    home_x = column_home // (2 * depth)
+    other_half = jnp.where(column_home // depth % 2 == y_lo, 0, line)
+    slot = jnp.where(column_home % depth == z, home_x + other_half, -1)
+    raw_part = lift(
+        slot[:, None], low_parts, plane_sum, up_line, up_other, rank, head_dim, model_width
+    )
     with jax.named_scope("sum_z"):
         by_depth = exchange(raw_part.reshape(depth, per_group, base_end), "z")
     raw = jnp.sum(by_depth.astype(jnp.float32), axis=0)
@@ -346,31 +456,31 @@
         adapter_out.reshape(task_count * rank, width_part),
     )
     mixed = mixed.astype(jnp.bfloat16)
-    half = every_row // 2
     core = lax.axis_index("core")
+    cores = lax.axis_size("core")
+    half = steps // cores
     with jax.named_scope("sum_core"):
         pair = lax.all_gather(mixed, "core", axis=0)
-    mine = lax.dynamic_slice_in_dim(pair, core * half, half, 1).astype(jnp.float32)
-    mine = (mine[0] + mine[1]).astype(jnp.bfloat16)
+    mine = lax.dynamic_slice_in_dim(
+        pair.reshape(cores, groups, steps, own_rows, width_part), core * half, half, 2
+    ).astype(jnp.float32)
+    mine = jnp.sum(mine, axis=0).astype(jnp.bfloat16)
+    mine = mine.transpose(1, 0, 2, 3).reshape(half, all_rows, width_part)
+    y_his = lax.axis_size("y_hi")
     with jax.named_scope("sum_y_hi"):
         mine = exchange(
-            jnp.broadcast_to(mine[None], (lax.axis_size("y_hi"), half, width_part)), "y_hi"
+            jnp.broadcast_to(mine[None], (y_his, half, all_rows, width_part)).reshape(
+                y_his * half, all_rows, width_part
+            ),
+            "y_hi",
         )
-    mine = jnp.sum(mine.astype(jnp.float32), axis=0)
-    residual = (
-        inputs.reshape(steps, groups, own_rows, width_part)
-        .transpose(1, 0, 2, 3)
-        .reshape(every_row, width_part)
-    )
-    residual = lax.dynamic_slice_in_dim(residual, core * half, half, 0)
-    finished = residual.astype(jnp.float32) + mine
+    mine = jnp.sum(
+        mine.reshape(y_his, half, all_rows, width_part).astype(jnp.float32), axis=0
+    )
+    residual = lax.dynamic_slice_in_dim(inputs, core * half, half, 0)
+    finished = (residual.astype(jnp.float32) + mine).astype(jnp.bfloat16)
     with jax.named_scope("gather_core"):
-        finished = lax.all_gather(finished.astype(jnp.bfloat16), "core", axis=0, tiled=True)
-    return (
-        finished.reshape(groups, steps, own_rows, width_part)
-        .transpose(1, 0, 2, 3)
-        .reshape(steps, all_rows, width_part)
-    )
+        return lax.all_gather(finished, "core", axis=0, tiled=True)
 
 
 def solution(mesh):

time: 167 us -> 139 us (0.83)
  blocking collectives: 22.3 us -> 65.6 us
  waiting for transfers between devices: 62.8 us -> 27.4 us
  between operations: 13.8 us -> 0.43 us
  starting transfers between devices: 40.5 us -> 27.2 us
  local copies, waits for them, and re-layouts: 12.3 us -> 4.87 us
  Pallas kernels: 4.15 us -> 8.78 us
  matrix products: 6.29 us -> 2.61 us
  other arithmetic: 3.69 us -> 1.33 us
    all_gather x1 -> x2, blocking collectives: 4.32 us -> 29.8 us  [the longest x1 25.8 us: on_device(): up_line = lax.all_gather(up, 'x', axis=0)]
    all_to_all x1 -> x2, blocking collectives: 10.4 us -> 25.4 us  [exchange(): return lax.all_to_all(blocks, axes, 0, 0, tiled=True)]
    ppermute x1, waiting for transfers between devices: 14 us -> 0.01 us  [on_device(): up_other = lax.ppermute(up_line, 'y_lo', [(0, 1), (1, 0)])]
    all_to_all x5 -> x4, starting transfers between devices: 37.1 us -> 24.5 us  [exchange(): return lax.all_to_all(blocks, axes, 0, 0, tiled=True)]
    all_gather x1 -> x0, waiting for transfers between devices: 12.1 us -> none  [on_device(): up_plane = lax.all_gather(up_pair, 'x', axis=0)]
    all_to_all x5 -> x4, waiting for transfers between devices: 36.7 us -> 27.4 us  [exchange(): return lax.all_to_all(blocks, axes, 0, 0, tiled=True)]
    unnamed x45 -> x32, local copies, waits for them, and re-layouts: 7.28 us -> 3.04 us
    dot_general x5 -> x2, matrix products: 4.46 us -> 0.77 us  [dot(): return jnp.dot(left, right, preferred_element_type=jnp.float32)]
  transfers between devices with their start and end apart: 7 -> 5, of which waited for: 6 -> 3; matrix products, arithmetic and copies ran while one was open for 3% -> 1% of each run, Pallas kernels for 0% -> 1%
where the time goes in v6:
time: 139 us; the launch traced here: 138 us
  blocking collectives  65.6 us (47%)
  waiting for transfers between devices  27.4 us (20%)
  starting transfers between devices  27.2 us (20%)
  Pallas kernels  8.78 us (6%)
  local copies, waits for them, and re-layouts  4.87 us (4%)
  matrix products  2.61 us (2%)
    all_to_all x4, waiting for transfers between devices, exchange(): return lax.all_to_all(blocks, axes, 0, 0, tiled=True)  27.4 us
    all_gather x1, blocking collectives, on_device(): up_line = lax.all_gather(up, 'x', axis=0)  25.8 us
    all_to_all x2, blocking collectives, exchange(): return lax.all_to_all(blocks, axes, 0, 0, tiled=True)  25.4 us
    all_to_all x4, starting transfers between devices, exchange(): return lax.all_to_all(blocks, axes, 0, 0, tiled=True)  24.5 us
    all_gather x1, blocking collectives, on_device(): pair = lax.all_gather(mixed, 'core', axis=0)  10.4 us
    pallas_call x1, Pallas kernels, project(): pl.pallas_call(functools.partial(project_kernel, own_rows), out_shape=jax...  5.16 us
    all_gather x1, blocking collectives, on_device(): return lax.all_gather(finished, 'core', axis=0, tiled=True)  4.01 us
    unnamed x32, local copies, waits for them, and re-layouts  3.04 us
  transfers between devices with their start and end apart: 5, of which 3 were waited for; matrix products, arithmetic and copies ran while one was open for 1% of the time, Pallas kernels for 1%

profile of v6, /device:TPU:1, one launch (start us, length us, event | category | flops | bytes accessed | tf_op | source)
XLA Modules:
  0.0 138.2 jit_solution(9285925963059531512)
XLA Ops:
  0.0 5.2 %shard_map.163 = bf16[512,1536]{1,0:T(8,128)(2,1)} custom-call(f32[1,128]{1,0:T(1,128)} %bitcast.116, s32[1,128]{1,0:T(1,128)} %bitcast.115, s32[2,16]{1,0:T(2,128)} %bitcast.114, bf16[4,128,128]{2,1,0:T(8,128)(2,1)} %inputs_ref.1, bf16[8,192,128]{2,1,0:T(8,128)(2,1)} %bitcast.99, bf16[128,1024]{1,0:T(8,128)(2,1)} %query_ref.1, bf16[128,128]{1,0:T(8,128)(2,1)} %key_ref.1, ...), custom_call_target="tpu_custom_call" | custom-call | flops 436207616 | bytes 3000000 | tf_op jit(solution)/shard_map/pallas_call | solution.py:161
  5.2 6.0 %all-to-all-start = ((bf16[8,64,1536]{2,1,0:T(8,128)(2,1)}), bf16[8,64,1536]{2,1,0:T(8,128)(2,1)S(1)}, u32[]{:S(2)}, u32[]{:S(2)}) async-start(bf16[8,64,1536]{2,1,0:T(8,128)(2,1)} %bitcast.91), calls=%async_computation | async-start | bytes 3145728 | tf_op jit(solution)/shard_map/sum_plane/all_to_all | solution.py:20
  11.3 25.8 %all-gather = bf16[256,1280]{1,0:T(8,128)(2,1)S(1)} all-gather(bf16[64,1280]{1,0:T(8,128)(2,1)S(1)} %pad_maximum_fusion), channel_id=2, replica_groups=mesh['x'=4,'y_lo'=2,'z'=8,'y_hi'=4,'core'=2] {'x'}, dimensions={0}, use_global_device_ids=true | all-gather | bytes 819200 | tf_op jit(solution)/shard_map/up_x/all_gather | solution.py:389
  37.1 2.6 %collective-permute-start = (bf16[4,64,1280]{2,1,0:T(8,128)(2,1)S(1)}, bf16[4,64,1280]{2,1,0:T(8,128)(2,1)}, u32[]{:S(2)}, u32[]{:S(2)}) collective-permute-start(bf16[4,64,1280]{2,1,0:T(8,128)(2,1)S(1)} %bitcast.89), channel_id=1, source_target_pairs={{0,64},{64,0},{1,65},{65,1},{2,66},{66,2},{3,67},{67,3},{4,68},{68... | collective-permute-start | bytes 1966088 | tf_op jit(solution)/shard_map/up_y_lo/ppermute | solution.py:391
  40.7 1.1 shard_map.164
  41.8 0.7 copy-done.1
  42.5 11.6 %all-to-all-start.1 = ((bf16[8,64,256]{2,1,0:T(8,128)(2,1)}), bf16[8,64,256]{2,1,0:T(8,128)(2,1)S(1)}, u32[]{:S(2)}, u32[]{:S(2)}) async-start(bf16[8,64,256]{2,1,0:T(8,128)(2,1)} %get-tuple-element.11), calls=%async_computation.1 | async-start | bytes 524288 | tf_op jit(solution)/shard_map/sum_low/all_to_all | solution.py:20
  54.3 9.1 %all-to-all-done.1.low_ref = bf16[8,64,256]{2,1,0:T(8,128)(2,1)S(1)} async-done(((bf16[8,64,256]{2,1,0:T(8,128)(2,1)}), bf16[8,64,256]{2,1,0:T(8,128)(2,1)S(1)}, u32[]{:S(2)}, u32[]{:S(2)}) %all-to-all-start.1) | async-done | bytes 262176 | tf_op jit(solution)/shard_map/sum_low/all_to_all | solution.py:20
  63.4 1.0 copy-done.2
  64.4 2.5 %shard_map.165 = bf16[64,1280]{1,0:T(8,128)(2,1)} custom-call(s32[64,1]{1,0:T(8,128)S(1)} %copy.39.slot_ref, bf16[8,64,256]{2,1,0:T(8,128)(2,1)S(1)} %all-to-all-done.1.low_ref, bf16[4,64,1280]{2,1,0:T(8,128)(2,1)S(1)} %bitcast.90, bf16[4,64,1280]{2,1,0:T(8,128)(2,1)} %collective-permute-done.other_ref, f32[64,1280]{1,0:T(8,128)S(1)} %copy-done.2), custom_call_target="tpu_custom_call" | custom-call | flops 83886080 | bytes 2000000 | tf_op jit(solution)/shard_map/pallas_call | solution.py:270
  66.9 3.4 %all-to-all-start.2 = ((bf16[8,8,1280]{2,1,0:T(8,128)(2,1)}), bf16[8,8,1280]{2,1,0:T(8,128)(2,1)S(1)}, u32[]{:S(2)}, u32[]{:S(2)}) async-start(bf16[8,8,1280]{2,1,0:T(8,128)(2,1)} %bitcast.10), calls=%async_computation.2 | async-start | bytes 327680 | tf_op jit(solution)/shard_map/sum_z/all_to_all | solution.py:20
  70.4 8.1 %all-to-all-done.2 = bf16[8,8,1280]{2,1,0:T(8,128)(2,1)S(1)} async-done(((bf16[8,8,1280]{2,1,0:T(8,128)(2,1)}), bf16[8,8,1280]{2,1,0:T(8,128)(2,1)S(1)}, u32[]{:S(2)}, u32[]{:S(2)}) %all-to-all-start.2) | async-done | bytes 163872 | tf_op jit(solution)/shard_map/sum_z/all_to_all | solution.py:20
  78.8 0.4 fusion.39
  80.2 10.3 %all_to_all.30 = bf16[8,8,1024]{2,1,0:T(8,128)(2,1)S(1)} all-to-all(bf16[8,8,1024]{2,1,0:T(8,128)(2,1)S(1)} %broadcast_in_dim.150), channel_id=1, replica_groups=mesh['x'=4,'y_lo'=2,'z'=8,'y_hi'=4,'core'=2] {'z'}, dimensions={0} | all-to-all | bytes 262144 | tf_op jit(solution)/shard_map/gather_z/all_to_all | solution.py:20
  90.6 1.1 broadcast_in_dim.152
  91.7 3.6 %all-to-all-start.4 = ((bf16[8,64,1024]{2,1,0:T(8,128)(2,1)}), bf16[8,64,1024]{2,1,0:T(8,128)(2,1)S(1)}, u32[]{:S(2)}, u32[]{:S(2)}) async-start(bf16[8,64,1024]{2,1,0:T(8,128)(2,1)} %broadcast_in_dim.152), calls=%async_computation.4 | async-start | bytes 2097152 | tf_op jit(solution)/shard_map/gather_plane/all_to_all | solution.py:20
  95.3 10.3 %all-to-all-done.4 = bf16[8,64,1024]{2,1,0:T(8,128)(2,1)S(1)} async-done(((bf16[8,64,1024]{2,1,0:T(8,128)(2,1)}), bf16[8,64,1024]{2,1,0:T(8,128)(2,1)S(1)}, u32[]{:S(2)}, u32[]{:S(2)}) %all-to-all-start.4) | async-done | bytes 1048608 | tf_op jit(solution)/shard_map/gather_plane/all_to_all | solution.py:20
  105.6 0.7 fusion.41
  106.8 0.5 copy-done.5
  107.3 0.4 fusion.1
  107.7 10.4 %all-gather.1 = bf16[1024,128]{1,0:T(8,128)(2,1)S(1)} all-gather(bf16[512,128]{1,0:T(8,128)(2,1)S(1)} %fusion.1), channel_id=3, replica_groups=mesh['x'=4,'y_lo'=2,'z'=8,'y_hi'=4,'core'=2] {'core'}, dimensions={0}, use_global_device_ids=true | all-gather | bytes 393216 | tf_op jit(solution)/shard_map/sum_core/all_gather | solution.py:463
  118.4 15.1 %all_to_all.31 = bf16[8,128,128]{2,1,0:T(8,128)(2,1)S(1)} all-to-all(bf16[8,128,128]{2,1,0:T(8,128)(2,1)S(1)} %bitcast.94), channel_id=1, replica_groups=mesh['x'=4,'y_lo'=2,'z'=8,'y_hi'=4,'core'=2] {'y_hi'}, dimensions={0} | all-to-all | bytes 524288 | tf_op jit(solution)/shard_map/sum_y_hi/all_to_all | solution.py:20
  133.5 4.0 %all_gather.19 = bf16[4,128,128]{2,1,0:T(8,128)(2,1)S(1)} all-gather(bf16[2,128,128]{2,1,0:T(8,128)(2,1)S(1)} %add_convert_fusion), channel_id=1, replica_groups=mesh['x'=4,'y_lo'=2,'z'=8,'y_hi'=4,'core'=2] {'core'}, dimensions={0}, use_global_device_ids=true | all-gather | bytes 196608 | tf_op jit(solution)/shard_map/gather_core/all_gather | solution.py:483
  137.6 0.7 copy.71
  (75 shorter events, 3.3 us)
Async XLA Ops:
  0.0 105.6 %copy-start = (bf16[8,1024,64]{1,2,0:T(8,128)(2,1)S(1)}, bf16[8,1024,64]{1,2,0:T(8,128)(2,1)}, u32[]{:S(2)}) copy-start(bf16[8,1024,64]{1,2,0:T(8,128)(2,1)} %param.24) | copy-start | bytes 3145732
  5.2 6.1 %copy-start.8 = (bf16[1,64,2,128]{3,2,1,0:T(2,128)(2,1)S(1)}, bf16[1,64,2,128]{3,2,1,0:T(2,128)(2,1)}, u32[]{:S(2)}) copy-start(bf16[1,64,2,128]{3,2,1,0:T(2,128)(2,1)} %param.27) | copy-start | bytes 98308
  5.2 6.1 %copy-start.6 = (bf16[1,64,1024]{2,1,0:T(8,128)(2,1)S(1)}, bf16[1,64,1024]{2,1,0:T(8,128)(2,1)}, u32[]{:S(2)}) copy-start(bf16[1,64,1024]{2,1,0:T(8,128)(2,1)} %param.26) | copy-start | bytes 393220
  5.2 34.5 %copy-start.11 = (s32[128]{0:T(128)S(1)}, s32[128]{0:T(128)}, u32[]{:S(2)}) copy-start(s32[128]{0:T(128)} %param.30) | copy-start | bytes 1540
  5.2 34.7 %copy-start.9 = (s32[16,2]{0,1:T(2,128)S(1)}, s32[16,2]{0,1:T(2,128)}, u32[]{:S(2)}) copy-start(s32[16,2]{0,1:T(2,128)} %param.32) | copy-start | bytes 388
  5.2 35.4 %all-to-all-start = ((bf16[8,64,1536]{2,1,0:T(8,128)(2,1)}), bf16[8,64,1536]{2,1,0:T(8,128)(2,1)S(1)}, u32[]{:S(2)}, u32[]{:S(2)}) async-start(bf16[8,64,1536]{2,1,0:T(8,128)(2,1)} %bitcast.91), calls=%async_computation | async-start | bytes 3145728 | tf_op jit(solution)/shard_map/sum_plane/all_to_all | solution.py:20
  11.2 29.2 %copy-start.10 = (s32[2]{0:T(128)S(1)}, s32[2]{0:T(128)}, u32[]{:S(2)}) copy-start(s32[2]{0:T(128)} %param.33) | copy-start | bytes 28
  11.2 29.3 %copy-start.12 = (s32[8]{0:T(128)S(1)}, s32[8]{0:T(128)}, u32[]{:S(2)}) copy-start(s32[8]{0:T(128)} %param.31) | copy-start | bytes 100
  37.1 17.3 %collective-permute-start = (bf16[4,64,1280]{2,1,0:T(8,128)(2,1)S(1)}, bf16[4,64,1280]{2,1,0:T(8,128)(2,1)}, u32[]{:S(2)}, u32[]{:S(2)}) collective-permute-start(bf16[4,64,1280]{2,1,0:T(8,128)(2,1)S(1)} %bitcast.89), channel_id=1, source_target_pairs={{0,64},{64,0},{1,65},{65,1},{2,66},{66,2},{3,67},{67,3},{4,68},{68... | collective-permute-start | bytes 1966088 | tf_op jit(solution)/shard_map/up_y_lo/ppermute | solution.py:391
  41.8 0.7 copy-start.1
  42.5 36.3 %copy-start.3 = (bf16[2,1,1024,128]{3,2,1,0:T(8,128)(2,1)S(1)}, bf16[2,1,1024,128]{3,2,1,0:T(8,128)(2,1)}, u32[]{:S(2)}) copy-start(bf16[2,1,1024,128]{3,2,1,0:T(8,128)(2,1)} %param.28) | copy-start | bytes 1572868
  42.5 20.9 %all-to-all-start.1 = ((bf16[8,64,256]{2,1,0:T(8,128)(2,1)}), bf16[8,64,256]{2,1,0:T(8,128)(2,1)S(1)}, u32[]{:S(2)}, u32[]{:S(2)}) async-start(bf16[8,64,256]{2,1,0:T(8,128)(2,1)} %get-tuple-element.11), calls=%async_computation.1 | async-start | bytes 524288 | tf_op jit(solution)/shard_map/sum_low/all_to_all | solution.py:20
  63.4 1.0 copy-start.2
  64.4 15.3 %copy-start.13 = (bf16[2,1,1024,128]{3,2,1,0:T(8,128)(2,1)S(1)}, bf16[2,1,1024,128]{3,2,1,0:T(8,128)(2,1)}, u32[]{:S(2)}) copy-start(bf16[2,1,1024,128]{3,2,1,0:T(8,128)(2,1)} %param.29) | copy-start | bytes 1572868
  66.9 11.6 %all-to-all-start.2 = ((bf16[8,8,1280]{2,1,0:T(8,128)(2,1)}), bf16[8,8,1280]{2,1,0:T(8,128)(2,1)S(1)}, u32[]{:S(2)}, u32[]{:S(2)}) async-start(bf16[8,8,1280]{2,1,0:T(8,128)(2,1)} %bitcast.10), calls=%async_computation.2 | async-start | bytes 327680 | tf_op jit(solution)/shard_map/sum_z/all_to_all | solution.py:20
  91.7 13.9 %all-to-all-start.4 = ((bf16[8,64,1024]{2,1,0:T(8,128)(2,1)}), bf16[8,64,1024]{2,1,0:T(8,128)(2,1)S(1)}, u32[]{:S(2)}, u32[]{:S(2)}) async-start(bf16[8,64,1024]{2,1,0:T(8,128)(2,1)} %broadcast_in_dim.152), calls=%async_computation.4 | async-start | bytes 2097152 | tf_op jit(solution)/shard_map/gather_plane/all_to_all | solution.py:20
  105.6 0.9 copy-start.7
  106.3 1.0 copy-start.5
  107.3 26.2 %copy-start.4 = (bf16[4,128,128]{2,1,0:T(8,128)(2,1)S(1)}, bf16[4,128,128]{2,1,0:T(8,128)(2,1)}, u32[]{:S(2)}) copy-start(bf16[4,128,128]{2,1,0:T(8,128)(2,1)} %inputs_ref.1) | copy-start | bytes 393220

commit v7 on v6

--- a/solution.py
+++ b/solution.py
@@ -386,7 +386,18 @@
         axis=1,
     )
     with jax.named_scope("up_x"):
-        up_line = lax.all_gather(up, "x", axis=0)
+        ahead = [(i, (i + 1) % line) for i in range(line)]
+        back = [(i, (i - 1) % line) for i in range(line)]
+        half_rank = rank // 2
+        from_left = lax.ppermute(up, "x", ahead)
+        from_right = lax.ppermute(up, "x", back)
+        from_far = jnp.concatenate(
+            [
+                lax.ppermute(from_left[:half_rank], "x", ahead),
+                lax.ppermute(from_right[half_rank:], "x", back),
+            ]
+        )
+        up_line = jnp.stack([up, from_left, from_right, from_far])
     with jax.named_scope("up_y_lo"):
         up_other = lax.ppermute(up_line, "y_lo", [(0, 1), (1, 0)])
     plane_sum, low_part = sum_plane(by_plane, base_end, 3 * rank, depth)
@@ -397,9 +408,10 @@
     column_home = lax.dynamic_slice_in_dim(
         row_home, (x * 2 + y_lo) * column_rows, column_rows, 0
     )
-    home_x = column_home // (2 * depth)
+    offset = (column_home // (2 * depth) - x) % line
+    near_slot = jnp.where(offset == line - 1, 1, jnp.where(offset == 0, 0, offset + 1))
     other_half = jnp.where(column_home // depth % 2 == y_lo, 0, line)
-    slot = jnp.where(column_home % depth == z, home_x + other_half, -1)
+    slot = jnp.where(column_home % depth == z, near_slot + other_half, -1)
     raw_part = lift(
         slot[:, None], low_parts, plane_sum, up_line, up_other, rank, head_dim, model_width
     )

time: 139 us -> 145 us (1.043)
  blocking collectives: 65.6 us -> 38 us
  waiting for transfers between devices: 27.4 us -> 44.8 us
  starting transfers between devices: 27.2 us -> 40.8 us
    all_gather x1 -> x0, blocking collectives: 25.8 us -> none  [on_device(): up_line = lax.all_gather(up, 'x', axis=0)]
    ppermute x0 -> x4, waiting for transfers between devices: none -> 17.1 us  [the longest x1 12.7 us: on_device(): from_right = lax.ppermute(up, 'x', back)]
    ppermute x0 -> x4, starting transfers between devices: none -> 11.9 us  [the longest x1 4.57 us: on_device(): from_right = lax.ppermute(up, 'x', back)]
    all_gather x1, blocking collectives: 10.4 us -> 8.6 us  [on_device(): pair = lax.all_gather(mixed, 'core', axis=0)]
    all_to_all x4, starting transfers between devices: 24.5 us -> 26.1 us  [exchange(): return lax.all_to_all(blocks, axes, 0, 0, tiled=True)]
    unnamed x32 -> x34, local copies, waits for them, and re-layouts: 3.04 us -> 3.07 us
  transfers between devices with their start and end apart: 5 -> 9, of which waited for: 3 -> 5; matrix products, arithmetic and copies ran while one was open for 1% -> 2% of each run, Pallas kernels for 1% -> 1%
where the time goes in v7:
time: 145 us; the launch traced here: 144 us
  waiting for transfers between devices  44.8 us (31%)
  starting transfers between devices  40.8 us (28%)
  blocking collectives  38 us (26%)
  Pallas kernels  8.73 us (6%)
  local copies, waits for them, and re-layouts  4.91 us (3%)
  matrix products  3.64 us (3%)
  other arithmetic  2.44 us (2%)
    all_to_all x4, waiting for transfers between devices, exchange(): return lax.all_to_all(blocks, axes, 0, 0, tiled=True)  27.7 us
    all_to_all x4, starting transfers between devices, exchange(): return lax.all_to_all(blocks, axes, 0, 0, tiled=True)  26.1 us
    all_to_all x2, blocking collectives, exchange(): return lax.all_to_all(blocks, axes, 0, 0, tiled=True)  25.4 us
    ppermute x1, waiting for transfers between devices, on_device(): from_right = lax.ppermute(up, 'x', back)  12.7 us
    all_gather x1, blocking collectives, on_device(): pair = lax.all_gather(mixed, 'core', axis=0)  8.6 us
    pallas_call x1, Pallas kernels, project(): pl.pallas_call(functools.partial(project_kernel, own_rows), out_shape=jax...  5.15 us
    ppermute x1, starting transfers between devices, on_device(): from_right = lax.ppermute(up, 'x', back)  4.57 us
    ppermute x1, waiting for transfers between devices, on_device(): lax.ppermute(from_left[:half_rank], 'x', ahead)  4.37 us
  transfers between devices with their start and end apart: 9, of which 5 were waited for; matrix products, arithmetic and copies ran while one was open for 2% of the time, Pallas kernels for 1%

profile of v7, /device:TPU:1, one launch (start us, length us, event | category | flops | bytes accessed | tf_op | source)
XLA Modules:
  0.0 143.8 jit_solution(4510267656940907562)
XLA Ops:
  0.0 5.2 %shard_map.163 = bf16[512,1536]{1,0:T(8,128)(2,1)} custom-call(f32[1,128]{1,0:T(1,128)} %bitcast.121, s32[1,128]{1,0:T(1,128)} %bitcast.120, s32[2,16]{1,0:T(2,128)} %bitcast.119, bf16[4,128,128]{2,1,0:T(8,128)(2,1)} %inputs_ref.1, bf16[8,192,128]{2,1,0:T(8,128)(2,1)} %bitcast.102, bf16[128,1024]{1,0:T(8,128)(2,1)} %query_ref.1, bf16[128,128]{1,0:T(8,128)(2,1)} %key_ref.1, ...), custom_call_target="tpu_custom_call" | custom-call | flops 436207616 | bytes 3000000 | tf_op jit(solution)/shard_map/pallas_call | solution.py:161
  5.2 6.0 %all-to-all-start = ((bf16[8,64,1536]{2,1,0:T(8,128)(2,1)}), bf16[8,64,1536]{2,1,0:T(8,128)(2,1)S(1)}, u32[]{:S(2)}, u32[]{:S(2)}) async-start(bf16[8,64,1536]{2,1,0:T(8,128)(2,1)} %bitcast.94), calls=%async_computation | async-start | bytes 3145728 | tf_op jit(solution)/shard_map/sum_plane/all_to_all | solution.py:20
  11.3 4.6 %collective-permute-start.1 = (bf16[64,1280]{1,0:T(8,128)(2,1)S(1)}, bf16[64,1280]{1,0:T(8,128)(2,1)S(1)}, u32[]{:S(2)}, u32[]{:S(2)}) collective-permute-start(bf16[64,1280]{1,0:T(8,128)(2,1)S(1)} %get-tuple-element.16), channel_id=1, source_target_pairs={{0,384},{128,0},{256,128},{384,256},{1,385},{129,1},{257,129},{385... | collective-permute-start | bytes 491528 | tf_op jit(solution)/shard_map/up_x/ppermute | solution.py:393
  15.9 1.9 %collective-permute-start = (bf16[64,1280]{1,0:T(8,128)(2,1)S(1)}, bf16[64,1280]{1,0:T(8,128)(2,1)S(1)}, u32[]{:S(2)}, u32[]{:S(2)}) collective-permute-start(bf16[64,1280]{1,0:T(8,128)(2,1)S(1)} %get-tuple-element.16), channel_id=1, source_target_pairs={{0,128},{128,256},{256,384},{384,0},{1,129},{129,257},{257,385},{3... | collective-permute-start | bytes 491528 | tf_op jit(solution)/shard_map/up_x/ppermute | solution.py:392
  18.6 12.7 %collective-permute-done.1 = bf16[64,1280]{1,0:T(8,128)(2,1)S(1)} collective-permute-done((bf16[64,1280]{1,0:T(8,128)(2,1)S(1)}, bf16[64,1280]{1,0:T(8,128)(2,1)S(1)}, u32[]{:S(2)}, u32[]{:S(2)}) %collective-permute-start.1) | collective-permute-done | bytes 163872 | tf_op jit(solution)/shard_map/up_x/ppermute | solution.py:393
  31.4 3.5 %collective-permute-start.3 = (bf16[32,1280]{1,0:T(8,128)(2,1)S(1)}, bf16[32,1280]{1,0:T(8,128)(2,1)S(1)}, u32[]{:S(2)}, u32[]{:S(2)}) collective-permute-start(bf16[32,1280]{1,0:T(8,128)(2,1)S(1)} %slice.46), channel_id=1, source_target_pairs={{0,384},{128,0},{256,128},{384,256},{1,385},{129,1},{257,129},{385... | collective-permute-start | bytes 245768 | tf_op jit(solution)/shard_map/up_x/ppermute | solution.py:397
  34.9 1.9 %collective-permute-start.2 = (bf16[32,1280]{1,0:T(8,128)(2,1)S(1)}, bf16[32,1280]{1,0:T(8,128)(2,1)S(1)}, u32[]{:S(2)}, u32[]{:S(2)}) collective-permute-start(bf16[32,1280]{1,0:T(8,128)(2,1)S(1)} %slice.45), channel_id=1, source_target_pairs={{0,128},{128,256},{256,384},{384,0},{1,129},{129,257},{257,385},{3... | collective-permute-start | bytes 245768 | tf_op jit(solution)/shard_map/up_x/ppermute | solution.py:396
  36.9 4.4 %collective-permute-done.2 = bf16[32,1280]{1,0:T(8,128)(2,1)S(1)} collective-permute-done((bf16[32,1280]{1,0:T(8,128)(2,1)S(1)}, bf16[32,1280]{1,0:T(8,128)(2,1)S(1)}, u32[]{:S(2)}, u32[]{:S(2)}) %collective-permute-start.2) | collective-permute-done | bytes 81952 | tf_op jit(solution)/shard_map/up_x/ppermute | solution.py:396
  41.3 1.1 pad_maximum_fusion.line_ref
  42.4 2.8 %collective-permute-start.4 = (bf16[4,64,1280]{2,1,0:T(8,128)(2,1)S(1)}, bf16[4,64,1280]{2,1,0:T(8,128)(2,1)}, u32[]{:S(2)}, u32[]{:S(2)}) collective-permute-start(bf16[4,64,1280]{2,1,0:T(8,128)(2,1)S(1)} %pad_maximum_fusion.line_ref), channel_id=1, source_target_pairs={{0,64},{64,0},{1,65},{65,1},{2,66},{66,2},{3,67},{67,3},{4,68},{68... | collective-permute-start | bytes 1966088 | tf_op jit(solution)/shard_map/up_y_lo/ppermute | solution.py:402
  45.2 1.1 shard_map.164
  47.1 13.1 %all-to-all-start.1 = ((bf16[8,64,256]{2,1,0:T(8,128)(2,1)}), bf16[8,64,256]{2,1,0:T(8,128)(2,1)S(1)}, u32[]{:S(2)}, u32[]{:S(2)}) async-start(bf16[8,64,256]{2,1,0:T(8,128)(2,1)} %get-tuple-element.11), calls=%async_computation.1 | async-start | bytes 524288 | tf_op jit(solution)/shard_map/sum_low/all_to_all | solution.py:20
  60.4 9.2 %all-to-all-done.1.low_ref = bf16[8,64,256]{2,1,0:T(8,128)(2,1)S(1)} async-done(((bf16[8,64,256]{2,1,0:T(8,128)(2,1)}), bf16[8,64,256]{2,1,0:T(8,128)(2,1)S(1)}, u32[]{:S(2)}, u32[]{:S(2)}) %all-to-all-start.1) | async-done | bytes 262176 | tf_op jit(solution)/shard_map/sum_low/all_to_all | solution.py:20
  70.5 2.5 %shard_map.165 = bf16[64,1280]{1,0:T(8,128)(2,1)} custom-call(s32[64,1]{1,0:T(8,128)S(1)} %copy.39.slot_ref, bf16[8,64,256]{2,1,0:T(8,128)(2,1)S(1)} %all-to-all-done.1.low_ref, bf16[4,64,1280]{2,1,0:T(8,128)(2,1)S(1)} %pad_maximum_fusion.line_ref, bf16[4,64,1280]{2,1,0:T(8,128)(2,1)} %collective-permute-done.4.other_ref, f32[64,1280]{1,0:T(8,128)S(1)} %copy-done.2), custom_call_target="tpu_custom_call" | custom-call | flops 83886080 | bytes 2000000 | tf_op jit(solution)/shard_map/pallas_call | solution.py:270
  73.0 3.5 %all-to-all-start.2 = ((bf16[8,8,1280]{2,1,0:T(8,128)(2,1)}), bf16[8,8,1280]{2,1,0:T(8,128)(2,1)S(1)}, u32[]{:S(2)}, u32[]{:S(2)}) async-start(bf16[8,8,1280]{2,1,0:T(8,128)(2,1)} %bitcast.13), calls=%async_computation.2 | async-start | bytes 327680 | tf_op jit(solution)/shard_map/sum_z/all_to_all | solution.py:20
  76.7 8.2 %all-to-all-done.2 = bf16[8,8,1280]{2,1,0:T(8,128)(2,1)S(1)} async-done(((bf16[8,8,1280]{2,1,0:T(8,128)(2,1)}), bf16[8,8,1280]{2,1,0:T(8,128)(2,1)S(1)}, u32[]{:S(2)}, u32[]{:S(2)}) %all-to-all-start.2) | async-done | bytes 163872 | tf_op jit(solution)/shard_map/sum_z/all_to_all | solution.py:20
  85.1 1.4 %fusion.41 = (f32[2,32]{1,0:T(2,128)S(1)}, f32[2,32,1024]{2,1,0:T(8,128)S(1)}) fusion(bf16[2,1,1024,128]{3,2,1,0:T(8,128)(2,1)} %param.28, pred[2,1024]{1,0:T(4,128)(4,1)S(1)} %iota_compare_fusion.2, bf16[4,2,8,64]{3,2,1,0:T(8,128)(2,1)S(1)} %bitcast.112, bf16[4,2,8,64]{3,2,1,0:T(8,128)(2,1)S(1)} %bitcast.110), kind=kOutput, calls=%fused_computation.109 | convolution fusion | flops 17006528 | bytes 805120 | tf_op jit(solution)/shard_map/rnd,rjd->rnj/dot_general | solution.py:289
  87.6 10.3 %all_to_all.30 = bf16[8,8,1024]{2,1,0:T(8,128)(2,1)S(1)} all-to-all(bf16[8,8,1024]{2,1,0:T(8,128)(2,1)S(1)} %broadcast_in_dim.153), channel_id=1, replica_groups=mesh['x'=4,'y_lo'=2,'z'=8,'y_hi'=4,'core'=2] {'z'}, dimensions={0} | all-to-all | bytes 262144 | tf_op jit(solution)/shard_map/gather_z/all_to_all | solution.py:20
  97.9 1.1 broadcast_in_dim.155
  99.0 3.6 %all-to-all-start.4 = ((bf16[8,64,1024]{2,1,0:T(8,128)(2,1)}), bf16[8,64,1024]{2,1,0:T(8,128)(2,1)S(1)}, u32[]{:S(2)}, u32[]{:S(2)}) async-start(bf16[8,64,1024]{2,1,0:T(8,128)(2,1)} %broadcast_in_dim.155), calls=%async_computation.4 | async-start | bytes 2097152 | tf_op jit(solution)/shard_map/gather_plane/all_to_all | solution.py:20
  102.6 10.3 %all-to-all-done.4 = bf16[8,64,1024]{2,1,0:T(8,128)(2,1)S(1)} async-done(((bf16[8,64,1024]{2,1,0:T(8,128)(2,1)}), bf16[8,64,1024]{2,1,0:T(8,128)(2,1)S(1)}, u32[]{:S(2)}, u32[]{:S(2)}) %all-to-all-start.4) | async-done | bytes 1048608 | tf_op jit(solution)/shard_map/gather_plane/all_to_all | solution.py:20
  115.1 8.6 %all-gather = bf16[1024,128]{1,0:T(8,128)(2,1)S(1)} all-gather(bf16[512,128]{1,0:T(8,128)(2,1)S(1)} %fusion.1), channel_id=2, replica_groups=mesh['x'=4,'y_lo'=2,'z'=8,'y_hi'=4,'core'=2] {'core'}, dimensions={0}, use_global_device_ids=true | all-gather | bytes 393216 | tf_op jit(solution)/shard_map/sum_core/all_gather | solution.py:475
  124.0 15.1 %all_to_all.31 = bf16[8,128,128]{2,1,0:T(8,128)(2,1)S(1)} all-to-all(bf16[8,128,128]{2,1,0:T(8,128)(2,1)S(1)} %bitcast.97), channel_id=1, replica_groups=mesh['x'=4,'y_lo'=2,'z'=8,'y_hi'=4,'core'=2] {'y_hi'}, dimensions={0} | all-to-all | bytes 524288 | tf_op jit(solution)/shard_map/sum_y_hi/all_to_all | solution.py:20
  139.1 4.0 %all_gather.11 = bf16[4,128,128]{2,1,0:T(8,128)(2,1)S(1)} all-gather(bf16[2,128,128]{2,1,0:T(8,128)(2,1)S(1)} %add_convert_fusion), channel_id=1, replica_groups=mesh['x'=4,'y_lo'=2,'z'=8,'y_hi'=4,'core'=2] {'core'}, dimensions={0}, use_global_device_ids=true | all-gather | bytes 196608 | tf_op jit(solution)/shard_map/gather_core/all_gather | solution.py:495
  (88 shorter events, 7.4 us)
Async XLA Ops:
  0.0 113.0 %copy-start = (bf16[8,1024,64]{1,2,0:T(8,128)(2,1)S(1)}, bf16[8,1024,64]{1,2,0:T(8,128)(2,1)}, u32[]{:S(2)}) copy-start(bf16[8,1024,64]{1,2,0:T(8,128)(2,1)} %param.24) | copy-start | bytes 3145732
  5.2 6.1 %copy-start.9 = (bf16[1,64,2,128]{3,2,1,0:T(2,128)(2,1)S(1)}, bf16[1,64,2,128]{3,2,1,0:T(2,128)(2,1)}, u32[]{:S(2)}) copy-start(bf16[1,64,2,128]{3,2,1,0:T(2,128)(2,1)} %param.27) | copy-start | bytes 98308
  5.2 6.1 %copy-start.7 = (bf16[1,64,1024]{2,1,0:T(8,128)(2,1)S(1)}, bf16[1,64,1024]{2,1,0:T(8,128)(2,1)}, u32[]{:S(2)}) copy-start(bf16[1,64,1024]{2,1,0:T(8,128)(2,1)} %param.26) | copy-start | bytes 393220
  5.2 12.6 %copy-start.12 = (s32[128]{0:T(128)S(1)}, s32[128]{0:T(128)}, u32[]{:S(2)}) copy-start(s32[128]{0:T(128)} %param.30) | copy-start | bytes 1540
  5.2 12.8 %copy-start.10 = (s32[16,2]{0,1:T(2,128)S(1)}, s32[16,2]{0,1:T(2,128)}, u32[]{:S(2)}) copy-start(s32[16,2]{0,1:T(2,128)} %param.32) | copy-start | bytes 388
  5.2 13.3 %copy-start.11 = (s32[2]{0:T(128)S(1)}, s32[2]{0:T(128)}, u32[]{:S(2)}) copy-start(s32[2]{0:T(128)} %param.33) | copy-start | bytes 28
  5.2 40.0 %all-to-all-start = ((bf16[8,64,1536]{2,1,0:T(8,128)(2,1)}), bf16[8,64,1536]{2,1,0:T(8,128)(2,1)S(1)}, u32[]{:S(2)}, u32[]{:S(2)}) async-start(bf16[8,64,1536]{2,1,0:T(8,128)(2,1)} %bitcast.94), calls=%async_computation | async-start | bytes 3145728 | tf_op jit(solution)/shard_map/sum_plane/all_to_all | solution.py:20
  11.2 25.6 %copy-start.13 = (s32[8]{0:T(128)S(1)}, s32[8]{0:T(128)}, u32[]{:S(2)}) copy-start(s32[8]{0:T(128)} %param.31) | copy-start | bytes 100
  11.3 20.1 %collective-permute-start.1 = (bf16[64,1280]{1,0:T(8,128)(2,1)S(1)}, bf16[64,1280]{1,0:T(8,128)(2,1)S(1)}, u32[]{:S(2)}, u32[]{:S(2)}) collective-permute-start(bf16[64,1280]{1,0:T(8,128)(2,1)S(1)} %get-tuple-element.16), channel_id=1, source_target_pairs={{0,384},{128,0},{256,128},{384,256},{1,385},{129,1},{257,129},{385... | collective-permute-start | bytes 491528 | tf_op jit(solution)/shard_map/up_x/ppermute | solution.py:393
  15.9 19.0 %collective-permute-start = (bf16[64,1280]{1,0:T(8,128)(2,1)S(1)}, bf16[64,1280]{1,0:T(8,128)(2,1)S(1)}, u32[]{:S(2)}, u32[]{:S(2)}) collective-permute-start(bf16[64,1280]{1,0:T(8,128)(2,1)S(1)} %get-tuple-element.16), channel_id=1, source_target_pairs={{0,128},{128,256},{256,384},{384,0},{1,129},{129,257},{257,385},{3... | collective-permute-start | bytes 491528 | tf_op jit(solution)/shard_map/up_x/ppermute | solution.py:392
  31.4 9.9 %copy-start.3 = (bf16[64,1280]{1,0:T(8,128)(2,1)}, bf16[64,1280]{1,0:T(8,128)(2,1)S(1)}, u32[]{:S(2)}) copy-start(bf16[64,1280]{1,0:T(8,128)(2,1)S(1)} %collective-permute-done.1) | copy-start | bytes 491524
  31.4 5.5 %collective-permute-start.3 = (bf16[32,1280]{1,0:T(8,128)(2,1)S(1)}, bf16[32,1280]{1,0:T(8,128)(2,1)S(1)}, u32[]{:S(2)}, u32[]{:S(2)}) collective-permute-start(bf16[32,1280]{1,0:T(8,128)(2,1)S(1)} %slice.46), channel_id=1, source_target_pairs={{0,384},{128,0},{256,128},{384,256},{1,385},{129,1},{257,129},{385... | collective-permute-start | bytes 245768 | tf_op jit(solution)/shard_map/up_x/ppermute | solution.py:397
  34.9 6.4 %copy-start.4 = (bf16[64,1280]{1,0:T(8,128)(2,1)}, bf16[64,1280]{1,0:T(8,128)(2,1)S(1)}, u32[]{:S(2)}) copy-start(bf16[64,1280]{1,0:T(8,128)(2,1)S(1)} %collective-permute-done) | copy-start | bytes 491524
  34.9 6.4 %collective-permute-start.2 = (bf16[32,1280]{1,0:T(8,128)(2,1)S(1)}, bf16[32,1280]{1,0:T(8,128)(2,1)S(1)}, u32[]{:S(2)}, u32[]{:S(2)}) collective-permute-start(bf16[32,1280]{1,0:T(8,128)(2,1)S(1)} %slice.45), channel_id=1, source_target_pairs={{0,128},{128,256},{256,384},{384,0},{1,129},{129,257},{257,385},{3... | collective-permute-start | bytes 245768 | tf_op jit(solution)/shard_map/up_x/ppermute | solution.py:396
  42.4 18.0 %collective-permute-start.4 = (bf16[4,64,1280]{2,1,0:T(8,128)(2,1)S(1)}, bf16[4,64,1280]{2,1,0:T(8,128)(2,1)}, u32[]{:S(2)}, u32[]{:S(2)}) collective-permute-start(bf16[4,64,1280]{2,1,0:T(8,128)(2,1)S(1)} %pad_maximum_fusion.line_ref), channel_id=1, source_target_pairs={{0,64},{64,0},{1,65},{65,1},{2,66},{66,2},{3,67},{67,3},{4,68},{68... | collective-permute-start | bytes 1966088 | tf_op jit(solution)/shard_map/up_y_lo/ppermute | solution.py:402
  46.3 0.7 copy-start.1
  47.1 22.5 %all-to-all-start.1 = ((bf16[8,64,256]{2,1,0:T(8,128)(2,1)}), bf16[8,64,256]{2,1,0:T(8,128)(2,1)S(1)}, u32[]{:S(2)}, u32[]{:S(2)}) async-start(bf16[8,64,256]{2,1,0:T(8,128)(2,1)} %get-tuple-element.11), calls=%async_computation.1 | async-start | bytes 524288 | tf_op jit(solution)/shard_map/sum_low/all_to_all | solution.py:20
  69.5 1.0 copy-start.2
  73.0 14.0 %copy-start.14 = (bf16[2,1,1024,128]{3,2,1,0:T(8,128)(2,1)S(1)}, bf16[2,1,1024,128]{3,2,1,0:T(8,128)(2,1)}, u32[]{:S(2)}) copy-start(bf16[2,1,1024,128]{3,2,1,0:T(8,128)(2,1)} %param.29) | copy-start | bytes 1572868
  73.0 11.8 %all-to-all-start.2 = ((bf16[8,8,1280]{2,1,0:T(8,128)(2,1)}), bf16[8,8,1280]{2,1,0:T(8,128)(2,1)S(1)}, u32[]{:S(2)}, u32[]{:S(2)}) async-start(bf16[8,8,1280]{2,1,0:T(8,128)(2,1)} %bitcast.13), calls=%async_computation.2 | async-start | bytes 327680 | tf_op jit(solution)/shard_map/sum_z/all_to_all | solution.py:20
  99.0 13.9 %all-to-all-start.4 = ((bf16[8,64,1024]{2,1,0:T(8,128)(2,1)}), bf16[8,64,1024]{2,1,0:T(8,128)(2,1)S(1)}, u32[]{:S(2)}, u32[]{:S(2)}) async-start(bf16[8,64,1024]{2,1,0:T(8,128)(2,1)} %broadcast_in_dim.155), calls=%async_computation.4 | async-start | bytes 2097152 | tf_op jit(solution)/shard_map/gather_plane/all_to_all | solution.py:20
  113.0 0.9 copy-start.8
  113.7 1.0 copy-start.6
  114.7 24.4 %copy-start.5 = (bf16[4,128,128]{2,1,0:T(8,128)(2,1)S(1)}, bf16[4,128,128]{2,1,0:T(8,128)(2,1)}, u32[]{:S(2)}) copy-start(bf16[4,128,128]{2,1,0:T(8,128)(2,1)} %inputs_ref.1) | copy-start | bytes 393220

commit v8 on v6

--- a/solution.py
+++ b/solution.py
@@ -174,44 +174,36 @@
     )(gain[None, :], tasks[None, :], moves.T, *large)
 
 
-def plane_kernel(low, parts_ref, base_ref, low_ref):
+def low_kernel(low, parts_ref, low_ref):
     sources, rows, columns = parts_ref.shape
-    base_end = base_ref.shape[1]
-    @pl.loop(0, rows // 16)
-    def _(index):
-        part = pl.ds(pl.multiple_of(index * 16, 16), 16)
-        total = parts_ref[0, part, :].astype(jnp.float32)
-        for source in range(1, sources):
-            total = total + parts_ref[source, part, :].astype(jnp.float32)
-        base_ref[part, :] = total[:, :base_end]
-        last = total[:, base_end:]
-        lane = lax.broadcasted_iota(jnp.int32, last.shape, 1)
-        squares = jnp.sum(jnp.where(lane >= low, last, 0.0), axis=1, keepdims=True)
-        squares_high = squares.astype(jnp.bfloat16).astype(jnp.float32)
-        last = jnp.where(
-            lane < low,
-            last,
-            jnp.where(
-                lane == low, squares_high, jnp.where(lane == low + 1, squares - squares_high, 0.0)
-            ),
-        ).astype(jnp.bfloat16)
-        for target in range(low_ref.shape[0]):
-            low_ref[target, part, :] = last
-
-
-def sum_plane(parts, base_end, low, depth):
-    sources, rows, columns = parts.shape
+    targets, _, width = low_ref.shape
+    total = parts_ref[0, :, columns - width :].astype(jnp.float32)
+    for source in range(1, sources):
+        total = total + parts_ref[source, :, columns - width :].astype(jnp.float32)
+    lane = lax.broadcasted_iota(jnp.int32, total.shape, 1)
+    squares = jnp.sum(jnp.where(lane >= low, total, 0.0), axis=1, keepdims=True)
+    squares_high = squares.astype(jnp.bfloat16).astype(jnp.float32)
+    total = jnp.where(
+        lane < low,
+        total,
+        jnp.where(
+            lane == low, squares_high, jnp.where(lane == low + 1, squares - squares_high, 0.0)
+        ),
+    ).astype(jnp.bfloat16)
+    for target in range(targets):
+        low_ref[target] = total
+
+
+def sum_low(parts, base_end, low, depth):
+    _, rows, columns = parts.shape
     return pl.pallas_call(
-        functools.partial(plane_kernel, low),
-        out_shape=[
-            jax.ShapeDtypeStruct((rows, base_end), jnp.float32),
-            jax.ShapeDtypeStruct((depth, rows, columns - base_end), jnp.bfloat16),
-        ],
+        functools.partial(low_kernel, low),
+        out_shape=jax.ShapeDtypeStruct((depth, rows, columns - base_end), jnp.bfloat16),
         in_specs=[pl.BlockSpec(memory_space=pltpu.VMEM)],
-        out_specs=[pl.BlockSpec(memory_space=pltpu.VMEM)] * 2,
+        out_specs=pl.BlockSpec(memory_space=pltpu.VMEM),
         compiler_params=pltpu.CompilerParams(vmem_limit_bytes=16 * 1024 * 1024),
         cost_estimate=pl.CostEstimate(
-            flops=parts.size, bytes_accessed=2 * parts.size, transcendentals=0
+            flops=parts.size // 6, bytes_accessed=parts.size // 3, transcendentals=0
         ),
     )(parts)
 
@@ -226,11 +218,7 @@
     other_ref,
     base_ref,
     out_ref,
-    held_base,
-    arrived,
 ):
-    copy = pltpu.make_async_copy(base_ref, held_base, arrived)
-    copy.start()
     rows, columns = out_ref.shape
     line = line_ref.shape[0]
     low = 3 * rank
@@ -255,7 +243,6 @@
                 for half in range(2)
             ]
         )
-    copy.wait()
     key_first, value_first = columns - 2 * head_dim, columns - head_dim
     bounds = ((0, key_first), (key_first, value_first), (value_first, columns))
     for (first, last), (near, far) in zip(bounds, spreads, strict=True):
@@ -263,17 +250,15 @@
         lifted = lifted + dot(
             far, other_ref[:, :, first:last].reshape(line * rank, last - first)
         )
-        out_ref[:, first:last] = (inverse * held_base[:, first:last] + lifted).astype(jnp.bfloat16)
+        out_ref[:, first:last] = (inverse * base_ref[:, first:last] + lifted).astype(jnp.bfloat16)
 
 
 def lift(slot, low_parts, base, up_line, up_other, rank, head_dim, model_width):
     return pl.pallas_call(
         functools.partial(lift_kernel, rank, head_dim, model_width),
         out_shape=jax.ShapeDtypeStruct(base.shape, jnp.bfloat16),
-        in_specs=[pl.BlockSpec(memory_space=pltpu.VMEM)] * 4
-        + [pl.BlockSpec(memory_space=pl.ANY)],
+        in_specs=[pl.BlockSpec(memory_space=pltpu.VMEM)] * 5,
         out_specs=pl.BlockSpec(memory_space=pltpu.VMEM),
-        scratch_shapes=[pltpu.VMEM(base.shape, jnp.float32), pltpu.SemaphoreType.DMA(())],
         compiler_params=pltpu.CompilerParams(vmem_limit_bytes=16 * 1024 * 1024),
         cost_estimate=pl.CostEstimate(
             flops=2 * base.size * up_line.shape[0] * 2 * rank,
@@ -361,6 +346,18 @@
     marks = active[:, None] == jnp.arange(task_count, dtype=jnp.int32)[None, :]
     row_home = jnp.sum(jnp.where(marks, homes[None, :], 0), axis=1)
 
+    up = jnp.concatenate(
+        [
+            pool_query.reshape(rank, query_width),
+            slot_keyvalue_matrices.reshape(rank, 2 * head_dim),
+        ],
+        axis=1,
+    )
+    with jax.named_scope("up_x"):
+        up_line = exchange(
+            jnp.broadcast_to(up[None], (line, rank, base_end)), "x"
+        )
+
     partial = project(
         inputs,
         gain,
@@ -372,24 +369,16 @@
         moves,
         own_rows,
     )
-    partial, pool_query, slot_keyvalue_matrices = lax.optimization_barrier(
-        (partial, pool_query, slot_keyvalue_matrices)
-    )
+    partial, up_line = lax.optimization_barrier((partial, up_line))
     with jax.named_scope("sum_plane"):
         by_plane = exchange(partial.reshape(planes, column_rows, -1), PLANE)
 
-    up = jnp.concatenate(
-        [
-            pool_query.reshape(rank, query_width),
-            slot_keyvalue_matrices.reshape(rank, 2 * head_dim),
-        ],
-        axis=1,
-    )
-    with jax.named_scope("up_x"):
-        up_line = lax.all_gather(up, "x", axis=0)
+    up_line, by_plane = lax.optimization_barrier((up_line, by_plane))
     with jax.named_scope("up_y_lo"):
         up_other = lax.ppermute(up_line, "y_lo", [(0, 1), (1, 0)])
-    plane_sum, low_part = sum_plane(by_plane, base_end, 3 * rank, depth)
+
+    low_part = sum_low(by_plane, base_end, 3 * rank, depth)
+    plane_sum = jnp.sum(by_plane[:, :, :base_end].astype(jnp.float32), axis=0)
     with jax.named_scope("sum_low"):
         low_parts = exchange(low_part, "z")
 

time: 139 us -> 143 us (1.029)
  blocking collectives: 65.6 us -> 37.5 us
  waiting for transfers between devices: 27.4 us -> 44.5 us
  starting transfers between devices: 27.2 us -> 35.2 us
  other arithmetic: 1.33 us -> 4.25 us
  local copies, waits for them, and re-layouts: 4.87 us -> 7.25 us
  matrix products: 2.61 us -> 4.69 us
    all_gather x1 -> x0, blocking collectives: 25.8 us -> none  [on_device(): up_line = lax.all_gather(up, 'x', axis=0)]
    all_to_all x4 -> x5, waiting for transfers between devices: 27.4 us -> 44.5 us  [exchange(): return lax.all_to_all(blocks, axes, 0, 0, tiled=True)]
    all_to_all x4 -> x5, starting transfers between devices: 24.5 us -> 32.8 us  [exchange(): return lax.all_to_all(blocks, axes, 0, 0, tiled=True)]
    all_gather x1, blocking collectives: 10.4 us -> 7.29 us  [on_device(): pair = lax.all_gather(mixed, 'core', axis=0)]
    unnamed x32 -> x28, local copies, waits for them, and re-layouts: 3.04 us -> 3.91 us
  transfers between devices with their start and end apart: 5 -> 6, of which waited for: 3 -> 5; matrix products, arithmetic and copies ran while one was open for 1% -> 3% of each run, Pallas kernels for 1% -> 4%
where the time goes in v8:
time: 143 us; the launch traced here: 142 us
  waiting for transfers between devices  44.5 us (31%)
  blocking collectives  37.5 us (26%)
  starting transfers between devices  35.2 us (25%)
  Pallas kernels  8.16 us (6%)
  local copies, waits for them, and re-layouts  7.25 us (5%)
  matrix products  4.69 us (3%)
  other arithmetic  4.25 us (3%)
    all_to_all x5, waiting for transfers between devices, exchange(): return lax.all_to_all(blocks, axes, 0, 0, tiled=True)  44.5 us
    all_to_all x5, starting transfers between devices, exchange(): return lax.all_to_all(blocks, axes, 0, 0, tiled=True)  32.8 us
    all_to_all x2, blocking collectives, exchange(): return lax.all_to_all(blocks, axes, 0, 0, tiled=True)  26.3 us
    all_gather x1, blocking collectives, on_device(): pair = lax.all_gather(mixed, 'core', axis=0)  7.29 us
    pallas_call x1, Pallas kernels, project(): pl.pallas_call(functools.partial(project_kernel, own_rows), out_shape=jax...  5.07 us
    all_gather x1, blocking collectives, on_device(): return lax.all_gather(finished, 'core', axis=0, tiled=True)  3.99 us
    unnamed x28, local copies, waits for them, and re-layouts  3.91 us
  transfers between devices with their start and end apart: 6, of which 5 were waited for; matrix products, arithmetic and copies ran while one was open for 3% of the time, Pallas kernels for 4%

profile of v8, /device:TPU:1, one launch (start us, length us, event | category | flops | bytes accessed | tf_op | source)
XLA Modules:
  0.0 142.0 jit_solution(7610283093684388947)
XLA Ops:
  0.9 0.9 pad_maximum_fusion
  1.8 0.9 broadcast_in_dim.152
  2.7 4.8 %all-to-all-start = ((bf16[4,64,1280]{2,1,0:T(8,128)(2,1)}), bf16[4,64,1280]{2,1,0:T(8,128)(2,1)S(1)}, u32[]{:S(2)}, u32[]{:S(2)}) async-start(bf16[4,64,1280]{2,1,0:T(8,128)(2,1)} %broadcast_in_dim.152), calls=%async_computation | async-start | bytes 1310720 | tf_op jit(solution)/shard_map/up_x/all_to_all | solution.py:20
  7.5 5.1 %shard_map.163 = bf16[512,1536]{1,0:T(8,128)(2,1)} custom-call(f32[1,128]{1,0:T(1,128)} %bitcast.113, s32[1,128]{1,0:T(1,128)} %bitcast.112, s32[2,16]{1,0:T(2,128)} %bitcast.111, bf16[4,128,128]{2,1,0:T(8,128)(2,1)} %inputs_ref.1, bf16[8,192,128]{2,1,0:T(8,128)(2,1)} %bitcast.96, bf16[128,1024]{1,0:T(8,128)(2,1)} %query_ref.1, bf16[128,128]{1,0:T(8,128)(2,1)} %key_ref.1, ...), custom_call_target="tpu_custom_call" | custom-call | flops 436207616 | bytes 3000000 | tf_op jit(solution)/shard_map/pallas_call | solution.py:161
  12.6 2.6 %all-to-all-done.line_ref = bf16[4,64,1280]{2,1,0:T(8,128)(2,1)S(1)} async-done(((bf16[4,64,1280]{2,1,0:T(8,128)(2,1)}), bf16[4,64,1280]{2,1,0:T(8,128)(2,1)S(1)}, u32[]{:S(2)}, u32[]{:S(2)}) %all-to-all-start) | async-done | bytes 655392 | tf_op jit(solution)/shard_map/up_x/all_to_all | solution.py:20
  15.2 5.7 %all-to-all-start.1 = ((bf16[8,64,1536]{2,1,0:T(8,128)(2,1)}), bf16[8,64,1536]{2,1,0:T(8,128)(2,1)S(1)}, u32[]{:S(2)}, u32[]{:S(2)}) async-start(bf16[8,64,1536]{2,1,0:T(8,128)(2,1)} %bitcast.88), calls=%async_computation.1 | async-start | bytes 3145728 | tf_op jit(solution)/shard_map/sum_plane/all_to_all | solution.py:20
  22.5 15.1 %all-to-all-done.1.parts_ref = bf16[8,64,1536]{2,1,0:T(8,128)(2,1)S(1)} async-done(((bf16[8,64,1536]{2,1,0:T(8,128)(2,1)}), bf16[8,64,1536]{2,1,0:T(8,128)(2,1)S(1)}, u32[]{:S(2)}, u32[]{:S(2)}) %all-to-all-start.1) | async-done | bytes 1572896 | tf_op jit(solution)/shard_map/sum_plane/all_to_all | solution.py:20
  37.6 2.5 %collective-permute-start = (bf16[4,64,1280]{2,1,0:T(8,128)(2,1)S(1)}, bf16[4,64,1280]{2,1,0:T(8,128)(2,1)}, u32[]{:S(2)}, u32[]{:S(2)}) collective-permute-start(bf16[4,64,1280]{2,1,0:T(8,128)(2,1)S(1)} %all-to-all-done.line_ref), channel_id=1, source_target_pairs={{0,64},{64,0},{1,65},{65,1},{2,66},{66,2},{3,67},{67,3},{4,68},{68... | collective-permute-start | bytes 1966088 | tf_op jit(solution)/shard_map/up_y_lo/ppermute | solution.py:378
  41.3 12.7 %all-to-all-start.2 = ((bf16[8,64,256]{2,1,0:T(8,128)(2,1)}), bf16[8,64,256]{2,1,0:T(8,128)(2,1)S(1)}, u32[]{:S(2)}, u32[]{:S(2)}) async-start(bf16[8,64,256]{2,1,0:T(8,128)(2,1)} %shard_map.164), calls=%async_computation.2 | async-start | bytes 524288 | tf_op jit(solution)/shard_map/sum_low/all_to_all | solution.py:20
  54.8 0.9 convert_reduce_fusion.base_ref
  55.8 7.7 %all-to-all-done.2.low_ref = bf16[8,64,256]{2,1,0:T(8,128)(2,1)S(1)} async-done(((bf16[8,64,256]{2,1,0:T(8,128)(2,1)}), bf16[8,64,256]{2,1,0:T(8,128)(2,1)S(1)}, u32[]{:S(2)}, u32[]{:S(2)}) %all-to-all-start.2) | async-done | bytes 262176 | tf_op jit(solution)/shard_map/sum_low/all_to_all | solution.py:20
  63.5 1.0 copy-done.1
  65.2 2.3 %shard_map.165 = bf16[64,1280]{1,0:T(8,128)(2,1)} custom-call(s32[64,1]{1,0:T(8,128)S(1)} %copy-done.2, bf16[8,64,256]{2,1,0:T(8,128)(2,1)S(1)} %all-to-all-done.2.low_ref, bf16[4,64,1280]{2,1,0:T(8,128)(2,1)S(1)} %all-to-all-done.line_ref, bf16[4,64,1280]{2,1,0:T(8,128)(2,1)} %collective-permute-done.other_ref, f32[64,1280]{1,0:T(8,128)S(1)} %copy-done.1), custom_call_target="tpu_custom_call" | custom-call | flops 83886080 | bytes 2000000 | tf_op jit(solution)/shard_map/pallas_call | solution.py:257
  67.5 3.4 %all-to-all-start.3 = ((bf16[8,8,1280]{2,1,0:T(8,128)(2,1)}), bf16[8,8,1280]{2,1,0:T(8,128)(2,1)S(1)}, u32[]{:S(2)}, u32[]{:S(2)}) async-start(bf16[8,8,1280]{2,1,0:T(8,128)(2,1)} %bitcast.9), calls=%async_computation.3 | async-start | bytes 327680 | tf_op jit(solution)/shard_map/sum_z/all_to_all | solution.py:20
  71.0 8.1 %all-to-all-done.3 = bf16[8,8,1280]{2,1,0:T(8,128)(2,1)S(1)} async-done(((bf16[8,8,1280]{2,1,0:T(8,128)(2,1)}), bf16[8,8,1280]{2,1,0:T(8,128)(2,1)S(1)}, u32[]{:S(2)}, u32[]{:S(2)}) %all-to-all-start.3) | async-done | bytes 163872 | tf_op jit(solution)/shard_map/sum_z/all_to_all | solution.py:20
  79.3 1.4 %fusion.39 = (f32[2,32]{1,0:T(2,128)S(1)}, f32[2,32,1024]{2,1,0:T(8,128)S(1)}) fusion(bf16[2,1,1024,128]{3,2,1,0:T(8,128)(2,1)} %param.28, pred[2,1024]{1,0:T(4,128)(4,1)S(1)} %iota_compare_fusion.2, bf16[4,2,8,64]{3,2,1,0:T(8,128)(2,1)S(1)} %bitcast.104, bf16[4,2,8,64]{3,2,1,0:T(8,128)(2,1)S(1)} %bitcast.102), kind=kOutput, calls=%fused_computation.101 | convolution fusion | flops 17006528 | bytes 805120 | tf_op jit(solution)/shard_map/rnd,rjd->rnj/dot_general | solution.py:274
  81.2 1.3 fusion.4
  82.8 10.3 %all_to_all.35 = bf16[8,8,1024]{2,1,0:T(8,128)(2,1)S(1)} all-to-all(bf16[8,8,1024]{2,1,0:T(8,128)(2,1)S(1)} %broadcast_in_dim.157), channel_id=1, replica_groups=mesh['x'=4,'y_lo'=2,'z'=8,'y_hi'=4,'core'=2] {'z'}, dimensions={0} | all-to-all | bytes 262144 | tf_op jit(solution)/shard_map/gather_z/all_to_all | solution.py:20
  93.2 1.1 broadcast_in_dim.159
  94.3 6.2 %all-to-all-start.5 = ((bf16[8,64,1024]{2,1,0:T(8,128)(2,1)}), bf16[8,64,1024]{2,1,0:T(8,128)(2,1)S(1)}, u32[]{:S(2)}, u32[]{:S(2)}) async-start(bf16[8,64,1024]{2,1,0:T(8,128)(2,1)} %broadcast_in_dim.159), calls=%async_computation.5 | async-start | bytes 2097152 | tf_op jit(solution)/shard_map/gather_plane/all_to_all | solution.py:20
  100.5 11.1 %all-to-all-done.5 = bf16[8,64,1024]{2,1,0:T(8,128)(2,1)S(1)} async-done(((bf16[8,64,1024]{2,1,0:T(8,128)(2,1)}), bf16[8,64,1024]{2,1,0:T(8,128)(2,1)S(1)}, u32[]{:S(2)}, u32[]{:S(2)}) %all-to-all-start.5) | async-done | bytes 1048608 | tf_op jit(solution)/shard_map/gather_plane/all_to_all | solution.py:20
  113.7 7.3 %all-gather = bf16[1024,128]{1,0:T(8,128)(2,1)S(1)} all-gather(bf16[512,128]{1,0:T(8,128)(2,1)S(1)} %fusion.1), channel_id=2, replica_groups=mesh['x'=4,'y_lo'=2,'z'=8,'y_hi'=4,'core'=2] {'core'}, dimensions={0}, use_global_device_ids=true | all-gather | bytes 393216 | tf_op jit(solution)/shard_map/sum_core/all_gather | solution.py:452
  121.3 16.0 %all_to_all.36 = bf16[8,128,128]{2,1,0:T(8,128)(2,1)S(1)} all-to-all(bf16[8,128,128]{2,1,0:T(8,128)(2,1)S(1)} %bitcast.91), channel_id=1, replica_groups=mesh['x'=4,'y_lo'=2,'z'=8,'y_hi'=4,'core'=2] {'y_hi'}, dimensions={0} | all-to-all | bytes 524288 | tf_op jit(solution)/shard_map/sum_y_hi/all_to_all | solution.py:20
  137.3 4.0 %all_gather.11 = bf16[4,128,128]{2,1,0:T(8,128)(2,1)S(1)} all-gather(bf16[2,128,128]{2,1,0:T(8,128)(2,1)S(1)} %add_convert_fusion), channel_id=1, replica_groups=mesh['x'=4,'y_lo'=2,'z'=8,'y_hi'=4,'core'=2] {'core'}, dimensions={0}, use_global_device_ids=true | all-gather | bytes 196608 | tf_op jit(solution)/shard_map/gather_core/all_gather | solution.py:472
  (74 shorter events, 9.5 us)
Async XLA Ops:
  0.0 111.6 %copy-start = (bf16[8,1024,64]{1,2,0:T(8,128)(2,1)S(1)}, bf16[8,1024,64]{1,2,0:T(8,128)(2,1)}, u32[]{:S(2)}) copy-start(bf16[8,1024,64]{1,2,0:T(8,128)(2,1)} %param.24) | copy-start | bytes 3145732
  2.7 12.5 %all-to-all-start = ((bf16[4,64,1280]{2,1,0:T(8,128)(2,1)}), bf16[4,64,1280]{2,1,0:T(8,128)(2,1)S(1)}, u32[]{:S(2)}, u32[]{:S(2)}) async-start(bf16[4,64,1280]{2,1,0:T(8,128)(2,1)} %broadcast_in_dim.152), calls=%async_computation | async-start | bytes 1310720 | tf_op jit(solution)/shard_map/up_x/all_to_all | solution.py:20
  15.1 5.7 %copy-start.9 = (s32[128]{0:T(128)S(1)}, s32[128]{0:T(128)}, u32[]{:S(2)}) copy-start(s32[128]{0:T(128)} %param.30) | copy-start | bytes 1540
  15.1 5.8 %copy-start.7 = (s32[2]{0:T(128)S(1)}, s32[2]{0:T(128)}, u32[]{:S(2)}) copy-start(s32[2]{0:T(128)} %param.33) | copy-start | bytes 28
  15.1 5.9 %copy-start.6 = (s32[16,2]{0,1:T(2,128)S(1)}, s32[16,2]{0,1:T(2,128)}, u32[]{:S(2)}) copy-start(s32[16,2]{0,1:T(2,128)} %param.32) | copy-start | bytes 388
  15.2 25.2 %copy-start.10 = (s32[8]{0:T(128)S(1)}, s32[8]{0:T(128)}, u32[]{:S(2)}) copy-start(s32[8]{0:T(128)} %param.31) | copy-start | bytes 100
  15.2 22.4 %all-to-all-start.1 = ((bf16[8,64,1536]{2,1,0:T(8,128)(2,1)}), bf16[8,64,1536]{2,1,0:T(8,128)(2,1)S(1)}, u32[]{:S(2)}, u32[]{:S(2)}) async-start(bf16[8,64,1536]{2,1,0:T(8,128)(2,1)} %bitcast.88), calls=%async_computation.1 | async-start | bytes 3145728 | tf_op jit(solution)/shard_map/sum_plane/all_to_all | solution.py:20
  37.6 25.8 %collective-permute-start = (bf16[4,64,1280]{2,1,0:T(8,128)(2,1)S(1)}, bf16[4,64,1280]{2,1,0:T(8,128)(2,1)}, u32[]{:S(2)}, u32[]{:S(2)}) collective-permute-start(bf16[4,64,1280]{2,1,0:T(8,128)(2,1)S(1)} %all-to-all-done.line_ref), channel_id=1, source_target_pairs={{0,64},{64,0},{1,65},{65,1},{2,66},{66,2},{3,67},{67,3},{4,68},{68... | collective-permute-start | bytes 1966088 | tf_op jit(solution)/shard_map/up_y_lo/ppermute | solution.py:378
  41.3 22.1 %all-to-all-start.2 = ((bf16[8,64,256]{2,1,0:T(8,128)(2,1)}), bf16[8,64,256]{2,1,0:T(8,128)(2,1)S(1)}, u32[]{:S(2)}, u32[]{:S(2)}) async-start(bf16[8,64,256]{2,1,0:T(8,128)(2,1)} %shard_map.164), calls=%async_computation.2 | async-start | bytes 524288 | tf_op jit(solution)/shard_map/sum_low/all_to_all | solution.py:20
  54.8 16.0 %copy-start.8 = (f32[8]{0:T(128)S(1)}, f32[8]{0:T(128)}, u32[]{:S(2)}) copy-start(f32[8]{0:T(128)} %fusion.33) | copy-start | bytes 100
  54.8 25.9 %copy-start.11 = (pred[32,4]{0,1:T(4,128)(4,1)S(1)}, pred[32,4]{0,1:T(4,128)(4,1)}, u32[]{:S(2)}) copy-start(pred[32,4]{0,1:T(4,128)(4,1)} %iota_compare_fusion.3) | copy-start | bytes 388
  63.4 1.0 copy-start.1
  64.4 0.8 copy-start.2
  67.5 11.6 %all-to-all-start.3 = ((bf16[8,8,1280]{2,1,0:T(8,128)(2,1)}), bf16[8,8,1280]{2,1,0:T(8,128)(2,1)S(1)}, u32[]{:S(2)}, u32[]{:S(2)}) async-start(bf16[8,8,1280]{2,1,0:T(8,128)(2,1)} %bitcast.9), calls=%async_computation.3 | async-start | bytes 327680 | tf_op jit(solution)/shard_map/sum_z/all_to_all | solution.py:20
  94.3 17.3 %all-to-all-start.5 = ((bf16[8,64,1024]{2,1,0:T(8,128)(2,1)}), bf16[8,64,1024]{2,1,0:T(8,128)(2,1)S(1)}, u32[]{:S(2)}, u32[]{:S(2)}) async-start(bf16[8,64,1024]{2,1,0:T(8,128)(2,1)} %broadcast_in_dim.159), calls=%async_computation.5 | async-start | bytes 2097152 | tf_op jit(solution)/shard_map/gather_plane/all_to_all | solution.py:20
  111.6 0.9 copy-start.5
  112.3 1.0 copy-start.4
  113.3 24.0 %copy-start.3 = (bf16[4,128,128]{2,1,0:T(8,128)(2,1)S(1)}, bf16[4,128,128]{2,1,0:T(8,128)(2,1)}, u32[]{:S(2)}) copy-start(bf16[4,128,128]{2,1,0:T(8,128)(2,1)} %inputs_ref.1) | copy-start | bytes 393220

commit v9 on v8

--- a/solution.py
+++ b/solution.py
@@ -95,7 +95,7 @@
     gathered = held_inputs[...].reshape(every_row, width)
     squares_of = []
     for first in range(0, every_row, block):
-        row = first + lax.broadcasted_iota(jnp.int32, (block, every_row), 0)
+        row = first + lax.broadcasted_iota(jnp.int32, (block, 1), 0)
         place = row % per_group // own_rows * all_rows + row // per_group * own_rows + row % own_rows
         order = jnp.where(lane(every_row) == place, 1.0, 0.0).astype(jnp.bfloat16)
         states = dot(order, gathered)
@@ -106,17 +106,13 @@
     for index, squares in enumerate(squares_of):
         first = index * block
 
-        def row_of(width):
-            return first + lax.broadcasted_iota(jnp.int32, (block, width), 0)
-
-        row = row_of(all_rows)
+        row = first + lax.broadcasted_iota(jnp.int32, (block, 1), 0)
         own = lane(all_rows) == row // per_group * own_rows + row % own_rows
         task = jnp.sum(jnp.where(own, tasks_ref[...], 0), axis=1, keepdims=True)
-        moves = moves_ref.shape[1]
-        here = moves_ref[1:2, :] == row_of(moves) // per_group
+        here = moves_ref[1:2, :] == row // per_group
         moved = jnp.sum(jnp.where(here, 1, 0), axis=1, keepdims=True) > 0
         chosen = jnp.sum(jnp.where(here, moves_ref[0:1, :], 0), axis=1, keepdims=True)
-        late = row_of(1) % per_group >= per_group // 2
+        late = row % per_group >= per_group // 2
         task = jnp.where(jnp.logical_and(late, moved), chosen, task)
         gained = gained_ref[first : first + block, :]
         total = jnp.zeros((block, low), jnp.float32)
@@ -346,18 +342,6 @@
     marks = active[:, None] == jnp.arange(task_count, dtype=jnp.int32)[None, :]
     row_home = jnp.sum(jnp.where(marks, homes[None, :], 0), axis=1)
 
-    up = jnp.concatenate(
-        [
-            pool_query.reshape(rank, query_width),
-            slot_keyvalue_matrices.reshape(rank, 2 * head_dim),
-        ],
-        axis=1,
-    )
-    with jax.named_scope("up_x"):
-        up_line = exchange(
-            jnp.broadcast_to(up[None], (line, rank, base_end)), "x"
-        )
-
     partial = project(
         inputs,
         gain,
@@ -369,14 +353,29 @@
         moves,
         own_rows,
     )
-    partial, up_line = lax.optimization_barrier((partial, up_line))
+    partial, pool_query, slot_keyvalue_matrices = lax.optimization_barrier(
+        (partial, pool_query, slot_keyvalue_matrices)
+    )
     with jax.named_scope("sum_plane"):
         by_plane = exchange(partial.reshape(planes, column_rows, -1), PLANE)
 
-    up_line, by_plane = lax.optimization_barrier((up_line, by_plane))
+    up = jnp.concatenate(
+        [
+            pool_query.reshape(rank, query_width),
+            slot_keyvalue_matrices.reshape(rank, 2 * head_dim),
+        ],
+        axis=1,
+    )
+    with jax.named_scope("up_x"):
+        ahead = [(i, (i + 1) % line) for i in range(line)]
+        back = [(i, (i - 1) % line) for i in range(line)]
+        across = [(i, (i + 2) % line) for i in range(line)]
+        from_left = lax.ppermute(up, "x", ahead)
+        from_right = lax.ppermute(up, "x", back)
+        from_far = lax.ppermute(up, "x", across)
+        up_line = jnp.stack([up, from_left, from_right, from_far])
     with jax.named_scope("up_y_lo"):
         up_other = lax.ppermute(up_line, "y_lo", [(0, 1), (1, 0)])
-
     low_part = sum_low(by_plane, base_end, 3 * rank, depth)
     plane_sum = jnp.sum(by_plane[:, :, :base_end].astype(jnp.float32), axis=0)
     with jax.named_scope("sum_low"):
@@ -386,9 +385,10 @@
     column_home = lax.dynamic_slice_in_dim(
         row_home, (x * 2 + y_lo) * column_rows, column_rows, 0
     )
-    home_x = column_home // (2 * depth)
+    offset = (column_home // (2 * depth) - x) % line
+    near_slot = jnp.where(offset == line - 1, 1, jnp.where(offset == 0, 0, offset + 1))
     other_half = jnp.where(column_home // depth % 2 == y_lo, 0, line)
-    slot = jnp.where(column_home % depth == z, home_x + other_half, -1)
+    slot = jnp.where(column_home % depth == z, near_slot + other_half, -1)
     raw_part = lift(
         slot[:, None], low_parts, plane_sum, up_line, up_other, rank, head_dim, model_width
     )

time: 143 us -> 140 us (0.979)
  starting transfers between devices: 35.2 us -> 39.8 us
  waiting for transfers between devices: 44.5 us -> 40.4 us
    all_to_all x5 -> x4, waiting for transfers between devices: 44.5 us -> 27.4 us  [exchange(): return lax.all_to_all(blocks, axes, 0, 0, tiled=True)]
    ppermute x0 -> x3, waiting for transfers between devices: none -> 13 us  [the longest x1 8.36 us: on_device(): from_right = lax.ppermute(up, 'x', back)]
    ppermute x0 -> x3, starting transfers between devices: none -> 10.1 us  [the longest x1 4.57 us: on_device(): from_right = lax.ppermute(up, 'x', back)]
    all_to_all x5 -> x4, starting transfers between devices: 32.8 us -> 25.8 us  [exchange(): return lax.all_to_all(blocks, axes, 0, 0, tiled=True)]
    ppermute x1, starting transfers between devices: 2.48 us -> 3.95 us  [on_device(): up_other = lax.ppermute(up_line, 'y_lo', [(0, 1), (1, 0)])]
    unnamed x28 -> x40, local copies, waits for them, and re-layouts: 3.91 us -> 3.76 us
  transfers between devices with their start and end apart: 6 -> 8, of which waited for: 5 -> 6; matrix products, arithmetic and copies ran while one was open for 3% -> 4% of each run, Pallas kernels for 4% -> 1%
where the time goes in v9:
time: 140 us; the launch traced here: 139 us
  waiting for transfers between devices  40.4 us (29%)
  starting transfers between devices  39.8 us (28%)
  blocking collectives  36.2 us (26%)
  Pallas kernels  8.33 us (6%)
  local copies, waits for them, and re-layouts  6.19 us (4%)
  other arithmetic  4.4 us (3%)
  matrix products  3.65 us (3%)
    all_to_all x4, waiting for transfers between devices, exchange(): return lax.all_to_all(blocks, axes, 0, 0, tiled=True)  27.4 us
    all_to_all x4, starting transfers between devices, exchange(): return lax.all_to_all(blocks, axes, 0, 0, tiled=True)  25.8 us
    all_to_all x2, blocking collectives, exchange(): return lax.all_to_all(blocks, axes, 0, 0, tiled=True)  25.4 us
    ppermute x1, waiting for transfers between devices, on_device(): from_right = lax.ppermute(up, 'x', back)  8.36 us
    all_gather x1, blocking collectives, on_device(): pair = lax.all_gather(mixed, 'core', axis=0)  6.78 us
    pallas_call x1, Pallas kernels, project(): pl.pallas_call(functools.partial(project_kernel, own_rows), out_shape=jax...  5.17 us
    ppermute x1, starting transfers between devices, on_device(): from_right = lax.ppermute(up, 'x', back)  4.57 us
    ppermute x1, waiting for transfers between devices, on_device(): from_left = lax.ppermute(up, 'x', ahead)  4.43 us
  transfers between devices with their start and end apart: 8, of which 6 were waited for; matrix products, arithmetic and copies ran while one was open for 4% of the time, Pallas kernels for 1%

profile of v9, /device:TPU:1, one launch (start us, length us, event | category | flops | bytes accessed | tf_op | source)
XLA Modules:
  0.0 139.4 jit_solution(12003446875886619910)
XLA Ops:
  0.0 5.2 %shard_map.163 = bf16[512,1536]{1,0:T(8,128)(2,1)} custom-call(f32[1,128]{1,0:T(1,128)} %bitcast.121, s32[1,128]{1,0:T(1,128)} %bitcast.120, s32[2,16]{1,0:T(2,128)} %bitcast.119, bf16[4,128,128]{2,1,0:T(8,128)(2,1)} %inputs_ref.1, bf16[8,192,128]{2,1,0:T(8,128)(2,1)} %bitcast.101, bf16[128,1024]{1,0:T(8,128)(2,1)} %query_ref.1, bf16[128,128]{1,0:T(8,128)(2,1)} %key_ref.1, ...), custom_call_target="tpu_custom_call" | custom-call | flops 436207616 | bytes 3000000 | tf_op jit(solution)/shard_map/pallas_call | solution.py:157
  5.2 6.0 %all-to-all-start = ((bf16[8,64,1536]{2,1,0:T(8,128)(2,1)}), bf16[8,64,1536]{2,1,0:T(8,128)(2,1)S(1)}, u32[]{:S(2)}, u32[]{:S(2)}) async-start(bf16[8,64,1536]{2,1,0:T(8,128)(2,1)} %bitcast.93), calls=%async_computation | async-start | bytes 3145728 | tf_op jit(solution)/shard_map/sum_plane/all_to_all | solution.py:20
  11.3 4.6 %collective-permute-start.1 = (bf16[64,1280]{1,0:T(8,128)(2,1)S(1)}, bf16[64,1280]{1,0:T(8,128)(2,1)S(1)}, u32[]{:S(2)}, u32[]{:S(2)}) collective-permute-start(bf16[64,1280]{1,0:T(8,128)(2,1)S(1)} %get-tuple-element.12), channel_id=1, source_target_pairs={{0,384},{128,0},{256,128},{384,256},{1,385},{129,1},{257,129},{385... | collective-permute-start | bytes 491528 | tf_op jit(solution)/shard_map/up_x/ppermute | solution.py:374
  15.9 1.9 %collective-permute-start = (bf16[64,1280]{1,0:T(8,128)(2,1)S(1)}, bf16[64,1280]{1,0:T(8,128)(2,1)S(1)}, u32[]{:S(2)}, u32[]{:S(2)}) collective-permute-start(bf16[64,1280]{1,0:T(8,128)(2,1)S(1)} %get-tuple-element.12), channel_id=1, source_target_pairs={{0,128},{128,256},{256,384},{384,0},{1,129},{129,257},{257,385},{3... | collective-permute-start | bytes 491528 | tf_op jit(solution)/shard_map/up_x/ppermute | solution.py:373
  17.8 3.7 %collective-permute-start.2 = (bf16[64,1280]{1,0:T(8,128)(2,1)S(1)}, bf16[64,1280]{1,0:T(8,128)(2,1)S(1)}, u32[]{:S(2)}, u32[]{:S(2)}) collective-permute-start(bf16[64,1280]{1,0:T(8,128)(2,1)S(1)} %get-tuple-element.12), channel_id=1, source_target_pairs={{0,256},{128,384},{256,0},{384,128},{1,257},{129,385},{257,1},{385... | collective-permute-start | bytes 491528 | tf_op jit(solution)/shard_map/up_x/ppermute | solution.py:375
  23.0 8.4 %collective-permute-done.1 = bf16[64,1280]{1,0:T(8,128)(2,1)S(1)} collective-permute-done((bf16[64,1280]{1,0:T(8,128)(2,1)S(1)}, bf16[64,1280]{1,0:T(8,128)(2,1)S(1)}, u32[]{:S(2)}, u32[]{:S(2)}) %collective-permute-start.1) | collective-permute-done | bytes 163872 | tf_op jit(solution)/shard_map/up_x/ppermute | solution.py:374
  31.4 4.4 %collective-permute-done = bf16[64,1280]{1,0:T(8,128)(2,1)S(1)} collective-permute-done((bf16[64,1280]{1,0:T(8,128)(2,1)S(1)}, bf16[64,1280]{1,0:T(8,128)(2,1)S(1)}, u32[]{:S(2)}, u32[]{:S(2)}) %collective-permute-start) | collective-permute-done | bytes 163872 | tf_op jit(solution)/shard_map/up_x/ppermute | solution.py:373
  36.7 1.2 pad_maximum_fusion.line_ref
  37.9 3.9 %collective-permute-start.3 = (bf16[4,64,1280]{2,1,0:T(8,128)(2,1)S(1)}, bf16[4,64,1280]{2,1,0:T(8,128)(2,1)}, u32[]{:S(2)}, u32[]{:S(2)}) collective-permute-start(bf16[4,64,1280]{2,1,0:T(8,128)(2,1)S(1)} %pad_maximum_fusion.line_ref), channel_id=1, source_target_pairs={{0,64},{64,0},{1,65},{65,1},{2,66},{66,2},{3,67},{67,3},{4,68},{68... | collective-permute-start | bytes 1966088 | tf_op jit(solution)/shard_map/up_y_lo/ppermute | solution.py:378
  43.1 11.2 %all-to-all-start.1 = ((bf16[8,64,256]{2,1,0:T(8,128)(2,1)}), bf16[8,64,256]{2,1,0:T(8,128)(2,1)S(1)}, u32[]{:S(2)}, u32[]{:S(2)}) async-start(bf16[8,64,256]{2,1,0:T(8,128)(2,1)} %shard_map.164), calls=%async_computation.1 | async-start | bytes 524288 | tf_op jit(solution)/shard_map/sum_low/all_to_all | solution.py:20
  55.1 0.9 convert_reduce_fusion.base_ref
  56.0 7.7 %all-to-all-done.1.low_ref = bf16[8,64,256]{2,1,0:T(8,128)(2,1)S(1)} async-done(((bf16[8,64,256]{2,1,0:T(8,128)(2,1)}), bf16[8,64,256]{2,1,0:T(8,128)(2,1)S(1)}, u32[]{:S(2)}, u32[]{:S(2)}) %all-to-all-start.1) | async-done | bytes 262176 | tf_op jit(solution)/shard_map/sum_low/all_to_all | solution.py:20
  63.7 1.0 copy-done.1
  65.4 2.3 %shard_map.165 = bf16[64,1280]{1,0:T(8,128)(2,1)} custom-call(s32[64,1]{1,0:T(8,128)S(1)} %copy-done.2, bf16[8,64,256]{2,1,0:T(8,128)(2,1)S(1)} %all-to-all-done.1.low_ref, bf16[4,64,1280]{2,1,0:T(8,128)(2,1)S(1)} %pad_maximum_fusion.line_ref, bf16[4,64,1280]{2,1,0:T(8,128)(2,1)} %collective-permute-done.3.other_ref, f32[64,1280]{1,0:T(8,128)S(1)} %copy-done.1), custom_call_target="tpu_custom_call" | custom-call | flops 83886080 | bytes 2000000 | tf_op jit(solution)/shard_map/pallas_call | solution.py:253
  67.8 3.4 %all-to-all-start.2 = ((bf16[8,8,1280]{2,1,0:T(8,128)(2,1)}), bf16[8,8,1280]{2,1,0:T(8,128)(2,1)S(1)}, u32[]{:S(2)}, u32[]{:S(2)}) async-start(bf16[8,8,1280]{2,1,0:T(8,128)(2,1)} %bitcast.13), calls=%async_computation.2 | async-start | bytes 327680 | tf_op jit(solution)/shard_map/sum_z/all_to_all | solution.py:20
  71.3 8.2 %all-to-all-done.2 = bf16[8,8,1280]{2,1,0:T(8,128)(2,1)S(1)} async-done(((bf16[8,8,1280]{2,1,0:T(8,128)(2,1)}), bf16[8,8,1280]{2,1,0:T(8,128)(2,1)S(1)}, u32[]{:S(2)}, u32[]{:S(2)}) %all-to-all-start.2) | async-done | bytes 163872 | tf_op jit(solution)/shard_map/sum_z/all_to_all | solution.py:20
  80.6 1.3 fusion.4
  82.2 10.3 %all_to_all.30 = bf16[8,8,1024]{2,1,0:T(8,128)(2,1)S(1)} all-to-all(bf16[8,8,1024]{2,1,0:T(8,128)(2,1)S(1)} %broadcast_in_dim.153), channel_id=1, replica_groups=mesh['x'=4,'y_lo'=2,'z'=8,'y_hi'=4,'core'=2] {'z'}, dimensions={0} | all-to-all | bytes 262144 | tf_op jit(solution)/shard_map/gather_z/all_to_all | solution.py:20
  92.5 1.1 broadcast_in_dim.155
  93.6 5.2 %all-to-all-start.4 = ((bf16[8,64,1024]{2,1,0:T(8,128)(2,1)}), bf16[8,64,1024]{2,1,0:T(8,128)(2,1)S(1)}, u32[]{:S(2)}, u32[]{:S(2)}) async-start(bf16[8,64,1024]{2,1,0:T(8,128)(2,1)} %broadcast_in_dim.155), calls=%async_computation.4 | async-start | bytes 2097152 | tf_op jit(solution)/shard_map/gather_plane/all_to_all | solution.py:20
  98.8 11.6 %all-to-all-done.4 = bf16[8,64,1024]{2,1,0:T(8,128)(2,1)S(1)} async-done(((bf16[8,64,1024]{2,1,0:T(8,128)(2,1)}), bf16[8,64,1024]{2,1,0:T(8,128)(2,1)S(1)}, u32[]{:S(2)}, u32[]{:S(2)}) %all-to-all-start.4) | async-done | bytes 1048608 | tf_op jit(solution)/shard_map/gather_plane/all_to_all | solution.py:20
  112.6 6.8 %all-gather = bf16[1024,128]{1,0:T(8,128)(2,1)S(1)} all-gather(bf16[512,128]{1,0:T(8,128)(2,1)S(1)} %fusion.1), channel_id=2, replica_groups=mesh['x'=4,'y_lo'=2,'z'=8,'y_hi'=4,'core'=2] {'core'}, dimensions={0}, use_global_device_ids=true | all-gather | bytes 393216 | tf_op jit(solution)/shard_map/sum_core/all_gather | solution.py:452
  119.6 15.1 %all_to_all.31 = bf16[8,128,128]{2,1,0:T(8,128)(2,1)S(1)} all-to-all(bf16[8,128,128]{2,1,0:T(8,128)(2,1)S(1)} %bitcast.96), channel_id=1, replica_groups=mesh['x'=4,'y_lo'=2,'z'=8,'y_hi'=4,'core'=2] {'y_hi'}, dimensions={0} | all-to-all | bytes 524288 | tf_op jit(solution)/shard_map/sum_y_hi/all_to_all | solution.py:20
  134.8 4.0 %all_gather.11 = bf16[4,128,128]{2,1,0:T(8,128)(2,1)S(1)} all-gather(bf16[2,128,128]{2,1,0:T(8,128)(2,1)S(1)} %add_convert_fusion), channel_id=1, replica_groups=mesh['x'=4,'y_lo'=2,'z'=8,'y_hi'=4,'core'=2] {'core'}, dimensions={0}, use_global_device_ids=true | all-gather | bytes 196608 | tf_op jit(solution)/shard_map/gather_core/all_gather | solution.py:472
  (90 shorter events, 9.9 us)
Async XLA Ops:
  0.0 110.4 %copy-start = (bf16[8,1024,64]{1,2,0:T(8,128)(2,1)S(1)}, bf16[8,1024,64]{1,2,0:T(8,128)(2,1)}, u32[]{:S(2)}) copy-start(bf16[8,1024,64]{1,2,0:T(8,128)(2,1)} %param.24) | copy-start | bytes 3145732
  5.2 6.1 %copy-start.11 = (bf16[1,64,2,128]{3,2,1,0:T(2,128)(2,1)S(1)}, bf16[1,64,2,128]{3,2,1,0:T(2,128)(2,1)}, u32[]{:S(2)}) copy-start(bf16[1,64,2,128]{3,2,1,0:T(2,128)(2,1)} %param.27) | copy-start | bytes 98308
  5.2 6.1 %copy-start.9 = (bf16[1,64,1024]{2,1,0:T(8,128)(2,1)S(1)}, bf16[1,64,1024]{2,1,0:T(8,128)(2,1)}, u32[]{:S(2)}) copy-start(bf16[1,64,1024]{2,1,0:T(8,128)(2,1)} %param.26) | copy-start | bytes 393220
  5.2 16.3 %copy-start.15 = (s32[128]{0:T(128)S(1)}, s32[128]{0:T(128)}, u32[]{:S(2)}) copy-start(s32[128]{0:T(128)} %param.30) | copy-start | bytes 1540
  5.2 16.4 %copy-start.13 = (s32[2]{0:T(128)S(1)}, s32[2]{0:T(128)}, u32[]{:S(2)}) copy-start(s32[2]{0:T(128)} %param.33) | copy-start | bytes 28
  5.2 16.5 %copy-start.12 = (s32[16,2]{0,1:T(2,128)S(1)}, s32[16,2]{0,1:T(2,128)}, u32[]{:S(2)}) copy-start(s32[16,2]{0,1:T(2,128)} %param.32) | copy-start | bytes 388
  5.2 37.0 %all-to-all-start = ((bf16[8,64,1536]{2,1,0:T(8,128)(2,1)}), bf16[8,64,1536]{2,1,0:T(8,128)(2,1)S(1)}, u32[]{:S(2)}, u32[]{:S(2)}) async-start(bf16[8,64,1536]{2,1,0:T(8,128)(2,1)} %bitcast.93), calls=%async_computation | async-start | bytes 3145728 | tf_op jit(solution)/shard_map/sum_plane/all_to_all | solution.py:20
  11.2 30.9 %copy-start.16 = (s32[8]{0:T(128)S(1)}, s32[8]{0:T(128)}, u32[]{:S(2)}) copy-start(s32[8]{0:T(128)} %param.31) | copy-start | bytes 100
  11.3 20.1 %collective-permute-start.1 = (bf16[64,1280]{1,0:T(8,128)(2,1)S(1)}, bf16[64,1280]{1,0:T(8,128)(2,1)S(1)}, u32[]{:S(2)}, u32[]{:S(2)}) collective-permute-start(bf16[64,1280]{1,0:T(8,128)(2,1)S(1)} %get-tuple-element.12), channel_id=1, source_target_pairs={{0,384},{128,0},{256,128},{384,256},{1,385},{129,1},{257,129},{385... | collective-permute-start | bytes 491528 | tf_op jit(solution)/shard_map/up_x/ppermute | solution.py:374
  15.9 19.9 %collective-permute-start = (bf16[64,1280]{1,0:T(8,128)(2,1)S(1)}, bf16[64,1280]{1,0:T(8,128)(2,1)S(1)}, u32[]{:S(2)}, u32[]{:S(2)}) collective-permute-start(bf16[64,1280]{1,0:T(8,128)(2,1)S(1)} %get-tuple-element.12), channel_id=1, source_target_pairs={{0,128},{128,256},{256,384},{384,0},{1,129},{129,257},{257,385},{3... | collective-permute-start | bytes 491528 | tf_op jit(solution)/shard_map/up_x/ppermute | solution.py:373
  17.8 18.3 %collective-permute-start.2 = (bf16[64,1280]{1,0:T(8,128)(2,1)S(1)}, bf16[64,1280]{1,0:T(8,128)(2,1)S(1)}, u32[]{:S(2)}, u32[]{:S(2)}) collective-permute-start(bf16[64,1280]{1,0:T(8,128)(2,1)S(1)} %get-tuple-element.12), channel_id=1, source_target_pairs={{0,256},{128,384},{256,0},{384,128},{1,257},{129,385},{257,1},{385... | collective-permute-start | bytes 491528 | tf_op jit(solution)/shard_map/up_x/ppermute | solution.py:375
  31.4 4.7 %copy-start.6 = (bf16[64,1280]{1,0:T(8,128)(2,1)}, bf16[64,1280]{1,0:T(8,128)(2,1)S(1)}, u32[]{:S(2)}) copy-start(bf16[64,1280]{1,0:T(8,128)(2,1)S(1)} %collective-permute-done.1) | copy-start | bytes 491524
  37.9 18.1 %collective-permute-start.3 = (bf16[4,64,1280]{2,1,0:T(8,128)(2,1)S(1)}, bf16[4,64,1280]{2,1,0:T(8,128)(2,1)}, u32[]{:S(2)}, u32[]{:S(2)}) collective-permute-start(bf16[4,64,1280]{2,1,0:T(8,128)(2,1)S(1)} %pad_maximum_fusion.line_ref), channel_id=1, source_target_pairs={{0,64},{64,0},{1,65},{65,1},{2,66},{66,2},{3,67},{67,3},{4,68},{68... | collective-permute-start | bytes 1966088 | tf_op jit(solution)/shard_map/up_y_lo/ppermute | solution.py:378
  43.1 20.6 %all-to-all-start.1 = ((bf16[8,64,256]{2,1,0:T(8,128)(2,1)}), bf16[8,64,256]{2,1,0:T(8,128)(2,1)S(1)}, u32[]{:S(2)}, u32[]{:S(2)}) async-start(bf16[8,64,256]{2,1,0:T(8,128)(2,1)} %shard_map.164), calls=%async_computation.1 | async-start | bytes 524288 | tf_op jit(solution)/shard_map/sum_low/all_to_all | solution.py:20
  55.1 16.0 %copy-start.14 = (f32[8]{0:T(128)S(1)}, f32[8]{0:T(128)}, u32[]{:S(2)}) copy-start(f32[8]{0:T(128)} %fusion.33) | copy-start | bytes 100
  55.1 25.0 %copy-start.17 = (pred[32,4]{0,1:T(4,128)(4,1)S(1)}, pred[32,4]{0,1:T(4,128)(4,1)}, u32[]{:S(2)}) copy-start(pred[32,4]{0,1:T(4,128)(4,1)} %iota_compare_fusion.3) | copy-start | bytes 388
  63.7 1.0 copy-start.1
  64.7 0.8 copy-start.2
  65.4 14.3 %copy-start.3 = (bf16[2,1,1024,128]{3,2,1,0:T(8,128)(2,1)S(1)}, bf16[2,1,1024,128]{3,2,1,0:T(8,128)(2,1)}, u32[]{:S(2)}) copy-start(bf16[2,1,1024,128]{3,2,1,0:T(8,128)(2,1)} %param.28) | copy-start | bytes 1572868
  67.8 11.7 %all-to-all-start.2 = ((bf16[8,8,1280]{2,1,0:T(8,128)(2,1)}), bf16[8,8,1280]{2,1,0:T(8,128)(2,1)S(1)}, u32[]{:S(2)}, u32[]{:S(2)}) async-start(bf16[8,8,1280]{2,1,0:T(8,128)(2,1)} %bitcast.13), calls=%async_computation.2 | async-start | bytes 327680 | tf_op jit(solution)/shard_map/sum_z/all_to_all | solution.py:20
  93.6 16.8 %all-to-all-start.4 = ((bf16[8,64,1024]{2,1,0:T(8,128)(2,1)}), bf16[8,64,1024]{2,1,0:T(8,128)(2,1)S(1)}, u32[]{:S(2)}, u32[]{:S(2)}) async-start(bf16[8,64,1024]{2,1,0:T(8,128)(2,1)} %broadcast_in_dim.155), calls=%async_computation.4 | async-start | bytes 2097152 | tf_op jit(solution)/shard_map/gather_plane/all_to_all | solution.py:20
  110.4 0.9 copy-start.10
  111.2 1.0 copy-start.5
  112.1 22.6 %copy-start.4 = (bf16[4,128,128]{2,1,0:T(8,128)(2,1)S(1)}, bf16[4,128,128]{2,1,0:T(8,128)(2,1)}, u32[]{:S(2)}) copy-start(bf16[4,128,128]{2,1,0:T(8,128)(2,1)} %inputs_ref.1) | copy-start | bytes 393220
  (2 other events, 1.3 us)

commit v10 on v9

--- a/solution.py
+++ b/solution.py
@@ -367,13 +367,7 @@
         axis=1,
     )
     with jax.named_scope("up_x"):
-        ahead = [(i, (i + 1) % line) for i in range(line)]
-        back = [(i, (i - 1) % line) for i in range(line)]
-        across = [(i, (i + 2) % line) for i in range(line)]
-        from_left = lax.ppermute(up, "x", ahead)
-        from_right = lax.ppermute(up, "x", back)
-        from_far = lax.ppermute(up, "x", across)
-        up_line = jnp.stack([up, from_left, from_right, from_far])
+        up_line = lax.all_gather(up, "x", axis=0)
     with jax.named_scope("up_y_lo"):
         up_other = lax.ppermute(up_line, "y_lo", [(0, 1), (1, 0)])
     low_part = sum_low(by_plane, base_end, 3 * rank, depth)
@@ -385,10 +379,9 @@
     column_home = lax.dynamic_slice_in_dim(
         row_home, (x * 2 + y_lo) * column_rows, column_rows, 0
     )
-    offset = (column_home // (2 * depth) - x) % line
-    near_slot = jnp.where(offset == line - 1, 1, jnp.where(offset == 0, 0, offset + 1))
+    home_x = column_home // (2 * depth)
     other_half = jnp.where(column_home // depth % 2 == y_lo, 0, line)
-    slot = jnp.where(column_home % depth == z, near_slot + other_half, -1)
+    slot = jnp.where(column_home % depth == z, home_x + other_half, -1)
     raw_part = lift(
         slot[:, None], low_parts, plane_sum, up_line, up_other, rank, head_dim, model_width
     )
@@ -453,19 +446,14 @@
     mine = lax.dynamic_slice_in_dim(
         pair.reshape(cores, groups, steps, own_rows, width_part), core * half, half, 2
     ).astype(jnp.float32)
-    mine = jnp.sum(mine, axis=0).astype(jnp.bfloat16)
+    mine = jnp.sum(mine, axis=0)
     mine = mine.transpose(1, 0, 2, 3).reshape(half, all_rows, width_part)
-    y_his = lax.axis_size("y_hi")
-    with jax.named_scope("sum_y_hi"):
-        mine = exchange(
-            jnp.broadcast_to(mine[None], (y_his, half, all_rows, width_part)).reshape(
-                y_his * half, all_rows, width_part
-            ),
-            "y_hi",
-        )
-    mine = jnp.sum(
-        mine.reshape(y_his, half, all_rows, width_part).astype(jnp.float32), axis=0
-    )
+    for pairs in ([[0, 1], [2, 3]], [[1, 2], [3, 0]]):
+        with jax.named_scope("sum_y_hi"):
+            both = lax.all_gather(
+                mine.astype(jnp.bfloat16), "y_hi", axis=0, axis_index_groups=pairs
+            )
+        mine = both[0].astype(jnp.float32) + both[1].astype(jnp.float32)
     residual = lax.dynamic_slice_in_dim(inputs, core * half, half, 0)
     finished = (residual.astype(jnp.float32) + mine).astype(jnp.bfloat16)
     with jax.named_scope("gather_core"):

time: 140 us -> 136 us (0.971)
  blocking collectives: 36.2 us -> 62.6 us
  waiting for transfers between devices: 40.4 us -> 25.9 us
  starting transfers between devices: 39.8 us -> 27 us
    all_gather x0 -> x3, blocking collectives: none -> 38.6 us  [the longest x1 25.8 us: on_device(): up_line = lax.all_gather(up, 'x', axis=0)]
    all_to_all x2 -> x1, blocking collectives: 25.4 us -> 10.3 us  [exchange(): return lax.all_to_all(blocks, axes, 0, 0, tiled=True)]
    ppermute x3 -> x0, waiting for transfers between devices: 13 us -> none  [the longest x1 8.36 us: on_device(): from_right = lax.ppermute(up, 'x', back)]
    ppermute x3 -> x0, starting transfers between devices: 10.1 us -> none  [the longest x1 4.57 us: on_device(): from_right = lax.ppermute(up, 'x', back)]
    all_gather x1, blocking collectives: 6.78 us -> 10.4 us  [on_device(): pair = lax.all_gather(mixed, 'core', axis=0)]
    all_to_all x4, waiting for transfers between devices: 27.4 us -> 25.9 us  [exchange(): return lax.all_to_all(blocks, axes, 0, 0, tiled=True)]
    unnamed x40 -> x36, local copies, waits for them, and re-layouts: 3.76 us -> 3.09 us
  transfers between devices with their start and end apart: 8 -> 5, of which waited for: 6 -> 3; matrix products, arithmetic and copies ran while one was open for 4% -> 3% of each run, Pallas kernels for 1% -> 1%
where the time goes in v10:
time: 136 us
  blocking collectives  62.6 us (46%)
  starting transfers between devices  27 us (20%)
  waiting for transfers between devices  25.9 us (19%)
  Pallas kernels  8.33 us (6%)
  local copies, waits for them, and re-layouts  5.5 us (4%)
  other arithmetic  3.35 us (2%)
  matrix products  2.6 us (2%)
    all_to_all x4, waiting for transfers between devices, exchange(): return lax.all_to_all(blocks, axes, 0, 0, tiled=True)  25.9 us
    all_gather x1, blocking collectives, on_device(): up_line = lax.all_gather(up, 'x', axis=0)  25.8 us
    all_to_all x4, starting transfers between devices, exchange(): return lax.all_to_all(blocks, axes, 0, 0, tiled=True)  24.4 us
    all_gather x2, blocking collectives, on_device(): lax.all_gather(mine.astype(jnp.bfloat16), 'y_hi', axis=0, axis_index_grou...  12.8 us
    all_gather x1, blocking collectives, on_device(): pair = lax.all_gather(mixed, 'core', axis=0)  10.4 us
    all_to_all x1, blocking collectives, exchange(): return lax.all_to_all(blocks, axes, 0, 0, tiled=True)  10.3 us
    pallas_call x1, Pallas kernels, project(): pl.pallas_call(functools.partial(project_kernel, own_rows), out_shape=jax...  5.16 us
    all_gather x1, blocking collectives, on_device(): return lax.all_gather(finished, 'core', axis=0, tiled=True)  3.33 us
  transfers between devices with their start and end apart: 5, of which 3 were waited for; matrix products, arithmetic and copies ran while one was open for 3% of the time, Pallas kernels for 1%

profile of v10, /device:TPU:1, one launch (start us, length us, event | category | flops | bytes accessed | tf_op | source)
XLA Modules:
  0.0 135.7 jit_solution(13328499724350965692)
XLA Ops:
  0.0 5.2 %shard_map.163 = bf16[512,1536]{1,0:T(8,128)(2,1)} custom-call(f32[1,128]{1,0:T(1,128)} %bitcast.115, s32[1,128]{1,0:T(1,128)} %bitcast.114, s32[2,16]{1,0:T(2,128)} %bitcast.113, bf16[4,128,128]{2,1,0:T(8,128)(2,1)} %inputs_ref.1, bf16[8,192,128]{2,1,0:T(8,128)(2,1)} %bitcast.98, bf16[128,1024]{1,0:T(8,128)(2,1)} %query_ref.1, bf16[128,128]{1,0:T(8,128)(2,1)} %key_ref.1, ...), custom_call_target="tpu_custom_call" | custom-call | flops 436207616 | bytes 3000000 | tf_op jit(solution)/shard_map/pallas_call | solution.py:157
  5.2 6.0 %all-to-all-start = ((bf16[8,64,1536]{2,1,0:T(8,128)(2,1)}), bf16[8,64,1536]{2,1,0:T(8,128)(2,1)S(1)}, u32[]{:S(2)}, u32[]{:S(2)}) async-start(bf16[8,64,1536]{2,1,0:T(8,128)(2,1)} %bitcast.92), calls=%async_computation | async-start | bytes 3145728 | tf_op jit(solution)/shard_map/sum_plane/all_to_all | solution.py:20
  11.3 25.8 %all-gather = bf16[256,1280]{1,0:T(8,128)(2,1)S(1)} all-gather(bf16[64,1280]{1,0:T(8,128)(2,1)S(1)} %pad_maximum_fusion), channel_id=2, replica_groups=mesh['x'=4,'y_lo'=2,'z'=8,'y_hi'=4,'core'=2] {'x'}, dimensions={0}, use_global_device_ids=true | all-gather | bytes 819200 | tf_op jit(solution)/shard_map/up_x/all_gather | solution.py:370
  37.1 2.6 %collective-permute-start = (bf16[4,64,1280]{2,1,0:T(8,128)(2,1)S(1)}, bf16[4,64,1280]{2,1,0:T(8,128)(2,1)}, u32[]{:S(2)}, u32[]{:S(2)}) collective-permute-start(bf16[4,64,1280]{2,1,0:T(8,128)(2,1)S(1)} %bitcast.90), channel_id=1, source_target_pairs={{0,64},{64,0},{1,65},{65,1},{2,66},{66,2},{3,67},{67,3},{4,68},{68... | collective-permute-start | bytes 1966088 | tf_op jit(solution)/shard_map/up_y_lo/ppermute | solution.py:372
  41.8 0.8 shard_map.164
  42.6 11.5 %all-to-all-start.1 = ((bf16[8,64,256]{2,1,0:T(8,128)(2,1)}), bf16[8,64,256]{2,1,0:T(8,128)(2,1)S(1)}, u32[]{:S(2)}, u32[]{:S(2)}) async-start(bf16[8,64,256]{2,1,0:T(8,128)(2,1)} %shard_map.164), calls=%async_computation.1 | async-start | bytes 524288 | tf_op jit(solution)/shard_map/sum_low/all_to_all | solution.py:20
  54.2 0.7 copy.50.slot_ref
  55.0 0.9 convert_reduce_fusion.base_ref
  55.9 7.6 %all-to-all-done.1.low_ref = bf16[8,64,256]{2,1,0:T(8,128)(2,1)S(1)} async-done(((bf16[8,64,256]{2,1,0:T(8,128)(2,1)}), bf16[8,64,256]{2,1,0:T(8,128)(2,1)S(1)}, u32[]{:S(2)}, u32[]{:S(2)}) %all-to-all-start.1) | async-done | bytes 262176 | tf_op jit(solution)/shard_map/sum_low/all_to_all | solution.py:20
  63.4 1.0 copy-done.1
  64.4 0.8 copy-done.2
  65.2 2.4 %shard_map.165 = bf16[64,1280]{1,0:T(8,128)(2,1)} custom-call(s32[64,1]{1,0:T(8,128)S(1)} %copy-done.2, bf16[8,64,256]{2,1,0:T(8,128)(2,1)S(1)} %all-to-all-done.1.low_ref, bf16[4,64,1280]{2,1,0:T(8,128)(2,1)S(1)} %bitcast.91, bf16[4,64,1280]{2,1,0:T(8,128)(2,1)} %collective-permute-done.other_ref, f32[64,1280]{1,0:T(8,128)S(1)} %copy-done.1), custom_call_target="tpu_custom_call" | custom-call | flops 83886080 | bytes 2000000 | tf_op jit(solution)/shard_map/pallas_call | solution.py:253
  67.5 3.4 %all-to-all-start.2 = ((bf16[8,8,1280]{2,1,0:T(8,128)(2,1)}), bf16[8,8,1280]{2,1,0:T(8,128)(2,1)S(1)}, u32[]{:S(2)}, u32[]{:S(2)}) async-start(bf16[8,8,1280]{2,1,0:T(8,128)(2,1)} %bitcast.10), calls=%async_computation.2 | async-start | bytes 327680 | tf_op jit(solution)/shard_map/sum_z/all_to_all | solution.py:20
  71.0 8.1 %all-to-all-done.2 = bf16[8,8,1280]{2,1,0:T(8,128)(2,1)S(1)} async-done(((bf16[8,8,1280]{2,1,0:T(8,128)(2,1)}), bf16[8,8,1280]{2,1,0:T(8,128)(2,1)S(1)}, u32[]{:S(2)}, u32[]{:S(2)}) %all-to-all-start.2) | async-done | bytes 163872 | tf_op jit(solution)/shard_map/sum_z/all_to_all | solution.py:20
  80.8 10.3 %all_to_all.25 = bf16[8,8,1024]{2,1,0:T(8,128)(2,1)S(1)} all-to-all(bf16[8,8,1024]{2,1,0:T(8,128)(2,1)S(1)} %broadcast_in_dim.143), channel_id=1, replica_groups=mesh['x'=4,'y_lo'=2,'z'=8,'y_hi'=4,'core'=2] {'z'}, dimensions={0} | all-to-all | bytes 262144 | tf_op jit(solution)/shard_map/gather_z/all_to_all | solution.py:20
  91.1 1.1 broadcast_in_dim.145
  92.2 3.6 %all-to-all-start.4 = ((bf16[8,64,1024]{2,1,0:T(8,128)(2,1)}), bf16[8,64,1024]{2,1,0:T(8,128)(2,1)S(1)}, u32[]{:S(2)}, u32[]{:S(2)}) async-start(bf16[8,64,1024]{2,1,0:T(8,128)(2,1)} %broadcast_in_dim.145), calls=%async_computation.4 | async-start | bytes 2097152 | tf_op jit(solution)/shard_map/gather_plane/all_to_all | solution.py:20
  95.8 10.3 %all-to-all-done.4 = bf16[8,64,1024]{2,1,0:T(8,128)(2,1)S(1)} async-done(((bf16[8,64,1024]{2,1,0:T(8,128)(2,1)}), bf16[8,64,1024]{2,1,0:T(8,128)(2,1)S(1)}, u32[]{:S(2)}, u32[]{:S(2)}) %all-to-all-start.4) | async-done | bytes 1048608 | tf_op jit(solution)/shard_map/gather_plane/all_to_all | solution.py:20
  106.1 0.7 fusion.42
  108.3 10.4 %all-gather.1 = bf16[1024,128]{1,0:T(8,128)(2,1)S(1)} all-gather(bf16[512,128]{1,0:T(8,128)(2,1)S(1)} %fusion.1), channel_id=3, replica_groups=mesh['x'=4,'y_lo'=2,'z'=8,'y_hi'=4,'core'=2] {'core'}, dimensions={0}, use_global_device_ids=true | all-gather | bytes 393216 | tf_op jit(solution)/shard_map/sum_core/all_gather | solution.py:445
  118.9 6.8 %all_gather.27 = bf16[2,2,128,128]{3,2,1,0:T(8,128)(2,1)S(1)} all-gather(bf16[1,2,128,128]{3,2,1,0:T(8,128)(2,1)S(1)} %bitcast.101), channel_id=1, replica_groups={{0,2},{4,6},{1,3},{5,7},{8,10},{12,14},{9,11},{13,15},{16,18},{20,22},{..., dimensions={0}, use_global_device_ids=true | all-gather | bytes 196608 | tf_op jit(solution)/shard_map/sum_y_hi/all_gather | solution.py:453
  125.7 6.0 %all_gather.28 = bf16[2,2,128,128]{3,2,1,0:T(8,128)(2,1)S(1)} all-gather(bf16[1,2,128,128]{3,2,1,0:T(8,128)(2,1)S(1)} %add_convert_fusion), channel_id=1, replica_groups={{2,4},{6,0},{3,5},{7,1},{10,12},{14,8},{11,13},{15,9},{18,20},{22,16},{..., dimensions={0}, use_global_device_ids=true | all-gather | bytes 196608 | tf_op jit(solution)/shard_map/sum_y_hi/all_gather | solution.py:453
  131.7 3.3 %all_gather.29 = bf16[4,128,128]{2,1,0:T(8,128)(2,1)S(1)} all-gather(bf16[2,128,128]{2,1,0:T(8,128)(2,1)S(1)} %fusion.10), channel_id=1, replica_groups=mesh['x'=4,'y_lo'=2,'z'=8,'y_hi'=4,'core'=2] {'core'}, dimensions={0}, use_global_device_ids=true | all-gather | bytes 196608 | tf_op jit(solution)/shard_map/gather_core/all_gather | solution.py:460
  135.1 0.7 copy.82
  (80 shorter events, 5.6 us)
Async XLA Ops:
  0.0 106.1 %copy-start = (bf16[8,1024,64]{1,2,0:T(8,128)(2,1)S(1)}, bf16[8,1024,64]{1,2,0:T(8,128)(2,1)}, u32[]{:S(2)}) copy-start(bf16[8,1024,64]{1,2,0:T(8,128)(2,1)} %param.24) | copy-start | bytes 3145732
  5.2 6.1 %copy-start.8 = (bf16[1,64,2,128]{3,2,1,0:T(2,128)(2,1)S(1)}, bf16[1,64,2,128]{3,2,1,0:T(2,128)(2,1)}, u32[]{:S(2)}) copy-start(bf16[1,64,2,128]{3,2,1,0:T(2,128)(2,1)} %param.27) | copy-start | bytes 98308
  5.2 6.1 %copy-start.6 = (bf16[1,64,1024]{2,1,0:T(8,128)(2,1)S(1)}, bf16[1,64,1024]{2,1,0:T(8,128)(2,1)}, u32[]{:S(2)}) copy-start(bf16[1,64,1024]{2,1,0:T(8,128)(2,1)} %param.26) | copy-start | bytes 393220
  5.2 34.6 %copy-start.12 = (s32[128]{0:T(128)S(1)}, s32[128]{0:T(128)}, u32[]{:S(2)}) copy-start(s32[128]{0:T(128)} %param.30) | copy-start | bytes 1540
  5.2 34.7 %copy-start.10 = (s32[2]{0:T(128)S(1)}, s32[2]{0:T(128)}, u32[]{:S(2)}) copy-start(s32[2]{0:T(128)} %param.33) | copy-start | bytes 28
  5.2 34.8 %copy-start.9 = (s32[16,2]{0,1:T(2,128)S(1)}, s32[16,2]{0,1:T(2,128)}, u32[]{:S(2)}) copy-start(s32[16,2]{0,1:T(2,128)} %param.32) | copy-start | bytes 388
  5.2 36.6 %all-to-all-start = ((bf16[8,64,1536]{2,1,0:T(8,128)(2,1)}), bf16[8,64,1536]{2,1,0:T(8,128)(2,1)S(1)}, u32[]{:S(2)}, u32[]{:S(2)}) async-start(bf16[8,64,1536]{2,1,0:T(8,128)(2,1)} %bitcast.92), calls=%async_computation | async-start | bytes 3145728 | tf_op jit(solution)/shard_map/sum_plane/all_to_all | solution.py:20
  11.2 30.5 %copy-start.13 = (s32[8]{0:T(128)S(1)}, s32[8]{0:T(128)}, u32[]{:S(2)}) copy-start(s32[8]{0:T(128)} %param.31) | copy-start | bytes 100
  37.1 18.8 %collective-permute-start = (bf16[4,64,1280]{2,1,0:T(8,128)(2,1)S(1)}, bf16[4,64,1280]{2,1,0:T(8,128)(2,1)}, u32[]{:S(2)}, u32[]{:S(2)}) collective-permute-start(bf16[4,64,1280]{2,1,0:T(8,128)(2,1)S(1)} %bitcast.90), channel_id=1, source_target_pairs={{0,64},{64,0},{1,65},{65,1},{2,66},{66,2},{3,67},{67,3},{4,68},{68... | collective-permute-start | bytes 1966088 | tf_op jit(solution)/shard_map/up_y_lo/ppermute | solution.py:372
  42.6 20.8 %all-to-all-start.1 = ((bf16[8,64,256]{2,1,0:T(8,128)(2,1)}), bf16[8,64,256]{2,1,0:T(8,128)(2,1)S(1)}, u32[]{:S(2)}, u32[]{:S(2)}) async-start(bf16[8,64,256]{2,1,0:T(8,128)(2,1)} %shard_map.164), calls=%async_computation.1 | async-start | bytes 524288 | tf_op jit(solution)/shard_map/sum_low/all_to_all | solution.py:20
  55.0 15.9 %copy-start.11 = (f32[8]{0:T(128)S(1)}, f32[8]{0:T(128)}, u32[]{:S(2)}) copy-start(f32[8]{0:T(128)} %fusion.34) | copy-start | bytes 100
  55.0 24.8 %copy-start.15 = (pred[32,4]{0,1:T(4,128)(4,1)S(1)}, pred[32,4]{0,1:T(4,128)(4,1)}, u32[]{:S(2)}) copy-start(pred[32,4]{0,1:T(4,128)(4,1)} %iota_compare_fusion.3) | copy-start | bytes 388
  63.4 1.0 copy-start.1
  64.4 0.8 copy-start.2
  65.1 14.2 %copy-start.3 = (bf16[2,1,1024,128]{3,2,1,0:T(8,128)(2,1)S(1)}, bf16[2,1,1024,128]{3,2,1,0:T(8,128)(2,1)}, u32[]{:S(2)}) copy-start(bf16[2,1,1024,128]{3,2,1,0:T(8,128)(2,1)} %param.28) | copy-start | bytes 1572868
  65.1 15.1 %copy-start.14 = (bf16[2,1,1024,128]{3,2,1,0:T(8,128)(2,1)S(1)}, bf16[2,1,1024,128]{3,2,1,0:T(8,128)(2,1)}, u32[]{:S(2)}) copy-start(bf16[2,1,1024,128]{3,2,1,0:T(8,128)(2,1)} %param.29) | copy-start | bytes 1572868
  67.5 11.6 %all-to-all-start.2 = ((bf16[8,8,1280]{2,1,0:T(8,128)(2,1)}), bf16[8,8,1280]{2,1,0:T(8,128)(2,1)S(1)}, u32[]{:S(2)}, u32[]{:S(2)}) async-start(bf16[8,8,1280]{2,1,0:T(8,128)(2,1)} %bitcast.10), calls=%async_computation.2 | async-start | bytes 327680 | tf_op jit(solution)/shard_map/sum_z/all_to_all | solution.py:20
  92.2 13.9 %all-to-all-start.4 = ((bf16[8,64,1024]{2,1,0:T(8,128)(2,1)}), bf16[8,64,1024]{2,1,0:T(8,128)(2,1)S(1)}, u32[]{:S(2)}, u32[]{:S(2)}) async-start(bf16[8,64,1024]{2,1,0:T(8,128)(2,1)} %broadcast_in_dim.145), calls=%async_computation.4 | async-start | bytes 2097152 | tf_op jit(solution)/shard_map/gather_plane/all_to_all | solution.py:20
  106.1 0.9 copy-start.7
  106.9 1.0 copy-start.5
  107.8 23.8 %copy-start.4 = (bf16[4,128,128]{2,1,0:T(8,128)(2,1)S(1)}, bf16[4,128,128]{2,1,0:T(8,128)(2,1)}, u32[]{:S(2)}) copy-start(bf16[4,128,128]{2,1,0:T(8,128)(2,1)} %inputs_ref.1) | copy-start | bytes 393220

commit v11 on v10

--- a/solution.py
+++ b/solution.py
@@ -342,6 +342,11 @@
     marks = active[:, None] == jnp.arange(task_count, dtype=jnp.int32)[None, :]
     row_home = jnp.sum(jnp.where(marks, homes[None, :], 0), axis=1)
 
+    near = [(0, 1), (1, 0), (2, 3), (3, 2)]
+    far = [(0, 3), (1, 2), (2, 1), (3, 0)]
+    with jax.named_scope("up_x"):
+        pool_near = lax.ppermute(pool_query, "x", near)
+
     partial = project(
         inputs,
         gain,
@@ -353,21 +358,25 @@
         moves,
         own_rows,
     )
-    partial, pool_query, slot_keyvalue_matrices = lax.optimization_barrier(
-        (partial, pool_query, slot_keyvalue_matrices)
+    partial, pool_near, slot_keyvalue_matrices = lax.optimization_barrier(
+        (partial, pool_near, slot_keyvalue_matrices)
     )
     with jax.named_scope("sum_plane"):
         by_plane = exchange(partial.reshape(planes, column_rows, -1), PLANE)
 
-    up = jnp.concatenate(
+    with jax.named_scope("up_x"):
+        keyvalue_near = lax.ppermute(slot_keyvalue_matrices, "x", near)
+        query_pair = jnp.concatenate([pool_query, pool_near])
+        keyvalue_pair = jnp.concatenate([slot_keyvalue_matrices, keyvalue_near])
+        query_far = lax.ppermute(query_pair, "x", far)
+        keyvalue_far = lax.ppermute(keyvalue_pair, "x", far)
+    up_line = jnp.concatenate(
         [
-            pool_query.reshape(rank, query_width),
-            slot_keyvalue_matrices.reshape(rank, 2 * head_dim),
+            jnp.concatenate([query_pair, query_far]),
+            jnp.concatenate([keyvalue_pair, keyvalue_far]).reshape(line, rank, 2 * head_dim),
         ],
-        axis=1,
-    )
-    with jax.named_scope("up_x"):
-        up_line = lax.all_gather(up, "x", axis=0)
+        axis=2,
+    )
     with jax.named_scope("up_y_lo"):
         up_other = lax.ppermute(up_line, "y_lo", [(0, 1), (1, 0)])
     low_part = sum_low(by_plane, base_end, 3 * rank, depth)
@@ -380,8 +389,10 @@
         row_home, (x * 2 + y_lo) * column_rows, column_rows, 0
     )
     home_x = column_home // (2 * depth)
+    order = jnp.stack([x, x ^ 1, 3 - x, (3 - x) ^ 1])
+    near_slot = jnp.sum(jnp.where(home_x[:, None] == order[None, :], jnp.arange(line), 0), axis=1)
     other_half = jnp.where(column_home // depth % 2 == y_lo, 0, line)
-    slot = jnp.where(column_home % depth == z, home_x + other_half, -1)
+    slot = jnp.where(column_home % depth == z, near_slot + other_half, -1)
     raw_part = lift(
         slot[:, None], low_parts, plane_sum, up_line, up_other, rank, head_dim, model_width
     )

time: 136 us -> 138 us (1.015)
  blocking collectives: 62.6 us -> 34.6 us
  waiting for transfers between devices: 25.9 us -> 41.5 us
  starting transfers between devices: 27 us -> 38.1 us
  other arithmetic: 3.35 us -> 6.49 us
    all_gather x1 -> x0, blocking collectives: 25.8 us -> none  [on_device(): up_line = lax.all_gather(up, 'x', axis=0)]
    ppermute x0 -> x4, waiting for transfers between devices: none -> 15.6 us  [the longest x1 11.2 us: on_device(): keyvalue_far = lax.ppermute(keyvalue_pair, 'x', far)]
    ppermute x0 -> x4, starting transfers between devices: none -> 13 us  [the longest x1 4.07 us: on_device(): pool_near = lax.ppermute(pool_query, 'x', near)]
    all_to_all x4, starting transfers between devices: 24.4 us -> 22.3 us  [exchange(): return lax.all_to_all(blocks, axes, 0, 0, tiled=True)]
    all_gather x1, blocking collectives: 10.4 us -> 8.55 us  [on_device(): pair = lax.all_gather(mixed, 'core', axis=0)]
    unnamed x36 -> x39, local copies, waits for them, and re-layouts: 3.09 us -> 3.1 us
  transfers between devices with their start and end apart: 5 -> 9, of which waited for: 3 -> 5; matrix products, arithmetic and copies ran while one was open for 3% -> 5% of each run, Pallas kernels for 1% -> 4%
where the time goes in v11:
time: 138 us
  waiting for transfers between devices  41.5 us (30%)
  starting transfers between devices  38.1 us (28%)
  blocking collectives  34.6 us (25%)
  Pallas kernels  8.25 us (6%)
  other arithmetic  6.49 us (5%)
  local copies, waits for them, and re-layouts  5.58 us (4%)
  matrix products  2.61 us (2%)
    all_to_all x4, waiting for transfers between devices, exchange(): return lax.all_to_all(blocks, axes, 0, 0, tiled=True)  25.9 us
    all_to_all x4, starting transfers between devices, exchange(): return lax.all_to_all(blocks, axes, 0, 0, tiled=True)  22.3 us
    all_gather x2, blocking collectives, on_device(): lax.all_gather(mine.astype(jnp.bfloat16), 'y_hi', axis=0, axis_index_grou...  12.6 us
    ppermute x1, waiting for transfers between devices, on_device(): keyvalue_far = lax.ppermute(keyvalue_pair, 'x', far)  11.2 us
    all_to_all x1, blocking collectives, exchange(): return lax.all_to_all(blocks, axes, 0, 0, tiled=True)  10.3 us
    all_gather x1, blocking collectives, on_device(): pair = lax.all_gather(mixed, 'core', axis=0)  8.55 us
    pallas_call x1, Pallas kernels, project(): pl.pallas_call(functools.partial(project_kernel, own_rows), out_shape=jax...  5.08 us
    ppermute x1, waiting for transfers between devices, on_device(): keyvalue_near = lax.ppermute(slot_keyvalue_matrices, 'x', near)  4.41 us
  transfers between devices with their start and end apart: 9, of which 5 were waited for; matrix products, arithmetic and copies ran while one was open for 5% of the time, Pallas kernels for 4%

profile of v11, /device:TPU:1, one launch (start us, length us, event | category | flops | bytes accessed | tf_op | source)
XLA Modules:
  0.0 137.6 jit_solution(16303852099765021961)
XLA Ops:
  0.0 4.1 %collective-permute-start = (bf16[1,64,1024]{2,1,0:T(8,128)(2,1)}, bf16[1,64,1024]{2,1,0:T(8,128)(2,1)S(1)}, u32[]{:S(2)}, u32[]{:S(2)}) collective-permute-start(bf16[1,64,1024]{2,1,0:T(8,128)(2,1)} %param.26), channel_id=1, source_target_pairs={{0,128},{128,0},{256,384},{384,256},{1,129},{129,1},{257,385},{385... | collective-permute-start | bytes 393224 | tf_op jit(solution)/shard_map/up_x/ppermute | solution.py:348
  4.1 5.1 %shard_map.163 = bf16[512,1536]{1,0:T(8,128)(2,1)} custom-call(f32[1,128]{1,0:T(1,128)} %bitcast.107, s32[1,128]{1,0:T(1,128)} %bitcast.106, s32[2,16]{1,0:T(2,128)} %bitcast.105, bf16[4,128,128]{2,1,0:T(8,128)(2,1)} %inputs_ref.1, bf16[8,192,128]{2,1,0:T(8,128)(2,1)} %bitcast.93, bf16[128,1024]{1,0:T(8,128)(2,1)} %query_ref.1, bf16[128,128]{1,0:T(8,128)(2,1)} %key_ref.1, ...), custom_call_target="tpu_custom_call" | custom-call | flops 436207616 | bytes 3000000 | tf_op jit(solution)/shard_map/pallas_call | solution.py:157
  9.3 4.9 %all-to-all-start = ((bf16[8,64,1536]{2,1,0:T(8,128)(2,1)}), bf16[8,64,1536]{2,1,0:T(8,128)(2,1)S(1)}, u32[]{:S(2)}, u32[]{:S(2)}) async-start(bf16[8,64,1536]{2,1,0:T(8,128)(2,1)} %bitcast.87), calls=%async_computation | async-start | bytes 3145728 | tf_op jit(solution)/shard_map/sum_plane/all_to_all | solution.py:20
  16.7 3.4 %collective-permute-start.2 = (bf16[1,64,2,128]{3,2,1,0:T(2,128)(2,1)S(1)}, bf16[1,64,2,128]{3,2,1,0:T(2,128)(2,1)S(1)}, u32[]{:S(2)}, u32[]{:S(2)}) collective-permute-start(bf16[1,64,2,128]{3,2,1,0:T(2,128)(2,1)S(1)} %copy-done.8), channel_id=1, source_target_pairs={{0,128},{128,0},{256,384},{384,256},{1,129},{129,1},{257,385},{385... | collective-permute-start | bytes 98312 | tf_op jit(solution)/shard_map/up_x/ppermute | solution.py:368
  20.1 3.7 %collective-permute-start.1 = (bf16[2,64,1024]{2,1,0:T(8,128)(2,1)S(1)}, bf16[2,64,1024]{2,1,0:T(8,128)(2,1)}, u32[]{:S(2)}, u32[]{:S(2)}) collective-permute-start(bf16[2,64,1024]{2,1,0:T(8,128)(2,1)S(1)} %pad_maximum_fusion.1), channel_id=1, source_target_pairs={{0,384},{128,256},{256,128},{384,0},{1,385},{129,257},{257,129},{3... | collective-permute-start | bytes 786440 | tf_op jit(solution)/shard_map/up_x/ppermute | solution.py:371
  23.8 4.4 %collective-permute-done.2 = bf16[1,64,2,128]{3,2,1,0:T(2,128)(2,1)S(1)} collective-permute-done((bf16[1,64,2,128]{3,2,1,0:T(2,128)(2,1)S(1)}, bf16[1,64,2,128]{3,2,1,0:T(2,128)(2,1)S(1)}, u32[]{:S(2)}, u32[]{:S(2)}) %collective-permute-start.2) | collective-permute-done | bytes 32800 | tf_op jit(solution)/shard_map/up_x/ppermute | solution.py:368
  28.3 1.9 %collective-permute-start.3 = (bf16[2,64,2,128]{3,2,1,0:T(2,128)(2,1)S(1)}, bf16[2,64,2,128]{3,2,1,0:T(2,128)(2,1)S(1)}, u32[]{:S(2)}, u32[]{:S(2)}) collective-permute-start(bf16[2,64,2,128]{3,2,1,0:T(2,128)(2,1)S(1)} %pad_maximum_fusion.3), channel_id=1, source_target_pairs={{0,384},{128,256},{256,128},{384,0},{1,385},{129,257},{257,129},{3... | collective-permute-start | bytes 196616 | tf_op jit(solution)/shard_map/up_x/ppermute | solution.py:372
  30.3 11.2 %collective-permute-done.3 = bf16[2,64,2,128]{3,2,1,0:T(2,128)(2,1)S(1)} collective-permute-done((bf16[2,64,2,128]{3,2,1,0:T(2,128)(2,1)S(1)}, bf16[2,64,2,128]{3,2,1,0:T(2,128)(2,1)S(1)}, u32[]{:S(2)}, u32[]{:S(2)}) %collective-permute-start.3) | collective-permute-done | bytes 65568 | tf_op jit(solution)/shard_map/up_x/ppermute | solution.py:372
  41.9 1.0 pad_maximum_fusion.line_ref
  42.9 2.8 %collective-permute-start.4 = (bf16[4,64,1280]{2,1,0:T(8,128)(2,1)S(1)}, bf16[4,64,1280]{2,1,0:T(8,128)(2,1)}, u32[]{:S(2)}, u32[]{:S(2)}) collective-permute-start(bf16[4,64,1280]{2,1,0:T(8,128)(2,1)S(1)} %pad_maximum_fusion.line_ref), channel_id=1, source_target_pairs={{0,64},{64,0},{1,65},{65,1},{2,66},{66,2},{3,67},{67,3},{4,68},{68... | collective-permute-start | bytes 1966088 | tf_op jit(solution)/shard_map/up_y_lo/ppermute | solution.py:381
  47.1 10.3 %all-to-all-start.1 = ((bf16[8,64,256]{2,1,0:T(8,128)(2,1)}), bf16[8,64,256]{2,1,0:T(8,128)(2,1)S(1)}, u32[]{:S(2)}, u32[]{:S(2)}) async-start(bf16[8,64,256]{2,1,0:T(8,128)(2,1)} %shard_map.164), calls=%async_computation.1 | async-start | bytes 524288 | tf_op jit(solution)/shard_map/sum_low/all_to_all | solution.py:20
  59.9 7.4 %all-to-all-done.1.low_ref = bf16[8,64,256]{2,1,0:T(8,128)(2,1)S(1)} async-done(((bf16[8,64,256]{2,1,0:T(8,128)(2,1)}), bf16[8,64,256]{2,1,0:T(8,128)(2,1)S(1)}, u32[]{:S(2)}, u32[]{:S(2)}) %all-to-all-start.1) | async-done | bytes 262176 | tf_op jit(solution)/shard_map/sum_low/all_to_all | solution.py:20
  67.3 1.0 copy-done.1
  69.0 2.3 %shard_map.165 = bf16[64,1280]{1,0:T(8,128)(2,1)} custom-call(s32[64,1]{1,0:T(8,128)S(1)} %copy-done.2, bf16[8,64,256]{2,1,0:T(8,128)(2,1)S(1)} %all-to-all-done.1.low_ref, bf16[4,64,1280]{2,1,0:T(8,128)(2,1)S(1)} %pad_maximum_fusion.line_ref, bf16[4,64,1280]{2,1,0:T(8,128)(2,1)} %collective-permute-done.4.other_ref, f32[64,1280]{1,0:T(8,128)S(1)} %copy-done.1), custom_call_target="tpu_custom_call" | custom-call | flops 83886080 | bytes 2000000 | tf_op jit(solution)/shard_map/pallas_call | solution.py:253
  71.4 3.5 %all-to-all-start.2 = ((bf16[8,8,1280]{2,1,0:T(8,128)(2,1)}), bf16[8,8,1280]{2,1,0:T(8,128)(2,1)S(1)}, u32[]{:S(2)}, u32[]{:S(2)}) async-start(bf16[8,8,1280]{2,1,0:T(8,128)(2,1)} %bitcast.12), calls=%async_computation.2 | async-start | bytes 327680 | tf_op jit(solution)/shard_map/sum_z/all_to_all | solution.py:20
  75.0 8.1 %all-to-all-done.2 = bf16[8,8,1280]{2,1,0:T(8,128)(2,1)S(1)} async-done(((bf16[8,8,1280]{2,1,0:T(8,128)(2,1)}), bf16[8,8,1280]{2,1,0:T(8,128)(2,1)S(1)}, u32[]{:S(2)}, u32[]{:S(2)}) %all-to-all-start.2) | async-done | bytes 163872 | tf_op jit(solution)/shard_map/sum_z/all_to_all | solution.py:20
  84.8 10.3 %all_to_all.25 = bf16[8,8,1024]{2,1,0:T(8,128)(2,1)S(1)} all-to-all(bf16[8,8,1024]{2,1,0:T(8,128)(2,1)S(1)} %broadcast_in_dim.155), channel_id=1, replica_groups=mesh['x'=4,'y_lo'=2,'z'=8,'y_hi'=4,'core'=2] {'z'}, dimensions={0} | all-to-all | bytes 262144 | tf_op jit(solution)/shard_map/gather_z/all_to_all | solution.py:20
  95.1 1.1 broadcast_in_dim.157
  96.2 3.6 %all-to-all-start.4 = ((bf16[8,64,1024]{2,1,0:T(8,128)(2,1)}), bf16[8,64,1024]{2,1,0:T(8,128)(2,1)S(1)}, u32[]{:S(2)}, u32[]{:S(2)}) async-start(bf16[8,64,1024]{2,1,0:T(8,128)(2,1)} %broadcast_in_dim.157), calls=%async_computation.4 | async-start | bytes 2097152 | tf_op jit(solution)/shard_map/gather_plane/all_to_all | solution.py:20
  99.8 10.4 %all-to-all-done.4 = bf16[8,64,1024]{2,1,0:T(8,128)(2,1)S(1)} async-done(((bf16[8,64,1024]{2,1,0:T(8,128)(2,1)}), bf16[8,64,1024]{2,1,0:T(8,128)(2,1)S(1)}, u32[]{:S(2)}, u32[]{:S(2)}) %all-to-all-start.4) | async-done | bytes 1048608 | tf_op jit(solution)/shard_map/gather_plane/all_to_all | solution.py:20
  112.4 8.5 %all-gather = bf16[1024,128]{1,0:T(8,128)(2,1)S(1)} all-gather(bf16[512,128]{1,0:T(8,128)(2,1)S(1)} %fusion.1), channel_id=2, replica_groups=mesh['x'=4,'y_lo'=2,'z'=8,'y_hi'=4,'core'=2] {'core'}, dimensions={0}, use_global_device_ids=true | all-gather | bytes 393216 | tf_op jit(solution)/shard_map/sum_core/all_gather | solution.py:456
  121.1 6.6 %all_gather.19 = bf16[2,2,128,128]{3,2,1,0:T(8,128)(2,1)S(1)} all-gather(bf16[1,2,128,128]{3,2,1,0:T(8,128)(2,1)S(1)} %bitcast.96), channel_id=1, replica_groups={{0,2},{4,6},{1,3},{5,7},{8,10},{12,14},{9,11},{13,15},{16,18},{20,22},{..., dimensions={0}, use_global_device_ids=true | all-gather | bytes 196608 | tf_op jit(solution)/shard_map/sum_y_hi/all_gather | solution.py:464
  127.8 6.0 %all_gather.20 = bf16[2,2,128,128]{3,2,1,0:T(8,128)(2,1)S(1)} all-gather(bf16[1,2,128,128]{3,2,1,0:T(8,128)(2,1)S(1)} %add_convert_fusion), channel_id=1, replica_groups={{2,4},{6,0},{3,5},{7,1},{10,12},{14,8},{11,13},{15,9},{18,20},{22,16},{..., dimensions={0}, use_global_device_ids=true | all-gather | bytes 196608 | tf_op jit(solution)/shard_map/sum_y_hi/all_gather | solution.py:464
  133.9 3.1 %all_gather.21 = bf16[4,128,128]{2,1,0:T(8,128)(2,1)S(1)} all-gather(bf16[2,128,128]{2,1,0:T(8,128)(2,1)S(1)} %fusion.10), channel_id=1, replica_groups=mesh['x'=4,'y_lo'=2,'z'=8,'y_hi'=4,'core'=2] {'core'}, dimensions={0}, use_global_device_ids=true | all-gather | bytes 196608 | tf_op jit(solution)/shard_map/gather_core/all_gather | solution.py:471
  (97 shorter events, 12.4 us)
Async XLA Ops:
  0.0 110.2 %copy-start = (bf16[8,1024,64]{1,2,0:T(8,128)(2,1)S(1)}, bf16[8,1024,64]{1,2,0:T(8,128)(2,1)}, u32[]{:S(2)}) copy-start(bf16[8,1024,64]{1,2,0:T(8,128)(2,1)} %param.24) | copy-start | bytes 3145732
  0.0 9.2 %collective-permute-start = (bf16[1,64,1024]{2,1,0:T(8,128)(2,1)}, bf16[1,64,1024]{2,1,0:T(8,128)(2,1)S(1)}, u32[]{:S(2)}, u32[]{:S(2)}) collective-permute-start(bf16[1,64,1024]{2,1,0:T(8,128)(2,1)} %param.26), channel_id=1, source_target_pairs={{0,128},{128,0},{256,384},{384,256},{1,129},{129,1},{257,385},{385... | collective-permute-start | bytes 393224 | tf_op jit(solution)/shard_map/up_x/ppermute | solution.py:348
  9.2 32.7 %copy-start.5 = (bf16[1,64,1024]{2,1,0:T(8,128)(2,1)}, bf16[1,64,1024]{2,1,0:T(8,128)(2,1)S(1)}, u32[]{:S(2)}) copy-start(bf16[1,64,1024]{2,1,0:T(8,128)(2,1)S(1)} %collective-permute-done) | copy-start | bytes 393220
  9.2 5.0 %copy-start.13 = (s32[128]{0:T(128)S(1)}, s32[128]{0:T(128)}, u32[]{:S(2)}) copy-start(s32[128]{0:T(128)} %param.30) | copy-start | bytes 1540
  9.2 5.1 %copy-start.11 = (s32[2]{0:T(128)S(1)}, s32[2]{0:T(128)}, u32[]{:S(2)}) copy-start(s32[2]{0:T(128)} %param.33) | copy-start | bytes 28
  9.2 5.2 %copy-start.10 = (s32[16,2]{0,1:T(2,128)S(1)}, s32[16,2]{0,1:T(2,128)}, u32[]{:S(2)}) copy-start(s32[16,2]{0,1:T(2,128)} %param.32) | copy-start | bytes 388
  9.2 5.7 %copy-start.14 = (s32[8]{0:T(128)S(1)}, s32[8]{0:T(128)}, u32[]{:S(2)}) copy-start(s32[8]{0:T(128)} %param.31) | copy-start | bytes 100
  9.2 7.5 %copy-start.8 = (bf16[1,64,2,128]{3,2,1,0:T(2,128)(2,1)S(1)}, bf16[1,64,2,128]{3,2,1,0:T(2,128)(2,1)}, u32[]{:S(2)}) copy-start(bf16[1,64,2,128]{3,2,1,0:T(2,128)(2,1)} %param.27) | copy-start | bytes 98308
  9.3 10.8 %copy-start.4 = (bf16[1,64,1024]{2,1,0:T(8,128)(2,1)S(1)}, bf16[1,64,1024]{2,1,0:T(8,128)(2,1)}, u32[]{:S(2)}) copy-start(bf16[1,64,1024]{2,1,0:T(8,128)(2,1)} %param.26) | copy-start | bytes 393220
  9.3 37.0 %all-to-all-start = ((bf16[8,64,1536]{2,1,0:T(8,128)(2,1)}), bf16[8,64,1536]{2,1,0:T(8,128)(2,1)S(1)}, u32[]{:S(2)}, u32[]{:S(2)}) async-start(bf16[8,64,1536]{2,1,0:T(8,128)(2,1)} %bitcast.87), calls=%async_computation | async-start | bytes 3145728 | tf_op jit(solution)/shard_map/sum_plane/all_to_all | solution.py:20
  16.7 11.5 %collective-permute-start.2 = (bf16[1,64,2,128]{3,2,1,0:T(2,128)(2,1)S(1)}, bf16[1,64,2,128]{3,2,1,0:T(2,128)(2,1)S(1)}, u32[]{:S(2)}, u32[]{:S(2)}) collective-permute-start(bf16[1,64,2,128]{3,2,1,0:T(2,128)(2,1)S(1)} %copy-done.8), channel_id=1, source_target_pairs={{0,128},{128,0},{256,384},{384,256},{1,129},{129,1},{257,385},{385... | collective-permute-start | bytes 98312 | tf_op jit(solution)/shard_map/up_x/ppermute | solution.py:368
  20.1 21.7 %collective-permute-start.1 = (bf16[2,64,1024]{2,1,0:T(8,128)(2,1)S(1)}, bf16[2,64,1024]{2,1,0:T(8,128)(2,1)}, u32[]{:S(2)}, u32[]{:S(2)}) collective-permute-start(bf16[2,64,1024]{2,1,0:T(8,128)(2,1)S(1)} %pad_maximum_fusion.1), channel_id=1, source_target_pairs={{0,384},{128,256},{256,128},{384,0},{1,385},{129,257},{257,129},{3... | collective-permute-start | bytes 786440 | tf_op jit(solution)/shard_map/up_x/ppermute | solution.py:371
  28.3 13.2 %collective-permute-start.3 = (bf16[2,64,2,128]{3,2,1,0:T(2,128)(2,1)S(1)}, bf16[2,64,2,128]{3,2,1,0:T(2,128)(2,1)S(1)}, u32[]{:S(2)}, u32[]{:S(2)}) collective-permute-start(bf16[2,64,2,128]{3,2,1,0:T(2,128)(2,1)S(1)} %pad_maximum_fusion.3), channel_id=1, source_target_pairs={{0,384},{128,256},{256,128},{384,0},{1,385},{129,257},{257,129},{3... | collective-permute-start | bytes 196616 | tf_op jit(solution)/shard_map/up_x/ppermute | solution.py:372
  41.8 3.9 %copy-start.16 = (s32[64]{0:T(128)S(1)}, s32[64]{0:T(128)}, u32[]{:S(2)}) copy-start(s32[64]{0:T(128)} %and_select_fusion.4) | copy-start | bytes 772
  42.9 17.0 %collective-permute-start.4 = (bf16[4,64,1280]{2,1,0:T(8,128)(2,1)S(1)}, bf16[4,64,1280]{2,1,0:T(8,128)(2,1)}, u32[]{:S(2)}, u32[]{:S(2)}) collective-permute-start(bf16[4,64,1280]{2,1,0:T(8,128)(2,1)S(1)} %pad_maximum_fusion.line_ref), channel_id=1, source_target_pairs={{0,64},{64,0},{1,65},{65,1},{2,66},{66,2},{3,67},{67,3},{4,68},{68... | collective-permute-start | bytes 1966088 | tf_op jit(solution)/shard_map/up_y_lo/ppermute | solution.py:381
  47.1 20.2 %all-to-all-start.1 = ((bf16[8,64,256]{2,1,0:T(8,128)(2,1)}), bf16[8,64,256]{2,1,0:T(8,128)(2,1)S(1)}, u32[]{:S(2)}, u32[]{:S(2)}) async-start(bf16[8,64,256]{2,1,0:T(8,128)(2,1)} %shard_map.164), calls=%async_computation.1 | async-start | bytes 524288 | tf_op jit(solution)/shard_map/sum_low/all_to_all | solution.py:20
  59.0 15.9 %copy-start.12 = (f32[8]{0:T(128)S(1)}, f32[8]{0:T(128)}, u32[]{:S(2)}) copy-start(f32[8]{0:T(128)} %fusion.34) | copy-start | bytes 100
  67.3 1.0 copy-start.1
  69.0 14.4 %copy-start.3 = (bf16[2,1,1024,128]{3,2,1,0:T(8,128)(2,1)S(1)}, bf16[2,1,1024,128]{3,2,1,0:T(8,128)(2,1)}, u32[]{:S(2)}) copy-start(bf16[2,1,1024,128]{3,2,1,0:T(8,128)(2,1)} %param.28) | copy-start | bytes 1572868
  71.4 12.4 %copy-start.17 = (pred[32,4]{0,1:T(4,128)(4,1)S(1)}, pred[32,4]{0,1:T(4,128)(4,1)}, u32[]{:S(2)}) copy-start(pred[32,4]{0,1:T(4,128)(4,1)} %iota_compare_fusion.3) | copy-start | bytes 388
  71.4 12.9 %copy-start.15 = (bf16[2,1,1024,128]{3,2,1,0:T(8,128)(2,1)S(1)}, bf16[2,1,1024,128]{3,2,1,0:T(8,128)(2,1)}, u32[]{:S(2)}) copy-start(bf16[2,1,1024,128]{3,2,1,0:T(8,128)(2,1)} %param.29) | copy-start | bytes 1572868
  71.4 11.7 %all-to-all-start.2 = ((bf16[8,8,1280]{2,1,0:T(8,128)(2,1)}), bf16[8,8,1280]{2,1,0:T(8,128)(2,1)S(1)}, u32[]{:S(2)}, u32[]{:S(2)}) async-start(bf16[8,8,1280]{2,1,0:T(8,128)(2,1)} %bitcast.12), calls=%async_computation.2 | async-start | bytes 327680 | tf_op jit(solution)/shard_map/sum_z/all_to_all | solution.py:20
  96.2 14.0 %all-to-all-start.4 = ((bf16[8,64,1024]{2,1,0:T(8,128)(2,1)}), bf16[8,64,1024]{2,1,0:T(8,128)(2,1)S(1)}, u32[]{:S(2)}, u32[]{:S(2)}) async-start(bf16[8,64,1024]{2,1,0:T(8,128)(2,1)} %broadcast_in_dim.157), calls=%async_computation.4 | async-start | bytes 2097152 | tf_op jit(solution)/shard_map/gather_plane/all_to_all | solution.py:20
  111.9 21.9 %copy-start.6 = (bf16[4,128,128]{2,1,0:T(8,128)(2,1)S(1)}, bf16[4,128,128]{2,1,0:T(8,128)(2,1)}, u32[]{:S(2)}) copy-start(bf16[4,128,128]{2,1,0:T(8,128)(2,1)} %inputs_ref.1) | copy-start | bytes 393220
  (3 other events, 2.6 us)

commit v12 on v10

--- a/solution.py
+++ b/solution.py
@@ -3,6 +3,7 @@
 
 import jax
 import jax.numpy as jnp
+import numpy as np
 from jax import lax
 from jax.experimental import pallas as pl
 from jax.experimental.pallas import tpu as pltpu
@@ -54,6 +55,7 @@
     gain_ref,
     tasks_ref,
     moves_ref,
+    homes_ref,
     inputs_ref,
     adapter_ref,
     query_ref,
@@ -114,6 +116,9 @@
         chosen = jnp.sum(jnp.where(here, moves_ref[0:1, :], 0), axis=1, keepdims=True)
         late = row % per_group >= per_group // 2
         task = jnp.where(jnp.logical_and(late, moved), chosen, task)
+        home = jnp.sum(
+            jnp.where(lane(adapters) == task, homes_ref[...], 0), axis=1, keepdims=True
+        ).astype(jnp.float32)
         gained = gained_ref[first : first + block, :]
         total = jnp.zeros((block, low), jnp.float32)
         for adapter in range(0, adapters, 2):
@@ -132,7 +137,9 @@
         extra = jnp.where(
             lane(rest) == 0,
             squares_high,
-            jnp.where(lane(rest) == 1, squares - squares_high, 0.0),
+            jnp.where(
+                lane(rest) == 1, squares - squares_high, jnp.where(lane(rest) == 2, home, 0.0)
+            ),
         )
         out_ref[first : first + block, base_end : base_end + PADDED_WIDTH] = jnp.concatenate(
             [total, extra], axis=1
@@ -150,14 +157,14 @@
         out_ref[rows, key_end:base_end] = dot(gained, held_value[...]).astype(jnp.bfloat16)
 
 
-def project(inputs, gain, w_query, w_key, w_value, adapter_in, tasks, moves, own_rows):
+def project(inputs, gain, w_query, w_key, w_value, adapter_in, tasks, moves, homes, own_rows):
     steps, all_rows, width = inputs.shape
     columns = w_query.shape[1] + w_key.shape[1] + w_value.shape[1] + PADDED_WIDTH
     large = (inputs, jnp.swapaxes(adapter_in, 1, 2), w_query, w_key, w_value)
     return pl.pallas_call(
         functools.partial(project_kernel, own_rows),
         out_shape=jax.ShapeDtypeStruct((steps * all_rows, columns), jnp.bfloat16),
-        in_specs=[pl.BlockSpec(memory_space=pltpu.VMEM)] * 3
+        in_specs=[pl.BlockSpec(memory_space=pltpu.VMEM)] * 4
         + [pl.BlockSpec(memory_space=pl.ANY)] * len(large),
         scratch_shapes=[pltpu.VMEM(array.shape, jnp.bfloat16) for array in large]
         + [
@@ -167,7 +174,7 @@
         cost_estimate=pl.CostEstimate(
             flops=2 * steps * all_rows * width * 3328, bytes_accessed=3_000_000, transcendentals=0
         ),
-    )(gain[None, :], tasks[None, :], moves.T, *large)
+    )(gain[None, :], tasks[None, :], moves.T, homes[None, :], *large)
 
 
 def low_kernel(low, parts_ref, low_ref):
@@ -177,14 +184,13 @@
     for source in range(1, sources):
         total = total + parts_ref[source, :, columns - width :].astype(jnp.float32)
     lane = lax.broadcasted_iota(jnp.int32, total.shape, 1)
-    squares = jnp.sum(jnp.where(lane >= low, total, 0.0), axis=1, keepdims=True)
+    terms = jnp.logical_or(lane == low, lane == low + 1)
+    squares = jnp.sum(jnp.where(terms, total, 0.0), axis=1, keepdims=True)
     squares_high = squares.astype(jnp.bfloat16).astype(jnp.float32)
     total = jnp.where(
-        lane < low,
-        total,
-        jnp.where(
-            lane == low, squares_high, jnp.where(lane == low + 1, squares - squares_high, 0.0)
-        ),
+        lane == low,
+        squares_high,
+        jnp.where(lane == low + 1, squares - squares_high, total),
     ).astype(jnp.bfloat16)
     for target in range(targets):
         low_ref[target] = total
@@ -208,7 +214,7 @@
     rank,
     head_dim,
     model_width,
-    slot_ref,
+    groups,
     low_ref,
     line_ref,
     other_ref,
@@ -222,13 +228,19 @@
     for source in range(1, low_ref.shape[0]):
         total = total + low_ref[source].astype(jnp.float32)
     lane = lax.broadcasted_iota(jnp.int32, total.shape, 1)
-    squares = jnp.sum(jnp.where(lane >= low, total, 0.0), axis=1, keepdims=True)
+    terms = jnp.logical_or(lane == low, lane == low + 1)
+    squares = jnp.sum(jnp.where(terms, total, 0.0), axis=1, keepdims=True)
     inverse = lax.rsqrt(squares / model_width + epsilon)
     lowrank = (inverse * total).astype(jnp.bfloat16)
     from_lane = lax.broadcasted_iota(jnp.int32, (PADDED_WIDTH, line * rank), 0)
     to_lane = lax.broadcasted_iota(jnp.int32, (PADDED_WIDTH, line * rank), 1)
     slot_lane = lax.broadcasted_iota(jnp.int32, (rows, line * rank), 1) // rank
-    slot = slot_ref[...]
+    home = jnp.sum(jnp.where(lane == low + 2, total, 0.0), axis=1, keepdims=True) / groups
+    home = home.astype(jnp.int32)
+    depth = low_ref.shape[0]
+    same_half = home // depth % 2 == lax.axis_index("y_lo")
+    slot = home // (2 * depth) + jnp.where(same_half, 0, line)
+    slot = jnp.where(home % depth == lax.axis_index("z"), slot, -1)
     spreads = []
     for number in range(3):
         pick = jnp.where(from_lane == number * rank + to_lane % rank, 1.0, 0.0)
@@ -249,11 +261,11 @@
         out_ref[:, first:last] = (inverse * base_ref[:, first:last] + lifted).astype(jnp.bfloat16)
 
 
-def lift(slot, low_parts, base, up_line, up_other, rank, head_dim, model_width):
+def lift(low_parts, base, up_line, up_other, rank, head_dim, model_width, groups):
     return pl.pallas_call(
-        functools.partial(lift_kernel, rank, head_dim, model_width),
+        functools.partial(lift_kernel, rank, head_dim, model_width, groups),
         out_shape=jax.ShapeDtypeStruct(base.shape, jnp.bfloat16),
-        in_specs=[pl.BlockSpec(memory_space=pltpu.VMEM)] * 5,
+        in_specs=[pl.BlockSpec(memory_space=pltpu.VMEM)] * 4,
         out_specs=pl.BlockSpec(memory_space=pltpu.VMEM),
         compiler_params=pltpu.CompilerParams(vmem_limit_bytes=16 * 1024 * 1024),
         cost_estimate=pl.CostEstimate(
@@ -261,7 +273,7 @@
             bytes_accessed=2_000_000,
             transcendentals=0,
         ),
-    )(slot, low_parts, up_line, up_other, base)
+    )(low_parts, up_line, up_other, base)
 
 
 def attend(queries, cache_keys, value_cache, fresh_keys, fresh_values, lengths, query_steps):
@@ -276,7 +288,7 @@
     )
     visible = jnp.arange(cache_keys.shape[1])[None, None, :] < lengths[:, None, None]
     old_scores = jnp.where(visible, old_scores, -1e30)
-    fresh = jnp.arange(fresh_keys.shape[1])[None, None, :] <= query_steps[None, :, None]
+    fresh = np.arange(fresh_keys.shape[1])[None, None, :] <= query_steps[None, :, None]
     new_scores = jnp.where(fresh, new_scores, -1e30)
     highest = jnp.maximum(jnp.max(old_scores, axis=-1), jnp.max(new_scores, axis=-1))[..., None]
     old_exp = jnp.exp(old_scores - highest)
@@ -332,16 +344,6 @@
     model_width = width_part * groups
     column_rows = depth * per_group
 
-    group_tasks = tasks.reshape(groups, own_rows)
-    matched = moves[:, 1][None, :] == jnp.arange(groups, dtype=jnp.int32)[:, None]
-    moved = jnp.any(matched, axis=1)
-    chosen = jnp.sum(jnp.where(matched, moves[:, 0][None, :], 0), axis=1)
-    late = jnp.where(moved[:, None], chosen[:, None], group_tasks)
-    active = jnp.stack([group_tasks if s < steps // 2 else late for s in range(steps)], axis=1)
-    active = active.reshape(every_row)
-    marks = active[:, None] == jnp.arange(task_count, dtype=jnp.int32)[None, :]
-    row_home = jnp.sum(jnp.where(marks, homes[None, :], 0), axis=1)
-
     partial = project(
         inputs,
         gain,
@@ -351,6 +353,7 @@
         adapter_in,
         tasks,
         moves,
+        homes,
         own_rows,
     )
     partial, pool_query, slot_keyvalue_matrices = lax.optimization_barrier(
@@ -375,15 +378,8 @@
     with jax.named_scope("sum_low"):
         low_parts = exchange(low_part, "z")
 
-    x, y_lo, z = (lax.axis_index(name) for name in GROUP)
-    column_home = lax.dynamic_slice_in_dim(
-        row_home, (x * 2 + y_lo) * column_rows, column_rows, 0
-    )
-    home_x = column_home // (2 * depth)
-    other_half = jnp.where(column_home // depth % 2 == y_lo, 0, line)
-    slot = jnp.where(column_home % depth == z, home_x + other_half, -1)
     raw_part = lift(
-        slot[:, None], low_parts, plane_sum, up_line, up_other, rank, head_dim, model_width
+        low_parts, plane_sum, up_line, up_other, rank, head_dim, model_width, groups
     )
     with jax.named_scope("sum_z"):
         by_depth = exchange(raw_part.reshape(depth, per_group, base_end), "z")
@@ -412,7 +408,7 @@
         by_row(new_keys),
         by_row(raw_value),
         lengths,
-        jnp.arange(steps * heads) // heads,
+        np.arange(steps * heads) // heads,
     )
     attended = (
         attended.reshape(own_rows, steps, query_width)
@@ -421,13 +417,23 @@
     )
 
     with jax.named_scope("gather_z"):
-        line = exchange(
+        column = exchange(
             jnp.broadcast_to(attended[None], (depth, per_group, query_width)), "z"
         ).reshape(depth * per_group, query_width)
+    column, tasks, moves = lax.optimization_barrier((column, tasks, moves))
     with jax.named_scope("gather_plane"):
         piece_rows = exchange(
-            jnp.broadcast_to(line[None], (planes, depth * per_group, query_width)), PLANE
+            jnp.broadcast_to(column[None], (planes, depth * per_group, query_width)), PLANE
         ).reshape(every_row, query_width)
+
+    group_tasks = tasks.reshape(groups, own_rows)
+    matched = moves[:, 1][None, :] == jnp.arange(groups, dtype=jnp.int32)[:, None]
+    moved = jnp.any(matched, axis=1)
+    chosen = jnp.sum(jnp.where(matched, moves[:, 0][None, :], 0), axis=1)
+    late = jnp.where(moved[:, None], chosen[:, None], group_tasks)
+    active = jnp.stack([group_tasks if s < steps // 2 else late for s in range(steps)], axis=1)
+    active = active.reshape(every_row)
+    marks = active[:, None] == jnp.arange(task_count, dtype=jnp.int32)[None, :]
 
     every_reduced = jnp.einsum(
         "rq,tqc->rtc", piece_rows, adapter_attn, preferred_element_type=jnp.float32

time: 136 us -> 134 us (0.985)
  local copies, waits for them, and re-layouts: 5.5 us -> 4.02 us
    unnamed x36 -> x30, local copies, waits for them, and re-layouts: 3.09 us -> 2.32 us
  transfers between devices with their start and end apart: 5 -> 5, of which waited for: 3 -> 3; matrix products, arithmetic and copies ran while one was open for 3% -> 1% of each run, Pallas kernels for 1% -> 1%
where the time goes in v12:
time: 134 us; the launch traced here: 133 us
  blocking collectives  62.6 us (47%)
  starting transfers between devices  27 us (20%)
  waiting for transfers between devices  26 us (19%)
  Pallas kernels  8.56 us (6%)
  local copies, waits for them, and re-layouts  4.02 us (3%)
  matrix products  2.61 us (2%)
  other arithmetic  2.03 us (2%)
    all_to_all x4, waiting for transfers between devices, exchange(): return lax.all_to_all(blocks, axes, 0, 0, tiled=True)  26 us
    all_gather x1, blocking collectives, on_device(): up_line = lax.all_gather(up, 'x', axis=0)  25.8 us
    all_to_all x4, starting transfers between devices, exchange(): return lax.all_to_all(blocks, axes, 0, 0, tiled=True)  24.4 us
    all_gather x2, blocking collectives, on_device(): lax.all_gather(mine.astype(jnp.bfloat16), 'y_hi', axis=0, axis_index_grou...  12.8 us
    all_gather x1, blocking collectives, on_device(): pair = lax.all_gather(mixed, 'core', axis=0)  10.4 us
    all_to_all x1, blocking collectives, exchange(): return lax.all_to_all(blocks, axes, 0, 0, tiled=True)  10.3 us
    pallas_call x1, Pallas kernels, project(): pl.pallas_call(functools.partial(project_kernel, own_rows), out_shape=jax...  5.39 us
    all_gather x1, blocking collectives, on_device(): return lax.all_gather(finished, 'core', axis=0, tiled=True)  3.33 us
  transfers between devices with their start and end apart: 5, of which 3 were waited for; matrix products, arithmetic and copies ran while one was open for 1% of the time, Pallas kernels for 1%

profile of v12, /device:TPU:1, one launch (start us, length us, event | category | flops | bytes accessed | tf_op | source)
XLA Modules:
  0.0 133.2 jit_solution(7538020908919431327)
XLA Ops:
  0.0 5.4 %shard_map.172 = bf16[512,1536]{1,0:T(8,128)(2,1)} custom-call(f32[1,128]{1,0:T(1,128)} %bitcast.114, s32[1,128]{1,0:T(1,128)} %bitcast.113, s32[2,16]{1,0:T(2,128)} %bitcast.112, s32[1,8]{1,0:T(1,128)} %bitcast.115, bf16[4,128,128]{2,1,0:T(8,128)(2,1)} %inputs_ref.1, bf16[8,192,128]{2,1,0:T(8,128)(2,1)} %bitcast.97, bf16[128,1024]{1,0:T(8,128)(2,1)} %query_ref.1, ...), custom_call_target="tpu_custom_call" | custom-call | flops 436207616 | bytes 3000000 | tf_op jit(solution)/shard_map/pallas_call | solution.py:164
  5.4 6.0 %all-to-all-start = ((bf16[8,64,1536]{2,1,0:T(8,128)(2,1)}), bf16[8,64,1536]{2,1,0:T(8,128)(2,1)S(1)}, u32[]{:S(2)}, u32[]{:S(2)}) async-start(bf16[8,64,1536]{2,1,0:T(8,128)(2,1)} %bitcast.91), calls=%async_computation | async-start | bytes 3145728 | tf_op jit(solution)/shard_map/sum_plane/all_to_all | solution.py:21
  11.5 25.8 %all-gather = bf16[256,1280]{1,0:T(8,128)(2,1)S(1)} all-gather(bf16[64,1280]{1,0:T(8,128)(2,1)S(1)} %pad_maximum_fusion), channel_id=2, replica_groups=mesh['x'=4,'y_lo'=2,'z'=8,'y_hi'=4,'core'=2] {'x'}, dimensions={0}, use_global_device_ids=true | all-gather | bytes 819200 | tf_op jit(solution)/shard_map/up_x/all_gather | solution.py:373
  37.3 2.6 %collective-permute-start = (bf16[4,64,1280]{2,1,0:T(8,128)(2,1)S(1)}, bf16[4,64,1280]{2,1,0:T(8,128)(2,1)}, u32[]{:S(2)}, u32[]{:S(2)}) collective-permute-start(bf16[4,64,1280]{2,1,0:T(8,128)(2,1)S(1)} %bitcast.89), channel_id=1, source_target_pairs={{0,64},{64,0},{1,65},{65,1},{2,66},{66,2},{3,67},{67,3},{4,68},{68... | collective-permute-start | bytes 1966088 | tf_op jit(solution)/shard_map/up_y_lo/ppermute | solution.py:375
  40.1 0.8 shard_map.173
  40.9 11.5 %all-to-all-start.1 = ((bf16[8,64,256]{2,1,0:T(8,128)(2,1)}), bf16[8,64,256]{2,1,0:T(8,128)(2,1)S(1)}, u32[]{:S(2)}, u32[]{:S(2)}) async-start(bf16[8,64,256]{2,1,0:T(8,128)(2,1)} %shard_map.173), calls=%async_computation.1 | async-start | bytes 524288 | tf_op jit(solution)/shard_map/sum_low/all_to_all | solution.py:21
  52.4 0.9 convert_reduce_fusion.base_ref
  53.3 8.4 %all-to-all-done.1.low_ref = bf16[8,64,256]{2,1,0:T(8,128)(2,1)S(1)} async-done(((bf16[8,64,256]{2,1,0:T(8,128)(2,1)}), bf16[8,64,256]{2,1,0:T(8,128)(2,1)S(1)}, u32[]{:S(2)}, u32[]{:S(2)}) %all-to-all-start.1) | async-done | bytes 262176 | tf_op jit(solution)/shard_map/sum_low/all_to_all | solution.py:21
  61.7 1.0 copy-done.1
  62.6 2.4 %shard_map.174 = bf16[64,1280]{1,0:T(8,128)(2,1)} custom-call(bf16[8,64,256]{2,1,0:T(8,128)(2,1)S(1)} %all-to-all-done.1.low_ref, bf16[4,64,1280]{2,1,0:T(8,128)(2,1)S(1)} %bitcast.90, bf16[4,64,1280]{2,1,0:T(8,128)(2,1)} %collective-permute-done.other_ref, f32[64,1280]{1,0:T(8,128)S(1)} %copy-done.1), custom_call_target="tpu_custom_call" | custom-call | flops 83886080 | bytes 2000000 | tf_op jit(solution)/shard_map/pallas_call | solution.py:265
  65.0 3.4 %all-to-all-start.2 = ((bf16[8,8,1280]{2,1,0:T(8,128)(2,1)}), bf16[8,8,1280]{2,1,0:T(8,128)(2,1)S(1)}, u32[]{:S(2)}, u32[]{:S(2)}) async-start(bf16[8,8,1280]{2,1,0:T(8,128)(2,1)} %bitcast.8), calls=%async_computation.2 | async-start | bytes 327680 | tf_op jit(solution)/shard_map/sum_z/all_to_all | solution.py:21
  68.5 8.1 %all-to-all-done.2 = bf16[8,8,1280]{2,1,0:T(8,128)(2,1)S(1)} async-done(((bf16[8,8,1280]{2,1,0:T(8,128)(2,1)}), bf16[8,8,1280]{2,1,0:T(8,128)(2,1)S(1)}, u32[]{:S(2)}, u32[]{:S(2)}) %all-to-all-start.2) | async-done | bytes 163872 | tf_op jit(solution)/shard_map/sum_z/all_to_all | solution.py:21
  78.3 10.3 %all_to_all.25 = bf16[8,8,1024]{2,1,0:T(8,128)(2,1)S(1)} all-to-all(bf16[8,8,1024]{2,1,0:T(8,128)(2,1)S(1)} %broadcast_in_dim.117), channel_id=1, replica_groups=mesh['x'=4,'y_lo'=2,'z'=8,'y_hi'=4,'core'=2] {'z'}, dimensions={0} | all-to-all | bytes 262144 | tf_op jit(solution)/shard_map/gather_z/all_to_all | solution.py:21
  88.6 1.1 broadcast_in_dim.118
  89.7 3.6 %all-to-all-start.4 = ((bf16[8,64,1024]{2,1,0:T(8,128)(2,1)}), bf16[8,64,1024]{2,1,0:T(8,128)(2,1)S(1)}, u32[]{:S(2)}, u32[]{:S(2)}) async-start(bf16[8,64,1024]{2,1,0:T(8,128)(2,1)} %broadcast_in_dim.118), calls=%async_computation.4 | async-start | bytes 2097152 | tf_op jit(solution)/shard_map/gather_plane/all_to_all | solution.py:21
  94.0 9.6 %all-to-all-done.4 = bf16[8,64,1024]{2,1,0:T(8,128)(2,1)S(1)} async-done(((bf16[8,64,1024]{2,1,0:T(8,128)(2,1)}), bf16[8,64,1024]{2,1,0:T(8,128)(2,1)S(1)}, u32[]{:S(2)}, u32[]{:S(2)}) %all-to-all-start.4) | async-done | bytes 1048608 | tf_op jit(solution)/shard_map/gather_plane/all_to_all | solution.py:21
  103.6 0.7 fusion.39
  104.9 0.5 copy-done.4
  105.4 0.4 fusion.1
  105.8 10.4 %all-gather.1 = bf16[1024,128]{1,0:T(8,128)(2,1)S(1)} all-gather(bf16[512,128]{1,0:T(8,128)(2,1)S(1)} %fusion.1), channel_id=3, replica_groups=mesh['x'=4,'y_lo'=2,'z'=8,'y_hi'=4,'core'=2] {'core'}, dimensions={0}, use_global_device_ids=true | all-gather | bytes 393216 | tf_op jit(solution)/shard_map/sum_core/all_gather | solution.py:451
  116.4 6.8 %all_gather.27 = bf16[2,2,128,128]{3,2,1,0:T(8,128)(2,1)S(1)} all-gather(bf16[1,2,128,128]{3,2,1,0:T(8,128)(2,1)S(1)} %bitcast.100), channel_id=1, replica_groups={{0,2},{4,6},{1,3},{5,7},{8,10},{12,14},{9,11},{13,15},{16,18},{20,22},{..., dimensions={0}, use_global_device_ids=true | all-gather | bytes 196608 | tf_op jit(solution)/shard_map/sum_y_hi/all_gather | solution.py:459
  123.2 6.0 %all_gather.28 = bf16[2,2,128,128]{3,2,1,0:T(8,128)(2,1)S(1)} all-gather(bf16[1,2,128,128]{3,2,1,0:T(8,128)(2,1)S(1)} %add_convert_fusion), channel_id=1, replica_groups={{2,4},{6,0},{3,5},{7,1},{10,12},{14,8},{11,13},{15,9},{18,20},{22,16},{..., dimensions={0}, use_global_device_ids=true | all-gather | bytes 196608 | tf_op jit(solution)/shard_map/sum_y_hi/all_gather | solution.py:459
  129.2 3.3 %all_gather.29 = bf16[4,128,128]{2,1,0:T(8,128)(2,1)S(1)} all-gather(bf16[2,128,128]{2,1,0:T(8,128)(2,1)S(1)} %fusion.10), channel_id=1, replica_groups=mesh['x'=4,'y_lo'=2,'z'=8,'y_hi'=4,'core'=2] {'core'}, dimensions={0}, use_global_device_ids=true | all-gather | bytes 196608 | tf_op jit(solution)/shard_map/gather_core/all_gather | solution.py:466
  132.6 0.7 copy.78
  (69 shorter events, 3.4 us)
Async XLA Ops:
  0.0 103.6 %copy-start = (bf16[8,1024,64]{1,2,0:T(8,128)(2,1)S(1)}, bf16[8,1024,64]{1,2,0:T(8,128)(2,1)}, u32[]{:S(2)}) copy-start(bf16[8,1024,64]{1,2,0:T(8,128)(2,1)} %param.25) | copy-start | bytes 3145732
  5.4 6.0 %copy-start.7 = (bf16[1,64,2,128]{3,2,1,0:T(2,128)(2,1)S(1)}, bf16[1,64,2,128]{3,2,1,0:T(2,128)(2,1)}, u32[]{:S(2)}) copy-start(bf16[1,64,2,128]{3,2,1,0:T(2,128)(2,1)} %param.28) | copy-start | bytes 98308
  5.4 6.1 %copy-start.5 = (bf16[1,64,1024]{2,1,0:T(8,128)(2,1)S(1)}, bf16[1,64,1024]{2,1,0:T(8,128)(2,1)}, u32[]{:S(2)}) copy-start(bf16[1,64,1024]{2,1,0:T(8,128)(2,1)} %param.27) | copy-start | bytes 393220
  5.4 34.5 %copy-start.10 = (s32[2]{0:T(128)S(1)}, s32[2]{0:T(128)}, u32[]{:S(2)}) copy-start(s32[2]{0:T(128)} %param.34) | copy-start | bytes 28
  5.4 34.6 %all-to-all-start = ((bf16[8,64,1536]{2,1,0:T(8,128)(2,1)}), bf16[8,64,1536]{2,1,0:T(8,128)(2,1)S(1)}, u32[]{:S(2)}, u32[]{:S(2)}) async-start(bf16[8,64,1536]{2,1,0:T(8,128)(2,1)} %bitcast.91), calls=%async_computation | async-start | bytes 3145728 | tf_op jit(solution)/shard_map/sum_plane/all_to_all | solution.py:21
  37.3 16.0 %collective-permute-start = (bf16[4,64,1280]{2,1,0:T(8,128)(2,1)S(1)}, bf16[4,64,1280]{2,1,0:T(8,128)(2,1)}, u32[]{:S(2)}, u32[]{:S(2)}) collective-permute-start(bf16[4,64,1280]{2,1,0:T(8,128)(2,1)S(1)} %bitcast.89), channel_id=1, source_target_pairs={{0,64},{64,0},{1,65},{65,1},{2,66},{66,2},{3,67},{67,3},{4,68},{68... | collective-permute-start | bytes 1966088 | tf_op jit(solution)/shard_map/up_y_lo/ppermute | solution.py:375
  40.9 20.8 %all-to-all-start.1 = ((bf16[8,64,256]{2,1,0:T(8,128)(2,1)}), bf16[8,64,256]{2,1,0:T(8,128)(2,1)S(1)}, u32[]{:S(2)}, u32[]{:S(2)}) async-start(bf16[8,64,256]{2,1,0:T(8,128)(2,1)} %shard_map.173), calls=%async_computation.1 | async-start | bytes 524288 | tf_op jit(solution)/shard_map/sum_low/all_to_all | solution.py:21
  52.4 24.9 %copy-start.12 = (pred[32,4]{0,1:T(4,128)(4,1)S(1)}, pred[32,4]{0,1:T(4,128)(4,1)}, u32[]{:S(2)}) copy-start(pred[32,4]{0,1:T(4,128)(4,1)} %constant.50) | copy-start | bytes 388
  61.7 1.0 copy-start.1
  62.6 14.2 %copy-start.2 = (bf16[2,1,1024,128]{3,2,1,0:T(8,128)(2,1)S(1)}, bf16[2,1,1024,128]{3,2,1,0:T(8,128)(2,1)}, u32[]{:S(2)}) copy-start(bf16[2,1,1024,128]{3,2,1,0:T(8,128)(2,1)} %param.29) | copy-start | bytes 1572868
  62.6 15.1 %copy-start.11 = (bf16[2,1,1024,128]{3,2,1,0:T(8,128)(2,1)S(1)}, bf16[2,1,1024,128]{3,2,1,0:T(8,128)(2,1)}, u32[]{:S(2)}) copy-start(bf16[2,1,1024,128]{3,2,1,0:T(8,128)(2,1)} %param.30) | copy-start | bytes 1572868
  65.0 11.6 %all-to-all-start.2 = ((bf16[8,8,1280]{2,1,0:T(8,128)(2,1)}), bf16[8,8,1280]{2,1,0:T(8,128)(2,1)S(1)}, u32[]{:S(2)}, u32[]{:S(2)}) async-start(bf16[8,8,1280]{2,1,0:T(8,128)(2,1)} %bitcast.8), calls=%async_computation.2 | async-start | bytes 327680 | tf_op jit(solution)/shard_map/sum_z/all_to_all | solution.py:21
  88.6 4.7 %copy-start.9 = (s32[128]{0:T(128)S(1)}, s32[128]{0:T(128)}, u32[]{:S(2)}) copy-start(s32[128]{0:T(128)} %param.31) | copy-start | bytes 1540
  88.6 4.8 %copy-start.8 = (s32[16,2]{0,1:T(2,128)S(1)}, s32[16,2]{0,1:T(2,128)}, u32[]{:S(2)}) copy-start(s32[16,2]{0,1:T(2,128)} %param.33) | copy-start | bytes 388
  89.7 13.9 %all-to-all-start.4 = ((bf16[8,64,1024]{2,1,0:T(8,128)(2,1)}), bf16[8,64,1024]{2,1,0:T(8,128)(2,1)S(1)}, u32[]{:S(2)}, u32[]{:S(2)}) async-start(bf16[8,64,1024]{2,1,0:T(8,128)(2,1)} %broadcast_in_dim.118), calls=%async_computation.4 | async-start | bytes 2097152 | tf_op jit(solution)/shard_map/gather_plane/all_to_all | solution.py:21
  103.6 0.9 copy-start.6
  104.4 1.0 copy-start.4
  105.4 23.8 %copy-start.3 = (bf16[4,128,128]{2,1,0:T(8,128)(2,1)S(1)}, bf16[4,128,128]{2,1,0:T(8,128)(2,1)}, u32[]{:S(2)}) copy-start(bf16[4,128,128]{2,1,0:T(8,128)(2,1)} %inputs_ref.1) | copy-start | bytes 393220

commit v13 on v12

--- a/solution.py
+++ b/solution.py
@@ -68,7 +68,9 @@
     held_key,
     held_value,
     gained_ref,
+    held_out,
     arrived,
+    left,
 ):
     steps, all_rows, width = inputs_ref.shape
     every_row = steps * all_rows
@@ -141,7 +143,7 @@
                 lane(rest) == 1, squares - squares_high, jnp.where(lane(rest) == 2, home, 0.0)
             ),
         )
-        out_ref[first : first + block, base_end : base_end + PADDED_WIDTH] = jnp.concatenate(
+        held_out[first : first + block, base_end : base_end + PADDED_WIDTH] = jnp.concatenate(
             [total, extra], axis=1
         ).astype(jnp.bfloat16)
 
@@ -152,9 +154,14 @@
     def _(index):
         rows = pl.ds(pl.multiple_of(index * block, block), block)
         gained = gained_ref[rows, :]
-        out_ref[rows, 0:query_width] = dot(gained, held_query[...]).astype(jnp.bfloat16)
-        out_ref[rows, query_width:key_end] = dot(gained, held_key[...]).astype(jnp.bfloat16)
-        out_ref[rows, key_end:base_end] = dot(gained, held_value[...]).astype(jnp.bfloat16)
+        held_out[rows, 0:query_width] = dot(gained, held_query[...]).astype(jnp.bfloat16)
+        held_out[rows, query_width:key_end] = dot(gained, held_key[...]).astype(jnp.bfloat16)
+        held_out[rows, key_end:base_end] = dot(gained, held_value[...]).astype(jnp.bfloat16)
+        pltpu.make_async_copy(held_out.at[rows], out_ref.at[rows], left.at[index]).start()
+
+    for index in range(every_row // block):
+        rows = pl.ds(index * block, block)
+        pltpu.make_async_copy(held_out.at[rows], out_ref.at[rows], left.at[index]).wait()
 
 
 def project(inputs, gain, w_query, w_key, w_value, adapter_in, tasks, moves, homes, own_rows):
@@ -166,10 +173,13 @@
         out_shape=jax.ShapeDtypeStruct((steps * all_rows, columns), jnp.bfloat16),
         in_specs=[pl.BlockSpec(memory_space=pltpu.VMEM)] * 4
         + [pl.BlockSpec(memory_space=pl.ANY)] * len(large),
+        out_specs=pl.BlockSpec(memory_space=pl.ANY),
         scratch_shapes=[pltpu.VMEM(array.shape, jnp.bfloat16) for array in large]
         + [
             pltpu.VMEM((steps * all_rows, width), jnp.bfloat16),
+            pltpu.VMEM((steps * all_rows, columns), jnp.bfloat16),
             pltpu.SemaphoreType.DMA((len(large),)),
+            pltpu.SemaphoreType.DMA((steps * all_rows // 128,)),
         ],
         cost_estimate=pl.CostEstimate(
             flops=2 * steps * all_rows * width * 3328, bytes_accessed=3_000_000, transcendentals=0
@@ -276,6 +286,25 @@
     )(low_parts, up_line, up_other, base)
 
 
+def repeat_kernel(rows_ref, out_ref):
+    rows = rows_ref[...]
+    for target in range(out_ref.shape[0]):
+        out_ref[target] = rows
+
+
+def repeat(rows, count):
+    return pl.pallas_call(
+        repeat_kernel,
+        out_shape=jax.ShapeDtypeStruct((count, *rows.shape), rows.dtype),
+        in_specs=[pl.BlockSpec(memory_space=pltpu.VMEM)],
+        out_specs=pl.BlockSpec(memory_space=pltpu.VMEM),
+        compiler_params=pltpu.CompilerParams(vmem_limit_bytes=16 * 1024 * 1024),
+        cost_estimate=pl.CostEstimate(
+            flops=0, bytes_accessed=2 * count * rows.size, transcendentals=0
+        ),
+    )(rows)
+
+
 def attend(queries, cache_keys, value_cache, fresh_keys, fresh_values, lengths, query_steps):
     scaling = 1.0 / math.sqrt(queries.shape[-1])
     old_scores = (
@@ -422,9 +451,7 @@
         ).reshape(depth * per_group, query_width)
     column, tasks, moves = lax.optimization_barrier((column, tasks, moves))
     with jax.named_scope("gather_plane"):
-        piece_rows = exchange(
-            jnp.broadcast_to(column[None], (planes, depth * per_group, query_width)), PLANE
-        ).reshape(every_row, query_width)
+        piece_rows = exchange(repeat(column, planes), PLANE).reshape(every_row, query_width)
 
     group_tasks = tasks.reshape(groups, own_rows)
     matched = moves[:, 1][None, :] == jnp.arange(groups, dtype=jnp.int32)[:, None]

time: 134 us -> 133 us (level)
  no operation moved by 1% of the time
where the time goes in v13:
time: 133 us
  blocking collectives  62.6 us (47%)
  starting transfers between devices  27 us (20%)
  waiting for transfers between devices  26 us (20%)
  Pallas kernels  9.25 us (7%)
  local copies, waits for them, and re-layouts  2.91 us (2%)
  matrix products  2.61 us (2%)
  other arithmetic  2.03 us (2%)
    all_to_all x4, waiting for transfers between devices, exchange(): return lax.all_to_all(blocks, axes, 0, 0, tiled=True)  26 us
    all_gather x1, blocking collectives, on_device(): up_line = lax.all_gather(up, 'x', axis=0)  25.8 us
    all_to_all x4, starting transfers between devices, exchange(): return lax.all_to_all(blocks, axes, 0, 0, tiled=True)  24.4 us
    all_gather x2, blocking collectives, on_device(): lax.all_gather(mine.astype(jnp.bfloat16), 'y_hi', axis=0, axis_index_grou...  12.8 us
    all_gather x1, blocking collectives, on_device(): pair = lax.all_gather(mixed, 'core', axis=0)  10.4 us
    all_to_all x1, blocking collectives, exchange(): return lax.all_to_all(blocks, axes, 0, 0, tiled=True)  10.3 us
    pallas_call x1, Pallas kernels, project(): pl.pallas_call(functools.partial(project_kernel, own_rows), out_shape=jax...  5.03 us
    all_gather x1, blocking collectives, on_device(): return lax.all_gather(finished, 'core', axis=0, tiled=True)  3.33 us
  transfers between devices with their start and end apart: 5, of which 3 were waited for; matrix products, arithmetic and copies ran while one was open for 1% of the time, Pallas kernels for 1%

profile of v13, /device:TPU:1, one launch (start us, length us, event | category | flops | bytes accessed | tf_op | source)
XLA Modules:
  0.0 132.8 jit_solution(11063361784629151226)
XLA Ops:
  0.0 5.0 %shard_map.172 = bf16[512,1536]{1,0:T(8,128)(2,1)} custom-call(f32[1,128]{1,0:T(1,128)} %bitcast.114, s32[1,128]{1,0:T(1,128)} %bitcast.113, s32[2,16]{1,0:T(2,128)} %bitcast.112, s32[1,8]{1,0:T(1,128)} %bitcast.115, bf16[4,128,128]{2,1,0:T(8,128)(2,1)} %inputs_ref.1, bf16[8,192,128]{2,1,0:T(8,128)(2,1)} %bitcast.97, bf16[128,1024]{1,0:T(8,128)(2,1)} %query_ref.1, ...), custom_call_target="tpu_custom_call" | custom-call | flops 436207616 | bytes 3000000 | tf_op jit(solution)/shard_map/pallas_call | solution.py:171
  5.1 6.0 %all-to-all-start = ((bf16[8,64,1536]{2,1,0:T(8,128)(2,1)}), bf16[8,64,1536]{2,1,0:T(8,128)(2,1)S(1)}, u32[]{:S(2)}, u32[]{:S(2)}) async-start(bf16[8,64,1536]{2,1,0:T(8,128)(2,1)} %bitcast.92), calls=%async_computation | async-start | bytes 3145728 | tf_op jit(solution)/shard_map/sum_plane/all_to_all | solution.py:21
  11.1 25.8 %all-gather = bf16[256,1280]{1,0:T(8,128)(2,1)S(1)} all-gather(bf16[64,1280]{1,0:T(8,128)(2,1)S(1)} %pad_maximum_fusion), channel_id=2, replica_groups=mesh['x'=4,'y_lo'=2,'z'=8,'y_hi'=4,'core'=2] {'x'}, dimensions={0}, use_global_device_ids=true | all-gather | bytes 819200 | tf_op jit(solution)/shard_map/up_x/all_gather | solution.py:402
  36.9 2.6 %collective-permute-start = (bf16[4,64,1280]{2,1,0:T(8,128)(2,1)S(1)}, bf16[4,64,1280]{2,1,0:T(8,128)(2,1)}, u32[]{:S(2)}, u32[]{:S(2)}) collective-permute-start(bf16[4,64,1280]{2,1,0:T(8,128)(2,1)S(1)} %bitcast.89), channel_id=1, source_target_pairs={{0,64},{64,0},{1,65},{65,1},{2,66},{66,2},{3,67},{67,3},{4,68},{68... | collective-permute-start | bytes 1966088 | tf_op jit(solution)/shard_map/up_y_lo/ppermute | solution.py:404
  39.7 0.8 shard_map.173
  40.5 11.5 %all-to-all-start.1 = ((bf16[8,64,256]{2,1,0:T(8,128)(2,1)}), bf16[8,64,256]{2,1,0:T(8,128)(2,1)S(1)}, u32[]{:S(2)}, u32[]{:S(2)}) async-start(bf16[8,64,256]{2,1,0:T(8,128)(2,1)} %shard_map.173), calls=%async_computation.1 | async-start | bytes 524288 | tf_op jit(solution)/shard_map/sum_low/all_to_all | solution.py:21
  52.1 0.9 convert_reduce_fusion.base_ref
  52.9 8.4 %all-to-all-done.1.low_ref = bf16[8,64,256]{2,1,0:T(8,128)(2,1)S(1)} async-done(((bf16[8,64,256]{2,1,0:T(8,128)(2,1)}), bf16[8,64,256]{2,1,0:T(8,128)(2,1)S(1)}, u32[]{:S(2)}, u32[]{:S(2)}) %all-to-all-start.1) | async-done | bytes 262176 | tf_op jit(solution)/shard_map/sum_low/all_to_all | solution.py:21
  61.3 1.0 copy-done.1
  62.3 2.4 %shard_map.174 = bf16[64,1280]{1,0:T(8,128)(2,1)} custom-call(bf16[8,64,256]{2,1,0:T(8,128)(2,1)S(1)} %all-to-all-done.1.low_ref, bf16[4,64,1280]{2,1,0:T(8,128)(2,1)S(1)} %bitcast.90, bf16[4,64,1280]{2,1,0:T(8,128)(2,1)} %collective-permute-done.other_ref, f32[64,1280]{1,0:T(8,128)S(1)} %copy-done.1), custom_call_target="tpu_custom_call" | custom-call | flops 83886080 | bytes 2000000 | tf_op jit(solution)/shard_map/pallas_call | solution.py:275
  64.6 3.4 %all-to-all-start.2 = ((bf16[8,8,1280]{2,1,0:T(8,128)(2,1)}), bf16[8,8,1280]{2,1,0:T(8,128)(2,1)S(1)}, u32[]{:S(2)}, u32[]{:S(2)}) async-start(bf16[8,8,1280]{2,1,0:T(8,128)(2,1)} %bitcast.8), calls=%async_computation.2 | async-start | bytes 327680 | tf_op jit(solution)/shard_map/sum_z/all_to_all | solution.py:21
  68.2 8.1 %all-to-all-done.2 = bf16[8,8,1280]{2,1,0:T(8,128)(2,1)S(1)} async-done(((bf16[8,8,1280]{2,1,0:T(8,128)(2,1)}), bf16[8,8,1280]{2,1,0:T(8,128)(2,1)S(1)}, u32[]{:S(2)}, u32[]{:S(2)}) %all-to-all-start.2) | async-done | bytes 163872 | tf_op jit(solution)/shard_map/sum_z/all_to_all | solution.py:21
  78.0 10.3 %all_to_all.25 = bf16[8,8,1024]{2,1,0:T(8,128)(2,1)S(1)} all-to-all(bf16[8,8,1024]{2,1,0:T(8,128)(2,1)S(1)} %broadcast_in_dim.111), channel_id=1, replica_groups=mesh['x'=4,'y_lo'=2,'z'=8,'y_hi'=4,'core'=2] {'z'}, dimensions={0} | all-to-all | bytes 262144 | tf_op jit(solution)/shard_map/gather_z/all_to_all | solution.py:21
  88.3 1.0 gather_plane.1
  89.3 3.6 %all-to-all-start.4 = ((bf16[8,64,1024]{2,1,0:T(8,128)(2,1)}), bf16[8,64,1024]{2,1,0:T(8,128)(2,1)S(1)}, u32[]{:S(2)}, u32[]{:S(2)}) async-start(bf16[8,64,1024]{2,1,0:T(8,128)(2,1)} %gather_plane.1), calls=%async_computation.4 | async-start | bytes 2097152 | tf_op jit(solution)/shard_map/gather_plane/all_to_all | solution.py:21
  93.6 9.6 %all-to-all-done.4 = bf16[8,64,1024]{2,1,0:T(8,128)(2,1)S(1)} async-done(((bf16[8,64,1024]{2,1,0:T(8,128)(2,1)}), bf16[8,64,1024]{2,1,0:T(8,128)(2,1)S(1)}, u32[]{:S(2)}, u32[]{:S(2)}) %all-to-all-start.4) | async-done | bytes 1048608 | tf_op jit(solution)/shard_map/gather_plane/all_to_all | solution.py:21
  103.2 0.7 fusion.39
  104.4 0.5 copy-done.4
  104.9 0.4 fusion.1
  105.4 10.4 %all-gather.1 = bf16[1024,128]{1,0:T(8,128)(2,1)S(1)} all-gather(bf16[512,128]{1,0:T(8,128)(2,1)S(1)} %fusion.1), channel_id=3, replica_groups=mesh['x'=4,'y_lo'=2,'z'=8,'y_hi'=4,'core'=2] {'core'}, dimensions={0}, use_global_device_ids=true | all-gather | bytes 393216 | tf_op jit(solution)/shard_map/sum_core/all_gather | solution.py:478
  116.0 6.8 %all_gather.27 = bf16[2,2,128,128]{3,2,1,0:T(8,128)(2,1)S(1)} all-gather(bf16[1,2,128,128]{3,2,1,0:T(8,128)(2,1)S(1)} %bitcast.100), channel_id=1, replica_groups={{0,2},{4,6},{1,3},{5,7},{8,10},{12,14},{9,11},{13,15},{16,18},{20,22},{..., dimensions={0}, use_global_device_ids=true | all-gather | bytes 196608 | tf_op jit(solution)/shard_map/sum_y_hi/all_gather | solution.py:486
  122.8 6.0 %all_gather.28 = bf16[2,2,128,128]{3,2,1,0:T(8,128)(2,1)S(1)} all-gather(bf16[1,2,128,128]{3,2,1,0:T(8,128)(2,1)S(1)} %add_convert_fusion), channel_id=1, replica_groups={{2,4},{6,0},{3,5},{7,1},{10,12},{14,8},{11,13},{15,9},{18,20},{22,16},{..., dimensions={0}, use_global_device_ids=true | all-gather | bytes 196608 | tf_op jit(solution)/shard_map/sum_y_hi/all_gather | solution.py:486
  128.8 3.3 %all_gather.29 = bf16[4,128,128]{2,1,0:T(8,128)(2,1)S(1)} all-gather(bf16[2,128,128]{2,1,0:T(8,128)(2,1)S(1)} %fusion.10), channel_id=1, replica_groups=mesh['x'=4,'y_lo'=2,'z'=8,'y_hi'=4,'core'=2] {'core'}, dimensions={0}, use_global_device_ids=true | all-gather | bytes 196608 | tf_op jit(solution)/shard_map/gather_core/all_gather | solution.py:493
  132.1 0.7 copy.78
  (69 shorter events, 3.4 us)
Async XLA Ops:
  0.0 103.2 %copy-start = (bf16[8,1024,64]{1,2,0:T(8,128)(2,1)S(1)}, bf16[8,1024,64]{1,2,0:T(8,128)(2,1)}, u32[]{:S(2)}) copy-start(bf16[8,1024,64]{1,2,0:T(8,128)(2,1)} %param.25) | copy-start | bytes 3145732
  5.0 6.0 %copy-start.7 = (bf16[1,64,2,128]{3,2,1,0:T(2,128)(2,1)S(1)}, bf16[1,64,2,128]{3,2,1,0:T(2,128)(2,1)}, u32[]{:S(2)}) copy-start(bf16[1,64,2,128]{3,2,1,0:T(2,128)(2,1)} %param.28) | copy-start | bytes 98308
  5.0 6.1 %copy-start.5 = (bf16[1,64,1024]{2,1,0:T(8,128)(2,1)S(1)}, bf16[1,64,1024]{2,1,0:T(8,128)(2,1)}, u32[]{:S(2)}) copy-start(bf16[1,64,1024]{2,1,0:T(8,128)(2,1)} %param.27) | copy-start | bytes 393220
  5.1 34.5 %copy-start.10 = (s32[2]{0:T(128)S(1)}, s32[2]{0:T(128)}, u32[]{:S(2)}) copy-start(s32[2]{0:T(128)} %param.34) | copy-start | bytes 28
  5.1 34.6 %all-to-all-start = ((bf16[8,64,1536]{2,1,0:T(8,128)(2,1)}), bf16[8,64,1536]{2,1,0:T(8,128)(2,1)S(1)}, u32[]{:S(2)}, u32[]{:S(2)}) async-start(bf16[8,64,1536]{2,1,0:T(8,128)(2,1)} %bitcast.92), calls=%async_computation | async-start | bytes 3145728 | tf_op jit(solution)/shard_map/sum_plane/all_to_all | solution.py:21
  36.9 16.0 %collective-permute-start = (bf16[4,64,1280]{2,1,0:T(8,128)(2,1)S(1)}, bf16[4,64,1280]{2,1,0:T(8,128)(2,1)}, u32[]{:S(2)}, u32[]{:S(2)}) collective-permute-start(bf16[4,64,1280]{2,1,0:T(8,128)(2,1)S(1)} %bitcast.89), channel_id=1, source_target_pairs={{0,64},{64,0},{1,65},{65,1},{2,66},{66,2},{3,67},{67,3},{4,68},{68... | collective-permute-start | bytes 1966088 | tf_op jit(solution)/shard_map/up_y_lo/ppermute | solution.py:404
  40.5 20.8 %all-to-all-start.1 = ((bf16[8,64,256]{2,1,0:T(8,128)(2,1)}), bf16[8,64,256]{2,1,0:T(8,128)(2,1)S(1)}, u32[]{:S(2)}, u32[]{:S(2)}) async-start(bf16[8,64,256]{2,1,0:T(8,128)(2,1)} %shard_map.173), calls=%async_computation.1 | async-start | bytes 524288 | tf_op jit(solution)/shard_map/sum_low/all_to_all | solution.py:21
  52.1 24.9 %copy-start.12 = (pred[32,4]{0,1:T(4,128)(4,1)S(1)}, pred[32,4]{0,1:T(4,128)(4,1)}, u32[]{:S(2)}) copy-start(pred[32,4]{0,1:T(4,128)(4,1)} %constant.50) | copy-start | bytes 388
  61.3 1.0 copy-start.1
  62.3 14.2 %copy-start.2 = (bf16[2,1,1024,128]{3,2,1,0:T(8,128)(2,1)S(1)}, bf16[2,1,1024,128]{3,2,1,0:T(8,128)(2,1)}, u32[]{:S(2)}) copy-start(bf16[2,1,1024,128]{3,2,1,0:T(8,128)(2,1)} %param.29) | copy-start | bytes 1572868
  62.3 15.1 %copy-start.11 = (bf16[2,1,1024,128]{3,2,1,0:T(8,128)(2,1)S(1)}, bf16[2,1,1024,128]{3,2,1,0:T(8,128)(2,1)}, u32[]{:S(2)}) copy-start(bf16[2,1,1024,128]{3,2,1,0:T(8,128)(2,1)} %param.30) | copy-start | bytes 1572868
  64.6 11.6 %all-to-all-start.2 = ((bf16[8,8,1280]{2,1,0:T(8,128)(2,1)}), bf16[8,8,1280]{2,1,0:T(8,128)(2,1)S(1)}, u32[]{:S(2)}, u32[]{:S(2)}) async-start(bf16[8,8,1280]{2,1,0:T(8,128)(2,1)} %bitcast.8), calls=%async_computation.2 | async-start | bytes 327680 | tf_op jit(solution)/shard_map/sum_z/all_to_all | solution.py:21
  88.3 4.6 %copy-start.9 = (s32[128]{0:T(128)S(1)}, s32[128]{0:T(128)}, u32[]{:S(2)}) copy-start(s32[128]{0:T(128)} %param.31) | copy-start | bytes 1540
  88.3 4.8 %copy-start.8 = (s32[16,2]{0,1:T(2,128)S(1)}, s32[16,2]{0,1:T(2,128)}, u32[]{:S(2)}) copy-start(s32[16,2]{0,1:T(2,128)} %param.33) | copy-start | bytes 388
  89.3 13.9 %all-to-all-start.4 = ((bf16[8,64,1024]{2,1,0:T(8,128)(2,1)}), bf16[8,64,1024]{2,1,0:T(8,128)(2,1)S(1)}, u32[]{:S(2)}, u32[]{:S(2)}) async-start(bf16[8,64,1024]{2,1,0:T(8,128)(2,1)} %gather_plane.1), calls=%async_computation.4 | async-start | bytes 2097152 | tf_op jit(solution)/shard_map/gather_plane/all_to_all | solution.py:21
  103.2 0.9 copy-start.6
  104.0 1.0 copy-start.4
  104.9 23.8 %copy-start.3 = (bf16[4,128,128]{2,1,0:T(8,128)(2,1)S(1)}, bf16[4,128,128]{2,1,0:T(8,128)(2,1)}, u32[]{:S(2)}) copy-start(bf16[4,128,128]{2,1,0:T(8,128)(2,1)} %inputs_ref.1) | copy-start | bytes 393220

commit v14 on v13

--- a/solution.py
+++ b/solution.py
@@ -48,6 +48,19 @@
     for copy in copies:
         copy.start()
     return copies
+
+
+def row_tasks(row, own_rows, per_group, tasks_ref, moves_ref):
+    group = row // per_group
+    tasks, moves = tasks_ref.shape[1], moves_ref.shape[1]
+    lane = lax.broadcasted_iota(jnp.int32, (row.shape[0], tasks), 1)
+    own = lane == group * own_rows + row % own_rows
+    task = jnp.sum(jnp.where(own, tasks_ref[...], 0), axis=1, keepdims=True)
+    here = moves_ref[1:2, :] == jnp.broadcast_to(group, (row.shape[0], moves))
+    moved = jnp.sum(jnp.where(here, 1, 0), axis=1, keepdims=True) > 0
+    chosen = jnp.sum(jnp.where(here, moves_ref[0:1, :], 0), axis=1, keepdims=True)
+    late = row % per_group >= per_group // 2
+    return jnp.where(jnp.logical_and(late, moved), chosen, task)
 
 
 def project_kernel(
@@ -111,13 +124,7 @@
         first = index * block
 
         row = first + lax.broadcasted_iota(jnp.int32, (block, 1), 0)
-        own = lane(all_rows) == row // per_group * own_rows + row % own_rows
-        task = jnp.sum(jnp.where(own, tasks_ref[...], 0), axis=1, keepdims=True)
-        here = moves_ref[1:2, :] == row // per_group
-        moved = jnp.sum(jnp.where(here, 1, 0), axis=1, keepdims=True) > 0
-        chosen = jnp.sum(jnp.where(here, moves_ref[0:1, :], 0), axis=1, keepdims=True)
-        late = row % per_group >= per_group // 2
-        task = jnp.where(jnp.logical_and(late, moved), chosen, task)
+        task = row_tasks(row, own_rows, per_group, tasks_ref, moves_ref)
         home = jnp.sum(
             jnp.where(lane(adapters) == task, homes_ref[...], 0), axis=1, keepdims=True
         ).astype(jnp.float32)
@@ -286,23 +293,79 @@
     )(low_parts, up_line, up_other, base)
 
 
-def repeat_kernel(rows_ref, out_ref):
-    rows = rows_ref[...]
-    for target in range(out_ref.shape[0]):
-        out_ref[target] = rows
-
-
-def repeat(rows, count):
+def output_kernel(
+    own_rows,
+    steps,
+    tasks_ref,
+    moves_ref,
+    rows_ref,
+    down_ref,
+    weight_ref,
+    up_ref,
+    out_ref,
+    held_weight,
+    held_up,
+    held_out,
+    arrived,
+):
+    copies = start_copies(((weight_ref, held_weight), (up_ref, held_up)), arrived)
+    every_row, _ = rows_ref.shape
+    adapters, rank, width = down_ref.shape
+    per_group = steps * own_rows
+    all_rows = every_row // steps
+    block = 128
+    down = down_ref[...].reshape(adapters * rank, width)
+    for first in range(0, every_row, block):
+        row = first + lax.broadcasted_iota(jnp.int32, (block, 1), 0)
+        task = row_tasks(row, own_rows, per_group, tasks_ref, moves_ref)
+        rows = rows_ref[first : first + block, :]
+        reduced = lax.dot_general(
+            rows, down, (((1,), (1,)), ((), ())), preferred_element_type=jnp.float32
+        )
+        owner = lax.broadcasted_iota(jnp.int32, reduced.shape, 1) // rank
+        reduced = jnp.where(owner == task, reduced, 0.0).astype(jnp.bfloat16)
+        if first == 0:
+            for copy in copies:
+                copy.wait()
+        total = dot(rows, held_weight[...]) + dot(
+            reduced, held_up[...].reshape(adapters * rank, out_ref.shape[1])
+        )
+        held_out[first : first + block, :] = total.astype(jnp.bfloat16)
+    for first in range(0, every_row, block):
+        row = first + lax.broadcasted_iota(jnp.int32, (block, 1), 0)
+        place = row % all_rows // own_rows * per_group + row // all_rows * own_rows + row % own_rows
+        lane = lax.broadcasted_iota(jnp.int32, (block, every_row), 1)
+        order = jnp.where(lane == place, 1.0, 0.0).astype(jnp.bfloat16)
+        out_ref[first : first + block, :] = dot(order, held_out[...]).astype(jnp.bfloat16)
+
+
+def output(rows, w_output, adapter_attn, adapter_out, tasks, moves, own_rows, steps):
+    every_row, width = rows.shape
+    columns = w_output.shape[1]
     return pl.pallas_call(
-        repeat_kernel,
-        out_shape=jax.ShapeDtypeStruct((count, *rows.shape), rows.dtype),
-        in_specs=[pl.BlockSpec(memory_space=pltpu.VMEM)],
+        functools.partial(output_kernel, own_rows, steps),
+        out_shape=jax.ShapeDtypeStruct((every_row, columns), jnp.bfloat16),
+        in_specs=[pl.BlockSpec(memory_space=pltpu.VMEM)] * 4
+        + [pl.BlockSpec(memory_space=pl.ANY)] * 2,
         out_specs=pl.BlockSpec(memory_space=pltpu.VMEM),
+        scratch_shapes=[
+            pltpu.VMEM(w_output.shape, jnp.bfloat16),
+            pltpu.VMEM(adapter_out.shape, jnp.bfloat16),
+            pltpu.VMEM((every_row, columns), jnp.bfloat16),
+            pltpu.SemaphoreType.DMA((2,)),
+        ],
         compiler_params=pltpu.CompilerParams(vmem_limit_bytes=16 * 1024 * 1024),
         cost_estimate=pl.CostEstimate(
-            flops=0, bytes_accessed=2 * count * rows.size, transcendentals=0
+            flops=2 * every_row * width * 640, bytes_accessed=3_000_000, transcendentals=0
         ),
-    )(rows)
+    )(
+        tasks[None, :],
+        moves.T,
+        rows,
+        jnp.swapaxes(adapter_attn, 1, 2),
+        w_output,
+        adapter_out,
+    )
 
 
 def attend(queries, cache_keys, value_cache, fresh_keys, fresh_values, lengths, query_steps):
@@ -449,48 +512,25 @@
         column = exchange(
             jnp.broadcast_to(attended[None], (depth, per_group, query_width)), "z"
         ).reshape(depth * per_group, query_width)
-    column, tasks, moves = lax.optimization_barrier((column, tasks, moves))
     with jax.named_scope("gather_plane"):
-        piece_rows = exchange(repeat(column, planes), PLANE).reshape(every_row, query_width)
-
-    group_tasks = tasks.reshape(groups, own_rows)
-    matched = moves[:, 1][None, :] == jnp.arange(groups, dtype=jnp.int32)[:, None]
-    moved = jnp.any(matched, axis=1)
-    chosen = jnp.sum(jnp.where(matched, moves[:, 0][None, :], 0), axis=1)
-    late = jnp.where(moved[:, None], chosen[:, None], group_tasks)
-    active = jnp.stack([group_tasks if s < steps // 2 else late for s in range(steps)], axis=1)
-    active = active.reshape(every_row)
-    marks = active[:, None] == jnp.arange(task_count, dtype=jnp.int32)[None, :]
-
-    every_reduced = jnp.einsum(
-        "rq,tqc->rtc", piece_rows, adapter_attn, preferred_element_type=jnp.float32
-    )
-    reduced = jnp.where(marks[:, :, None], every_reduced, 0).astype(jnp.bfloat16)
-    mixed = dot(piece_rows, w_output) + dot(
-        reduced.reshape(every_row, task_count * rank),
-        adapter_out.reshape(task_count * rank, width_part),
-    )
-    mixed = mixed.astype(jnp.bfloat16)
-    core = lax.axis_index("core")
-    cores = lax.axis_size("core")
-    half = steps // cores
+        piece_rows = exchange(
+            jnp.broadcast_to(column[None], (planes, depth * per_group, query_width)), PLANE
+        ).reshape(every_row, query_width)
+
+    mixed = output(
+        piece_rows, w_output, adapter_attn, adapter_out, tasks, moves, own_rows, steps
+    )
     with jax.named_scope("sum_core"):
-        pair = lax.all_gather(mixed, "core", axis=0)
-    mine = lax.dynamic_slice_in_dim(
-        pair.reshape(cores, groups, steps, own_rows, width_part), core * half, half, 2
-    ).astype(jnp.float32)
-    mine = jnp.sum(mine, axis=0)
-    mine = mine.transpose(1, 0, 2, 3).reshape(half, all_rows, width_part)
+        both = lax.all_gather(mixed, "core", axis=0)
+    total = both[0].astype(jnp.float32) + both[1].astype(jnp.float32)
     for pairs in ([[0, 1], [2, 3]], [[1, 2], [3, 0]]):
         with jax.named_scope("sum_y_hi"):
             both = lax.all_gather(
-                mine.astype(jnp.bfloat16), "y_hi", axis=0, axis_index_groups=pairs
+                total.astype(jnp.bfloat16), "y_hi", axis=0, axis_index_groups=pairs
             )
-        mine = both[0].astype(jnp.float32) + both[1].astype(jnp.float32)
-    residual = lax.dynamic_slice_in_dim(inputs, core * half, half, 0)
-    finished = (residual.astype(jnp.float32) + mine).astype(jnp.bfloat16)
-    with jax.named_scope("gather_core"):
-        return lax.all_gather(finished, "core", axis=0, tiled=True)
+        total = both[0].astype(jnp.float32) + both[1].astype(jnp.float32)
+    finished = inputs.astype(jnp.float32) + total.reshape(inputs.shape)
+    return finished.astype(jnp.bfloat16)
 
 
 def solution(mesh):

time: 133 us -> 134 us (level); the launches traced: 133 us -> 132 us
  blocking collectives: 62.6 us -> 76.7 us
  waiting for transfers between devices: 26 us -> 17.1 us
  starting transfers between devices: 27 us -> 23.5 us
  local copies, waits for them, and re-layouts: 2.91 us -> 0.36 us
  Pallas kernels: 9.25 us -> 11 us
  matrix products: 2.61 us -> 1.09 us
    all_to_all x1 -> x2, blocking collectives: 10.3 us -> 23.2 us  [exchange(): return lax.all_to_all(blocks, axes, 0, 0, tiled=True)]
    all_to_all x4 -> x3, waiting for transfers between devices: 26 us -> 17.1 us  [exchange(): return lax.all_to_all(blocks, axes, 0, 0, tiled=True)]
    all_to_all x4 -> x3, starting transfers between devices: 24.4 us -> 20.9 us  [exchange(): return lax.all_to_all(blocks, axes, 0, 0, tiled=True)]
    unnamed x30 -> x27, local copies, waits for them, and re-layouts: 2.32 us -> 0.08 us
    pallas_call x1, Pallas kernels: 1.05 us -> 2.89 us  [output(): pl.pallas_call(functools.partial(output_kernel, own_rows, steps), out_sha...]
    all_gather x4 -> x3, blocking collectives: 26.5 us -> 27.6 us  [the longest x2 16.7 us: on_device(): lax.all_gather(total.astype(jnp.bfloat16), 'y_hi', axis=0, axis_index_gro...]
  transfers between devices with their start and end apart: 5 -> 4, of which waited for: 3 -> 2; matrix products, arithmetic and copies ran while one was open for 1% -> 0% of each run, Pallas kernels for 1% -> 1%
where the time goes in v14:
time: 134 us; the launch traced here: 132 us
  blocking collectives  76.7 us (57%)
  starting transfers between devices  23.5 us (18%)
  waiting for transfers between devices  17.1 us (13%)
  Pallas kernels  11 us (8%)
  other arithmetic  1.62 us (1%)
    all_gather x1, blocking collectives, on_device(): up_line = lax.all_gather(up, 'x', axis=0)  25.8 us
    all_to_all x2, blocking collectives, exchange(): return lax.all_to_all(blocks, axes, 0, 0, tiled=True)  23.2 us
    all_to_all x3, starting transfers between devices, exchange(): return lax.all_to_all(blocks, axes, 0, 0, tiled=True)  20.9 us
    all_to_all x3, waiting for transfers between devices, exchange(): return lax.all_to_all(blocks, axes, 0, 0, tiled=True)  17.1 us
    all_gather x2, blocking collectives, on_device(): lax.all_gather(total.astype(jnp.bfloat16), 'y_hi', axis=0, axis_index_gro...  16.7 us
    all_gather x1, blocking collectives, on_device(): both = lax.all_gather(mixed, 'core', axis=0)  11 us
    pallas_call x1, Pallas kernels, project(): pl.pallas_call(functools.partial(project_kernel, own_rows), out_shape=jax...  4.99 us
    pallas_call x1, Pallas kernels, output(): pl.pallas_call(functools.partial(output_kernel, own_rows, steps), out_sha...  2.89 us
  transfers between devices with their start and end apart: 4, of which 2 were waited for; matrix products, arithmetic and copies ran while one was open for 0% of the time, Pallas kernels for 1%

profile of v14, /device:TPU:1, one launch (start us, length us, event | category | flops | bytes accessed | tf_op | source)
XLA Modules:
  0.0 131.6 jit_solution(7175141029124651624)
XLA Ops:
  0.0 5.0 %shard_map.172 = bf16[512,1536]{1,0:T(8,128)(2,1)} custom-call(f32[1,128]{1,0:T(1,128)} %bitcast.94, s32[1,128]{1,0:T(1,128)} %bitcast.76, s32[2,16]{1,0:T(2,128)} %bitcast.74, s32[1,8]{1,0:T(1,128)} %bitcast.95, bf16[4,128,128]{2,1,0:T(8,128)(2,1)} %inputs_ref.1, bf16[8,192,128]{2,1,0:T(8,128)(2,1)} %bitcast.81, bf16[128,1024]{1,0:T(8,128)(2,1)} %query_ref.1, ...), custom_call_target="tpu_custom_call" | custom-call | flops 436207616 | bytes 3000000 | tf_op jit(solution)/shard_map/pallas_call | solution.py:178
  5.0 6.0 %all-to-all-start = ((bf16[8,64,1536]{2,1,0:T(8,128)(2,1)}), bf16[8,64,1536]{2,1,0:T(8,128)(2,1)S(1)}, u32[]{:S(2)}, u32[]{:S(2)}) async-start(bf16[8,64,1536]{2,1,0:T(8,128)(2,1)} %bitcast.78), calls=%async_computation | async-start | bytes 3145728 | tf_op jit(solution)/shard_map/sum_plane/all_to_all | solution.py:21
  11.1 25.8 %all-gather = bf16[256,1280]{1,0:T(8,128)(2,1)S(1)} all-gather(bf16[64,1280]{1,0:T(8,128)(2,1)S(1)} %pad_maximum_fusion), channel_id=2, replica_groups=mesh['x'=4,'y_lo'=2,'z'=8,'y_hi'=4,'core'=2] {'x'}, dimensions={0}, use_global_device_ids=true | all-gather | bytes 819200 | tf_op jit(solution)/shard_map/up_x/all_gather | solution.py:465
  36.9 2.6 %collective-permute-start = (bf16[4,64,1280]{2,1,0:T(8,128)(2,1)S(1)}, bf16[4,64,1280]{2,1,0:T(8,128)(2,1)}, u32[]{:S(2)}, u32[]{:S(2)}) collective-permute-start(bf16[4,64,1280]{2,1,0:T(8,128)(2,1)S(1)} %bitcast.71), channel_id=1, source_target_pairs={{0,64},{64,0},{1,65},{65,1},{2,66},{66,2},{3,67},{67,3},{4,68},{68... | collective-permute-start | bytes 1966088 | tf_op jit(solution)/shard_map/up_y_lo/ppermute | solution.py:467
  39.6 0.8 shard_map.173
  40.5 11.5 %all-to-all-start.1 = ((bf16[8,64,256]{2,1,0:T(8,128)(2,1)}), bf16[8,64,256]{2,1,0:T(8,128)(2,1)S(1)}, u32[]{:S(2)}, u32[]{:S(2)}) async-start(bf16[8,64,256]{2,1,0:T(8,128)(2,1)} %shard_map.173), calls=%async_computation.1 | async-start | bytes 524288 | tf_op jit(solution)/shard_map/sum_low/all_to_all | solution.py:21
  52.0 0.2 convert_reduce_fusion.base_ref
  52.2 9.0 %all-to-all-done.1.low_ref = bf16[8,64,256]{2,1,0:T(8,128)(2,1)S(1)} async-done(((bf16[8,64,256]{2,1,0:T(8,128)(2,1)}), bf16[8,64,256]{2,1,0:T(8,128)(2,1)S(1)}, u32[]{:S(2)}, u32[]{:S(2)}) %all-to-all-start.1) | async-done | bytes 262176 | tf_op jit(solution)/shard_map/sum_low/all_to_all | solution.py:21
  61.3 2.3 %shard_map.174 = bf16[64,1280]{1,0:T(8,128)(2,1)} custom-call(bf16[8,64,256]{2,1,0:T(8,128)(2,1)S(1)} %all-to-all-done.1.low_ref, bf16[4,64,1280]{2,1,0:T(8,128)(2,1)S(1)} %bitcast.72, bf16[4,64,1280]{2,1,0:T(8,128)(2,1)} %collective-permute-done.other_ref, f32[64,1280]{1,0:T(8,128)S(1)} %convert_reduce_fusion.base_ref), custom_call_target="tpu_custom_call" | custom-call | flops 83886080 | bytes 2000000 | tf_op jit(solution)/shard_map/pallas_call | solution.py:282
  63.6 3.4 %all-to-all-start.2 = ((bf16[8,8,1280]{2,1,0:T(8,128)(2,1)}), bf16[8,8,1280]{2,1,0:T(8,128)(2,1)S(1)}, u32[]{:S(2)}, u32[]{:S(2)}) async-start(bf16[8,8,1280]{2,1,0:T(8,128)(2,1)} %bitcast.8), calls=%async_computation.2 | async-start | bytes 327680 | tf_op jit(solution)/shard_map/sum_z/all_to_all | solution.py:21
  67.1 8.1 %all-to-all-done.2 = bf16[8,8,1280]{2,1,0:T(8,128)(2,1)S(1)} async-done(((bf16[8,8,1280]{2,1,0:T(8,128)(2,1)}), bf16[8,8,1280]{2,1,0:T(8,128)(2,1)S(1)}, u32[]{:S(2)}, u32[]{:S(2)}) %all-to-all-start.2) | async-done | bytes 163872 | tf_op jit(solution)/shard_map/sum_z/all_to_all | solution.py:21
  75.4 0.4 fusion.32
  75.9 0.2 fusion.33
  76.1 0.2 fusion.6
  76.3 0.3 fusion.3
  76.6 0.2 fusion.1
  76.9 10.3 %all_to_all.25 = bf16[8,8,1024]{2,1,0:T(8,128)(2,1)S(1)} all-to-all(bf16[8,8,1024]{2,1,0:T(8,128)(2,1)S(1)} %broadcast_in_dim.72), channel_id=1, replica_groups=mesh['x'=4,'y_lo'=2,'z'=8,'y_hi'=4,'core'=2] {'z'}, dimensions={0} | all-to-all | bytes 262144 | tf_op jit(solution)/shard_map/gather_z/all_to_all | solution.py:21
  87.2 0.1 broadcast_in_dim.74
  87.3 12.9 %all_to_all.26 = bf16[8,64,1024]{2,1,0:T(8,128)(2,1)S(1)} all-to-all(bf16[8,64,1024]{2,1,0:T(8,128)(2,1)S(1)} %broadcast_in_dim.74), channel_id=1, replica_groups=mesh['x'=4,'y_lo'=2,'z'=8,'y_hi'=4,'core'=2] {'x','y_lo'}, dimensions={0} | all-to-all | bytes 2097152 | tf_op jit(solution)/shard_map/gather_plane/all_to_all | solution.py:21
  100.3 2.9 %shard_map.175 = bf16[512,128]{1,0:T(8,128)(2,1)S(1)} custom-call(s32[1,128]{1,0:T(1,128)S(1)} %bitcast.77, s32[2,16]{1,0:T(2,128)S(1)} %bitcast.75, bf16[512,1024]{1,0:T(8,128)(2,1)S(1)} %bitcast.70, bf16[8,64,1024]{2,1,0:T(8,128)(2,1)S(1)} %bitcast.73, bf16[1024,128]{1,0:T(8,128)(2,1)S(1)} %copy-done.2, bf16[8,64,128]{2,1,0:T(8,128)(2,1)S(1)} %copy-done.3), custom_call_target="tpu_custom_call" | custom-call | flops 671088640 | bytes 3000000 | tf_op jit(solution)/shard_map/pallas_call | solution.py:345
  103.2 11.0 %all-gather.1 = bf16[1024,128]{1,0:T(8,128)(2,1)S(1)} all-gather(bf16[512,128]{1,0:T(8,128)(2,1)S(1)} %shard_map.175), channel_id=3, replica_groups=mesh['x'=4,'y_lo'=2,'z'=8,'y_hi'=4,'core'=2] {'core'}, dimensions={0}, use_global_device_ids=true | all-gather | bytes 393216 | tf_op jit(solution)/shard_map/sum_core/all_gather | solution.py:524
  114.2 9.5 %all_gather.24 = bf16[2,512,128]{2,1,0:T(8,128)(2,1)S(1)} all-gather(bf16[1,512,128]{2,1,0:T(8,128)(2,1)S(1)} %fusion.7), channel_id=1, replica_groups={{0,2},{4,6},{1,3},{5,7},{8,10},{12,14},{9,11},{13,15},{16,18},{20,22},{..., dimensions={0}, use_global_device_ids=true | all-gather | bytes 393216 | tf_op jit(solution)/shard_map/sum_y_hi/all_gather | solution.py:528
  123.8 7.1 %all_gather.25 = bf16[2,512,128]{2,1,0:T(8,128)(2,1)S(1)} all-gather(bf16[1,512,128]{2,1,0:T(8,128)(2,1)S(1)} %add_convert_fusion.2), channel_id=1, replica_groups={{2,4},{6,0},{3,5},{7,1},{10,12},{14,8},{11,13},{15,9},{18,20},{22,16},{..., dimensions={0}, use_global_device_ids=true | all-gather | bytes 393216 | tf_op jit(solution)/shard_map/sum_y_hi/all_gather | solution.py:528
  131.0 0.7 add_convert_fusion.1
  (53 shorter events, 0.8 us)
Async XLA Ops:
  0.0 75.4 %copy-start = (bf16[2,1,1024,128]{3,2,1,0:T(8,128)(2,1)S(1)}, bf16[2,1,1024,128]{3,2,1,0:T(8,128)(2,1)}, u32[]{:S(2)}) copy-start(bf16[2,1,1024,128]{3,2,1,0:T(8,128)(2,1)} %param.29) | copy-start | bytes 1572868
  5.0 6.0 %copy-start.8 = (bf16[1,64,2,128]{3,2,1,0:T(2,128)(2,1)S(1)}, bf16[1,64,2,128]{3,2,1,0:T(2,128)(2,1)}, u32[]{:S(2)}) copy-start(bf16[1,64,2,128]{3,2,1,0:T(2,128)(2,1)} %param.28) | copy-start | bytes 98308
  5.0 6.1 %copy-start.7 = (bf16[1,64,1024]{2,1,0:T(8,128)(2,1)S(1)}, bf16[1,64,1024]{2,1,0:T(8,128)(2,1)}, u32[]{:S(2)}) copy-start(bf16[1,64,1024]{2,1,0:T(8,128)(2,1)} %param.27) | copy-start | bytes 393220
  5.0 34.5 %copy-start.9 = (s32[2]{0:T(128)S(1)}, s32[2]{0:T(128)}, u32[]{:S(2)}) copy-start(s32[2]{0:T(128)} %param.34) | copy-start | bytes 28
  5.0 34.6 %all-to-all-start = ((bf16[8,64,1536]{2,1,0:T(8,128)(2,1)}), bf16[8,64,1536]{2,1,0:T(8,128)(2,1)S(1)}, u32[]{:S(2)}, u32[]{:S(2)}) async-start(bf16[8,64,1536]{2,1,0:T(8,128)(2,1)} %bitcast.78), calls=%async_computation | async-start | bytes 3145728 | tf_op jit(solution)/shard_map/sum_plane/all_to_all | solution.py:21
  36.9 15.3 %collective-permute-start = (bf16[4,64,1280]{2,1,0:T(8,128)(2,1)S(1)}, bf16[4,64,1280]{2,1,0:T(8,128)(2,1)}, u32[]{:S(2)}, u32[]{:S(2)}) collective-permute-start(bf16[4,64,1280]{2,1,0:T(8,128)(2,1)S(1)} %bitcast.71), channel_id=1, source_target_pairs={{0,64},{64,0},{1,65},{65,1},{2,66},{66,2},{3,67},{67,3},{4,68},{68... | collective-permute-start | bytes 1966088 | tf_op jit(solution)/shard_map/up_y_lo/ppermute | solution.py:467
  40.5 20.8 %all-to-all-start.1 = ((bf16[8,64,256]{2,1,0:T(8,128)(2,1)}), bf16[8,64,256]{2,1,0:T(8,128)(2,1)S(1)}, u32[]{:S(2)}, u32[]{:S(2)}) async-start(bf16[8,64,256]{2,1,0:T(8,128)(2,1)} %shard_map.173), calls=%async_computation.1 | async-start | bytes 524288 | tf_op jit(solution)/shard_map/sum_low/all_to_all | solution.py:21
  52.2 23.6 %copy-start.11 = (pred[32,4]{0,1:T(4,128)(4,1)S(1)}, pred[32,4]{0,1:T(4,128)(4,1)}, u32[]{:S(2)}) copy-start(pred[32,4]{0,1:T(4,128)(4,1)} %constant.37) | copy-start | bytes 388
  52.2 24.1 %copy-start.10 = (bf16[2,1,1024,128]{3,2,1,0:T(8,128)(2,1)S(1)}, bf16[2,1,1024,128]{3,2,1,0:T(8,128)(2,1)}, u32[]{:S(2)}) copy-start(bf16[2,1,1024,128]{3,2,1,0:T(8,128)(2,1)} %param.30) | copy-start | bytes 1572868
  63.6 11.6 %all-to-all-start.2 = ((bf16[8,8,1280]{2,1,0:T(8,128)(2,1)}), bf16[8,8,1280]{2,1,0:T(8,128)(2,1)S(1)}, u32[]{:S(2)}, u32[]{:S(2)}) async-start(bf16[8,8,1280]{2,1,0:T(8,128)(2,1)} %bitcast.8), calls=%async_computation.2 | async-start | bytes 327680 | tf_op jit(solution)/shard_map/sum_z/all_to_all | solution.py:21
  87.2 13.1 %copy-start.1 = (bf16[8,1024,64]{1,2,0:T(8,128)(2,1)S(1)}, bf16[8,1024,64]{1,2,0:T(8,128)(2,1)}, u32[]{:S(2)}) copy-start(bf16[8,1024,64]{1,2,0:T(8,128)(2,1)} %param.25) | copy-start | bytes 3145732
  87.2 13.1 %copy-start.2 = (bf16[1024,128]{1,0:T(8,128)(2,1)S(1)}, bf16[1024,128]{1,0:T(8,128)(2,1)}, u32[]{:S(2)}) copy-start(bf16[1024,128]{1,0:T(8,128)(2,1)} %weight_ref.1) | copy-start | bytes 786436
  87.2 13.1 %copy-start.3 = (bf16[8,64,128]{2,1,0:T(8,128)(2,1)S(1)}, bf16[8,64,128]{2,1,0:T(8,128)(2,1)}, u32[]{:S(2)}) copy-start(bf16[8,64,128]{2,1,0:T(8,128)(2,1)} %up_ref.1) | copy-start | bytes 393220
  87.2 13.1 %copy-start.4 = (s32[16,2]{0,1:T(2,128)S(1)}, s32[16,2]{0,1:T(2,128)}, u32[]{:S(2)}) copy-start(s32[16,2]{0,1:T(2,128)} %param.33) | copy-start | bytes 388
  87.2 13.1 %copy-start.5 = (s32[128]{0:T(128)S(1)}, s32[128]{0:T(128)}, u32[]{:S(2)}) copy-start(s32[128]{0:T(128)} %param.31) | copy-start | bytes 1540
  103.2 27.8 %copy-start.6 = (bf16[4,128,128]{2,1,0:T(8,128)(2,1)S(1)}, bf16[4,128,128]{2,1,0:T(8,128)(2,1)}, u32[]{:S(2)}) copy-start(bf16[4,128,128]{2,1,0:T(8,128)(2,1)} %inputs_ref.1) | copy-start | bytes 393220

commit v15 on v14

--- a/solution.py
+++ b/solution.py
@@ -313,7 +313,7 @@
     adapters, rank, width = down_ref.shape
     per_group = steps * own_rows
     all_rows = every_row // steps
-    block = 128
+    block = 256
     down = down_ref[...].reshape(adapters * rank, width)
     for first in range(0, every_row, block):
         row = first + lax.broadcasted_iota(jnp.int32, (block, 1), 0)
@@ -473,6 +473,7 @@
     raw_part = lift(
         low_parts, plane_sum, up_line, up_other, rank, head_dim, model_width, groups
     )
+    raw_part, first_core = lax.optimization_barrier((raw_part, lax.axis_index("core") == 0))
     with jax.named_scope("sum_z"):
         by_depth = exchange(raw_part.reshape(depth, per_group, base_end), "z")
     raw = jnp.sum(by_depth.astype(jnp.float32), axis=0)
@@ -522,6 +523,8 @@
     )
     with jax.named_scope("sum_core"):
         both = lax.all_gather(mixed, "core", axis=0)
+    half = every_row // 2
+    both = jnp.where(first_core, both[:, :half], both[:, half:])
     total = both[0].astype(jnp.float32) + both[1].astype(jnp.float32)
     for pairs in ([[0, 1], [2, 3]], [[1, 2], [3, 0]]):
         with jax.named_scope("sum_y_hi"):
@@ -529,8 +532,12 @@
                 total.astype(jnp.bfloat16), "y_hi", axis=0, axis_index_groups=pairs
             )
         total = both[0].astype(jnp.float32) + both[1].astype(jnp.float32)
-    finished = inputs.astype(jnp.float32) + total.reshape(inputs.shape)
-    return finished.astype(jnp.bfloat16)
+    total, residual = lax.optimization_barrier((total, inputs.reshape(every_row, width_part)))
+    residual = jnp.where(first_core, residual[:half], residual[half:])
+    finished = (residual.astype(jnp.float32) + total).astype(jnp.bfloat16)
+    with jax.named_scope("gather_core"):
+        finished = lax.all_gather(finished, "core", axis=0, tiled=True)
+    return finished.reshape(inputs.shape)
 
 
 def solution(mesh):

time: 134 us -> 131 us (0.978); the launches traced: 132 us -> 130 us
    all_gather x2, blocking collectives: 16.7 us -> 12.7 us  [on_device(): lax.all_gather(total.astype(jnp.bfloat16), 'y_hi', axis=0, axis_index_gro...]
    all_gather x0 -> x1, blocking collectives: none -> 3.36 us  [on_device(): finished = lax.all_gather(finished, 'core', axis=0, tiled=True)]
where the time goes in v15:
time: 131 us; the launch traced here: 130 us
  blocking collectives  76.1 us (58%)
  starting transfers between devices  23.5 us (18%)
  waiting for transfers between devices  17.1 us (13%)
  Pallas kernels  10 us (8%)
    all_gather x1, blocking collectives, on_device(): up_line = lax.all_gather(up, 'x', axis=0)  25.8 us
    all_to_all x2, blocking collectives, exchange(): return lax.all_to_all(blocks, axes, 0, 0, tiled=True)  23.2 us
    all_to_all x3, starting transfers between devices, exchange(): return lax.all_to_all(blocks, axes, 0, 0, tiled=True)  20.9 us
    all_to_all x3, waiting for transfers between devices, exchange(): return lax.all_to_all(blocks, axes, 0, 0, tiled=True)  17.1 us
    all_gather x2, blocking collectives, on_device(): lax.all_gather(total.astype(jnp.bfloat16), 'y_hi', axis=0, axis_index_gro...  12.7 us
    all_gather x1, blocking collectives, on_device(): both = lax.all_gather(mixed, 'core', axis=0)  11 us
    pallas_call x1, Pallas kernels, project(): pl.pallas_call(functools.partial(project_kernel, own_rows), out_shape=jax...  4.99 us
    all_gather x1, blocking collectives, on_device(): finished = lax.all_gather(finished, 'core', axis=0, tiled=True)  3.36 us
  transfers between devices with their start and end apart: 4, of which 2 were waited for; matrix products, arithmetic and copies ran while one was open for 0% of the time, Pallas kernels for 1%

profile of v15, /device:TPU:1, one launch (start us, length us, event | category | flops | bytes accessed | tf_op | source)
XLA Modules:
  0.0 130.1 jit_solution(3463308840690245051)
XLA Ops:
  0.0 5.0 %shard_map.172 = bf16[512,1536]{1,0:T(8,128)(2,1)} custom-call(f32[1,128]{1,0:T(1,128)} %bitcast.98, s32[1,128]{1,0:T(1,128)} %bitcast.78, s32[2,16]{1,0:T(2,128)} %bitcast.76, s32[1,8]{1,0:T(1,128)} %bitcast.99, bf16[4,128,128]{2,1,0:T(8,128)(2,1)} %inputs_ref.1, bf16[8,192,128]{2,1,0:T(8,128)(2,1)} %bitcast.85, bf16[128,1024]{1,0:T(8,128)(2,1)} %query_ref.1, ...), custom_call_target="tpu_custom_call" | custom-call | flops 436207616 | bytes 3000000 | tf_op jit(solution)/shard_map/pallas_call | solution.py:178
  5.0 6.0 %all-to-all-start = ((bf16[8,64,1536]{2,1,0:T(8,128)(2,1)}), bf16[8,64,1536]{2,1,0:T(8,128)(2,1)S(1)}, u32[]{:S(2)}, u32[]{:S(2)}) async-start(bf16[8,64,1536]{2,1,0:T(8,128)(2,1)} %bitcast.80), calls=%async_computation | async-start | bytes 3145728 | tf_op jit(solution)/shard_map/sum_plane/all_to_all | solution.py:21
  11.1 25.8 %all-gather = bf16[256,1280]{1,0:T(8,128)(2,1)S(1)} all-gather(bf16[64,1280]{1,0:T(8,128)(2,1)S(1)} %pad_maximum_fusion), channel_id=2, replica_groups=mesh['x'=4,'y_lo'=2,'z'=8,'y_hi'=4,'core'=2] {'x'}, dimensions={0}, use_global_device_ids=true | all-gather | bytes 819200 | tf_op jit(solution)/shard_map/up_x/all_gather | solution.py:465
  36.9 2.6 %collective-permute-start = (bf16[4,64,1280]{2,1,0:T(8,128)(2,1)S(1)}, bf16[4,64,1280]{2,1,0:T(8,128)(2,1)}, u32[]{:S(2)}, u32[]{:S(2)}) collective-permute-start(bf16[4,64,1280]{2,1,0:T(8,128)(2,1)S(1)} %bitcast.73), channel_id=1, source_target_pairs={{0,64},{64,0},{1,65},{65,1},{2,66},{66,2},{3,67},{67,3},{4,68},{68... | collective-permute-start | bytes 1966088 | tf_op jit(solution)/shard_map/up_y_lo/ppermute | solution.py:467
  39.6 0.8 shard_map.173
  40.5 11.5 %all-to-all-start.1 = ((bf16[8,64,256]{2,1,0:T(8,128)(2,1)}), bf16[8,64,256]{2,1,0:T(8,128)(2,1)S(1)}, u32[]{:S(2)}, u32[]{:S(2)}) async-start(bf16[8,64,256]{2,1,0:T(8,128)(2,1)} %shard_map.173), calls=%async_computation.1 | async-start | bytes 524288 | tf_op jit(solution)/shard_map/sum_low/all_to_all | solution.py:21
  52.0 0.2 convert_reduce_fusion.base_ref
  52.2 9.0 %all-to-all-done.1.low_ref = bf16[8,64,256]{2,1,0:T(8,128)(2,1)S(1)} async-done(((bf16[8,64,256]{2,1,0:T(8,128)(2,1)}), bf16[8,64,256]{2,1,0:T(8,128)(2,1)S(1)}, u32[]{:S(2)}, u32[]{:S(2)}) %all-to-all-start.1) | async-done | bytes 262176 | tf_op jit(solution)/shard_map/sum_low/all_to_all | solution.py:21
  61.3 2.3 %shard_map.174 = bf16[64,1280]{1,0:T(8,128)(2,1)} custom-call(bf16[8,64,256]{2,1,0:T(8,128)(2,1)S(1)} %all-to-all-done.1.low_ref, bf16[4,64,1280]{2,1,0:T(8,128)(2,1)S(1)} %bitcast.74, bf16[4,64,1280]{2,1,0:T(8,128)(2,1)} %collective-permute-done.other_ref, f32[64,1280]{1,0:T(8,128)S(1)} %convert_reduce_fusion.base_ref), custom_call_target="tpu_custom_call" | custom-call | flops 83886080 | bytes 2000000 | tf_op jit(solution)/shard_map/pallas_call | solution.py:282
  63.6 3.4 %all-to-all-start.2 = ((bf16[8,8,1280]{2,1,0:T(8,128)(2,1)}), bf16[8,8,1280]{2,1,0:T(8,128)(2,1)S(1)}, u32[]{:S(2)}, u32[]{:S(2)}) async-start(bf16[8,8,1280]{2,1,0:T(8,128)(2,1)} %bitcast.8), calls=%async_computation.2 | async-start | bytes 327680 | tf_op jit(solution)/shard_map/sum_z/all_to_all | solution.py:21
  67.1 8.1 %all-to-all-done.2 = bf16[8,8,1280]{2,1,0:T(8,128)(2,1)S(1)} async-done(((bf16[8,8,1280]{2,1,0:T(8,128)(2,1)}), bf16[8,8,1280]{2,1,0:T(8,128)(2,1)S(1)}, u32[]{:S(2)}, u32[]{:S(2)}) %all-to-all-start.2) | async-done | bytes 163872 | tf_op jit(solution)/shard_map/sum_z/all_to_all | solution.py:21
  75.4 0.4 fusion.31
  75.9 0.2 fusion.32
  76.1 0.2 fusion.6
  76.3 0.3 fusion.3
  76.6 0.2 fusion.1
  76.9 10.3 %all_to_all.25 = bf16[8,8,1024]{2,1,0:T(8,128)(2,1)S(1)} all-to-all(bf16[8,8,1024]{2,1,0:T(8,128)(2,1)S(1)} %broadcast_in_dim.72), channel_id=1, replica_groups=mesh['x'=4,'y_lo'=2,'z'=8,'y_hi'=4,'core'=2] {'z'}, dimensions={0} | all-to-all | bytes 262144 | tf_op jit(solution)/shard_map/gather_z/all_to_all | solution.py:21
  87.3 12.9 %all_to_all.26 = bf16[8,64,1024]{2,1,0:T(8,128)(2,1)S(1)} all-to-all(bf16[8,64,1024]{2,1,0:T(8,128)(2,1)S(1)} %broadcast_in_dim.74), channel_id=1, replica_groups=mesh['x'=4,'y_lo'=2,'z'=8,'y_hi'=4,'core'=2] {'x','y_lo'}, dimensions={0} | all-to-all | bytes 2097152 | tf_op jit(solution)/shard_map/gather_plane/all_to_all | solution.py:21
  100.3 1.9 %shard_map.175 = bf16[512,128]{1,0:T(8,128)(2,1)S(1)} custom-call(s32[1,128]{1,0:T(1,128)S(1)} %bitcast.79, s32[2,16]{1,0:T(2,128)S(1)} %bitcast.77, bf16[512,1024]{1,0:T(8,128)(2,1)S(1)} %bitcast.72, bf16[8,64,1024]{2,1,0:T(8,128)(2,1)S(1)} %bitcast.75, bf16[1024,128]{1,0:T(8,128)(2,1)S(1)} %copy-done.2, bf16[8,64,128]{2,1,0:T(8,128)(2,1)S(1)} %copy-done.3), custom_call_target="tpu_custom_call" | custom-call | flops 671088640 | bytes 3000000 | tf_op jit(solution)/shard_map/pallas_call | solution.py:345
  102.2 11.0 %all-gather.1 = bf16[1024,128]{1,0:T(8,128)(2,1)S(1)} all-gather(bf16[512,128]{1,0:T(8,128)(2,1)S(1)} %shard_map.175), channel_id=3, replica_groups=mesh['x'=4,'y_lo'=2,'z'=8,'y_hi'=4,'core'=2] {'core'}, dimensions={0}, use_global_device_ids=true | all-gather | bytes 393216 | tf_op jit(solution)/shard_map/sum_core/all_gather | solution.py:525
  113.3 6.7 %all_gather.27 = bf16[2,256,128]{2,1,0:T(8,128)(2,1)S(1)} all-gather(bf16[1,256,128]{2,1,0:T(8,128)(2,1)S(1)} %add_convert_fusion.2), channel_id=1, replica_groups={{0,2},{4,6},{1,3},{5,7},{8,10},{12,14},{9,11},{13,15},{16,18},{20,22},{..., dimensions={0}, use_global_device_ids=true | all-gather | bytes 196608 | tf_op jit(solution)/shard_map/sum_y_hi/all_gather | solution.py:531
  120.0 6.0 %all_gather.28 = bf16[2,256,128]{2,1,0:T(8,128)(2,1)S(1)} all-gather(bf16[1,256,128]{2,1,0:T(8,128)(2,1)S(1)} %add_convert_fusion.1), channel_id=1, replica_groups={{2,4},{6,0},{3,5},{7,1},{10,12},{14,8},{11,13},{15,9},{18,20},{22,16},{..., dimensions={0}, use_global_device_ids=true | all-gather | bytes 196608 | tf_op jit(solution)/shard_map/sum_y_hi/all_gather | solution.py:531
  126.1 3.4 %all_gather.29 = bf16[512,128]{1,0:T(8,128)(2,1)S(1)} all-gather(bf16[256,128]{1,0:T(8,128)(2,1)S(1)} %add_convert_fusion), channel_id=1, replica_groups=mesh['x'=4,'y_lo'=2,'z'=8,'y_hi'=4,'core'=2] {'core'}, dimensions={0}, use_global_device_ids=true | all-gather | bytes 196608 | tf_op jit(solution)/shard_map/gather_core/all_gather | solution.py:539
  129.4 0.7 copy.54
  (56 shorter events, 0.9 us)
Async XLA Ops:
  0.0 75.4 %copy-start = (bf16[2,1,1024,128]{3,2,1,0:T(8,128)(2,1)S(1)}, bf16[2,1,1024,128]{3,2,1,0:T(8,128)(2,1)}, u32[]{:S(2)}) copy-start(bf16[2,1,1024,128]{3,2,1,0:T(8,128)(2,1)} %param.29) | copy-start | bytes 1572868
  5.0 6.0 %copy-start.8 = (bf16[1,64,2,128]{3,2,1,0:T(2,128)(2,1)S(1)}, bf16[1,64,2,128]{3,2,1,0:T(2,128)(2,1)}, u32[]{:S(2)}) copy-start(bf16[1,64,2,128]{3,2,1,0:T(2,128)(2,1)} %param.28) | copy-start | bytes 98308
  5.0 6.1 %copy-start.7 = (bf16[1,64,1024]{2,1,0:T(8,128)(2,1)S(1)}, bf16[1,64,1024]{2,1,0:T(8,128)(2,1)}, u32[]{:S(2)}) copy-start(bf16[1,64,1024]{2,1,0:T(8,128)(2,1)} %param.27) | copy-start | bytes 393220
  5.0 34.5 %copy-start.9 = (s32[2]{0:T(128)S(1)}, s32[2]{0:T(128)}, u32[]{:S(2)}) copy-start(s32[2]{0:T(128)} %param.34) | copy-start | bytes 28
  5.0 34.6 %all-to-all-start = ((bf16[8,64,1536]{2,1,0:T(8,128)(2,1)}), bf16[8,64,1536]{2,1,0:T(8,128)(2,1)S(1)}, u32[]{:S(2)}, u32[]{:S(2)}) async-start(bf16[8,64,1536]{2,1,0:T(8,128)(2,1)} %bitcast.80), calls=%async_computation | async-start | bytes 3145728 | tf_op jit(solution)/shard_map/sum_plane/all_to_all | solution.py:21
  36.9 15.3 %collective-permute-start = (bf16[4,64,1280]{2,1,0:T(8,128)(2,1)S(1)}, bf16[4,64,1280]{2,1,0:T(8,128)(2,1)}, u32[]{:S(2)}, u32[]{:S(2)}) collective-permute-start(bf16[4,64,1280]{2,1,0:T(8,128)(2,1)S(1)} %bitcast.73), channel_id=1, source_target_pairs={{0,64},{64,0},{1,65},{65,1},{2,66},{66,2},{3,67},{67,3},{4,68},{68... | collective-permute-start | bytes 1966088 | tf_op jit(solution)/shard_map/up_y_lo/ppermute | solution.py:467
  40.5 20.8 %all-to-all-start.1 = ((bf16[8,64,256]{2,1,0:T(8,128)(2,1)}), bf16[8,64,256]{2,1,0:T(8,128)(2,1)S(1)}, u32[]{:S(2)}, u32[]{:S(2)}) async-start(bf16[8,64,256]{2,1,0:T(8,128)(2,1)} %shard_map.173), calls=%async_computation.1 | async-start | bytes 524288 | tf_op jit(solution)/shard_map/sum_low/all_to_all | solution.py:21
  52.2 23.6 %copy-start.11 = (pred[32,4]{0,1:T(4,128)(4,1)S(1)}, pred[32,4]{0,1:T(4,128)(4,1)}, u32[]{:S(2)}) copy-start(pred[32,4]{0,1:T(4,128)(4,1)} %constant.42) | copy-start | bytes 388
  52.2 24.1 %copy-start.10 = (bf16[2,1,1024,128]{3,2,1,0:T(8,128)(2,1)S(1)}, bf16[2,1,1024,128]{3,2,1,0:T(8,128)(2,1)}, u32[]{:S(2)}) copy-start(bf16[2,1,1024,128]{3,2,1,0:T(8,128)(2,1)} %param.30) | copy-start | bytes 1572868
  63.6 11.6 %all-to-all-start.2 = ((bf16[8,8,1280]{2,1,0:T(8,128)(2,1)}), bf16[8,8,1280]{2,1,0:T(8,128)(2,1)S(1)}, u32[]{:S(2)}, u32[]{:S(2)}) async-start(bf16[8,8,1280]{2,1,0:T(8,128)(2,1)} %bitcast.8), calls=%async_computation.2 | async-start | bytes 327680 | tf_op jit(solution)/shard_map/sum_z/all_to_all | solution.py:21
  87.2 13.1 %copy-start.1 = (bf16[8,1024,64]{1,2,0:T(8,128)(2,1)S(1)}, bf16[8,1024,64]{1,2,0:T(8,128)(2,1)}, u32[]{:S(2)}) copy-start(bf16[8,1024,64]{1,2,0:T(8,128)(2,1)} %param.25) | copy-start | bytes 3145732
  87.2 13.1 %copy-start.2 = (bf16[1024,128]{1,0:T(8,128)(2,1)S(1)}, bf16[1024,128]{1,0:T(8,128)(2,1)}, u32[]{:S(2)}) copy-start(bf16[1024,128]{1,0:T(8,128)(2,1)} %weight_ref.1) | copy-start | bytes 786436
  87.2 13.1 %copy-start.3 = (bf16[8,64,128]{2,1,0:T(8,128)(2,1)S(1)}, bf16[8,64,128]{2,1,0:T(8,128)(2,1)}, u32[]{:S(2)}) copy-start(bf16[8,64,128]{2,1,0:T(8,128)(2,1)} %up_ref.1) | copy-start | bytes 393220
  87.2 13.1 %copy-start.4 = (s32[16,2]{0,1:T(2,128)S(1)}, s32[16,2]{0,1:T(2,128)}, u32[]{:S(2)}) copy-start(s32[16,2]{0,1:T(2,128)} %param.33) | copy-start | bytes 388
  87.2 13.1 %copy-start.5 = (s32[128]{0:T(128)S(1)}, s32[128]{0:T(128)}, u32[]{:S(2)}) copy-start(s32[128]{0:T(128)} %param.31) | copy-start | bytes 1540
  102.2 23.8 %copy-start.6 = (bf16[4,128,128]{2,1,0:T(8,128)(2,1)S(1)}, bf16[4,128,128]{2,1,0:T(8,128)(2,1)}, u32[]{:S(2)}) copy-start(bf16[4,128,128]{2,1,0:T(8,128)(2,1)} %inputs_ref.1) | copy-start | bytes 393220

commit v16 on v15

--- a/solution.py
+++ b/solution.py
@@ -93,7 +93,7 @@
     adapters, low, _ = adapter_ref.shape
     key_end = query_width + head_dim
     base_end = key_end + head_dim
-    block = 128
+    block = 256
     copies = start_copies(
         (
             (inputs_ref, held_inputs),
@@ -186,7 +186,7 @@
             pltpu.VMEM((steps * all_rows, width), jnp.bfloat16),
             pltpu.VMEM((steps * all_rows, columns), jnp.bfloat16),
             pltpu.SemaphoreType.DMA((len(large),)),
-            pltpu.SemaphoreType.DMA((steps * all_rows // 128,)),
+            pltpu.SemaphoreType.DMA((steps * all_rows // 256,)),
         ],
         cost_estimate=pl.CostEstimate(
             flops=2 * steps * all_rows * width * 3328, bytes_accessed=3_000_000, transcendentals=0

time: 131 us -> 130 us (level)
  no operation moved by 1% of the time
where the time goes in v16:
time: 130 us
  blocking collectives  76.1 us (59%)
  starting transfers between devices  23.5 us (18%)
  waiting for transfers between devices  17.1 us (13%)
  Pallas kernels  9.61 us (7%)
    all_gather x1, blocking collectives, on_device(): up_line = lax.all_gather(up, 'x', axis=0)  25.8 us
    all_to_all x2, blocking collectives, exchange(): return lax.all_to_all(blocks, axes, 0, 0, tiled=True)  23.2 us
    all_to_all x3, starting transfers between devices, exchange(): return lax.all_to_all(blocks, axes, 0, 0, tiled=True)  20.9 us
    all_to_all x3, waiting for transfers between devices, exchange(): return lax.all_to_all(blocks, axes, 0, 0, tiled=True)  17.1 us
    all_gather x2, blocking collectives, on_device(): lax.all_gather(total.astype(jnp.bfloat16), 'y_hi', axis=0, axis_index_gro...  12.7 us
    all_gather x1, blocking collectives, on_device(): both = lax.all_gather(mixed, 'core', axis=0)  11 us
    pallas_call x1, Pallas kernels, project(): pl.pallas_call(functools.partial(project_kernel, own_rows), out_shape=jax...  4.56 us
    all_gather x1, blocking collectives, on_device(): finished = lax.all_gather(finished, 'core', axis=0, tiled=True)  3.35 us
  transfers between devices with their start and end apart: 4, of which 2 were waited for; matrix products, arithmetic and copies ran while one was open for 0% of the time, Pallas kernels for 1%

profile of v16, /device:TPU:1, one launch (start us, length us, event | category | flops | bytes accessed | tf_op | source)
XLA Modules:
  0.0 129.7 jit_solution(5181187147789210924)
XLA Ops:
  0.0 4.6 %shard_map.172 = bf16[512,1536]{1,0:T(8,128)(2,1)} custom-call(f32[1,128]{1,0:T(1,128)} %bitcast.98, s32[1,128]{1,0:T(1,128)} %bitcast.78, s32[2,16]{1,0:T(2,128)} %bitcast.76, s32[1,8]{1,0:T(1,128)} %bitcast.99, bf16[4,128,128]{2,1,0:T(8,128)(2,1)} %inputs_ref.1, bf16[8,192,128]{2,1,0:T(8,128)(2,1)} %bitcast.85, bf16[128,1024]{1,0:T(8,128)(2,1)} %query_ref.1, ...), custom_call_target="tpu_custom_call" | custom-call | flops 436207616 | bytes 3000000 | tf_op jit(solution)/shard_map/pallas_call | solution.py:178
  4.6 6.0 %all-to-all-start = ((bf16[8,64,1536]{2,1,0:T(8,128)(2,1)}), bf16[8,64,1536]{2,1,0:T(8,128)(2,1)S(1)}, u32[]{:S(2)}, u32[]{:S(2)}) async-start(bf16[8,64,1536]{2,1,0:T(8,128)(2,1)} %bitcast.80), calls=%async_computation | async-start | bytes 3145728 | tf_op jit(solution)/shard_map/sum_plane/all_to_all | solution.py:21
  10.7 25.8 %all-gather = bf16[256,1280]{1,0:T(8,128)(2,1)S(1)} all-gather(bf16[64,1280]{1,0:T(8,128)(2,1)S(1)} %pad_maximum_fusion), channel_id=2, replica_groups=mesh['x'=4,'y_lo'=2,'z'=8,'y_hi'=4,'core'=2] {'x'}, dimensions={0}, use_global_device_ids=true | all-gather | bytes 819200 | tf_op jit(solution)/shard_map/up_x/all_gather | solution.py:465
  36.5 2.6 %collective-permute-start = (bf16[4,64,1280]{2,1,0:T(8,128)(2,1)S(1)}, bf16[4,64,1280]{2,1,0:T(8,128)(2,1)}, u32[]{:S(2)}, u32[]{:S(2)}) collective-permute-start(bf16[4,64,1280]{2,1,0:T(8,128)(2,1)S(1)} %bitcast.73), channel_id=1, source_target_pairs={{0,64},{64,0},{1,65},{65,1},{2,66},{66,2},{3,67},{67,3},{4,68},{68... | collective-permute-start | bytes 1966088 | tf_op jit(solution)/shard_map/up_y_lo/ppermute | solution.py:467
  39.2 0.8 shard_map.173
  40.0 11.5 %all-to-all-start.1 = ((bf16[8,64,256]{2,1,0:T(8,128)(2,1)}), bf16[8,64,256]{2,1,0:T(8,128)(2,1)S(1)}, u32[]{:S(2)}, u32[]{:S(2)}) async-start(bf16[8,64,256]{2,1,0:T(8,128)(2,1)} %shard_map.173), calls=%async_computation.1 | async-start | bytes 524288 | tf_op jit(solution)/shard_map/sum_low/all_to_all | solution.py:21
  51.6 0.2 convert_reduce_fusion.base_ref
  51.8 9.0 %all-to-all-done.1.low_ref = bf16[8,64,256]{2,1,0:T(8,128)(2,1)S(1)} async-done(((bf16[8,64,256]{2,1,0:T(8,128)(2,1)}), bf16[8,64,256]{2,1,0:T(8,128)(2,1)S(1)}, u32[]{:S(2)}, u32[]{:S(2)}) %all-to-all-start.1) | async-done | bytes 262176 | tf_op jit(solution)/shard_map/sum_low/all_to_all | solution.py:21
  60.8 2.3 %shard_map.174 = bf16[64,1280]{1,0:T(8,128)(2,1)} custom-call(bf16[8,64,256]{2,1,0:T(8,128)(2,1)S(1)} %all-to-all-done.1.low_ref, bf16[4,64,1280]{2,1,0:T(8,128)(2,1)S(1)} %bitcast.74, bf16[4,64,1280]{2,1,0:T(8,128)(2,1)} %collective-permute-done.other_ref, f32[64,1280]{1,0:T(8,128)S(1)} %convert_reduce_fusion.base_ref), custom_call_target="tpu_custom_call" | custom-call | flops 83886080 | bytes 2000000 | tf_op jit(solution)/shard_map/pallas_call | solution.py:282
  63.1 3.4 %all-to-all-start.2 = ((bf16[8,8,1280]{2,1,0:T(8,128)(2,1)}), bf16[8,8,1280]{2,1,0:T(8,128)(2,1)S(1)}, u32[]{:S(2)}, u32[]{:S(2)}) async-start(bf16[8,8,1280]{2,1,0:T(8,128)(2,1)} %bitcast.8), calls=%async_computation.2 | async-start | bytes 327680 | tf_op jit(solution)/shard_map/sum_z/all_to_all | solution.py:21
  66.6 8.1 %all-to-all-done.2 = bf16[8,8,1280]{2,1,0:T(8,128)(2,1)S(1)} async-done(((bf16[8,8,1280]{2,1,0:T(8,128)(2,1)}), bf16[8,8,1280]{2,1,0:T(8,128)(2,1)S(1)}, u32[]{:S(2)}, u32[]{:S(2)}) %all-to-all-start.2) | async-done | bytes 163872 | tf_op jit(solution)/shard_map/sum_z/all_to_all | solution.py:21
  75.0 0.4 fusion.31
  75.4 0.2 fusion.32
  75.7 0.2 fusion.6
  75.9 0.3 fusion.3
  76.2 0.2 fusion.1
  76.5 10.3 %all_to_all.25 = bf16[8,8,1024]{2,1,0:T(8,128)(2,1)S(1)} all-to-all(bf16[8,8,1024]{2,1,0:T(8,128)(2,1)S(1)} %broadcast_in_dim.72), channel_id=1, replica_groups=mesh['x'=4,'y_lo'=2,'z'=8,'y_hi'=4,'core'=2] {'z'}, dimensions={0} | all-to-all | bytes 262144 | tf_op jit(solution)/shard_map/gather_z/all_to_all | solution.py:21
  86.9 12.9 %all_to_all.26 = bf16[8,64,1024]{2,1,0:T(8,128)(2,1)S(1)} all-to-all(bf16[8,64,1024]{2,1,0:T(8,128)(2,1)S(1)} %broadcast_in_dim.74), channel_id=1, replica_groups=mesh['x'=4,'y_lo'=2,'z'=8,'y_hi'=4,'core'=2] {'x','y_lo'}, dimensions={0} | all-to-all | bytes 2097152 | tf_op jit(solution)/shard_map/gather_plane/all_to_all | solution.py:21
  99.8 1.9 %shard_map.175 = bf16[512,128]{1,0:T(8,128)(2,1)S(1)} custom-call(s32[1,128]{1,0:T(1,128)S(1)} %bitcast.79, s32[2,16]{1,0:T(2,128)S(1)} %bitcast.77, bf16[512,1024]{1,0:T(8,128)(2,1)S(1)} %bitcast.72, bf16[8,64,1024]{2,1,0:T(8,128)(2,1)S(1)} %bitcast.75, bf16[1024,128]{1,0:T(8,128)(2,1)S(1)} %copy-done.2, bf16[8,64,128]{2,1,0:T(8,128)(2,1)S(1)} %copy-done.3), custom_call_target="tpu_custom_call" | custom-call | flops 671088640 | bytes 3000000 | tf_op jit(solution)/shard_map/pallas_call | solution.py:345
  101.8 11.0 %all-gather.1 = bf16[1024,128]{1,0:T(8,128)(2,1)S(1)} all-gather(bf16[512,128]{1,0:T(8,128)(2,1)S(1)} %shard_map.175), channel_id=3, replica_groups=mesh['x'=4,'y_lo'=2,'z'=8,'y_hi'=4,'core'=2] {'core'}, dimensions={0}, use_global_device_ids=true | all-gather | bytes 393216 | tf_op jit(solution)/shard_map/sum_core/all_gather | solution.py:525
  112.8 6.7 %all_gather.27 = bf16[2,256,128]{2,1,0:T(8,128)(2,1)S(1)} all-gather(bf16[1,256,128]{2,1,0:T(8,128)(2,1)S(1)} %add_convert_fusion.2), channel_id=1, replica_groups={{0,2},{4,6},{1,3},{5,7},{8,10},{12,14},{9,11},{13,15},{16,18},{20,22},{..., dimensions={0}, use_global_device_ids=true | all-gather | bytes 196608 | tf_op jit(solution)/shard_map/sum_y_hi/all_gather | solution.py:531
  119.6 6.0 %all_gather.28 = bf16[2,256,128]{2,1,0:T(8,128)(2,1)S(1)} all-gather(bf16[1,256,128]{2,1,0:T(8,128)(2,1)S(1)} %add_convert_fusion.1), channel_id=1, replica_groups={{2,4},{6,0},{3,5},{7,1},{10,12},{14,8},{11,13},{15,9},{18,20},{22,16},{..., dimensions={0}, use_global_device_ids=true | all-gather | bytes 196608 | tf_op jit(solution)/shard_map/sum_y_hi/all_gather | solution.py:531
  125.7 3.4 %all_gather.29 = bf16[512,128]{1,0:T(8,128)(2,1)S(1)} all-gather(bf16[256,128]{1,0:T(8,128)(2,1)S(1)} %add_convert_fusion), channel_id=1, replica_groups=mesh['x'=4,'y_lo'=2,'z'=8,'y_hi'=4,'core'=2] {'core'}, dimensions={0}, use_global_device_ids=true | all-gather | bytes 196608 | tf_op jit(solution)/shard_map/gather_core/all_gather | solution.py:539
  129.0 0.7 copy.54
  (56 shorter events, 0.9 us)
Async XLA Ops:
  0.0 75.0 %copy-start = (bf16[2,1,1024,128]{3,2,1,0:T(8,128)(2,1)S(1)}, bf16[2,1,1024,128]{3,2,1,0:T(8,128)(2,1)}, u32[]{:S(2)}) copy-start(bf16[2,1,1024,128]{3,2,1,0:T(8,128)(2,1)} %param.29) | copy-start | bytes 1572868
  4.6 6.0 %copy-start.8 = (bf16[1,64,2,128]{3,2,1,0:T(2,128)(2,1)S(1)}, bf16[1,64,2,128]{3,2,1,0:T(2,128)(2,1)}, u32[]{:S(2)}) copy-start(bf16[1,64,2,128]{3,2,1,0:T(2,128)(2,1)} %param.28) | copy-start | bytes 98308
  4.6 6.1 %copy-start.7 = (bf16[1,64,1024]{2,1,0:T(8,128)(2,1)S(1)}, bf16[1,64,1024]{2,1,0:T(8,128)(2,1)}, u32[]{:S(2)}) copy-start(bf16[1,64,1024]{2,1,0:T(8,128)(2,1)} %param.27) | copy-start | bytes 393220
  4.6 34.5 %copy-start.9 = (s32[2]{0:T(128)S(1)}, s32[2]{0:T(128)}, u32[]{:S(2)}) copy-start(s32[2]{0:T(128)} %param.34) | copy-start | bytes 28
  4.6 34.6 %all-to-all-start = ((bf16[8,64,1536]{2,1,0:T(8,128)(2,1)}), bf16[8,64,1536]{2,1,0:T(8,128)(2,1)S(1)}, u32[]{:S(2)}, u32[]{:S(2)}) async-start(bf16[8,64,1536]{2,1,0:T(8,128)(2,1)} %bitcast.80), calls=%async_computation | async-start | bytes 3145728 | tf_op jit(solution)/shard_map/sum_plane/all_to_all | solution.py:21
  36.5 15.3 %collective-permute-start = (bf16[4,64,1280]{2,1,0:T(8,128)(2,1)S(1)}, bf16[4,64,1280]{2,1,0:T(8,128)(2,1)}, u32[]{:S(2)}, u32[]{:S(2)}) collective-permute-start(bf16[4,64,1280]{2,1,0:T(8,128)(2,1)S(1)} %bitcast.73), channel_id=1, source_target_pairs={{0,64},{64,0},{1,65},{65,1},{2,66},{66,2},{3,67},{67,3},{4,68},{68... | collective-permute-start | bytes 1966088 | tf_op jit(solution)/shard_map/up_y_lo/ppermute | solution.py:467
  40.0 20.8 %all-to-all-start.1 = ((bf16[8,64,256]{2,1,0:T(8,128)(2,1)}), bf16[8,64,256]{2,1,0:T(8,128)(2,1)S(1)}, u32[]{:S(2)}, u32[]{:S(2)}) async-start(bf16[8,64,256]{2,1,0:T(8,128)(2,1)} %shard_map.173), calls=%async_computation.1 | async-start | bytes 524288 | tf_op jit(solution)/shard_map/sum_low/all_to_all | solution.py:21
  51.8 23.6 %copy-start.11 = (pred[32,4]{0,1:T(4,128)(4,1)S(1)}, pred[32,4]{0,1:T(4,128)(4,1)}, u32[]{:S(2)}) copy-start(pred[32,4]{0,1:T(4,128)(4,1)} %constant.42) | copy-start | bytes 388
  51.8 24.1 %copy-start.10 = (bf16[2,1,1024,128]{3,2,1,0:T(8,128)(2,1)S(1)}, bf16[2,1,1024,128]{3,2,1,0:T(8,128)(2,1)}, u32[]{:S(2)}) copy-start(bf16[2,1,1024,128]{3,2,1,0:T(8,128)(2,1)} %param.30) | copy-start | bytes 1572868
  63.1 11.6 %all-to-all-start.2 = ((bf16[8,8,1280]{2,1,0:T(8,128)(2,1)}), bf16[8,8,1280]{2,1,0:T(8,128)(2,1)S(1)}, u32[]{:S(2)}, u32[]{:S(2)}) async-start(bf16[8,8,1280]{2,1,0:T(8,128)(2,1)} %bitcast.8), calls=%async_computation.2 | async-start | bytes 327680 | tf_op jit(solution)/shard_map/sum_z/all_to_all | solution.py:21
  86.8 13.1 %copy-start.1 = (bf16[8,1024,64]{1,2,0:T(8,128)(2,1)S(1)}, bf16[8,1024,64]{1,2,0:T(8,128)(2,1)}, u32[]{:S(2)}) copy-start(bf16[8,1024,64]{1,2,0:T(8,128)(2,1)} %param.25) | copy-start | bytes 3145732
  86.8 13.1 %copy-start.2 = (bf16[1024,128]{1,0:T(8,128)(2,1)S(1)}, bf16[1024,128]{1,0:T(8,128)(2,1)}, u32[]{:S(2)}) copy-start(bf16[1024,128]{1,0:T(8,128)(2,1)} %weight_ref.1) | copy-start | bytes 786436
  86.8 13.1 %copy-start.3 = (bf16[8,64,128]{2,1,0:T(8,128)(2,1)S(1)}, bf16[8,64,128]{2,1,0:T(8,128)(2,1)}, u32[]{:S(2)}) copy-start(bf16[8,64,128]{2,1,0:T(8,128)(2,1)} %up_ref.1) | copy-start | bytes 393220
  86.8 13.1 %copy-start.4 = (s32[16,2]{0,1:T(2,128)S(1)}, s32[16,2]{0,1:T(2,128)}, u32[]{:S(2)}) copy-start(s32[16,2]{0,1:T(2,128)} %param.33) | copy-start | bytes 388
  86.8 13.1 %copy-start.5 = (s32[128]{0:T(128)S(1)}, s32[128]{0:T(128)}, u32[]{:S(2)}) copy-start(s32[128]{0:T(128)} %param.31) | copy-start | bytes 1540
  101.8 23.8 %copy-start.6 = (bf16[4,128,128]{2,1,0:T(8,128)(2,1)S(1)}, bf16[4,128,128]{2,1,0:T(8,128)(2,1)}, u32[]{:S(2)}) copy-start(bf16[4,128,128]{2,1,0:T(8,128)(2,1)} %inputs_ref.1) | copy-start | bytes 393220

commit v17 on v16

--- a/solution.py
+++ b/solution.py
@@ -21,14 +21,18 @@
     return lax.all_to_all(blocks, axes, 0, 0, tiled=True)
 
 
-def apply_rotary(vectors, token_positions):
+def rotary_tables(token_positions, width):
+    half_width = width // 2
+    frequency = jnp.exp(
+        -jnp.log(500000.0) * jnp.arange(half_width, dtype=jnp.float32) * (2.0 / width)
+    )
+    angles = token_positions.astype(jnp.float32)[:, None] * frequency[None, :]
+    return jnp.cos(angles), jnp.sin(angles)
+
+
+def apply_rotary(vectors, cosine, sine_part):
     half_width = vectors.shape[-1] // 2
-    frequency = jnp.exp(
-        -jnp.log(500000.0) * jnp.arange(half_width, dtype=jnp.float32) * (2.0 / vectors.shape[-1])
-    )
-    angles = token_positions.astype(jnp.float32)[:, None] * frequency[None, :]
-    cosine = jnp.cos(angles)[:, None, :]
-    sine_part = jnp.sin(angles)[:, None, :]
+    cosine, sine_part = cosine[:, None, :], sine_part[:, None, :]
     leading = vectors[..., :half_width]
     trailing = vectors[..., half_width:]
     return jnp.concatenate(
@@ -368,7 +372,7 @@
     )
 
 
-def attend(queries, cache_keys, value_cache, fresh_keys, fresh_values, lengths, query_steps):
+def attend(queries, cache_keys, value_cache, fresh_keys, fresh_values, visible, query_steps):
     scaling = 1.0 / math.sqrt(queries.shape[-1])
     old_scores = (
         jnp.einsum("rnd,rjd->rnj", queries, cache_keys, preferred_element_type=jnp.float32)
@@ -378,8 +382,7 @@
         jnp.einsum("rnd,rjd->rnj", queries, fresh_keys, preferred_element_type=jnp.float32)
         * scaling
     )
-    visible = jnp.arange(cache_keys.shape[1])[None, None, :] < lengths[:, None, None]
-    old_scores = jnp.where(visible, old_scores, -1e30)
+    old_scores = jnp.where(visible[:, None, :], old_scores, -1e30)
     fresh = np.arange(fresh_keys.shape[1])[None, None, :] <= query_steps[None, :, None]
     new_scores = jnp.where(fresh, new_scores, -1e30)
     highest = jnp.maximum(jnp.max(old_scores, axis=-1), jnp.max(new_scores, axis=-1))[..., None]
@@ -465,6 +468,7 @@
         up_line = lax.all_gather(up, "x", axis=0)
     with jax.named_scope("up_y_lo"):
         up_other = lax.ppermute(up_line, "y_lo", [(0, 1), (1, 0)])
+    by_plane, lengths = lax.optimization_barrier((by_plane, lengths))
     low_part = sum_low(by_plane, base_end, 3 * rank, depth)
     plane_sum = jnp.sum(by_plane[:, :, :base_end].astype(jnp.float32), axis=0)
     with jax.named_scope("sum_low"):
@@ -473,16 +477,21 @@
     raw_part = lift(
         low_parts, plane_sum, up_line, up_other, rank, head_dim, model_width, groups
     )
-    raw_part, first_core = lax.optimization_barrier((raw_part, lax.axis_index("core") == 0))
+    positions = jnp.tile(lengths, steps) + jnp.arange(per_group) // own_rows
+    cosine, sine_part = rotary_tables(positions, head_dim)
+    visible = jnp.arange(cache_keys.shape[2])[None, :] < lengths[:, None]
+    raw_part, cosine, sine_part, visible, first_core = lax.optimization_barrier(
+        (raw_part, cosine, sine_part, visible, lax.axis_index("core") == 0)
+    )
     with jax.named_scope("sum_z"):
         by_depth = exchange(raw_part.reshape(depth, per_group, base_end), "z")
     raw = jnp.sum(by_depth.astype(jnp.float32), axis=0)
 
-    row_step = jnp.arange(per_group) // own_rows
-    positions = jnp.tile(lengths, steps) + row_step
-    queries = apply_rotary(raw[:, :query_width].reshape(per_group, heads, head_dim), positions)
+    queries = apply_rotary(
+        raw[:, :query_width].reshape(per_group, heads, head_dim), cosine, sine_part
+    )
     new_keys = apply_rotary(
-        raw[:, query_width:key_end].reshape(per_group, 1, head_dim), positions
+        raw[:, query_width:key_end].reshape(per_group, 1, head_dim), cosine, sine_part
     )
     raw_value = raw[:, key_end:]
 
@@ -500,7 +509,7 @@
         value_cache.reshape(own_rows, -1, head_dim),
         by_row(new_keys),
         by_row(raw_value),
-        lengths,
+        visible,
         np.arange(steps * heads) // heads,
     )
     attended = (

time: 130 us -> 129 us (level)
  blocking collectives: 76.1 us -> 86.7 us
  waiting for transfers between devices: 17.1 us -> 8.95 us
  starting transfers between devices: 23.5 us -> 20.1 us
    all_to_all x2 -> x3, blocking collectives: 23.2 us -> 34.3 us  [exchange(): return lax.all_to_all(blocks, axes, 0, 0, tiled=True)]
    all_to_all x3 -> x2, waiting for transfers between devices: 17.1 us -> 8.94 us  [exchange(): return lax.all_to_all(blocks, axes, 0, 0, tiled=True)]
    all_to_all x3 -> x2, starting transfers between devices: 20.9 us -> 17.5 us  [exchange(): return lax.all_to_all(blocks, axes, 0, 0, tiled=True)]
  transfers between devices with their start and end apart: 4 -> 3, of which waited for: 2 -> 1; matrix products, arithmetic and copies ran while one was open for 0% -> 0% of each run, Pallas kernels for 1% -> 1%
where the time goes in v17:
time: 129 us; the launch traced here: 128 us
  blocking collectives  86.7 us (67%)
  starting transfers between devices  20.1 us (16%)
  waiting for transfers between devices  8.95 us (7%)
  Pallas kernels  8.93 us (7%)
    all_to_all x3, blocking collectives, exchange(): return lax.all_to_all(blocks, axes, 0, 0, tiled=True)  34.3 us
    all_gather x1, blocking collectives, on_device(): up_line = lax.all_gather(up, 'x', axis=0)  25.8 us
    all_to_all x2, starting transfers between devices, exchange(): return lax.all_to_all(blocks, axes, 0, 0, tiled=True)  17.5 us
    all_gather x2, blocking collectives, on_device(): lax.all_gather(total.astype(jnp.bfloat16), 'y_hi', axis=0, axis_index_gro...  12.7 us
    all_gather x1, blocking collectives, on_device(): both = lax.all_gather(mixed, 'core', axis=0)  10.6 us
    all_to_all x2, waiting for transfers between devices, exchange(): return lax.all_to_all(blocks, axes, 0, 0, tiled=True)  8.94 us
    pallas_call x1, Pallas kernels, project(): pl.pallas_call(functools.partial(project_kernel, own_rows), out_shape=jax...  4.57 us
    all_gather x1, blocking collectives, on_device(): finished = lax.all_gather(finished, 'core', axis=0, tiled=True)  3.37 us
  transfers between devices with their start and end apart: 3, of which 1 were waited for; matrix products, arithmetic and copies ran while one was open for 0% of the time, Pallas kernels for 1%

profile of v17, /device:TPU:1, one launch (start us, length us, event | category | flops | bytes accessed | tf_op | source)
XLA Modules:
  0.0 128.1 jit_solution(16422318318479012429)
XLA Ops:
  0.0 4.6 %shard_map.172 = bf16[512,1536]{1,0:T(8,128)(2,1)} custom-call(f32[1,128]{1,0:T(1,128)} %bitcast.117, s32[1,128]{1,0:T(1,128)} %bitcast.97, s32[2,16]{1,0:T(2,128)} %bitcast.95, s32[1,8]{1,0:T(1,128)} %bitcast.118, bf16[4,128,128]{2,1,0:T(8,128)(2,1)} %inputs_ref.1, bf16[8,192,128]{2,1,0:T(8,128)(2,1)} %bitcast.104, bf16[128,1024]{1,0:T(8,128)(2,1)} %query_ref.1, ...), custom_call_target="tpu_custom_call" | custom-call | flops 436207616 | bytes 3000000 | tf_op jit(solution)/shard_map/pallas_call | solution.py:182
  4.6 6.0 %all-to-all-start = ((bf16[8,64,1536]{2,1,0:T(8,128)(2,1)}), bf16[8,64,1536]{2,1,0:T(8,128)(2,1)S(1)}, u32[]{:S(2)}, u32[]{:S(2)}) async-start(bf16[8,64,1536]{2,1,0:T(8,128)(2,1)} %bitcast.99), calls=%async_computation | async-start | bytes 3145728 | tf_op jit(solution)/shard_map/sum_plane/all_to_all | solution.py:21
  10.7 25.8 %all-gather = bf16[256,1280]{1,0:T(8,128)(2,1)S(1)} all-gather(bf16[64,1280]{1,0:T(8,128)(2,1)S(1)} %pad_maximum_fusion), channel_id=2, replica_groups=mesh['x'=4,'y_lo'=2,'z'=8,'y_hi'=4,'core'=2] {'x'}, dimensions={0}, use_global_device_ids=true | all-gather | bytes 819200 | tf_op jit(solution)/shard_map/up_x/all_gather | solution.py:468
  36.5 2.6 %collective-permute-start = (bf16[4,64,1280]{2,1,0:T(8,128)(2,1)S(1)}, bf16[4,64,1280]{2,1,0:T(8,128)(2,1)}, u32[]{:S(2)}, u32[]{:S(2)}) collective-permute-start(bf16[4,64,1280]{2,1,0:T(8,128)(2,1)S(1)} %bitcast.91), channel_id=1, source_target_pairs={{0,64},{64,0},{1,65},{65,1},{2,66},{66,2},{3,67},{67,3},{4,68},{68... | collective-permute-start | bytes 1966088 | tf_op jit(solution)/shard_map/up_y_lo/ppermute | solution.py:470
  39.3 0.8 shard_map.173
  40.1 11.5 %all-to-all-start.1 = ((bf16[8,64,256]{2,1,0:T(8,128)(2,1)}), bf16[8,64,256]{2,1,0:T(8,128)(2,1)S(1)}, u32[]{:S(2)}, u32[]{:S(2)}) async-start(bf16[8,64,256]{2,1,0:T(8,128)(2,1)} %shard_map.173), calls=%async_computation.1 | async-start | bytes 524288 | tf_op jit(solution)/shard_map/sum_low/all_to_all | solution.py:21
  51.5 0.2 convert_reduce_fusion.base_ref
  51.9 8.9 %all-to-all-done.1.low_ref = bf16[8,64,256]{2,1,0:T(8,128)(2,1)S(1)} async-done(((bf16[8,64,256]{2,1,0:T(8,128)(2,1)}), bf16[8,64,256]{2,1,0:T(8,128)(2,1)S(1)}, u32[]{:S(2)}, u32[]{:S(2)}) %all-to-all-start.1) | async-done | bytes 262176 | tf_op jit(solution)/shard_map/sum_low/all_to_all | solution.py:21
  60.9 1.6 %shard_map.174 = bf16[64,1280]{1,0:T(8,128)(2,1)S(1)} custom-call(bf16[8,64,256]{2,1,0:T(8,128)(2,1)S(1)} %all-to-all-done.1.low_ref, bf16[4,64,1280]{2,1,0:T(8,128)(2,1)S(1)} %bitcast.92, bf16[4,64,1280]{2,1,0:T(8,128)(2,1)} %collective-permute-done.other_ref, f32[64,1280]{1,0:T(8,128)S(1)} %convert_reduce_fusion.base_ref), custom_call_target="tpu_custom_call" | custom-call | flops 83886080 | bytes 2000000 | tf_op jit(solution)/shard_map/pallas_call | solution.py:286
  62.5 10.7 %all_to_all.25 = bf16[8,8,1280]{2,1,0:T(8,128)(2,1)S(1)} all-to-all(bf16[8,8,1280]{2,1,0:T(8,128)(2,1)S(1)} %bitcast.94), channel_id=1, replica_groups=mesh['x'=4,'y_lo'=2,'z'=8,'y_hi'=4,'core'=2] {'z'}, dimensions={0} | all-to-all | bytes 327680 | tf_op jit(solution)/shard_map/sum_z/all_to_all | solution.py:21
  73.4 0.4 select_reduce_fusion
  73.8 0.2 fusion.29
  74.1 0.2 fusion.5
  74.3 0.3 fusion.2
  74.6 0.2 fusion
  74.9 10.3 %all_to_all.26 = bf16[8,8,1024]{2,1,0:T(8,128)(2,1)S(1)} all-to-all(bf16[8,8,1024]{2,1,0:T(8,128)(2,1)S(1)} %broadcast_in_dim.77), channel_id=1, replica_groups=mesh['x'=4,'y_lo'=2,'z'=8,'y_hi'=4,'core'=2] {'z'}, dimensions={0} | all-to-all | bytes 262144 | tf_op jit(solution)/shard_map/gather_z/all_to_all | solution.py:21
  85.2 0.1 broadcast_in_dim.79
  85.3 13.3 %all_to_all.27 = bf16[8,64,1024]{2,1,0:T(8,128)(2,1)S(1)} all-to-all(bf16[8,64,1024]{2,1,0:T(8,128)(2,1)S(1)} %broadcast_in_dim.79), channel_id=1, replica_groups=mesh['x'=4,'y_lo'=2,'z'=8,'y_hi'=4,'core'=2] {'x','y_lo'}, dimensions={0} | all-to-all | bytes 2097152 | tf_op jit(solution)/shard_map/gather_plane/all_to_all | solution.py:21
  98.6 1.9 %shard_map.175 = bf16[512,128]{1,0:T(8,128)(2,1)S(1)} custom-call(s32[1,128]{1,0:T(1,128)S(1)} %bitcast.98, s32[2,16]{1,0:T(2,128)S(1)} %bitcast.96, bf16[512,1024]{1,0:T(8,128)(2,1)S(1)} %bitcast.90, bf16[8,64,1024]{2,1,0:T(8,128)(2,1)S(1)} %bitcast.93, bf16[1024,128]{1,0:T(8,128)(2,1)S(1)} %copy-done.2, bf16[8,64,128]{2,1,0:T(8,128)(2,1)S(1)} %copy-done.3), custom_call_target="tpu_custom_call" | custom-call | flops 671088640 | bytes 3000000 | tf_op jit(solution)/shard_map/pallas_call | solution.py:349
  100.6 10.6 %all-gather.1 = bf16[1024,128]{1,0:T(8,128)(2,1)S(1)} all-gather(bf16[512,128]{1,0:T(8,128)(2,1)S(1)} %shard_map.175), channel_id=3, replica_groups=mesh['x'=4,'y_lo'=2,'z'=8,'y_hi'=4,'core'=2] {'core'}, dimensions={0}, use_global_device_ids=true | all-gather | bytes 393216 | tf_op jit(solution)/shard_map/sum_core/all_gather | solution.py:534
  111.2 6.7 %all_gather.27 = bf16[2,256,128]{2,1,0:T(8,128)(2,1)S(1)} all-gather(bf16[1,256,128]{2,1,0:T(8,128)(2,1)S(1)} %add_convert_fusion.2), channel_id=1, replica_groups={{0,2},{4,6},{1,3},{5,7},{8,10},{12,14},{9,11},{13,15},{16,18},{20,22},{..., dimensions={0}, use_global_device_ids=true | all-gather | bytes 196608 | tf_op jit(solution)/shard_map/sum_y_hi/all_gather | solution.py:540
  118.0 6.0 %all_gather.28 = bf16[2,256,128]{2,1,0:T(8,128)(2,1)S(1)} all-gather(bf16[1,256,128]{2,1,0:T(8,128)(2,1)S(1)} %add_convert_fusion.1), channel_id=1, replica_groups={{2,4},{6,0},{3,5},{7,1},{10,12},{14,8},{11,13},{15,9},{18,20},{22,16},{..., dimensions={0}, use_global_device_ids=true | all-gather | bytes 196608 | tf_op jit(solution)/shard_map/sum_y_hi/all_gather | solution.py:540
  124.0 3.4 %all_gather.29 = bf16[512,128]{1,0:T(8,128)(2,1)S(1)} all-gather(bf16[256,128]{1,0:T(8,128)(2,1)S(1)} %add_convert_fusion), channel_id=1, replica_groups=mesh['x'=4,'y_lo'=2,'z'=8,'y_hi'=4,'core'=2] {'core'}, dimensions={0}, use_global_device_ids=true | all-gather | bytes 196608 | tf_op jit(solution)/shard_map/gather_core/all_gather | solution.py:548
  127.4 0.7 copy.54
  (55 shorter events, 0.8 us)
Async XLA Ops:
  0.0 73.4 %copy-start = (bf16[2,1,1024,128]{3,2,1,0:T(8,128)(2,1)S(1)}, bf16[2,1,1024,128]{3,2,1,0:T(8,128)(2,1)}, u32[]{:S(2)}) copy-start(bf16[2,1,1024,128]{3,2,1,0:T(8,128)(2,1)} %param.29) | copy-start | bytes 1572868
  4.6 6.0 %copy-start.8 = (bf16[1,64,2,128]{3,2,1,0:T(2,128)(2,1)S(1)}, bf16[1,64,2,128]{3,2,1,0:T(2,128)(2,1)}, u32[]{:S(2)}) copy-start(bf16[1,64,2,128]{3,2,1,0:T(2,128)(2,1)} %param.28) | copy-start | bytes 98308
  4.6 6.1 %copy-start.7 = (bf16[1,64,1024]{2,1,0:T(8,128)(2,1)S(1)}, bf16[1,64,1024]{2,1,0:T(8,128)(2,1)}, u32[]{:S(2)}) copy-start(bf16[1,64,1024]{2,1,0:T(8,128)(2,1)} %param.27) | copy-start | bytes 393220
  4.6 34.5 %copy-start.9 = (s32[2]{0:T(128)S(1)}, s32[2]{0:T(128)}, u32[]{:S(2)}) copy-start(s32[2]{0:T(128)} %param.34) | copy-start | bytes 28
  4.6 34.5 %all-to-all-start = ((bf16[8,64,1536]{2,1,0:T(8,128)(2,1)}), bf16[8,64,1536]{2,1,0:T(8,128)(2,1)S(1)}, u32[]{:S(2)}, u32[]{:S(2)}) async-start(bf16[8,64,1536]{2,1,0:T(8,128)(2,1)} %bitcast.99), calls=%async_computation | async-start | bytes 3145728 | tf_op jit(solution)/shard_map/sum_plane/all_to_all | solution.py:21
  36.5 15.5 %collective-permute-start = (bf16[4,64,1280]{2,1,0:T(8,128)(2,1)S(1)}, bf16[4,64,1280]{2,1,0:T(8,128)(2,1)}, u32[]{:S(2)}, u32[]{:S(2)}) collective-permute-start(bf16[4,64,1280]{2,1,0:T(8,128)(2,1)S(1)} %bitcast.91), channel_id=1, source_target_pairs={{0,64},{64,0},{1,65},{65,1},{2,66},{66,2},{3,67},{67,3},{4,68},{68... | collective-permute-start | bytes 1966088 | tf_op jit(solution)/shard_map/up_y_lo/ppermute | solution.py:470
  40.1 20.8 %all-to-all-start.1 = ((bf16[8,64,256]{2,1,0:T(8,128)(2,1)}), bf16[8,64,256]{2,1,0:T(8,128)(2,1)S(1)}, u32[]{:S(2)}, u32[]{:S(2)}) async-start(bf16[8,64,256]{2,1,0:T(8,128)(2,1)} %shard_map.173), calls=%async_computation.1 | async-start | bytes 524288 | tf_op jit(solution)/shard_map/sum_low/all_to_all | solution.py:21
  51.9 21.9 %copy-start.11 = (pred[32,4]{0,1:T(4,128)(4,1)S(1)}, pred[32,4]{0,1:T(4,128)(4,1)}, u32[]{:S(2)}) copy-start(pred[32,4]{0,1:T(4,128)(4,1)} %constant.42) | copy-start | bytes 388
  51.9 22.4 %copy-start.10 = (bf16[2,1,1024,128]{3,2,1,0:T(8,128)(2,1)S(1)}, bf16[2,1,1024,128]{3,2,1,0:T(8,128)(2,1)}, u32[]{:S(2)}) copy-start(bf16[2,1,1024,128]{3,2,1,0:T(8,128)(2,1)} %param.30) | copy-start | bytes 1572868
  85.2 13.4 %copy-start.1 = (bf16[8,1024,64]{1,2,0:T(8,128)(2,1)S(1)}, bf16[8,1024,64]{1,2,0:T(8,128)(2,1)}, u32[]{:S(2)}) copy-start(bf16[8,1024,64]{1,2,0:T(8,128)(2,1)} %param.25) | copy-start | bytes 3145732
  85.2 13.4 %copy-start.2 = (bf16[1024,128]{1,0:T(8,128)(2,1)S(1)}, bf16[1024,128]{1,0:T(8,128)(2,1)}, u32[]{:S(2)}) copy-start(bf16[1024,128]{1,0:T(8,128)(2,1)} %weight_ref.1) | copy-start | bytes 786436
  85.2 13.4 %copy-start.3 = (bf16[8,64,128]{2,1,0:T(8,128)(2,1)S(1)}, bf16[8,64,128]{2,1,0:T(8,128)(2,1)}, u32[]{:S(2)}) copy-start(bf16[8,64,128]{2,1,0:T(8,128)(2,1)} %up_ref.1) | copy-start | bytes 393220
  85.2 13.4 %copy-start.4 = (s32[16,2]{0,1:T(2,128)S(1)}, s32[16,2]{0,1:T(2,128)}, u32[]{:S(2)}) copy-start(s32[16,2]{0,1:T(2,128)} %param.33) | copy-start | bytes 388
  85.2 13.4 %copy-start.5 = (s32[128]{0:T(128)S(1)}, s32[128]{0:T(128)}, u32[]{:S(2)}) copy-start(s32[128]{0:T(128)} %param.31) | copy-start | bytes 1540
  100.6 23.4 %copy-start.6 = (bf16[4,128,128]{2,1,0:T(8,128)(2,1)S(1)}, bf16[4,128,128]{2,1,0:T(8,128)(2,1)}, u32[]{:S(2)}) copy-start(bf16[4,128,128]{2,1,0:T(8,128)(2,1)} %inputs_ref.1) | copy-start | bytes 393220
